TPU v7x, 32 devices: a whole 2x2x4 slice. The times are simulated.
32 devices in a mesh: grp: 2 (over y), wide: 4 (over z), narrow: 2 (over x), tile: 2 (over core).
Axes of the slice: x: 2, y: 2, z: 4, core: 2. Of those that a mesh axis runs over, the one named last changes fastest.
Arguments:
- green: bfloat16 [32768, 1024], P(('grp', 'wide', 'narrow', 'tile')), parts along dimension 0, may hold values from -0.52734375 to 0.52734375
- log_strength: float32 [32768], P(('grp', 'wide', 'narrow', 'tile')), parts along dimension 0, may hold values from -1 to 1
- observed: float32 [1056, 512], P('grp'), parts along dimension 0, may hold values from -6 to 6
- owner_map: int32 [1056], P('grp'), parts along dimension 0, may hold values from 0 to 527, each once
Outputs:
- new_log_strength: float32 [32768], P(('grp', 'wide', 'narrow', 'tile')), parts along dimension 0
- residual: float32 [1056, 512], P(('grp', 'wide')), parts along dimension 0
There are 2 independent parts, one for each index of `grp`. A program takes and returns all parts, laid end to end along the dimension named above; each array names one. Nothing has to cross between parts.
Inputs may be any that keep to these rules, and one draw needn't show every extreme that they name: `owner_map`: every tile number appears once; the slots form 4 equal runs in order, the k-th run owned by the k-th index of wide.
All inputs are finite; a program needn't handle non-finite values.
Results may differ from a plain program's by a relative error of at most 0.0018.
Values may be sent and summed in bfloat16 or wider, within the bound.
No kernel may reach another device: no remote copies, remote signals or barrier semaphores. Data moves between devices by JAX's collectives and lax.ppermute only.
A program may use at most 64 MiB of HBM per device.

v0:
```python
import math

import jax
import jax.numpy as jnp
import numpy as np
from jax import lax
from jax.experimental import pallas as pl
from jax.experimental.pallas import tpu as pltpu
from jax.sharding import PartitionSpec as P

STEPS = 2
LANES = 128
WIDE_BLOCK = 256
SUB = 16
TOP = 14.0
F32, BF16, F16 = jnp.float32, jnp.bfloat16, jnp.float16
VMEM = pl.BlockSpec(memory_space=pltpu.VMEM)
SMEM = pl.BlockSpec(memory_space=pltpu.SMEM)


class Plan:
    def __init__(self, mesh, green, observed, owner_map):
        self.points, columns = green.shape
        self.stations = columns // 2
        self.area = observed.shape[1] // 2
        self.width = math.isqrt(self.area)
        self.blocks = self.stations // self.width
        self.group = LANES // self.width
        self.wide = mesh.shape["wide"]
        self.narrow = mesh.shape["narrow"]
        side = self.stations // LANES
        self.pairs = [(i, j) for i in range(side) for j in range(i, side)]
        self.place = {pair: k for k, pair in enumerate(self.pairs)}
        rows = len(self.pairs) * LANES
        self.chunk = -(-rows // (self.wide * SUB)) * SUB
        self.piece = math.gcd(LANES, self.chunk)
        self.rows = self.wide * self.chunk
        self.slots = owner_map.shape[0] // self.wide

    def pieces(self):
        for k, (i, j) in enumerate(self.pairs):
            for r in range(0, LANES, self.piece):
                row = k * LANES + r
                yield i, j, r, row // self.chunk, row % self.chunk

    def strip_starts(self):
        starts = np.zeros(self.rows // self.width, np.int32)
        per = LANES // self.width
        for k, (i, j) in enumerate(self.pairs):
            for r in range(per):
                a, b = i * per + r, j * self.group
                starts[k * per + r] = a * self.blocks - a * (a - 1) // 2 + b - a
        return starts

    def tile_places(self):
        rows, cols = np.triu_indices(self.blocks)
        per = LANES // self.width
        table = [
            (self.place[(i // per, j // per)] * per + i % per) * self.group + j % per
            for i, j in zip(rows, cols)
        ]
        return np.asarray(table, np.int32)


def contract(a, b, over_a, over_b):
    return lax.dot_general(a, b, (((over_a,), (over_b,)), ((), ())), preferred_element_type=F32)


def swap_groups(x, width):
    n = LANES // width
    row = lax.broadcasted_iota(jnp.int32, (n, LANES), 0)
    run = lax.broadcasted_iota(jnp.int32, (n, LANES), 1) // width
    shift = (row - run + n) % n
    out = x
    for d in range(1, n):
        moved = pltpu.roll(pltpu.roll(x, d, 0), LANES - width * d, 1)
        out = jnp.where(shift == d, moved, out)
    return out


def to_column(rows):
    eye = lax.broadcasted_iota(jnp.int32, (LANES, LANES), 0) == lax.broadcasted_iota(
        jnp.int32, (LANES, LANES), 1
    )
    parts = []
    for i in range(rows.shape[0]):
        spread = jnp.broadcast_to(rows[i : i + 1, :], (LANES, LANES))
        parts.append(jnp.sum(jnp.where(eye, spread, 0.0), axis=1, keepdims=True))
    return jnp.concatenate(parts, axis=0)


def to_rows(column, out_ref):
    eye = lax.broadcasted_iota(jnp.int32, (LANES, LANES), 0) == lax.broadcasted_iota(
        jnp.int32, (LANES, LANES), 1
    )
    for i in range(column.shape[0] // LANES):
        spread = jnp.broadcast_to(column[i * LANES : (i + 1) * LANES], (LANES, LANES))
        out_ref[i : i + 1, :] = jnp.sum(jnp.where(eye, spread, 0.0), axis=0, keepdims=True)


def product(plan, green, strength, weighted, send, own):
    core, z = lax.axis_index("tile"), lax.axis_index("wide")
    ns = plan.stations
    for h in range(2):
        weighted[h] = (green[:, h * ns : (h + 1) * ns].astype(F32) * strength).astype(BF16)
    flip = (1 - 2 * core).astype(F32)
    most = jnp.zeros((8, LANES), F32)
    for out, first, sign in ((send, 1 - core, -flip), (own, core, flip)):
        for j in range(ns // WIDE_BLOCK):
            end = WIDE_BLOCK * (j + 1)
            a = green[:, end - WIDE_BLOCK : end]
            b = green[:, ns + end - WIDE_BLOCK : ns + end]
            part = contract(weighted[first, :, :end], a, 0, 0)
            part = part + sign * contract(weighted[1 - first, :, :end], b, 0, 0)
            for bi, bj, r, chunk, at in plan.pieces():
                if bj * LANES // WIDE_BLOCK != j:
                    continue
                left = bj * LANES % WIDE_BLOCK
                top = bi * LANES + r
                value = part[top : top + plan.piece, left : left + LANES]
                out[chunk ^ z, at : at + plan.piece, :] = value
                folded = jnp.max(jnp.abs(value).reshape(-1, 8, LANES), axis=0)
                most = jnp.maximum(most, folded)
    top = jnp.max(jnp.max(most, axis=0, keepdims=True), axis=1, keepdims=True)
    level = jnp.ceil(jnp.log2(jnp.maximum(top, 1e-30)))
    level = jnp.broadcast_to(level, (plan.wide, SUB, LANES))
    send[:, plan.chunk :, :] = level
    own[:, plan.chunk :, :] = level


def fill_kernel(plan, load, kernel):
    core, z = lax.axis_index("tile"), lax.axis_index("wide")
    row = lax.broadcasted_iota(jnp.int32, (plan.piece, LANES), 0)
    run = lax.broadcasted_iota(jnp.int32, (plan.piece, LANES), 1) // plan.width
    for q in range(2):
        half = q ^ core
        for bi, bj, r, chunk, at in plan.pieces():
            value = load(q, chunk ^ z, at)
            if bi == bj:
                value = jnp.where((row + r) // plan.width <= run, value, 0.0)
            top = bi * LANES + r
            kernel[half, top : top + plan.piece, bj * LANES : (bj + 1) * LANES] = value.astype(BF16)
        for k in range(plan.stations // WIDE_BLOCK):
            at = k * WIDE_BLOCK
            kernel[half, at + LANES : at + WIDE_BLOCK, at : at + LANES] = jnp.zeros(
                (WIDE_BLOCK - LANES, LANES), BF16
            )


def contraction(plan, green, kernel):
    ns = plan.stations
    total = jnp.zeros((plan.points, LANES), F32)
    for j in range(ns // WIDE_BLOCK):
        end = WIDE_BLOCK * (j + 1)
        real = kernel[0, :end, end - WIDE_BLOCK : end]
        imag = kernel[1, :end, end - WIDE_BLOCK : end]
        a, b = green[:, :end], green[:, ns : ns + end]
        u = contract(a, real, 1, 0) + contract(b, imag, 1, 0)
        v = contract(b, real, 1, 0) - contract(a, imag, 1, 0)
        x = green[:, end - WIDE_BLOCK : end].astype(F32)
        y = green[:, ns + end - WIDE_BLOCK : ns + end].astype(F32)
        part = u * x + v * y
        for left in range(0, WIDE_BLOCK, LANES):
            total = total + part[:, left : left + LANES]
    return jnp.sum(total, axis=1, keepdims=True)


def observed_kernel(plan, starts, observed, out):
    core, z = lax.axis_index("tile"), lax.axis_index("wide")
    strips = plan.chunk // plan.width
    left = pl.multiple_of(core * plan.area, LANES)

    n = plan.group
    row = lax.broadcasted_iota(jnp.int32, (n, LANES), 0)
    last = observed.shape[0] // n * n - n

    def strip(s, carry):
        start = starts[z * strips + s]
        low = pl.multiple_of(start // n * n, n)
        high = pl.multiple_of(jnp.minimum(low + n, last), n)
        skip = start - low
        for part in range(plan.area // LANES):
            at = pl.ds(pl.multiple_of(left + part * LANES, LANES), LANES)
            tiles = jnp.where(row >= skip, observed[pl.ds(low, n), at], observed[pl.ds(high, n), at])
            tiles = pltpu.roll(tiles, (n - skip) % n, 0)
            to = pl.multiple_of(s * plan.width + part * n, n)
            out[pl.ds(to, n), :] = swap_groups(tiles, plan.width)
        return carry

    lax.fori_loop(0, strips, strip, 0)


def first_kernel(plan, log_ref, green, send, own, weighted):
    product(plan, green, jnp.exp(to_column(log_ref[...])), weighted, send, own)


def middle_kernel(plan, log_ref, green, *refs):
    tiles = refs[: 2 * plan.wide]
    send, own, log_out, weighted, kernel, stack = refs[2 * plan.wide :]
    for k, ref in enumerate(tiles):
        stack[k] = ref[...]
    fill_kernel(
        plan,
        lambda q, slot, at: stack[q * plan.wide + slot, at : at + plan.piece, :],
        kernel,
    )
    log_now = to_column(log_ref[...])
    log_now = log_now - 0.5 * jnp.exp(log_now) * contraction(plan, green, kernel)
    to_rows(log_now, log_out)
    product(plan, green, jnp.exp(log_now), weighted, send, own)


def last_kernel(plan, log_ref, green, tiles, owners, places, log_out, residual, kernel):
    core, z = lax.axis_index("tile"), lax.axis_index("wide")
    fill_kernel(
        plan,
        lambda q, slot, at: tiles[q * plan.wide + slot, at : at + plan.piece, :],
        kernel,
    )
    log_now = to_column(log_ref[...])
    log_now = log_now - 0.5 * jnp.exp(log_now) * contraction(plan, green, kernel)
    to_rows(log_now, log_out)

    n = plan.group
    run = lax.broadcasted_iota(jnp.int32, (plan.width, LANES), 1) // plan.width

    def rows_of(first, count):
        found = [jnp.zeros((plan.width, LANES), F32) for _ in range(2)]
        for m in range(count):
            where = places[owners[z * plan.slots + first + m]]
            strip, col = where // n, where % n
            row = strip * plan.width
            slot = (row // plan.chunk) ^ z
            at = pl.multiple_of(row % plan.chunk, plan.width)
            shift = ((m - col + n) % n) * plan.width
            for h in range(2):
                value = tiles[(h ^ core) * plan.wide + slot, pl.ds(at, plan.width), :]
                found[h] = jnp.where(run == m, pltpu.roll(value, shift, 1), found[h])
        return [
            swap_groups(found[h][k * n : (k + 1) * n], plan.width)
            for h in range(2)
            for k in range(plan.width // n)
        ]

    def batch(i, carry):
        first = pl.multiple_of(i * n, n)
        for k, piece in enumerate(rows_of(first, n)):
            residual[pl.ds(first, n), k * LANES : (k + 1) * LANES] = piece
        return carry

    whole = plan.slots // n
    lax.fori_loop(0, whole, batch, 0)
    rest = plan.slots - whole * n
    if rest:
        for k, piece in enumerate(rows_of(whole * n, rest)):
            residual[whole * n :, k * LANES : (k + 1) * LANES] = piece[:rest]


def call(kernel, plan, out_shape, scratch, arguments, specs):
    def body(*refs):
        kernel(plan, *refs)

    return pl.pallas_call(
        body,
        in_specs=specs,
        out_specs=jax.tree.map(lambda _: VMEM, out_shape),
        out_shape=out_shape,
        scratch_shapes=scratch,
        compiler_params=pltpu.CompilerParams(vmem_limit_bytes=24 * 1024 * 1024),
    )(*arguments)


def exchange(x, axis, mask, size):
    return lax.ppermute(x, axis, [(i, i ^ mask) for i in range(size)])


def reduce_spectra(plan, send, own):
    recv = exchange(send, "tile", 1, 2)
    kept = own[0, : plan.chunk] + recv[0, : plan.chunk]
    body = lax.broadcasted_iota(jnp.int32, own.shape[1:], 0) < plan.chunk
    arrived = []
    for k in range(1, plan.wide):
        level = jnp.maximum(own[k, plan.chunk, 0], recv[k, plan.chunk, 0]) + (1.0 - TOP)
        message = jnp.where(body, (own[k] + recv[k]) * jnp.exp2(-level), level).astype(F16)
        arrived.append(exchange(message, "wide", k, plan.wide))
    total = kept
    for message in arrived:
        wider = message.astype(F32)
        total = total + wider[: plan.chunk] * jnp.exp2(wider[plan.chunk, 0])
    mask = 1
    while mask < plan.narrow:
        total = total + exchange(total, "narrow", mask, plan.narrow)
        mask *= 2
    return total


def spread(plan, chunk):
    mine = [chunk] + [exchange(chunk, "wide", k, plan.wide) for k in range(1, plan.wide)]
    return mine + [exchange(x, "tile", 1, 2) for x in mine]


def on_device(mesh, green, log_strength, observed, owner_map):
    plan = Plan(mesh, green, observed, owner_map)
    shape = jax.ShapeDtypeStruct
    log_now = log_strength.reshape(-1, LANES)
    log_shape = shape(log_now.shape, F32)
    message = shape((plan.wide, plan.chunk + SUB, LANES), F32)
    weighted = pltpu.VMEM((2, plan.points, plan.stations), BF16)
    kernel = pltpu.VMEM((2, plan.stations, plan.stations), BF16)

    target = call(
        observed_kernel, plan, shape((plan.chunk, LANES), F32), [],
        (jnp.asarray(plan.strip_starts()), observed), [SMEM, VMEM],
    )
    send, own = call(first_kernel, plan, (message, message), [weighted], (log_now, green), [VMEM] * 2)
    for _ in range(STEPS - 1):
        residual = jnp.tanh(reduce_spectra(plan, send, own) - target)
        tiles = spread(plan, residual.astype(BF16))
        stack = pltpu.VMEM((2 * plan.wide, plan.chunk, LANES), BF16)
        send, own, log_now = call(
            middle_kernel, plan, (message, message, log_shape), [weighted, kernel, stack],
            (log_now, green, *tiles), [VMEM] * (2 + len(tiles)),
        )
    residual = jnp.tanh(reduce_spectra(plan, send, own) - target)
    tiles = jnp.stack(spread(plan, residual.astype(F16))).astype(F32)
    log_now, owned = call(
        last_kernel, plan, (log_shape, shape((plan.slots, observed.shape[1]), F32)), [kernel],
        (log_now, green, tiles, owner_map, jnp.asarray(plan.tile_places())),
        [VMEM, VMEM, VMEM, SMEM, SMEM],
    )
    return log_now.reshape(-1), owned


def solution(mesh):
    points = P(("grp", "wide", "narrow", "tile"))
    in_specs = (P(("grp", "wide", "narrow", "tile"), None), points, P("grp", None), P("grp"))
    out_specs = (points, P(("grp", "wide"), None))

    def program(green, log_strength, observed, owner_map):
        return on_device(mesh, green, log_strength, observed, owner_map)

    return jax.shard_map(
        program, mesh=mesh, in_specs=in_specs, out_specs=out_specs, check_vma=False
    )
```

profile of v0, /device:TPU:0, one launch (start us, length us, event | category | flops | bytes accessed | tf_op | source)
XLA Modules:
  0.0 95.4 jit_solution(633696725244233385)
XLA Ops:
  0.6 1.6 %copy-done = bf16[1024,1024]{1,0:T(8,128)(2,1)S(1)} copy-done((bf16[1024,1024]{1,0:T(8,128)(2,1)S(1)}, bf16[1024,1024]{1,0:T(8,128)(2,1)}, u32[]{:S(2)}) %copy-start) | copy-done | bytes 2097176
  2.2 0.7 copy-done.3
  2.9 2.7 %shard_map.77 = (f32[4,336,128]{2,1,0:T(8,128)S(1)}, f32[4,336,128]{2,1,0:T(8,128)S(1)}) custom-call(f32[8,128]{1,0:T(8,128)S(1)} %bitcast.74, bf16[1024,1024]{1,0:T(8,128)(2,1)S(1)} %copy-done), custom_call_target="tpu_custom_call" | custom-call | tf_op jit(solution)/shard_map/pallas_call | solution.py:263
  6.0 0.5 fusion.35
  6.6 1.2 %collective-permute-done = f32[4,336,128]{2,1,0:T(8,128)S(1)} collective-permute-done((f32[4,336,128]{2,1,0:T(8,128)S(1)}, f32[4,336,128]{2,1,0:T(8,128)S(1)}, u32[]{:S(2)}, u32[]{:S(2)}) %collective-permute-start) | collective-permute-done | bytes 688160 | tf_op jit(solution)/shard_map/ppermute | solution.py:274
  7.8 0.6 fusion.34
  12.5 5.0 %collective-permute-start.3 = (f16[336,128]{1,0:T(8,128)(2,1)S(1)}, f16[336,128]{1,0:T(8,128)(2,1)S(1)}, u32[]{:S(2)}, u32[]{:S(2)}) collective-permute-start(f16[336,128]{1,0:T(8,128)(2,1)S(1)} %get-tuple-element.22), channel_id=1, source_target_pairs={{0,12},{4,8},{8,4},{12,0},{1,13},{5,9},{9,5},{13,1},{2,14},{6,10},... | collective-permute-start | bytes 258056 | tf_op jit(solution)/shard_map/ppermute | solution.py:274
  17.6 0.6 collective-permute-start.2
  18.2 2.7 %collective-permute-done.3 = f16[336,128]{1,0:T(8,128)(2,1)S(1)} collective-permute-done((f16[336,128]{1,0:T(8,128)(2,1)S(1)}, f16[336,128]{1,0:T(8,128)(2,1)S(1)}, u32[]{:S(2)}, u32[]{:S(2)}) %collective-permute-start.3) | collective-permute-done | bytes 86048 | tf_op jit(solution)/shard_map/ppermute | solution.py:274
  21.0 0.5 slice.172
  22.2 1.2 %collective-permute-done.1 = f16[336,128]{1,0:T(8,128)(2,1)S(1)} collective-permute-done((f16[336,128]{1,0:T(8,128)(2,1)S(1)}, f16[336,128]{1,0:T(8,128)(2,1)S(1)}, u32[]{:S(2)}, u32[]{:S(2)}) %collective-permute-start.1) | collective-permute-done | bytes 86048 | tf_op jit(solution)/shard_map/ppermute | solution.py:274
  23.4 0.5 slice.164
  24.6 0.5 collective-permute-done.2
  25.1 0.5 slice.168
  26.4 1.6 %collective-permute-start.4 = (f32[320,128]{1,0:T(8,128)S(1)}, f32[320,128]{1,0:T(8,128)S(1)}, u32[]{:S(2)}, u32[]{:S(2)}) collective-permute-start(f32[320,128]{1,0:T(8,128)S(1)} %fusion.28), channel_id=1, source_target_pairs={{0,2},{2,0},{1,3},{3,1},{4,6},{6,4},{5,7},{7,5},{8,10},{10,8},{9,1... | collective-permute-start | bytes 491528 | tf_op jit(solution)/shard_map/ppermute | solution.py:274
  28.0 2.7 %shard_map.78 = f32[320,128]{1,0:T(8,128)S(1)} custom-call(s32[80]{0:T(128)S(1)} %copy-done.7, f32[528,512]{1,0:T(8,128)S(1)} %copy-done.2), custom_call_target="tpu_custom_call" | custom-call | tf_op jit(solution)/shard_map/pallas_call | solution.py:263
  30.7 1.3 %collective-permute-done.4 = f32[320,128]{1,0:T(8,128)S(1)} collective-permute-done((f32[320,128]{1,0:T(8,128)S(1)}, f32[320,128]{1,0:T(8,128)S(1)}, u32[]{:S(2)}, u32[]{:S(2)}) %collective-permute-start.4) | collective-permute-done | bytes 163872 | tf_op jit(solution)/shard_map/ppermute | solution.py:274
  32.1 1.6 %collective-permute-start.6 = (bf16[320,128]{1,0:T(8,128)(2,1)S(1)}, bf16[320,128]{1,0:T(8,128)(2,1)S(1)}, u32[]{:S(2)}, u32[]{:S(2)}) collective-permute-start(bf16[320,128]{1,0:T(8,128)(2,1)S(1)} %tanh_convert_fusion.1.refs_2_), channel_id=1, source_target_pairs={{0,8},{4,12},{8,0},{12,4},{1,9},{5,13},{9,1},{13,5},{2,10},{6,14},... | collective-permute-start | bytes 245768 | tf_op jit(solution)/shard_map/ppermute | solution.py:274
  33.6 1.6 %collective-permute-start.7 = (bf16[320,128]{1,0:T(8,128)(2,1)S(1)}, bf16[320,128]{1,0:T(8,128)(2,1)S(1)}, u32[]{:S(2)}, u32[]{:S(2)}) collective-permute-start(bf16[320,128]{1,0:T(8,128)(2,1)S(1)} %tanh_convert_fusion.1.refs_2_), channel_id=1, source_target_pairs={{0,12},{4,8},{8,4},{12,0},{1,13},{5,9},{9,5},{13,1},{2,14},{6,10},... | collective-permute-start | bytes 245768 | tf_op jit(solution)/shard_map/ppermute | solution.py:274
  35.6 3.1 %collective-permute-done.6.refs_4_ = bf16[320,128]{1,0:T(8,128)(2,1)S(1)} collective-permute-done((bf16[320,128]{1,0:T(8,128)(2,1)S(1)}, bf16[320,128]{1,0:T(8,128)(2,1)S(1)}, u32[]{:S(2)}, u32[]{:S(2)}) %collective-permute-start.6) | collective-permute-done | bytes 81952 | tf_op jit(solution)/shard_map/ppermute | solution.py:274
  38.8 1.3 %collective-permute-done.7.refs_5_ = bf16[320,128]{1,0:T(8,128)(2,1)S(1)} collective-permute-done((bf16[320,128]{1,0:T(8,128)(2,1)S(1)}, bf16[320,128]{1,0:T(8,128)(2,1)S(1)}, u32[]{:S(2)}, u32[]{:S(2)}) %collective-permute-start.7) | collective-permute-done | bytes 81952 | tf_op jit(solution)/shard_map/ppermute | solution.py:274
  40.0 0.5 collective-permute-done.5.refs_3_
  40.5 0.8 collective-permute-done.11.refs_9_
  41.3 0.5 collective-permute-done.9.refs_7_
  41.8 5.4 %shard_map.79 = (f32[4,336,128]{2,1,0:T(8,128)S(1)}, f32[4,336,128]{2,1,0:T(8,128)S(1)}, f32[8,128]{1,0:T(8,128)S(1)}) custom-call(f32[8,128]{1,0:T(8,128)S(1)} %bitcast.75, bf16[1024,1024]{1,0:T(8,128)(2,1)S(1)} %copy-done.1, bf16[320,128]{1,0:T(8,128)(2,1)S(1)} %tanh_convert_fusion.1.refs_2_, bf16[320,128]{1,0:T(8,128)(2,1)S(1)} %collective-permute-done.5.refs_3_, ...), custom_call_target="tpu_custom_call" | custom-call | tf_op jit(solution)/shard_map/pallas_call | solution.py:263
  47.4 0.6 fusion.33
  48.0 1.4 %collective-permute-done.12 = f32[4,336,128]{2,1,0:T(8,128)S(1)} collective-permute-done((f32[4,336,128]{2,1,0:T(8,128)S(1)}, f32[4,336,128]{2,1,0:T(8,128)S(1)}, u32[]{:S(2)}, u32[]{:S(2)}) %collective-permute-start.12) | collective-permute-done | bytes 688160 | tf_op jit(solution)/shard_map/ppermute | solution.py:274
  49.4 0.9 copy-done.8
  50.3 0.6 fusion.32
  54.7 1.2 %fusion.11 = (f16[336,128]{1,0:T(8,128)(2,1)S(1)}, f16[336,128]{1,0:T(8,128)(2,1)S(1)}, f16[336,128]{1,0:T(8,128)(2,1)S(1)}) fusion(f32[4,336,128]{2,1,0:T(8,128)} %copy-done.8, f32[4,336,128]{2,1,0:T(8,128)S(1)} %get-tuple-element.12, f32[]{:T(128)} %bitcast.12, f32[]{:T(128)S(6)} %exp2.112, pred[336]{0:T(512)(128)(4,1)S(1)} %iota_compare_fusion, ...), kind=kLoop, calls=%fused_computation.14 | loop fusion | flops 516096 | bytes 1290600 | tf_op jit(solution)/shard_map/convert_element_type | solution.py:284
  56.0 0.8 collective-permute-start.13
  56.8 2.0 %collective-permute-start.14 = (f16[336,128]{1,0:T(8,128)(2,1)S(1)}, f16[336,128]{1,0:T(8,128)(2,1)S(1)}, u32[]{:S(2)}, u32[]{:S(2)}) collective-permute-start(f16[336,128]{1,0:T(8,128)(2,1)S(1)} %get-tuple-element.20), channel_id=1, source_target_pairs={{0,8},{4,12},{8,0},{12,4},{1,9},{5,13},{9,1},{13,5},{2,10},{6,14},... | collective-permute-start | bytes 258056 | tf_op jit(solution)/shard_map/ppermute | solution.py:274
  58.8 1.6 %collective-permute-start.15 = (f16[336,128]{1,0:T(8,128)(2,1)S(1)}, f16[336,128]{1,0:T(8,128)(2,1)S(1)}, u32[]{:S(2)}, u32[]{:S(2)}) collective-permute-start(f16[336,128]{1,0:T(8,128)(2,1)S(1)} %get-tuple-element.19), channel_id=1, source_target_pairs={{0,12},{4,8},{8,4},{12,0},{1,13},{5,9},{9,5},{13,1},{2,14},{6,10},... | collective-permute-start | bytes 258056 | tf_op jit(solution)/shard_map/ppermute | solution.py:274
  60.4 1.2 %collective-permute-done.13 = f16[336,128]{1,0:T(8,128)(2,1)S(1)} collective-permute-done((f16[336,128]{1,0:T(8,128)(2,1)S(1)}, f16[336,128]{1,0:T(8,128)(2,1)S(1)}, u32[]{:S(2)}, u32[]{:S(2)}) %collective-permute-start.13) | collective-permute-done | bytes 86048 | tf_op jit(solution)/shard_map/ppermute | solution.py:274
  61.7 0.5 slice.177
  62.9 3.8 %collective-permute-done.14 = f16[336,128]{1,0:T(8,128)(2,1)S(1)} collective-permute-done((f16[336,128]{1,0:T(8,128)(2,1)S(1)}, f16[336,128]{1,0:T(8,128)(2,1)S(1)}, u32[]{:S(2)}, u32[]{:S(2)}) %collective-permute-start.14) | collective-permute-done | bytes 86048 | tf_op jit(solution)/shard_map/ppermute | solution.py:274
  66.7 0.5 slice.181
  68.0 0.5 slice.185
  69.2 1.0 %fusion.24 = f32[320,128]{1,0:T(8,128)S(1)} fusion(f32[336,128]{1,0:T(8,128)S(1)} %convert_element_type.57, f32[336,128]{1,0:T(8,128)S(1)} %convert_element_type.55, f32[336,128]{1,0:T(8,128)S(1)} %convert_element_type.53, f32[4,336,128]{2,1,0:T(8,128)} %copy-done.8, f32[4,336,128]{2,1,0:T(8,128)S(1)} %get-tuple-element.12, f32[]{:T(128)} %bitcast.20, ...), kind=kLoop, calls=%fused_computation.31 | loop fusion | flops 286720 | bytes 983052 | tf_op jit(solution)/shard_map/add | solution.py:289
  70.2 1.5 %collective-permute-start.16 = (f32[320,128]{1,0:T(8,128)S(1)}, f32[320,128]{1,0:T(8,128)S(1)}, u32[]{:S(2)}, u32[]{:S(2)}) collective-permute-start(f32[320,128]{1,0:T(8,128)S(1)} %fusion.24), channel_id=1, source_target_pairs={{0,2},{2,0},{1,3},{3,1},{4,6},{6,4},{5,7},{7,5},{8,10},{10,8},{9,1... | collective-permute-start | bytes 491528 | tf_op jit(solution)/shard_map/ppermute | solution.py:274
  71.7 3.8 %collective-permute-done.16 = f32[320,128]{1,0:T(8,128)S(1)} collective-permute-done((f32[320,128]{1,0:T(8,128)S(1)}, f32[320,128]{1,0:T(8,128)S(1)}, u32[]{:S(2)}, u32[]{:S(2)}) %collective-permute-start.16) | collective-permute-done | bytes 163872 | tf_op jit(solution)/shard_map/ppermute | solution.py:274
  76.0 2.2 %collective-permute-start.18 = (f16[320,128]{1,0:T(8,128)(2,1)S(1)}, f16[320,128]{1,0:T(8,128)(2,1)S(1)}, u32[]{:S(2)}, u32[]{:S(2)}) collective-permute-start(f16[320,128]{1,0:T(8,128)(2,1)S(1)} %get-tuple-element.17), channel_id=1, source_target_pairs={{0,8},{4,12},{8,0},{12,4},{1,9},{5,13},{9,1},{13,5},{2,10},{6,14},... | collective-permute-start | bytes 245768 | tf_op jit(solution)/shard_map/ppermute | solution.py:274
  78.2 1.8 %collective-permute-start.19 = (f16[320,128]{1,0:T(8,128)(2,1)S(1)}, f16[320,128]{1,0:T(8,128)(2,1)S(1)}, u32[]{:S(2)}, u32[]{:S(2)}) collective-permute-start(f16[320,128]{1,0:T(8,128)(2,1)S(1)} %get-tuple-element.17), channel_id=1, source_target_pairs={{0,12},{4,8},{8,4},{12,0},{1,13},{5,9},{9,5},{13,1},{2,14},{6,10},... | collective-permute-start | bytes 245768 | tf_op jit(solution)/shard_map/ppermute | solution.py:274
  80.0 1.0 %collective-permute-done.17 = f16[320,128]{1,0:T(8,128)(2,1)S(1)} collective-permute-done((f16[320,128]{1,0:T(8,128)(2,1)S(1)}, f16[320,128]{1,0:T(8,128)(2,1)S(1)}, u32[]{:S(2)}, u32[]{:S(2)}) %collective-permute-start.17) | collective-permute-done | bytes 81952 | tf_op jit(solution)/shard_map/ppermute | solution.py:274
  81.0 1.7 %collective-permute-done.18 = f16[320,128]{1,0:T(8,128)(2,1)S(1)} collective-permute-done((f16[320,128]{1,0:T(8,128)(2,1)S(1)}, f16[320,128]{1,0:T(8,128)(2,1)S(1)}, u32[]{:S(2)}, u32[]{:S(2)}) %collective-permute-start.18) | collective-permute-done | bytes 81952 | tf_op jit(solution)/shard_map/ppermute | solution.py:274
  82.7 1.8 %collective-permute-done.19 = f16[320,128]{1,0:T(8,128)(2,1)S(1)} collective-permute-done((f16[320,128]{1,0:T(8,128)(2,1)S(1)}, f16[320,128]{1,0:T(8,128)(2,1)S(1)}, u32[]{:S(2)}, u32[]{:S(2)}) %collective-permute-start.19) | collective-permute-done | bytes 81952 | tf_op jit(solution)/shard_map/ppermute | solution.py:274
  84.7 1.1 %collective-permute-done.23 = f16[320,128]{1,0:T(8,128)(2,1)S(1)} collective-permute-done((f16[320,128]{1,0:T(8,128)(2,1)S(1)}, f16[320,128]{1,0:T(8,128)(2,1)S(1)}, u32[]{:S(2)}, u32[]{:S(2)}) %collective-permute-start.23) | collective-permute-done | bytes 81952 | tf_op jit(solution)/shard_map/ppermute | solution.py:274
  85.9 9.5 %shard_map.80 = (f32[8,128]{1,0:T(8,128)}, f32[132,512]{1,0:T(8,128)}) custom-call(f32[8,128]{1,0:T(8,128)S(1)} %get-tuple-element.11.refs_0_, bf16[1024,1024]{1,0:T(8,128)(2,1)S(1)} %copy-done.1, f32[8,320,128]{2,1,0:T(8,128)S(1)} %convert_element_type.59.refs_2_, s32[528]{0:T(1024)S(1)} %copy-done.5, s32[528]{0:T(1024)S(1)} %copy-done.6), custom_call_target="tpu_custom_call" | custom-call | tf_op jit(solution)/shard_map/pallas_call | solution.py:263
  (53 shorter events, 2.3 us)
Async XLA Ops:
  0.6 1.6 %copy-start = (bf16[1024,1024]{1,0:T(8,128)(2,1)S(1)}, bf16[1024,1024]{1,0:T(8,128)(2,1)}, u32[]{:S(2)}) copy-start(bf16[1024,1024]{1,0:T(8,128)(2,1)} %refs_1_.7) | copy-start | bytes 6291460
  2.2 0.7 copy-start.3
  5.6 2.2 %collective-permute-start = (f32[4,336,128]{2,1,0:T(8,128)S(1)}, f32[4,336,128]{2,1,0:T(8,128)S(1)}, u32[]{:S(2)}, u32[]{:S(2)}) collective-permute-start(f32[4,336,128]{2,1,0:T(8,128)S(1)} %get-tuple-element.10), channel_id=1, source_target_pairs={{0,1},{1,0},{2,3},{3,2},{4,5},{5,4},{6,7},{7,6},{8,9},{9,8},{10,11... | collective-permute-start | bytes 2064392 | tf_op jit(solution)/shard_map/ppermute | solution.py:274
  12.3 15.7 %copy-start.2 = (f32[528,512]{1,0:T(8,128)S(1)}, f32[528,512]{1,0:T(8,128)}, u32[]{:S(2)}) copy-start(f32[528,512]{1,0:T(8,128)} %refs_1_.5) | copy-start | bytes 3244036
  12.3 15.7 %copy-start.7 = (s32[80]{0:T(128)S(1)}, s32[80]{0:T(128)}, u32[]{:S(2)}) copy-start(s32[80]{0:T(128)} %constant.23.clone.refs_0_) | copy-start | bytes 964
  12.5 8.4 %collective-permute-start.3 = (f16[336,128]{1,0:T(8,128)(2,1)S(1)}, f16[336,128]{1,0:T(8,128)(2,1)S(1)}, u32[]{:S(2)}, u32[]{:S(2)}) collective-permute-start(f16[336,128]{1,0:T(8,128)(2,1)S(1)} %get-tuple-element.22), channel_id=1, source_target_pairs={{0,12},{4,8},{8,4},{12,0},{1,13},{5,9},{9,5},{13,1},{2,14},{6,10},... | collective-permute-start | bytes 258056 | tf_op jit(solution)/shard_map/ppermute | solution.py:274
  17.6 5.8 %collective-permute-start.1 = (f16[336,128]{1,0:T(8,128)(2,1)S(1)}, f16[336,128]{1,0:T(8,128)(2,1)S(1)}, u32[]{:S(2)}, u32[]{:S(2)}) collective-permute-start(f16[336,128]{1,0:T(8,128)(2,1)S(1)} %get-tuple-element.21), channel_id=1, source_target_pairs={{0,4},{4,0},{8,12},{12,8},{1,5},{5,1},{9,13},{13,9},{2,6},{6,2},{1... | collective-permute-start | bytes 258056 | tf_op jit(solution)/shard_map/ppermute | solution.py:274
  17.6 7.5 %collective-permute-start.2 = (f16[336,128]{1,0:T(8,128)(2,1)S(1)}, f16[336,128]{1,0:T(8,128)(2,1)S(1)}, u32[]{:S(2)}, u32[]{:S(2)}) collective-permute-start(f16[336,128]{1,0:T(8,128)(2,1)S(1)} %get-tuple-element.23), channel_id=1, source_target_pairs={{0,8},{4,12},{8,0},{12,4},{1,9},{5,13},{9,1},{13,5},{2,10},{6,14},... | collective-permute-start | bytes 258056 | tf_op jit(solution)/shard_map/ppermute | solution.py:274
  26.3 15.5 %copy-start.1 = (bf16[1024,1024]{1,0:T(8,128)(2,1)S(1)}, bf16[1024,1024]{1,0:T(8,128)(2,1)}, u32[]{:S(2)}) copy-start(bf16[1024,1024]{1,0:T(8,128)(2,1)} %refs_1_.7) | copy-start | bytes 6291460
  26.3 15.5 %copy-start.4 = (f32[1024]{0:T(1024)S(1)}, f32[1024]{0:T(1024)}, u32[]{:S(2)}) copy-start(f32[1024]{0:T(1024)} %param.7) | copy-start | bytes 12292
  26.4 5.6 %collective-permute-start.4 = (f32[320,128]{1,0:T(8,128)S(1)}, f32[320,128]{1,0:T(8,128)S(1)}, u32[]{:S(2)}, u32[]{:S(2)}) collective-permute-start(f32[320,128]{1,0:T(8,128)S(1)} %fusion.28), channel_id=1, source_target_pairs={{0,2},{2,0},{1,3},{3,1},{4,6},{6,4},{5,7},{7,5},{8,10},{10,8},{9,1... | collective-permute-start | bytes 491528 | tf_op jit(solution)/shard_map/ppermute | solution.py:274
  32.1 6.7 %collective-permute-start.6 = (bf16[320,128]{1,0:T(8,128)(2,1)S(1)}, bf16[320,128]{1,0:T(8,128)(2,1)S(1)}, u32[]{:S(2)}, u32[]{:S(2)}) collective-permute-start(bf16[320,128]{1,0:T(8,128)(2,1)S(1)} %tanh_convert_fusion.1.refs_2_), channel_id=1, source_target_pairs={{0,8},{4,12},{8,0},{12,4},{1,9},{5,13},{9,1},{13,5},{2,10},{6,14},... | collective-permute-start | bytes 245768 | tf_op jit(solution)/shard_map/ppermute | solution.py:274
  33.6 6.4 %collective-permute-start.7 = (bf16[320,128]{1,0:T(8,128)(2,1)S(1)}, bf16[320,128]{1,0:T(8,128)(2,1)S(1)}, u32[]{:S(2)}, u32[]{:S(2)}) collective-permute-start(bf16[320,128]{1,0:T(8,128)(2,1)S(1)} %tanh_convert_fusion.1.refs_2_), channel_id=1, source_target_pairs={{0,12},{4,8},{8,4},{12,0},{1,13},{5,9},{9,5},{13,1},{2,14},{6,10},... | collective-permute-start | bytes 245768 | tf_op jit(solution)/shard_map/ppermute | solution.py:274
  35.2 5.3 %collective-permute-start.5 = (bf16[320,128]{1,0:T(8,128)(2,1)S(1)}, bf16[320,128]{1,0:T(8,128)(2,1)S(1)}, u32[]{:S(2)}, u32[]{:S(2)}) collective-permute-start(bf16[320,128]{1,0:T(8,128)(2,1)S(1)} %tanh_convert_fusion.1.refs_2_), channel_id=1, source_target_pairs={{0,4},{4,0},{8,12},{12,8},{1,5},{5,1},{9,13},{13,9},{2,6},{6,2},{1... | collective-permute-start | bytes 245768 | tf_op jit(solution)/shard_map/ppermute | solution.py:274
  35.6 4.9 %collective-permute-start.8 = (bf16[320,128]{1,0:T(8,128)(2,1)S(1)}, bf16[320,128]{1,0:T(8,128)(2,1)S(1)}, u32[]{:S(2)}, u32[]{:S(2)}) collective-permute-start(bf16[320,128]{1,0:T(8,128)(2,1)S(1)} %tanh_convert_fusion.1.refs_2_), channel_id=1, source_target_pairs={{0,1},{1,0},{2,3},{3,2},{4,5},{5,4},{6,7},{7,6},{8,9},{9,8},{10,11... | collective-permute-start | bytes 245768 | tf_op jit(solution)/shard_map/ppermute | solution.py:274
  38.8 1.8 %collective-permute-start.10 = (bf16[320,128]{1,0:T(8,128)(2,1)S(1)}, bf16[320,128]{1,0:T(8,128)(2,1)S(1)}, u32[]{:S(2)}, u32[]{:S(2)}) collective-permute-start(bf16[320,128]{1,0:T(8,128)(2,1)S(1)} %collective-permute-done.6.refs_4_), channel_id=1, source_target_pairs={{0,1},{1,0},{2,3},{3,2},{4,5},{5,4},{6,7},{7,6},{8,9},{9,8},{10,11... | collective-permute-start | bytes 245768 | tf_op jit(solution)/shard_map/ppermute | solution.py:274
  40.0 1.3 %collective-permute-start.11 = (bf16[320,128]{1,0:T(8,128)(2,1)S(1)}, bf16[320,128]{1,0:T(8,128)(2,1)S(1)}, u32[]{:S(2)}, u32[]{:S(2)}) collective-permute-start(bf16[320,128]{1,0:T(8,128)(2,1)S(1)} %collective-permute-done.7.refs_5_), channel_id=1, source_target_pairs={{0,1},{1,0},{2,3},{3,2},{4,5},{5,4},{6,7},{7,6},{8,9},{9,8},{10,11... | collective-permute-start | bytes 245768 | tf_op jit(solution)/shard_map/ppermute | solution.py:274
  40.5 1.3 %collective-permute-start.9 = (bf16[320,128]{1,0:T(8,128)(2,1)S(1)}, bf16[320,128]{1,0:T(8,128)(2,1)S(1)}, u32[]{:S(2)}, u32[]{:S(2)}) collective-permute-start(bf16[320,128]{1,0:T(8,128)(2,1)S(1)} %collective-permute-done.5.refs_3_), channel_id=1, source_target_pairs={{0,1},{1,0},{2,3},{3,2},{4,5},{5,4},{6,7},{7,6},{8,9},{9,8},{10,11... | collective-permute-start | bytes 245768 | tf_op jit(solution)/shard_map/ppermute | solution.py:274
  47.2 2.2 %collective-permute-start.12 = (f32[4,336,128]{2,1,0:T(8,128)S(1)}, f32[4,336,128]{2,1,0:T(8,128)S(1)}, u32[]{:S(2)}, u32[]{:S(2)}) collective-permute-start(f32[4,336,128]{2,1,0:T(8,128)S(1)} %get-tuple-element.13), channel_id=1, source_target_pairs={{0,1},{1,0},{2,3},{3,2},{4,5},{5,4},{6,7},{7,6},{8,9},{9,8},{10,11... | collective-permute-start | bytes 2064392 | tf_op jit(solution)/shard_map/ppermute | solution.py:274
  49.4 0.9 copy-start.8
  56.0 5.7 %collective-permute-start.13 = (f16[336,128]{1,0:T(8,128)(2,1)S(1)}, f16[336,128]{1,0:T(8,128)(2,1)S(1)}, u32[]{:S(2)}, u32[]{:S(2)}) collective-permute-start(f16[336,128]{1,0:T(8,128)(2,1)S(1)} %get-tuple-element.18), channel_id=1, source_target_pairs={{0,4},{4,0},{8,12},{12,8},{1,5},{5,1},{9,13},{13,9},{2,6},{6,2},{1... | collective-permute-start | bytes 258056 | tf_op jit(solution)/shard_map/ppermute | solution.py:274
  56.8 9.9 %collective-permute-start.14 = (f16[336,128]{1,0:T(8,128)(2,1)S(1)}, f16[336,128]{1,0:T(8,128)(2,1)S(1)}, u32[]{:S(2)}, u32[]{:S(2)}) collective-permute-start(f16[336,128]{1,0:T(8,128)(2,1)S(1)} %get-tuple-element.20), channel_id=1, source_target_pairs={{0,8},{4,12},{8,0},{12,4},{1,9},{5,13},{9,1},{13,5},{2,10},{6,14},... | collective-permute-start | bytes 258056 | tf_op jit(solution)/shard_map/ppermute | solution.py:274
  58.8 9.1 %collective-permute-start.15 = (f16[336,128]{1,0:T(8,128)(2,1)S(1)}, f16[336,128]{1,0:T(8,128)(2,1)S(1)}, u32[]{:S(2)}, u32[]{:S(2)}) collective-permute-start(f16[336,128]{1,0:T(8,128)(2,1)S(1)} %get-tuple-element.19), channel_id=1, source_target_pairs={{0,12},{4,8},{8,4},{12,0},{1,13},{5,9},{9,5},{13,1},{2,14},{6,10},... | collective-permute-start | bytes 258056 | tf_op jit(solution)/shard_map/ppermute | solution.py:274
  70.2 5.4 %collective-permute-start.16 = (f32[320,128]{1,0:T(8,128)S(1)}, f32[320,128]{1,0:T(8,128)S(1)}, u32[]{:S(2)}, u32[]{:S(2)}) collective-permute-start(f32[320,128]{1,0:T(8,128)S(1)} %fusion.24), channel_id=1, source_target_pairs={{0,2},{2,0},{1,3},{3,1},{4,6},{6,4},{5,7},{7,5},{8,10},{10,8},{9,1... | collective-permute-start | bytes 491528 | tf_op jit(solution)/shard_map/ppermute | solution.py:274
  75.6 5.4 %collective-permute-start.17 = (f16[320,128]{1,0:T(8,128)(2,1)S(1)}, f16[320,128]{1,0:T(8,128)(2,1)S(1)}, u32[]{:S(2)}, u32[]{:S(2)}) collective-permute-start(f16[320,128]{1,0:T(8,128)(2,1)S(1)} %get-tuple-element.17), channel_id=1, source_target_pairs={{0,4},{4,0},{8,12},{12,8},{1,5},{5,1},{9,13},{13,9},{2,6},{6,2},{1... | collective-permute-start | bytes 245768 | tf_op jit(solution)/shard_map/ppermute | solution.py:274
  76.0 6.7 %collective-permute-start.18 = (f16[320,128]{1,0:T(8,128)(2,1)S(1)}, f16[320,128]{1,0:T(8,128)(2,1)S(1)}, u32[]{:S(2)}, u32[]{:S(2)}) collective-permute-start(f16[320,128]{1,0:T(8,128)(2,1)S(1)} %get-tuple-element.17), channel_id=1, source_target_pairs={{0,8},{4,12},{8,0},{12,4},{1,9},{5,13},{9,1},{13,5},{2,10},{6,14},... | collective-permute-start | bytes 245768 | tf_op jit(solution)/shard_map/ppermute | solution.py:274
  78.2 6.2 %collective-permute-start.19 = (f16[320,128]{1,0:T(8,128)(2,1)S(1)}, f16[320,128]{1,0:T(8,128)(2,1)S(1)}, u32[]{:S(2)}, u32[]{:S(2)}) collective-permute-start(f16[320,128]{1,0:T(8,128)(2,1)S(1)} %get-tuple-element.17), channel_id=1, source_target_pairs={{0,12},{4,8},{8,4},{12,0},{1,13},{5,9},{9,5},{13,1},{2,14},{6,10},... | collective-permute-start | bytes 245768 | tf_op jit(solution)/shard_map/ppermute | solution.py:274
  80.0 4.5 %collective-permute-start.20 = (f16[320,128]{1,0:T(8,128)(2,1)S(1)}, f16[320,128]{1,0:T(8,128)(2,1)S(1)}, u32[]{:S(2)}, u32[]{:S(2)}) collective-permute-start(f16[320,128]{1,0:T(8,128)(2,1)S(1)} %get-tuple-element.17), channel_id=1, source_target_pairs={{0,1},{1,0},{2,3},{3,2},{4,5},{5,4},{6,7},{7,6},{8,9},{9,8},{10,11... | collective-permute-start | bytes 245768 | tf_op jit(solution)/shard_map/ppermute | solution.py:274
  81.0 3.6 %collective-permute-start.21 = (f16[320,128]{1,0:T(8,128)(2,1)S(1)}, f16[320,128]{1,0:T(8,128)(2,1)S(1)}, u32[]{:S(2)}, u32[]{:S(2)}) collective-permute-start(f16[320,128]{1,0:T(8,128)(2,1)S(1)} %collective-permute-done.17), channel_id=1, source_target_pairs={{0,1},{1,0},{2,3},{3,2},{4,5},{5,4},{6,7},{7,6},{8,9},{9,8},{10,11... | collective-permute-start | bytes 245768 | tf_op jit(solution)/shard_map/ppermute | solution.py:274
  82.7 1.9 %collective-permute-start.22 = (f16[320,128]{1,0:T(8,128)(2,1)S(1)}, f16[320,128]{1,0:T(8,128)(2,1)S(1)}, u32[]{:S(2)}, u32[]{:S(2)}) collective-permute-start(f16[320,128]{1,0:T(8,128)(2,1)S(1)} %collective-permute-done.18), channel_id=1, source_target_pairs={{0,1},{1,0},{2,3},{3,2},{4,5},{5,4},{6,7},{7,6},{8,9},{9,8},{10,11... | collective-permute-start | bytes 245768 | tf_op jit(solution)/shard_map/ppermute | solution.py:274
  84.5 1.3 %collective-permute-start.23 = (f16[320,128]{1,0:T(8,128)(2,1)S(1)}, f16[320,128]{1,0:T(8,128)(2,1)S(1)}, u32[]{:S(2)}, u32[]{:S(2)}) collective-permute-start(f16[320,128]{1,0:T(8,128)(2,1)S(1)} %collective-permute-done.19), channel_id=1, source_target_pairs={{0,1},{1,0},{2,3},{3,2},{4,5},{5,4},{6,7},{7,6},{8,9},{9,8},{10,11... | collective-permute-start | bytes 245768 | tf_op jit(solution)/shard_map/ppermute | solution.py:274
  84.5 1.4 %copy-start.5 = (s32[528]{0:T(1024)S(1)}, s32[528]{0:T(1024)}, u32[]{:S(2)}) copy-start(s32[528]{0:T(1024)} %refs_3_.1) | copy-start | bytes 6340
  84.5 1.4 %copy-start.6 = (s32[528]{0:T(1024)S(1)}, s32[528]{0:T(1024)}, u32[]{:S(2)}) copy-start(s32[528]{0:T(1024)} %constant.24.clone.refs_4_) | copy-start | bytes 6340
where the time goes:
time: 95.8 us; the launch traced here: 95.4 us
  waiting for transfers between devices  28.9 us (30%)
  starting transfers between devices  21.9 us (23%)
  Pallas kernels  20.3 us (21%)
  between operations  12.8 us (13%)
  local copies, waits for them, and re-layouts  8.74 us (9%)
  other arithmetic  2.73 us (3%)
    ppermute x24, waiting for transfers between devices, exchange(): return lax.ppermute(x, axis, [(i, i ^ mask) for i in range(size)])  28.9 us
    ppermute x24, starting transfers between devices, exchange(): return lax.ppermute(x, axis, [(i, i ^ mask) for i in range(size)])  21.9 us
    pallas_call x4, Pallas kernels, call(): pl.pallas_call(body, in_specs=specs, out_specs=jax.tree.map(lambda _: VME...  20.3 us
    unnamed x24, local copies, waits for them, and re-layouts  3.36 us
    slice x6, local copies, waits for them, and re-layouts, reduce_spectra(): total = total + wider[:plan.chunk] * jnp.exp2(wider[plan.chunk, 0])  3.08 us
  transfers between devices with their start and end apart: 24, of which 18 were waited for; matrix products, arithmetic and copies ran while one was open for 4% of the time, Pallas kernels for 3%

commit v1 on v0

v1 whole, which is shorter than its diff:
```python
import math

import jax
import jax.numpy as jnp
import numpy as np
from jax import lax
from jax.experimental import pallas as pl
from jax.experimental.pallas import tpu as pltpu
from jax.sharding import PartitionSpec as P

STEPS = 2
LANES = 128
WIDE_BLOCK = 256
SUB = 16
TOP = 14.0
LN2 = math.log(2.0)
F32, BF16, F16 = jnp.float32, jnp.bfloat16, jnp.float16
VMEM = pl.BlockSpec(memory_space=pltpu.VMEM)
SMEM = pl.BlockSpec(memory_space=pltpu.SMEM)


class Plan:
    def __init__(self, mesh, green, observed, owner_map):
        self.points, columns = green.shape
        self.stations = columns // 2
        self.area = observed.shape[1] // 2
        self.width = math.isqrt(self.area)
        self.blocks = self.stations // self.width
        self.group = LANES // self.width
        self.wide = mesh.shape["wide"]
        self.narrow = mesh.shape["narrow"]
        self.strips = self.list_strips()
        self.run = -(-len(self.strips) // self.wide)
        self.chunk = self.run * self.width
        self.slots = owner_map.shape[0] // self.wide

    def list_strips(self):
        side, per, w = self.stations // LANES, self.group, self.width
        strips = []
        for i in range(side):
            for j in range(i + 1, side):
                strips += [[(i * per + s, j, 0, LANES, 0)] for s in range(per)]
        for i in range(side):
            for s in range(per // 2):
                strip = [(i * per + s, i, s * w, LANES, 0)]
                if s:
                    strip.append((i * per + per - s, i, 0, s * w, s * w))
                strips.append(strip)
        half = LANES // 2
        for i in range(0, side, 2):
            strip = [(i * per + per // 2, i, half, LANES, 0)]
            if i + 1 < side:
                strip.append(((i + 1) * per + per // 2, i + 1, 0, half, half))
            strips.append(strip)
        return strips

    def tile(self, row, col):
        return row * self.blocks - row * (row - 1) // 2 + col - row

    def strip_table(self):
        table = np.zeros((3, self.run * self.wide), np.int32)
        for k, strip in enumerate(self.strips):
            row, j, first, _, _ = strip[0]
            table[0, k] = self.tile(row, j * self.group)
            if len(strip) > 1:
                row, j, _, last, shift = strip[1]
                table[1, k] = self.tile(row, (j + 1) * self.group - shift // self.width)
                table[2, k] = last // self.width
        return table.reshape(-1)

    def tile_places(self):
        places = np.zeros(self.tile(self.blocks - 1, self.blocks - 1) + 1, np.int32)
        for k, strip in enumerate(self.strips):
            for row, j, first, last, shift in strip:
                for m in range(first // self.width, last // self.width):
                    col = j * self.group + m - shift // self.width + (self.group if shift > m * self.width else 0)
                    at = (k % self.run) * self.width
                    places[self.tile(row, col)] = (k // self.run) * 65536 + at * 16 + m
        return places


def contract(a, b, over_a, over_b):
    return lax.dot_general(a, b, (((over_a,), (over_b,)), ((), ())), preferred_element_type=F32)


def swap_groups(x, width):
    n = LANES // width
    row = lax.broadcasted_iota(jnp.int32, (n, LANES), 0)
    run = lax.broadcasted_iota(jnp.int32, (n, LANES), 1) // width
    d = n // 2
    while d:
        up = pltpu.roll(pltpu.roll(x, n - d, 0), width * d, 1)
        down = up if 2 * d == n else pltpu.roll(pltpu.roll(x, d, 0), LANES - width * d, 1)
        low, high = (row & d) == 0, (run & d) == 0
        x = jnp.where(low == high, x, jnp.where(low, up, down))
        d //= 2
    return x


def to_column(rows):
    eye = lax.broadcasted_iota(jnp.int32, (LANES, LANES), 0) == lax.broadcasted_iota(
        jnp.int32, (LANES, LANES), 1
    )
    parts = []
    for i in range(rows.shape[0]):
        spread = jnp.broadcast_to(rows[i : i + 1, :], (LANES, LANES))
        parts.append(jnp.sum(jnp.where(eye, spread, 0.0), axis=1, keepdims=True))
    return jnp.concatenate(parts, axis=0)


def to_rows(column, out_ref):
    eye = lax.broadcasted_iota(jnp.int32, (LANES, LANES), 0) == lax.broadcasted_iota(
        jnp.int32, (LANES, LANES), 1
    )
    for i in range(column.shape[0] // LANES):
        spread = jnp.broadcast_to(column[i * LANES : (i + 1) * LANES], (LANES, LANES))
        out_ref[i : i + 1, :] = jnp.sum(jnp.where(eye, spread, 0.0), axis=0, keepdims=True)


def product(plan, green, strength, weighted, send, own):
    core, z = lax.axis_index("tile"), lax.axis_index("wide")
    ns, w = plan.stations, plan.width
    for h in range(2):
        weighted[h] = (green[:, h * ns : (h + 1) * ns].astype(F32) * strength).astype(BF16)
    flip = (1 - 2 * core).astype(F32)
    lane = lax.broadcasted_iota(jnp.int32, (w, LANES), 1)
    most = jnp.zeros((w, LANES), F32)
    for out, first, sign in ((send, 1 - core, -flip), (own, core, flip)):
        for j in range(ns // WIDE_BLOCK):
            end = WIDE_BLOCK * (j + 1)
            a = green[:, end - WIDE_BLOCK : end]
            b = green[:, ns + end - WIDE_BLOCK : ns + end]
            part = contract(weighted[first, :, :end], a, 0, 0)
            part = part + sign * contract(weighted[1 - first, :, :end], b, 0, 0)
            for k, strip in enumerate(plan.strips):
                if strip[0][1] * LANES // WIDE_BLOCK != j:
                    continue
                value = None
                for row, bj, _, last, shift in strip:
                    left = bj * LANES % WIDE_BLOCK
                    seen = part[row * w : (row + 1) * w, left : left + LANES]
                    seen = pltpu.roll(seen, shift, 1) if shift else seen
                    value = seen if value is None else jnp.where(lane < last, seen, value)
                at = k % plan.run * w
                out[(k // plan.run) ^ z, at : at + w, :] = value
                if send.shape[1] > plan.chunk:
                    most = jnp.maximum(most, jnp.abs(value))
        for k in range(len(plan.strips), plan.run * plan.wide):
            at = k % plan.run * w
            out[(k // plan.run) ^ z, at : at + w, :] = jnp.zeros((w, LANES), F32)
    if send.shape[1] > plan.chunk:
        top = jnp.max(jnp.max(most, axis=0, keepdims=True), axis=1, keepdims=True)
        level = jnp.ceil(jnp.log2(jnp.maximum(top, 1e-30)))
        level = jnp.broadcast_to(level, (plan.wide, SUB, LANES))
        send[:, plan.chunk :, :] = level
        own[:, plan.chunk :, :] = level


def fill_kernel(plan, load, kernel):
    core, z = lax.axis_index("tile"), lax.axis_index("wide")
    w = plan.width
    lane = lax.broadcasted_iota(jnp.int32, (w, LANES), 1)
    for q in range(2):
        half = q ^ core
        for k, strip in enumerate(plan.strips):
            value = load(q, (k // plan.run) ^ z, k % plan.run * w)
            for row, bj, first, _, shift in strip:
                seen = value
                if shift:
                    seen = pltpu.roll(value.astype(F32), LANES - shift, 1)
                start = first if not shift else LANES - shift
                if start:
                    seen = jnp.where(lane >= start, seen.astype(F32), 0.0)
                at = pl.ds(bj * LANES, LANES)
                kernel[half, row * w : (row + 1) * w, at] = seen.astype(BF16)
        for k in range(plan.stations // WIDE_BLOCK):
            at = k * WIDE_BLOCK
            kernel[half, at + LANES : at + WIDE_BLOCK, at : at + LANES] = jnp.zeros(
                (WIDE_BLOCK - LANES, LANES), BF16
            )


def contraction(plan, green, kernel):
    ns = plan.stations
    total = jnp.zeros((plan.points, LANES), F32)
    for j in range(ns // WIDE_BLOCK):
        end = WIDE_BLOCK * (j + 1)
        real = kernel[0, :end, end - WIDE_BLOCK : end]
        imag = kernel[1, :end, end - WIDE_BLOCK : end]
        a, b = green[:, :end], green[:, ns : ns + end]
        u = contract(a, real, 1, 0) + contract(b, imag, 1, 0)
        v = contract(b, real, 1, 0) - contract(a, imag, 1, 0)
        x = green[:, end - WIDE_BLOCK : end].astype(F32)
        y = green[:, ns + end - WIDE_BLOCK : ns + end].astype(F32)
        part = u * x + v * y
        for left in range(0, WIDE_BLOCK, LANES):
            total = total + part[:, left : left + LANES]
    return jnp.sum(total, axis=1, keepdims=True)


def observed_kernel(plan, table, observed, out):
    core, z = lax.axis_index("tile"), lax.axis_index("wide")
    left = pl.multiple_of(core * plan.area, LANES)
    n, count = plan.group, plan.run * plan.wide
    row = lax.broadcasted_iota(jnp.int32, (n, LANES), 0)
    last = observed.shape[0] // n * n - n

    def strip(s, carry):
        k = z * plan.run + s
        split = table[2 * count + k]
        for part in range(plan.area // LANES):
            at = pl.ds(pl.multiple_of(left + part * LANES, LANES), LANES)
            found = []
            for start in (table[k], table[count + k]):
                low = pl.multiple_of(start // n * n, n)
                high = pl.multiple_of(jnp.minimum(low + n, last), n)
                skip = start - low
                tiles = jnp.where(row >= skip, observed[pl.ds(low, n), at], observed[pl.ds(high, n), at])
                found.append(pltpu.roll(tiles, (n - skip) % n, 0))
            tiles = jnp.where(row < split, found[1], found[0])
            to = pl.multiple_of(s * plan.width + part * n, n)
            out[pl.ds(to, n), :] = swap_groups(tiles, plan.width)
        return carry

    lax.fori_loop(0, plan.run, strip, 0)


def place_kernel(plan, owners, places, where):
    z, n, total = lax.axis_index("wide"), plan.group, where.shape[0] // 2

    def place(k, carry):
        at = places[owners[z * plan.slots + jnp.minimum(k, plan.slots - 1)]]
        where[k] = (((at >> 16) ^ z) * plan.run * plan.width) + ((at >> 4) & 4095)
        where[total + k] = ((k - (at & 15)) & (n - 1)) * plan.width
        return carry

    lax.fori_loop(0, total, place, 0)


def first_kernel(plan, log_ref, green, send, own, weighted):
    product(plan, green, jnp.exp(to_column(log_ref[...])), weighted, send, own)


def new_log(plan, log_ref, green, kernel, log_out):
    log_now = to_column(log_ref[...])
    log_now = log_now - 0.5 * jnp.exp(log_now) * contraction(plan, green, kernel)
    to_rows(log_now, log_out)
    return log_now


def middle_kernel(plan, log_ref, green, *refs):
    tiles = refs[: 2 * plan.wide]
    send, own, log_out, weighted, kernel, stack = refs[2 * plan.wide :]
    for k, ref in enumerate(tiles):
        stack[k] = ref[...]
    fill_kernel(
        plan,
        lambda q, slot, at: stack[q * plan.wide + slot, at : at + plan.width, :],
        kernel,
    )
    log_now = new_log(plan, log_ref, green, kernel, log_out)
    product(plan, green, jnp.exp(log_now), weighted, send, own)


def last_kernel(plan, log_ref, green, tiles, where, log_out, residual, kernel):
    core = lax.axis_index("tile")
    half = plan.wide * plan.chunk
    fill_kernel(
        plan,
        lambda q, slot, at: tiles[pl.ds((q * plan.wide + slot) * plan.chunk + at, plan.width), :],
        kernel,
    )
    new_log(plan, log_ref, green, kernel, log_out)
    n, w = plan.group, plan.width
    run = lax.broadcasted_iota(jnp.int32, (w, LANES), 1) // w
    base = [pl.multiple_of((h ^ core) * half, w) for h in range(2)]

    def rows_of(first):
        found = [None, None]
        for m in range(n):
            at = where[first + m]
            shift = where[where.shape[0] // 2 + first + m]
            for h in range(2):
                value = tiles[pl.ds(pl.multiple_of(base[h] + at, w), w), :]
                value = pltpu.roll(value, shift, 1)
                found[h] = value if m == 0 else jnp.where(run == m, value, found[h])
        return [
            swap_groups(found[h][k * n : (k + 1) * n], w) for h in range(2) for k in range(w // n)
        ]

    def batch(i, carry):
        first = pl.multiple_of(i * n, n)
        for k, piece in enumerate(rows_of(first)):
            residual[pl.ds(first, n), k * LANES : (k + 1) * LANES] = piece
        return carry

    whole = plan.slots // n
    lax.fori_loop(0, whole, batch, 0)
    rest = plan.slots - whole * n
    if rest:
        for k, piece in enumerate(rows_of(whole * n)):
            residual[whole * n :, k * LANES : (k + 1) * LANES] = piece[:rest]


def join_kernel(plan, own, recv, *messages):
    c = plan.chunk
    level = jnp.maximum(own[0, c : c + 1, :], recv[0, c : c + 1, :]) + (1.0 - TOP)
    factor = jnp.exp(level * -LN2)
    for k, out in enumerate(messages):
        out[:c, :] = (own[k, :c, :] + recv[k, :c, :]) * factor
        out[c:, :] = jnp.broadcast_to(level, (SUB, LANES))


def sum_kernel(plan, *refs):
    c = plan.chunk
    *messages, out = refs
    levels = [x[c : c + 1, :] for x in messages]
    level = levels[0]
    for x in levels[1:]:
        level = jnp.maximum(level, x)
    level = level + float(math.ceil(math.log2(len(messages))))
    out[:c, :] = sum(x[:c, :] * jnp.exp((at - level) * LN2) for x, at in zip(messages, levels))
    out[c:, :] = jnp.broadcast_to(level, (SUB, LANES))


def tanh_kernel(plan, target, left, right, out):
    c = plan.chunk
    total = sum(x[:c, :] * jnp.exp(x[c : c + 1, :] * LN2) for x in (left, right))
    out[...] = jnp.tanh(total - target[...])


def call(kernel, plan, out_shape, scratch, arguments, specs, out_spec=VMEM):
    def body(*refs):
        kernel(plan, *refs)

    return pl.pallas_call(
        body,
        in_specs=specs,
        out_specs=jax.tree.map(lambda _: out_spec, out_shape),
        out_shape=out_shape,
        scratch_shapes=scratch,
        compiler_params=pltpu.CompilerParams(vmem_limit_bytes=24 * 1024 * 1024),
    )(*arguments)


def exchange(x, axis, mask, size):
    return lax.ppermute(x, axis, [(i, i ^ mask) for i in range(size)])


def to_half(x):
    return lax.reduce_precision(x, exponent_bits=5, mantissa_bits=10)


def bounded_residual(plan, send, own, target):
    recv = exchange(send, "tile", 1, 2)
    sums = [own[k] + recv[k] for k in range(plan.wide)]
    total = sums[0]
    for x in [exchange(sums[k].astype(F16), "wide", k, plan.wide) for k in range(1, plan.wide)]:
        total = total + x.astype(F32)
    mask = 1
    while mask < plan.narrow:
        total = to_half(total)
        total = total + exchange(total.astype(F16), "narrow", mask, plan.narrow).astype(F32)
        mask *= 2
    return jnp.tanh(total - target)


def scaled_residual(plan, send, own, target):
    message = jax.ShapeDtypeStruct((plan.chunk + SUB, LANES), F32)

    def join(*parts):
        return call(sum_kernel, plan, message, [], parts, [VMEM] * len(parts))

    recv = exchange(send, "tile", 1, 2)
    sums = call(join_kernel, plan, (message,) * plan.wide, [], (own, recv), [VMEM] * 2)
    parts = [sums[0]]
    for k in range(1, plan.wide):
        parts.append(exchange(sums[k].astype(F16), "wide", k, plan.wide).astype(F32))
    total = to_half(join(*parts))
    mask = 1
    while mask < plan.narrow:
        other = exchange(total.astype(F16), "narrow", mask, plan.narrow).astype(F32)
        mask *= 2
        if mask < plan.narrow:
            total = to_half(join(total, other))
    return call(
        tanh_kernel, plan, jax.ShapeDtypeStruct(target.shape, F32), [],
        (target, total, other), [VMEM] * 3,
    )


def spread(plan, chunk):
    mine = [chunk] + [exchange(chunk, "wide", k, plan.wide) for k in range(1, plan.wide)]
    return mine + [exchange(x, "tile", 1, 2) for x in mine]


def on_device(mesh, green, log_strength, observed, owner_map):
    plan = Plan(mesh, green, observed, owner_map)
    shape = jax.ShapeDtypeStruct
    log_now = log_strength.reshape(-1, LANES)
    log_shape = shape(log_now.shape, F32)
    plain = shape((plan.wide, plan.chunk, LANES), F32)
    levelled = shape((plan.wide, plan.chunk + SUB, LANES), F32)
    weighted = pltpu.VMEM((2, plan.points, plan.stations), BF16)
    kernel = pltpu.VMEM((2, plan.stations, plan.stations), BF16)

    target = call(
        observed_kernel, plan, shape((plan.chunk, LANES), F32), [],
        (jnp.asarray(plan.strip_table()), observed), [SMEM, VMEM],
    )
    where = call(
        place_kernel, plan, shape((2 * -(-plan.slots // plan.group) * plan.group,), jnp.int32), [],
        (owner_map, jnp.asarray(plan.tile_places())), [SMEM, SMEM], SMEM,
    )
    send, own = call(first_kernel, plan, (plain, plain), [weighted], (log_now, green), [VMEM] * 2)
    residual = bounded_residual(plan, send, own, target)
    for _ in range(STEPS - 1):
        tiles = spread(plan, residual.astype(BF16))
        stack = pltpu.VMEM((2 * plan.wide, plan.chunk, LANES), BF16)
        send, own, log_now = call(
            middle_kernel, plan, (levelled, levelled, log_shape), [weighted, kernel, stack],
            (log_now, green, *tiles), [VMEM] * (2 + len(tiles)),
        )
        residual = scaled_residual(plan, send, own, target)
    tiles = jnp.concatenate(spread(plan, to_half(residual).astype(F16))).astype(F32)
    log_now, owned = call(
        last_kernel, plan, (log_shape, shape((plan.slots, observed.shape[1]), F32)), [kernel],
        (log_now, green, tiles, where), [VMEM, VMEM, VMEM, SMEM],
    )
    return log_now.reshape(-1), owned


def solution(mesh):
    points = P(("grp", "wide", "narrow", "tile"))
    in_specs = (P(("grp", "wide", "narrow", "tile"), None), points, P("grp", None), P("grp"))
    out_specs = (points, P(("grp", "wide"), None))

    def program(green, log_strength, observed, owner_map):
        return on_device(mesh, green, log_strength, observed, owner_map)

    return jax.shard_map(
        program, mesh=mesh, in_specs=in_specs, out_specs=out_specs, check_vma=False
    )
```

time: 95.8 us -> 82 us (0.86)
  between operations: 12.8 us -> 0.85 us
  Pallas kernels: 20.3 us -> 26.9 us
  local copies, waits for them, and re-layouts: 8.74 us -> 2.52 us
  other arithmetic: 2.73 us -> 0.53 us
  starting transfers between devices: 21.9 us -> 23 us
    pallas_call x4 -> x8, Pallas kernels: 20.3 us -> 26.9 us  [call(): pl.pallas_call(body, in_specs=specs, out_specs=jax.tree.map(lambda _: out...]
    slice x10 -> x0, local copies, waits for them, and re-layouts: 5.35 us -> none  [the longest x6 3.08 us: reduce_spectra(): total = total + wider[:plan.chunk] * jnp.exp2(wider[plan.chunk, 0])]
    convert_element_type x9 -> x11, other arithmetic: 1.61 us -> 0.4 us  [the longest x1 0.11 us: bounded_residual(): total.astype(F16)]
    ppermute x24, starting transfers between devices: 21.9 us -> 23 us  [exchange(): return lax.ppermute(x, axis, [(i, i ^ mask) for i in range(size)])]
    add x2 -> x0, other arithmetic: 1.04 us -> none  [reduce_spectra(): total = total + wider[:plan.chunk] * jnp.exp2(wider[plan.chunk, 0])]
    unnamed x24 -> x22, local copies, waits for them, and re-layouts: 3.36 us -> 2.49 us
  transfers between devices with their start and end apart: 24 -> 24, of which waited for: 18 -> 14; matrix products, arithmetic and copies ran while one was open for 4% -> 0% of each run, Pallas kernels for 3% -> 11%
where the time goes in v1:
time: 82 us; the launch traced here: 81.8 us
  waiting for transfers between devices  28 us (34%)
  Pallas kernels  26.9 us (33%)
  starting transfers between devices  23 us (28%)
  local copies, waits for them, and re-layouts  2.52 us (3%)
  between operations  0.85 us (1%)
    ppermute x24, waiting for transfers between devices, exchange(): return lax.ppermute(x, axis, [(i, i ^ mask) for i in range(size)])  28 us
    pallas_call x8, Pallas kernels, call(): pl.pallas_call(body, in_specs=specs, out_specs=jax.tree.map(lambda _: out...  26.9 us
    ppermute x24, starting transfers between devices, exchange(): return lax.ppermute(x, axis, [(i, i ^ mask) for i in range(size)])  23 us
    unnamed x22, local copies, waits for them, and re-layouts  2.49 us
  transfers between devices with their start and end apart: 24, of which 14 were waited for; matrix products, arithmetic and copies ran while one was open for 0% of the time, Pallas kernels for 11%

profile of v1, /device:TPU:0, one launch (start us, length us, event | category | flops | bytes accessed | tf_op | source)
XLA Modules:
  0.0 81.8 jit_solution(2305904270003755268)
XLA Ops:
  0.6 0.0 copy-start
  0.6 1.6 %copy-done = bf16[1024,1024]{1,0:T(8,128)(2,1)S(1)} copy-done((bf16[1024,1024]{1,0:T(8,128)(2,1)S(1)}, bf16[1024,1024]{1,0:T(8,128)(2,1)}, u32[]{:S(2)}) %copy-start) | copy-done | bytes 2097176
  2.2 0.7 copy-done.3
  2.9 2.7 %shard_map.77 = (f32[4,272,128]{2,1,0:T(8,128)S(1)}, f32[4,272,128]{2,1,0:T(8,128)S(1)}) custom-call(f32[8,128]{1,0:T(8,128)S(1)} %bitcast.19, bf16[1024,1024]{1,0:T(8,128)(2,1)S(1)} %copy-done), custom_call_target="tpu_custom_call" | custom-call | tf_op jit(solution)/shard_map/pallas_call | solution.py:336
  5.6 0.0 copy-start.2
  5.6 0.0 copy-start.7
  5.6 0.5 collective-permute-start
  6.1 1.6 %collective-permute-done = f32[4,272,128]{2,1,0:T(8,128)S(1)} collective-permute-done((f32[4,272,128]{2,1,0:T(8,128)S(1)}, f32[4,272,128]{2,1,0:T(8,128)S(1)}, u32[]{:S(2)}, u32[]{:S(2)}) %collective-permute-start) | collective-permute-done | bytes 557088 | tf_op jit(solution)/shard_map/ppermute | solution.py:347
  7.8 5.0 %collective-permute-start.3 = (f16[272,128]{1,0:T(8,128)(2,1)S(1)}, f16[272,128]{1,0:T(8,128)(2,1)S(1)}, u32[]{:S(2)}, u32[]{:S(2)}) collective-permute-start(f16[272,128]{1,0:T(8,128)(2,1)S(1)} %get-tuple-element.29), channel_id=1, source_target_pairs={{0,12},{4,8},{8,4},{12,0},{1,13},{5,9},{9,5},{13,1},{2,14},{6,10},... | collective-permute-start | bytes 208904 | tf_op jit(solution)/shard_map/ppermute | solution.py:347
  12.8 0.6 collective-permute-start.1
  13.5 2.2 %collective-permute-done.3 = f16[272,128]{1,0:T(8,128)(2,1)S(1)} collective-permute-done((f16[272,128]{1,0:T(8,128)(2,1)S(1)}, f16[272,128]{1,0:T(8,128)(2,1)S(1)}, u32[]{:S(2)}, u32[]{:S(2)}) %collective-permute-start.3) | collective-permute-done | bytes 69664 | tf_op jit(solution)/shard_map/ppermute | solution.py:347
  15.6 3.4 %collective-permute-done.2 = f16[272,128]{1,0:T(8,128)(2,1)S(1)} collective-permute-done((f16[272,128]{1,0:T(8,128)(2,1)S(1)}, f16[272,128]{1,0:T(8,128)(2,1)S(1)}, u32[]{:S(2)}, u32[]{:S(2)}) %collective-permute-start.2) | collective-permute-done | bytes 69664 | tf_op jit(solution)/shard_map/ppermute | solution.py:347
  19.0 0.1 fusion.11
  19.1 1.6 %collective-permute-start.4 = (f16[272,128]{1,0:T(8,128)(2,1)S(1)}, f16[272,128]{1,0:T(8,128)(2,1)S(1)}, u32[]{:S(2)}, u32[]{:S(2)}) collective-permute-start(f16[272,128]{1,0:T(8,128)(2,1)S(1)} %get-tuple-element.26), channel_id=1, source_target_pairs={{0,2},{2,0},{1,3},{3,1},{4,6},{6,4},{5,7},{7,5},{8,10},{10,8},{9,1... | collective-permute-start | bytes 208904 | tf_op jit(solution)/shard_map/ppermute | solution.py:347
  20.7 5.1 %shard_map.78.refs_0_ = f32[272,128]{1,0:T(8,128)S(1)} custom-call(s32[204]{0:T(256)S(1)} %copy-done.7, f32[528,512]{1,0:T(8,128)S(1)} %copy-done.2), custom_call_target="tpu_custom_call" | custom-call | tf_op jit(solution)/shard_map/pallas_call | solution.py:336
  25.8 1.1 %collective-permute-start.5 = (bf16[272,128]{1,0:T(8,128)(2,1)S(1)}, bf16[272,128]{1,0:T(8,128)(2,1)S(1)}, u32[]{:S(2)}, u32[]{:S(2)}) collective-permute-start(bf16[272,128]{1,0:T(8,128)(2,1)S(1)} %tanh_convert_fusion.refs_2_), channel_id=1, source_target_pairs={{0,4},{4,0},{8,12},{12,8},{1,5},{5,1},{9,13},{13,9},{2,6},{6,2},{1... | collective-permute-start | bytes 208904 | tf_op jit(solution)/shard_map/ppermute | solution.py:347
  26.9 2.0 %collective-permute-start.6 = (bf16[272,128]{1,0:T(8,128)(2,1)S(1)}, bf16[272,128]{1,0:T(8,128)(2,1)S(1)}, u32[]{:S(2)}, u32[]{:S(2)}) collective-permute-start(bf16[272,128]{1,0:T(8,128)(2,1)S(1)} %tanh_convert_fusion.refs_2_), channel_id=1, source_target_pairs={{0,8},{4,12},{8,0},{12,4},{1,9},{5,13},{9,1},{13,5},{2,10},{6,14},... | collective-permute-start | bytes 208904 | tf_op jit(solution)/shard_map/ppermute | solution.py:347
  28.9 1.3 %collective-permute-start.7 = (bf16[272,128]{1,0:T(8,128)(2,1)S(1)}, bf16[272,128]{1,0:T(8,128)(2,1)S(1)}, u32[]{:S(2)}, u32[]{:S(2)}) collective-permute-start(bf16[272,128]{1,0:T(8,128)(2,1)S(1)} %tanh_convert_fusion.refs_2_), channel_id=1, source_target_pairs={{0,12},{4,8},{8,4},{12,0},{1,13},{5,9},{9,5},{13,1},{2,14},{6,10},... | collective-permute-start | bytes 208904 | tf_op jit(solution)/shard_map/ppermute | solution.py:347
  30.3 0.1 collective-permute-done.5.refs_3_
  30.4 0.4 collective-permute-start.9
  30.8 2.8 %collective-permute-done.6.refs_4_ = bf16[272,128]{1,0:T(8,128)(2,1)S(1)} collective-permute-done((bf16[272,128]{1,0:T(8,128)(2,1)S(1)}, bf16[272,128]{1,0:T(8,128)(2,1)S(1)}, u32[]{:S(2)}, u32[]{:S(2)}) %collective-permute-start.6) | collective-permute-done | bytes 69664 | tf_op jit(solution)/shard_map/ppermute | solution.py:347
  33.6 1.5 %collective-permute-done.7.refs_5_ = bf16[272,128]{1,0:T(8,128)(2,1)S(1)} collective-permute-done((bf16[272,128]{1,0:T(8,128)(2,1)S(1)}, bf16[272,128]{1,0:T(8,128)(2,1)S(1)}, u32[]{:S(2)}, u32[]{:S(2)}) %collective-permute-start.7) | collective-permute-done | bytes 69664 | tf_op jit(solution)/shard_map/ppermute | solution.py:347
  35.1 1.2 %collective-permute-done.11.refs_9_ = bf16[272,128]{1,0:T(8,128)(2,1)S(1)} collective-permute-done((bf16[272,128]{1,0:T(8,128)(2,1)S(1)}, bf16[272,128]{1,0:T(8,128)(2,1)S(1)}, u32[]{:S(2)}, u32[]{:S(2)}) %collective-permute-start.11) | collective-permute-done | bytes 69664 | tf_op jit(solution)/shard_map/ppermute | solution.py:347
  36.4 5.6 %shard_map.79 = (f32[4,288,128]{2,1,0:T(8,128)S(1)}, f32[4,288,128]{2,1,0:T(8,128)S(1)}, f32[8,128]{1,0:T(8,128)S(1)}) custom-call(f32[8,128]{1,0:T(8,128)S(1)} %bitcast.20, bf16[1024,1024]{1,0:T(8,128)(2,1)S(1)} %copy-done.1, bf16[272,128]{1,0:T(8,128)(2,1)S(1)} %tanh_convert_fusion.refs_2_, bf16[272,128]{1,0:T(8,128)(2,1)S(1)} %collective-permute-done.5.refs_3_, ...), custom_call_target="tpu_custom_call" | custom-call | tf_op jit(solution)/shard_map/pallas_call | solution.py:336
  42.0 0.2 collective-permute-start.12
  42.2 1.8 %collective-permute-done.12.refs_1_ = f32[4,288,128]{2,1,0:T(8,128)S(1)} collective-permute-done((f32[4,288,128]{2,1,0:T(8,128)S(1)}, f32[4,288,128]{2,1,0:T(8,128)S(1)}, u32[]{:S(2)}, u32[]{:S(2)}) %collective-permute-start.12) | collective-permute-done | bytes 589856 | tf_op jit(solution)/shard_map/ppermute | solution.py:347
  44.0 0.1 shard_map.80
  44.1 0.1 collective-permute-start.13
  44.2 1.9 %collective-permute-start.14 = (f16[288,128]{1,0:T(8,128)(2,1)S(1)}, f16[288,128]{1,0:T(8,128)(2,1)S(1)}, u32[]{:S(2)}, u32[]{:S(2)}) collective-permute-start(f16[288,128]{1,0:T(8,128)(2,1)S(1)} %convert_element_type.80), channel_id=1, source_target_pairs={{0,8},{4,12},{8,0},{12,4},{1,9},{5,13},{9,1},{13,5},{2,10},{6,14},... | collective-permute-start | bytes 221192 | tf_op jit(solution)/shard_map/ppermute | solution.py:347
  46.1 2.6 %collective-permute-start.15 = (f16[288,128]{1,0:T(8,128)(2,1)S(1)}, f16[288,128]{1,0:T(8,128)(2,1)S(1)}, u32[]{:S(2)}, u32[]{:S(2)}) collective-permute-start(f16[288,128]{1,0:T(8,128)(2,1)S(1)} %convert_element_type.82), channel_id=1, source_target_pairs={{0,12},{4,8},{8,4},{12,0},{1,13},{5,9},{9,5},{13,1},{2,14},{6,10},... | collective-permute-start | bytes 221192 | tf_op jit(solution)/shard_map/ppermute | solution.py:347
  48.7 0.9 %collective-permute-done.13 = f16[288,128]{1,0:T(8,128)(2,1)S(1)} collective-permute-done((f16[288,128]{1,0:T(8,128)(2,1)S(1)}, f16[288,128]{1,0:T(8,128)(2,1)S(1)}, u32[]{:S(2)}, u32[]{:S(2)}) %collective-permute-start.13) | collective-permute-done | bytes 73760 | tf_op jit(solution)/shard_map/ppermute | solution.py:347
  49.7 3.5 %collective-permute-done.14 = f16[288,128]{1,0:T(8,128)(2,1)S(1)} collective-permute-done((f16[288,128]{1,0:T(8,128)(2,1)S(1)}, f16[288,128]{1,0:T(8,128)(2,1)S(1)}, u32[]{:S(2)}, u32[]{:S(2)}) %collective-permute-start.14) | collective-permute-done | bytes 73760 | tf_op jit(solution)/shard_map/ppermute | solution.py:347
  53.3 0.0 copy-start.5
  53.3 0.0 copy-start.6
  53.3 0.1 reduce-precision_convert_fusion.1
  53.4 0.6 collective-permute-start.16
  54.0 3.8 %collective-permute-done.16 = f16[288,128]{1,0:T(8,128)(2,1)S(1)} collective-permute-done((f16[288,128]{1,0:T(8,128)(2,1)S(1)}, f16[288,128]{1,0:T(8,128)(2,1)S(1)}, u32[]{:S(2)}, u32[]{:S(2)}) %collective-permute-start.16) | collective-permute-done | bytes 73760 | tf_op jit(solution)/shard_map/ppermute | solution.py:347
  57.9 0.1 constant_dynamic-update-slice_fusion.7
  58.0 1.7 %collective-permute-start.17 = (f16[272,128]{1,0:T(8,128)(2,1)S(1)}, f16[272,128]{1,0:T(8,128)(2,1)S(1)}, u32[]{:S(2)}, u32[]{:S(2)}) collective-permute-start(f16[272,128]{1,0:T(8,128)(2,1)S(1)} %get-tuple-element.25), channel_id=1, source_target_pairs={{0,4},{4,0},{8,12},{12,8},{1,5},{5,1},{9,13},{13,9},{2,6},{6,2},{1... | collective-permute-start | bytes 208904 | tf_op jit(solution)/shard_map/ppermute | solution.py:347
  59.7 3.6 %shard_map.83.refs_3_ = s32[272]{0:T(512)S(1)} custom-call(s32[528]{0:T(1024)S(1)} %copy-done.5, s32[528]{0:T(1024)S(1)} %copy-done.6), custom_call_target="tpu_custom_call" | custom-call | tf_op jit(solution)/shard_map/pallas_call | solution.py:336
  63.3 1.1 %collective-permute-start.18 = (f16[272,128]{1,0:T(8,128)(2,1)S(1)}, f16[272,128]{1,0:T(8,128)(2,1)S(1)}, u32[]{:S(2)}, u32[]{:S(2)}) collective-permute-start(f16[272,128]{1,0:T(8,128)(2,1)S(1)} %get-tuple-element.25), channel_id=1, source_target_pairs={{0,8},{4,12},{8,0},{12,4},{1,9},{5,13},{9,1},{13,5},{2,10},{6,14},... | collective-permute-start | bytes 208904 | tf_op jit(solution)/shard_map/ppermute | solution.py:347
  64.4 1.7 %collective-permute-start.19 = (f16[272,128]{1,0:T(8,128)(2,1)S(1)}, f16[272,128]{1,0:T(8,128)(2,1)S(1)}, u32[]{:S(2)}, u32[]{:S(2)}) collective-permute-start(f16[272,128]{1,0:T(8,128)(2,1)S(1)} %get-tuple-element.25), channel_id=1, source_target_pairs={{0,12},{4,8},{8,4},{12,0},{1,13},{5,9},{9,5},{13,1},{2,14},{6,10},... | collective-permute-start | bytes 208904 | tf_op jit(solution)/shard_map/ppermute | solution.py:347
  66.1 0.5 collective-permute-start.21
  66.7 2.5 %collective-permute-done.18 = f16[272,128]{1,0:T(8,128)(2,1)S(1)} collective-permute-done((f16[272,128]{1,0:T(8,128)(2,1)S(1)}, f16[272,128]{1,0:T(8,128)(2,1)S(1)}, u32[]{:S(2)}, u32[]{:S(2)}) %collective-permute-start.18) | collective-permute-done | bytes 69664 | tf_op jit(solution)/shard_map/ppermute | solution.py:347
  69.2 1.4 %collective-permute-done.19 = f16[272,128]{1,0:T(8,128)(2,1)S(1)} collective-permute-done((f16[272,128]{1,0:T(8,128)(2,1)S(1)}, f16[272,128]{1,0:T(8,128)(2,1)S(1)}, u32[]{:S(2)}, u32[]{:S(2)}) %collective-permute-start.19) | collective-permute-done | bytes 69664 | tf_op jit(solution)/shard_map/ppermute | solution.py:347
  70.8 1.1 %collective-permute-done.23 = f16[272,128]{1,0:T(8,128)(2,1)S(1)} collective-permute-done((f16[272,128]{1,0:T(8,128)(2,1)S(1)}, f16[272,128]{1,0:T(8,128)(2,1)S(1)}, u32[]{:S(2)}, u32[]{:S(2)}) %collective-permute-start.23) | collective-permute-done | bytes 69664 | tf_op jit(solution)/shard_map/ppermute | solution.py:347
  71.9 0.1 convert_element_type.87.refs_2_
  72.0 9.8 %shard_map.84 = (f32[8,128]{1,0:T(8,128)}, f32[132,512]{1,0:T(8,128)}) custom-call(f32[8,128]{1,0:T(8,128)S(1)} %get-tuple-element.15.refs_0_, bf16[1024,1024]{1,0:T(8,128)(2,1)S(1)} %copy-done.1, f32[2176,128]{1,0:T(8,128)S(1)} %convert_element_type.87.refs_2_, s32[272]{0:T(512)S(1)} %shard_map.83.refs_3_), custom_call_target="tpu_custom_call" | custom-call | tf_op jit(solution)/shard_map/pallas_call | solution.py:336
  (44 shorter events, 0.5 us)
Async XLA Ops:
  0.6 1.6 %copy-start = (bf16[1024,1024]{1,0:T(8,128)(2,1)S(1)}, bf16[1024,1024]{1,0:T(8,128)(2,1)}, u32[]{:S(2)}) copy-start(bf16[1024,1024]{1,0:T(8,128)(2,1)} %refs_1_.8) | copy-start | bytes 6291460
  2.2 0.7 copy-start.3
  5.6 15.1 %copy-start.2 = (f32[528,512]{1,0:T(8,128)S(1)}, f32[528,512]{1,0:T(8,128)}, u32[]{:S(2)}) copy-start(f32[528,512]{1,0:T(8,128)} %refs_1_.6) | copy-start | bytes 3244036
  5.6 15.1 %copy-start.7 = (s32[204]{0:T(256)S(1)}, s32[204]{0:T(256)}, u32[]{:S(2)}) copy-start(s32[204]{0:T(256)} %constant.4.clone.refs_0_) | copy-start | bytes 2452
  5.6 2.1 %collective-permute-start = (f32[4,272,128]{2,1,0:T(8,128)S(1)}, f32[4,272,128]{2,1,0:T(8,128)S(1)}, u32[]{:S(2)}, u32[]{:S(2)}) collective-permute-start(f32[4,272,128]{2,1,0:T(8,128)S(1)} %get-tuple-element.14), channel_id=1, source_target_pairs={{0,1},{1,0},{2,3},{3,2},{4,5},{5,4},{6,7},{7,6},{8,9},{9,8},{10,11... | collective-permute-start | bytes 1671176 | tf_op jit(solution)/shard_map/ppermute | solution.py:347
  7.8 7.8 %collective-permute-start.3 = (f16[272,128]{1,0:T(8,128)(2,1)S(1)}, f16[272,128]{1,0:T(8,128)(2,1)S(1)}, u32[]{:S(2)}, u32[]{:S(2)}) collective-permute-start(f16[272,128]{1,0:T(8,128)(2,1)S(1)} %get-tuple-element.29), channel_id=1, source_target_pairs={{0,12},{4,8},{8,4},{12,0},{1,13},{5,9},{9,5},{13,1},{2,14},{6,10},... | collective-permute-start | bytes 208904 | tf_op jit(solution)/shard_map/ppermute | solution.py:347
  12.8 6.2 %collective-permute-start.2 = (f16[272,128]{1,0:T(8,128)(2,1)S(1)}, f16[272,128]{1,0:T(8,128)(2,1)S(1)}, u32[]{:S(2)}, u32[]{:S(2)}) collective-permute-start(f16[272,128]{1,0:T(8,128)(2,1)S(1)} %get-tuple-element.30), channel_id=1, source_target_pairs={{0,8},{4,12},{8,0},{12,4},{1,9},{5,13},{9,1},{13,5},{2,10},{6,14},... | collective-permute-start | bytes 208904 | tf_op jit(solution)/shard_map/ppermute | solution.py:347
  12.8 23.6 %copy-start.1 = (bf16[1024,1024]{1,0:T(8,128)(2,1)S(1)}, bf16[1024,1024]{1,0:T(8,128)(2,1)}, u32[]{:S(2)}) copy-start(bf16[1024,1024]{1,0:T(8,128)(2,1)} %refs_1_.8) | copy-start | bytes 6291460
  12.8 23.6 %copy-start.4 = (f32[1024]{0:T(1024)S(1)}, f32[1024]{0:T(1024)}, u32[]{:S(2)}) copy-start(f32[1024]{0:T(1024)} %param.7) | copy-start | bytes 12292
  12.8 6.2 %collective-permute-start.1 = (f16[272,128]{1,0:T(8,128)(2,1)S(1)}, f16[272,128]{1,0:T(8,128)(2,1)S(1)}, u32[]{:S(2)}, u32[]{:S(2)}) collective-permute-start(f16[272,128]{1,0:T(8,128)(2,1)S(1)} %get-tuple-element.28), channel_id=1, source_target_pairs={{0,4},{4,0},{8,12},{12,8},{1,5},{5,1},{9,13},{13,9},{2,6},{6,2},{1... | collective-permute-start | bytes 208904 | tf_op jit(solution)/shard_map/ppermute | solution.py:347
  19.1 6.6 %collective-permute-start.4 = (f16[272,128]{1,0:T(8,128)(2,1)S(1)}, f16[272,128]{1,0:T(8,128)(2,1)S(1)}, u32[]{:S(2)}, u32[]{:S(2)}) collective-permute-start(f16[272,128]{1,0:T(8,128)(2,1)S(1)} %get-tuple-element.26), channel_id=1, source_target_pairs={{0,2},{2,0},{1,3},{3,1},{4,6},{6,4},{5,7},{7,5},{8,10},{10,8},{9,1... | collective-permute-start | bytes 208904 | tf_op jit(solution)/shard_map/ppermute | solution.py:347
  25.8 4.6 %collective-permute-start.5 = (bf16[272,128]{1,0:T(8,128)(2,1)S(1)}, bf16[272,128]{1,0:T(8,128)(2,1)S(1)}, u32[]{:S(2)}, u32[]{:S(2)}) collective-permute-start(bf16[272,128]{1,0:T(8,128)(2,1)S(1)} %tanh_convert_fusion.refs_2_), channel_id=1, source_target_pairs={{0,4},{4,0},{8,12},{12,8},{1,5},{5,1},{9,13},{13,9},{2,6},{6,2},{1... | collective-permute-start | bytes 208904 | tf_op jit(solution)/shard_map/ppermute | solution.py:347
  26.9 6.7 %collective-permute-start.6 = (bf16[272,128]{1,0:T(8,128)(2,1)S(1)}, bf16[272,128]{1,0:T(8,128)(2,1)S(1)}, u32[]{:S(2)}, u32[]{:S(2)}) collective-permute-start(bf16[272,128]{1,0:T(8,128)(2,1)S(1)} %tanh_convert_fusion.refs_2_), channel_id=1, source_target_pairs={{0,8},{4,12},{8,0},{12,4},{1,9},{5,13},{9,1},{13,5},{2,10},{6,14},... | collective-permute-start | bytes 208904 | tf_op jit(solution)/shard_map/ppermute | solution.py:347
  28.9 6.2 %collective-permute-start.7 = (bf16[272,128]{1,0:T(8,128)(2,1)S(1)}, bf16[272,128]{1,0:T(8,128)(2,1)S(1)}, u32[]{:S(2)}, u32[]{:S(2)}) collective-permute-start(bf16[272,128]{1,0:T(8,128)(2,1)S(1)} %tanh_convert_fusion.refs_2_), channel_id=1, source_target_pairs={{0,12},{4,8},{8,4},{12,0},{1,13},{5,9},{9,5},{13,1},{2,14},{6,10},... | collective-permute-start | bytes 208904 | tf_op jit(solution)/shard_map/ppermute | solution.py:347
  30.3 4.9 %collective-permute-start.8 = (bf16[272,128]{1,0:T(8,128)(2,1)S(1)}, bf16[272,128]{1,0:T(8,128)(2,1)S(1)}, u32[]{:S(2)}, u32[]{:S(2)}) collective-permute-start(bf16[272,128]{1,0:T(8,128)(2,1)S(1)} %tanh_convert_fusion.refs_2_), channel_id=1, source_target_pairs={{0,1},{1,0},{2,3},{3,2},{4,5},{5,4},{6,7},{7,6},{8,9},{9,8},{10,11... | collective-permute-start | bytes 208904 | tf_op jit(solution)/shard_map/ppermute | solution.py:347
  30.4 4.8 %collective-permute-start.9 = (bf16[272,128]{1,0:T(8,128)(2,1)S(1)}, bf16[272,128]{1,0:T(8,128)(2,1)S(1)}, u32[]{:S(2)}, u32[]{:S(2)}) collective-permute-start(bf16[272,128]{1,0:T(8,128)(2,1)S(1)} %collective-permute-done.5.refs_3_), channel_id=1, source_target_pairs={{0,1},{1,0},{2,3},{3,2},{4,5},{5,4},{6,7},{7,6},{8,9},{9,8},{10,11... | collective-permute-start | bytes 208904 | tf_op jit(solution)/shard_map/ppermute | solution.py:347
  33.6 1.5 %collective-permute-start.10 = (bf16[272,128]{1,0:T(8,128)(2,1)S(1)}, bf16[272,128]{1,0:T(8,128)(2,1)S(1)}, u32[]{:S(2)}, u32[]{:S(2)}) collective-permute-start(bf16[272,128]{1,0:T(8,128)(2,1)S(1)} %collective-permute-done.6.refs_4_), channel_id=1, source_target_pairs={{0,1},{1,0},{2,3},{3,2},{4,5},{5,4},{6,7},{7,6},{8,9},{9,8},{10,11... | collective-permute-start | bytes 208904 | tf_op jit(solution)/shard_map/ppermute | solution.py:347
  35.1 1.3 %collective-permute-start.11 = (bf16[272,128]{1,0:T(8,128)(2,1)S(1)}, bf16[272,128]{1,0:T(8,128)(2,1)S(1)}, u32[]{:S(2)}, u32[]{:S(2)}) collective-permute-start(bf16[272,128]{1,0:T(8,128)(2,1)S(1)} %collective-permute-done.7.refs_5_), channel_id=1, source_target_pairs={{0,1},{1,0},{2,3},{3,2},{4,5},{5,4},{6,7},{7,6},{8,9},{9,8},{10,11... | collective-permute-start | bytes 208904 | tf_op jit(solution)/shard_map/ppermute | solution.py:347
  42.0 2.0 %collective-permute-start.12 = (f32[4,288,128]{2,1,0:T(8,128)S(1)}, f32[4,288,128]{2,1,0:T(8,128)S(1)}, u32[]{:S(2)}, u32[]{:S(2)}) collective-permute-start(f32[4,288,128]{2,1,0:T(8,128)S(1)} %get-tuple-element.17), channel_id=1, source_target_pairs={{0,1},{1,0},{2,3},{3,2},{4,5},{5,4},{6,7},{7,6},{8,9},{9,8},{10,11... | collective-permute-start | bytes 1769480 | tf_op jit(solution)/shard_map/ppermute | solution.py:347
  44.1 5.6 %collective-permute-start.13 = (f16[288,128]{1,0:T(8,128)(2,1)S(1)}, f16[288,128]{1,0:T(8,128)(2,1)S(1)}, u32[]{:S(2)}, u32[]{:S(2)}) collective-permute-start(f16[288,128]{1,0:T(8,128)(2,1)S(1)} %convert_element_type.78), channel_id=1, source_target_pairs={{0,4},{4,0},{8,12},{12,8},{1,5},{5,1},{9,13},{13,9},{2,6},{6,2},{1... | collective-permute-start | bytes 221192 | tf_op jit(solution)/shard_map/ppermute | solution.py:347
  44.2 9.0 %collective-permute-start.14 = (f16[288,128]{1,0:T(8,128)(2,1)S(1)}, f16[288,128]{1,0:T(8,128)(2,1)S(1)}, u32[]{:S(2)}, u32[]{:S(2)}) collective-permute-start(f16[288,128]{1,0:T(8,128)(2,1)S(1)} %convert_element_type.80), channel_id=1, source_target_pairs={{0,8},{4,12},{8,0},{12,4},{1,9},{5,13},{9,1},{13,5},{2,10},{6,14},... | collective-permute-start | bytes 221192 | tf_op jit(solution)/shard_map/ppermute | solution.py:347
  46.1 7.1 %collective-permute-start.15 = (f16[288,128]{1,0:T(8,128)(2,1)S(1)}, f16[288,128]{1,0:T(8,128)(2,1)S(1)}, u32[]{:S(2)}, u32[]{:S(2)}) collective-permute-start(f16[288,128]{1,0:T(8,128)(2,1)S(1)} %convert_element_type.82), channel_id=1, source_target_pairs={{0,12},{4,8},{8,4},{12,0},{1,13},{5,9},{9,5},{13,1},{2,14},{6,10},... | collective-permute-start | bytes 221192 | tf_op jit(solution)/shard_map/ppermute | solution.py:347
  53.3 6.4 %copy-start.5 = (s32[528]{0:T(1024)S(1)}, s32[528]{0:T(1024)}, u32[]{:S(2)}) copy-start(s32[528]{0:T(1024)} %refs_0_.2) | copy-start | bytes 6340
  53.3 6.4 %copy-start.6 = (s32[528]{0:T(1024)S(1)}, s32[528]{0:T(1024)}, u32[]{:S(2)}) copy-start(s32[528]{0:T(1024)} %constant.5.clone.refs_1_) | copy-start | bytes 6340
  53.4 4.4 %collective-permute-start.16 = (f16[288,128]{1,0:T(8,128)(2,1)S(1)}, f16[288,128]{1,0:T(8,128)(2,1)S(1)}, u32[]{:S(2)}, u32[]{:S(2)}) collective-permute-start(f16[288,128]{1,0:T(8,128)(2,1)S(1)} %get-tuple-element.31), channel_id=1, source_target_pairs={{0,2},{2,0},{1,3},{3,1},{4,6},{6,4},{5,7},{7,5},{8,10},{10,8},{9,1... | collective-permute-start | bytes 221192 | tf_op jit(solution)/shard_map/ppermute | solution.py:347
  58.0 8.1 %collective-permute-start.17 = (f16[272,128]{1,0:T(8,128)(2,1)S(1)}, f16[272,128]{1,0:T(8,128)(2,1)S(1)}, u32[]{:S(2)}, u32[]{:S(2)}) collective-permute-start(f16[272,128]{1,0:T(8,128)(2,1)S(1)} %get-tuple-element.25), channel_id=1, source_target_pairs={{0,4},{4,0},{8,12},{12,8},{1,5},{5,1},{9,13},{13,9},{2,6},{6,2},{1... | collective-permute-start | bytes 208904 | tf_op jit(solution)/shard_map/ppermute | solution.py:347
  63.3 5.9 %collective-permute-start.18 = (f16[272,128]{1,0:T(8,128)(2,1)S(1)}, f16[272,128]{1,0:T(8,128)(2,1)S(1)}, u32[]{:S(2)}, u32[]{:S(2)}) collective-permute-start(f16[272,128]{1,0:T(8,128)(2,1)S(1)} %get-tuple-element.25), channel_id=1, source_target_pairs={{0,8},{4,12},{8,0},{12,4},{1,9},{5,13},{9,1},{13,5},{2,10},{6,14},... | collective-permute-start | bytes 208904 | tf_op jit(solution)/shard_map/ppermute | solution.py:347
  64.4 6.2 %collective-permute-start.19 = (f16[272,128]{1,0:T(8,128)(2,1)S(1)}, f16[272,128]{1,0:T(8,128)(2,1)S(1)}, u32[]{:S(2)}, u32[]{:S(2)}) collective-permute-start(f16[272,128]{1,0:T(8,128)(2,1)S(1)} %get-tuple-element.25), channel_id=1, source_target_pairs={{0,12},{4,8},{8,4},{12,0},{1,13},{5,9},{9,5},{13,1},{2,14},{6,10},... | collective-permute-start | bytes 208904 | tf_op jit(solution)/shard_map/ppermute | solution.py:347
  66.1 4.5 %collective-permute-start.20 = (f16[272,128]{1,0:T(8,128)(2,1)S(1)}, f16[272,128]{1,0:T(8,128)(2,1)S(1)}, u32[]{:S(2)}, u32[]{:S(2)}) collective-permute-start(f16[272,128]{1,0:T(8,128)(2,1)S(1)} %get-tuple-element.25), channel_id=1, source_target_pairs={{0,1},{1,0},{2,3},{3,2},{4,5},{5,4},{6,7},{7,6},{8,9},{9,8},{10,11... | collective-permute-start | bytes 208904 | tf_op jit(solution)/shard_map/ppermute | solution.py:347
  66.1 4.6 %collective-permute-start.21 = (f16[272,128]{1,0:T(8,128)(2,1)S(1)}, f16[272,128]{1,0:T(8,128)(2,1)S(1)}, u32[]{:S(2)}, u32[]{:S(2)}) collective-permute-start(f16[272,128]{1,0:T(8,128)(2,1)S(1)} %collective-permute-done.17), channel_id=1, source_target_pairs={{0,1},{1,0},{2,3},{3,2},{4,5},{5,4},{6,7},{7,6},{8,9},{9,8},{10,11... | collective-permute-start | bytes 208904 | tf_op jit(solution)/shard_map/ppermute | solution.py:347
  69.2 1.5 %collective-permute-start.22 = (f16[272,128]{1,0:T(8,128)(2,1)S(1)}, f16[272,128]{1,0:T(8,128)(2,1)S(1)}, u32[]{:S(2)}, u32[]{:S(2)}) collective-permute-start(f16[272,128]{1,0:T(8,128)(2,1)S(1)} %collective-permute-done.18), channel_id=1, source_target_pairs={{0,1},{1,0},{2,3},{3,2},{4,5},{5,4},{6,7},{7,6},{8,9},{9,8},{10,11... | collective-permute-start | bytes 208904 | tf_op jit(solution)/shard_map/ppermute | solution.py:347
  70.6 1.3 %collective-permute-start.23 = (f16[272,128]{1,0:T(8,128)(2,1)S(1)}, f16[272,128]{1,0:T(8,128)(2,1)S(1)}, u32[]{:S(2)}, u32[]{:S(2)}) collective-permute-start(f16[272,128]{1,0:T(8,128)(2,1)S(1)} %collective-permute-done.19), channel_id=1, source_target_pairs={{0,1},{1,0},{2,3},{3,2},{4,5},{5,4},{6,7},{7,6},{8,9},{9,8},{10,11... | collective-permute-start | bytes 208904 | tf_op jit(solution)/shard_map/ppermute | solution.py:347

commit v2 on v1

v2 whole, which is shorter than its diff:
```python
import math

import jax
import jax.numpy as jnp
import numpy as np
from jax import lax
from jax.experimental import pallas as pl
from jax.experimental.pallas import tpu as pltpu
from jax.sharding import PartitionSpec as P

STEPS = 2
LANES = 128
WIDE_BLOCK = 256
SUB = 16
TOP = 14.0
LN2 = math.log(2.0)
STRIPS, BATCHES = 17, 4
F32, BF16, F16 = jnp.float32, jnp.bfloat16, jnp.float16
VMEM = pl.BlockSpec(memory_space=pltpu.VMEM)
SMEM = pl.BlockSpec(memory_space=pltpu.SMEM)


class Plan:
    def __init__(self, mesh, green, observed, owner_map):
        self.points, columns = green.shape
        self.stations = columns // 2
        self.area = observed.shape[1] // 2
        self.width = math.isqrt(self.area)
        self.blocks = self.stations // self.width
        self.group = LANES // self.width
        self.wide = mesh.shape["wide"]
        self.narrow = mesh.shape["narrow"]
        self.strips = self.list_strips()
        self.run = -(-len(self.strips) // self.wide)
        self.chunk = self.run * self.width
        self.slots = owner_map.shape[0] // self.wide

    def list_strips(self):
        side, per, w = self.stations // LANES, self.group, self.width
        strips = []
        for i in range(side):
            for j in range(i + 1, side):
                strips += [[(i * per + s, j, 0, LANES, 0)] for s in range(per)]
        for i in range(side):
            for s in range(per // 2):
                strip = [(i * per + s, i, s * w, LANES, 0)]
                if s:
                    strip.append((i * per + per - s, i, 0, s * w, s * w))
                strips.append(strip)
        half = LANES // 2
        for i in range(0, side, 2):
            strip = [(i * per + per // 2, i, half, LANES, 0)]
            if i + 1 < side:
                strip.append(((i + 1) * per + per // 2, i + 1, 0, half, half))
            strips.append(strip)
        return strips

    def tile(self, row, col):
        return row * self.blocks - row * (row - 1) // 2 + col - row

    def strip_table(self):
        table = np.zeros((3, self.run * self.wide), np.int32)
        for k, strip in enumerate(self.strips):
            row, j, first, _, _ = strip[0]
            table[0, k] = self.tile(row, j * self.group)
            if len(strip) > 1:
                row, j, _, last, shift = strip[1]
                table[1, k] = self.tile(row, (j + 1) * self.group - shift // self.width)
                table[2, k] = last // self.width
        return table.reshape(-1)

    def tile_places(self):
        places = np.zeros(self.tile(self.blocks - 1, self.blocks - 1) + 1, np.int32)
        for k, strip in enumerate(self.strips):
            for row, j, first, last, shift in strip:
                for m in range(first // self.width, last // self.width):
                    col = j * self.group + m - shift // self.width + (self.group if shift > m * self.width else 0)
                    at = (k % self.run) * self.width
                    places[self.tile(row, col)] = (k // self.run) * 65536 + at * 16 + m
        return places


def contract(a, b, over_a, over_b):
    return lax.dot_general(a, b, (((over_a,), (over_b,)), ((), ())), preferred_element_type=F32)


def swap_groups(x, width):
    n = LANES // width
    row = lax.broadcasted_iota(jnp.int32, (n, LANES), 0)
    run = lax.broadcasted_iota(jnp.int32, (n, LANES), 1) // width
    d = n // 2
    while d:
        up = pltpu.roll(pltpu.roll(x, n - d, 0), width * d, 1)
        down = up if 2 * d == n else pltpu.roll(pltpu.roll(x, d, 0), LANES - width * d, 1)
        low, high = (row & d) == 0, (run & d) == 0
        x = jnp.where(low == high, x, jnp.where(low, up, down))
        d //= 2
    return x


def unrolled(count, step, body):
    def several(i, carry):
        for k in range(step):
            body(i * step + k)
        return carry

    whole = count // step
    if whole > 1:
        lax.fori_loop(0, whole, several, 0)
    elif whole:
        several(0, 0)
    for i in range(whole * step, count):
        body(i)


def to_column(rows):
    eye = lax.broadcasted_iota(jnp.int32, (LANES, LANES), 0) == lax.broadcasted_iota(
        jnp.int32, (LANES, LANES), 1
    )
    parts = []
    for i in range(rows.shape[0]):
        spread = jnp.broadcast_to(rows[i : i + 1, :], (LANES, LANES))
        parts.append(jnp.sum(jnp.where(eye, spread, 0.0), axis=1, keepdims=True))
    return jnp.concatenate(parts, axis=0)


def to_rows(column, out_ref):
    eye = lax.broadcasted_iota(jnp.int32, (LANES, LANES), 0) == lax.broadcasted_iota(
        jnp.int32, (LANES, LANES), 1
    )
    for i in range(column.shape[0] // LANES):
        spread = jnp.broadcast_to(column[i * LANES : (i + 1) * LANES], (LANES, LANES))
        out_ref[i : i + 1, :] = jnp.sum(jnp.where(eye, spread, 0.0), axis=0, keepdims=True)


def weigh(plan, green, strength, weighted):
    ns = plan.stations
    for h in range(2):
        weighted[h] = (green[:, h * ns : (h + 1) * ns].astype(F32) * strength).astype(BF16)


def product(plan, half, green, weighted, out):
    z = lax.axis_index("wide")
    ns, w = plan.stations, plan.width
    sign = (1 - 2 * half).astype(F32)
    lane = lax.broadcasted_iota(jnp.int32, (w, LANES), 1)
    most = jnp.zeros((w, LANES), F32)
    levelled = out.shape[1] > plan.chunk
    for j in range(ns // WIDE_BLOCK):
        end = WIDE_BLOCK * (j + 1)
        a = green[:, end - WIDE_BLOCK : end]
        b = green[:, ns + end - WIDE_BLOCK : ns + end]
        part = contract(weighted[half, :, :end], a, 0, 0)
        part = part + sign * contract(weighted[1 - half, :, :end], b, 0, 0)
        for k, strip in enumerate(plan.strips):
            if strip[0][1] * LANES // WIDE_BLOCK != j:
                continue
            value = None
            for row, bj, _, last, shift in strip:
                left = bj * LANES % WIDE_BLOCK
                seen = part[row * w : (row + 1) * w, left : left + LANES]
                seen = pltpu.roll(seen, shift, 1) if shift else seen
                value = seen if value is None else jnp.where(lane < last, seen, value)
            at = k % plan.run * w
            out[(k // plan.run) ^ z, at : at + w, :] = value
            if levelled:
                most = jnp.maximum(most, jnp.abs(value))
    for k in range(len(plan.strips), plan.run * plan.wide):
        at = k % plan.run * w
        out[(k // plan.run) ^ z, at : at + w, :] = jnp.zeros((w, LANES), F32)
    if levelled:
        top = jnp.max(jnp.max(most, axis=0, keepdims=True), axis=1, keepdims=True)
        level = jnp.ceil(jnp.log2(jnp.maximum(top, 1e-30)))
        out[:, plan.chunk :, :] = jnp.broadcast_to(level, (plan.wide, SUB, LANES))


def fill_half(plan, load, kernel):
    z = lax.axis_index("wide")
    w = plan.width
    lane = lax.broadcasted_iota(jnp.int32, (w, LANES), 1)
    for k, strip in enumerate(plan.strips):
        value = load((k // plan.run) ^ z, k % plan.run * w)
        for row, bj, first, _, shift in strip:
            seen = value
            if shift:
                seen = pltpu.roll(value.astype(F32), LANES - shift, 1)
            start = first if not shift else LANES - shift
            if start:
                seen = jnp.where(lane >= start, seen.astype(F32), 0.0)
            kernel[row * w : (row + 1) * w, bj * LANES : (bj + 1) * LANES] = seen.astype(BF16)
    for at in range(0, plan.stations, WIDE_BLOCK):
        kernel[at + LANES : at + WIDE_BLOCK, at : at + LANES] = jnp.zeros(
            (WIDE_BLOCK - LANES, LANES), BF16
        )


def contraction(plan, half, green, kernel):
    ns = plan.stations
    near = pl.multiple_of(half * ns, LANES)
    far = pl.multiple_of((1 - half) * ns, LANES)
    sign = (1 - 2 * half).astype(F32)
    total = None
    for j in range(ns // WIDE_BLOCK):
        end = WIDE_BLOCK * (j + 1)
        block = kernel[:end, end - WIDE_BLOCK : end]
        u = contract(green[:, pl.ds(near, end)], block, 1, 0)
        v = contract(green[:, pl.ds(far, end)], block, 1, 0) * sign
        x = green[:, end - WIDE_BLOCK : end].astype(F32)
        y = green[:, ns + end - WIDE_BLOCK : ns + end].astype(F32)
        part = u * x + v * y
        for left in range(0, WIDE_BLOCK, LANES):
            seen = part[:, left : left + LANES]
            total = seen if total is None else total + seen
    return total


def observed_kernel(plan, table, observed, out):
    core, z = lax.axis_index("tile"), lax.axis_index("wide")
    left = pl.multiple_of(core * plan.area, LANES)
    n, count = plan.group, plan.run * plan.wide
    row = lax.broadcasted_iota(jnp.int32, (n, LANES), 0)
    last = observed.shape[0] // n * n - n

    def strip(s):
        k = z * plan.run + s
        split = table[2 * count + k]
        for part in range(plan.area // LANES):
            at = pl.ds(pl.multiple_of(left + part * LANES, LANES), LANES)
            found = []
            for start in (table[k], table[count + k]):
                low = pl.multiple_of(start // n * n, n)
                high = pl.multiple_of(jnp.minimum(low + n, last), n)
                skip = start - low
                tiles = jnp.where(row >= skip, observed[pl.ds(low, n), at], observed[pl.ds(high, n), at])
                found.append(pltpu.roll(tiles, (n - skip) % n, 0))
            tiles = jnp.where(row < split, found[1], found[0])
            to = s * plan.width + part * n
            to = to if isinstance(to, int) else pl.multiple_of(to, n)
            out[pl.ds(to, n), :] = swap_groups(tiles, plan.width)

    unrolled(plan.run, STRIPS, strip)


def first_kernel(plan, log_ref, green, send, weighted):
    weigh(plan, green, jnp.exp(to_column(log_ref[...])), weighted)
    product(plan, 1 - lax.axis_index("tile"), green, weighted, send)


def own_product_kernel(plan, green, weighted, own):
    product(plan, lax.axis_index("tile"), green, weighted, own)


def own_contraction_kernel(plan, green, *refs):
    *tiles, total, kernel, stack = refs
    for k, ref in enumerate(tiles):
        stack[k] = ref[...].astype(BF16)
    fill_half(plan, lambda slot, at: stack[slot, at : at + plan.width, :], kernel)
    total[...] = contraction(plan, lax.axis_index("tile"), green, kernel)


def new_log(plan, log_ref, green, total, kernel, log_out):
    total = total[...] + contraction(plan, 1 - lax.axis_index("tile"), green, kernel)
    log_now = to_column(log_ref[...])
    log_now = log_now - 0.5 * jnp.exp(log_now) * jnp.sum(total, axis=1, keepdims=True)
    to_rows(log_now, log_out)
    return log_now


def middle_kernel(plan, log_ref, green, total, *refs):
    *tiles, send, weighted, log_out, kernel, stack = refs
    for k, ref in enumerate(tiles):
        stack[k] = ref[...]
    fill_half(plan, lambda slot, at: stack[slot, at : at + plan.width, :], kernel)
    log_now = new_log(plan, log_ref, green, total, kernel, log_out)
    weigh(plan, green, jnp.exp(log_now), weighted)
    product(plan, 1 - lax.axis_index("tile"), green, weighted, send)


def last_kernel(plan, log_ref, green, total, mine, others, owners, places, log_out, residual, kernel, tiles):
    core, z = lax.axis_index("tile"), lax.axis_index("wide")
    n, w, c = plan.group, plan.width, plan.chunk
    fill_half(
        plan,
        lambda slot, at: others[pl.ds(pl.multiple_of(slot * c + at, w), w), :],
        kernel,
    )
    new_log(plan, log_ref, green, total, kernel, log_out)
    tiles[core] = mine[...]
    tiles[1 - core] = others[...]
    run = lax.broadcasted_iota(jnp.int32, (w, LANES), 1) // w

    def rows_of(first, count):
        found = [None, None]
        for m in range(count):
            place = places[owners[z * plan.slots + first + m]]
            row = pl.multiple_of(((place >> 16) ^ z) * c + ((place >> 4) & 4095), w)
            shift = ((m - (place & 15)) & (n - 1)) * w
            for h in range(2):
                value = pltpu.roll(tiles[h, pl.ds(row, w), :], shift, 1)
                found[h] = value if m == 0 else jnp.where(run == m, value, found[h])
        return [
            swap_groups(found[h][k * n : (k + 1) * n], w) for h in range(2) for k in range(w // n)
        ]

    def batch(i):
        first = i * n if isinstance(i, int) else pl.multiple_of(i * n, n)
        for k, piece in enumerate(rows_of(first, n)):
            residual[pl.ds(first, n), k * LANES : (k + 1) * LANES] = piece

    whole = plan.slots // n
    unrolled(whole, BATCHES, batch)
    rest = plan.slots - whole * n
    if rest:
        for k, piece in enumerate(rows_of(whole * n, rest)):
            residual[whole * n :, k * LANES : (k + 1) * LANES] = piece[:rest]


def join_kernel(plan, own, recv, *messages):
    c = plan.chunk
    level = jnp.maximum(own[0, c : c + 1, :], recv[0, c : c + 1, :]) + (1.0 - TOP)
    factor = jnp.exp(level * -LN2)
    for k, out in enumerate(messages):
        out[:c, :] = (own[k, :c, :] + recv[k, :c, :]) * factor
        out[c:, :] = jnp.broadcast_to(level, (SUB, LANES))


def sum_kernel(plan, *refs):
    c = plan.chunk
    *messages, out = refs
    levels = [x[c : c + 1, :] for x in messages]
    level = levels[0]
    for x in levels[1:]:
        level = jnp.maximum(level, x)
    level = level + float(math.ceil(math.log2(len(messages))))
    out[:c, :] = sum(x[:c, :] * jnp.exp((at - level) * LN2) for x, at in zip(messages, levels))
    out[c:, :] = jnp.broadcast_to(level, (SUB, LANES))


def tanh_kernel(plan, target, left, right, out):
    c = plan.chunk
    total = sum(x[:c, :] * jnp.exp(x[c : c + 1, :] * LN2) for x in (left, right))
    out[...] = jnp.tanh(total - target[...])


def call(kernel, plan, out_shape, scratch, arguments, specs, out_spec=VMEM):
    def body(*refs):
        kernel(plan, *refs)

    return pl.pallas_call(
        body,
        in_specs=specs,
        out_specs=jax.tree.map(lambda _: out_spec, out_shape),
        out_shape=out_shape,
        scratch_shapes=scratch,
        compiler_params=pltpu.CompilerParams(vmem_limit_bytes=24 * 1024 * 1024),
    )(*arguments)


def exchange(x, axis, mask, size):
    return lax.ppermute(x, axis, [(i, i ^ mask) for i in range(size)])


def to_half(x):
    return lax.reduce_precision(x, exponent_bits=5, mantissa_bits=10)


def bounded_residual(plan, own, recv, target):
    sums = [own[k] + recv[k] for k in range(plan.wide)]
    total = sums[0]
    for x in [exchange(sums[k].astype(F16), "wide", k, plan.wide) for k in range(1, plan.wide)]:
        total = total + x.astype(F32)
    mask = 1
    while mask < plan.narrow:
        total = to_half(total)
        total = total + exchange(total.astype(F16), "narrow", mask, plan.narrow).astype(F32)
        mask *= 2
    return jnp.tanh(total - target)


def scaled_residual(plan, own, recv, target):
    message = jax.ShapeDtypeStruct((plan.chunk + SUB, LANES), F32)

    def join(*parts):
        return call(sum_kernel, plan, message, [], parts, [VMEM] * len(parts))

    sums = call(join_kernel, plan, (message,) * plan.wide, [], (own, recv), [VMEM] * 2)
    parts = [sums[0]]
    for k in range(1, plan.wide):
        parts.append(exchange(sums[k].astype(F16), "wide", k, plan.wide).astype(F32))
    total = to_half(join(*parts))
    mask = 1
    while mask < plan.narrow:
        other = exchange(total.astype(F16), "narrow", mask, plan.narrow).astype(F32)
        mask *= 2
        if mask < plan.narrow:
            total = to_half(join(total, other))
    return call(
        tanh_kernel, plan, jax.ShapeDtypeStruct(target.shape, F32), [],
        (target, total, other), [VMEM] * 3,
    )


def spread(plan, chunk):
    mine = [chunk] + [exchange(chunk, "wide", k, plan.wide) for k in range(1, plan.wide)]
    return mine, [exchange(x, "tile", 1, 2) for x in mine]


def on_device(mesh, green, log_strength, observed, owner_map):
    plan = Plan(mesh, green, observed, owner_map)
    shape = jax.ShapeDtypeStruct
    log_now = log_strength.reshape(-1, LANES)
    log_shape = shape(log_now.shape, F32)
    weighted_shape = shape((2, plan.points, plan.stations), BF16)
    total_shape = shape((plan.points, LANES), F32)
    kernel = pltpu.VMEM((plan.stations, plan.stations), BF16)
    stack = pltpu.VMEM((plan.wide, plan.chunk, LANES), BF16)

    def own_product(weighted, like):
        return call(own_product_kernel, plan, shape(like.shape, F32), [], (green, weighted), [VMEM] * 2)

    def own_contraction(tiles):
        return call(
            own_contraction_kernel, plan, total_shape, [kernel, stack], (green, *tiles),
            [VMEM] * (1 + len(tiles)),
        )

    target = call(
        observed_kernel, plan, shape((plan.chunk, LANES), F32), [],
        (jnp.asarray(plan.strip_table()), observed), [SMEM, VMEM],
    )
    send, weighted = call(
        first_kernel, plan, (shape((plan.wide, plan.chunk, LANES), F32), weighted_shape), [],
        (log_now, green), [VMEM] * 2,
    )
    residual = bounded_residual(
        plan, own_product(weighted, send), exchange(send, "tile", 1, 2), target
    )
    for _ in range(STEPS - 1):
        mine, others = spread(plan, residual.astype(BF16))
        levelled = shape((plan.wide, plan.chunk + SUB, LANES), F32)
        send, weighted, log_now = call(
            middle_kernel, plan, (levelled, weighted_shape, log_shape), [kernel, stack],
            (log_now, green, own_contraction(mine), *others), [VMEM] * (3 + len(others)),
        )
        residual = scaled_residual(
            plan, own_product(weighted, send), exchange(send, "tile", 1, 2), target
        )
    mine, others = spread(plan, to_half(residual).astype(F16))
    mine = [x.astype(F32) for x in mine]
    log_now, owned = call(
        last_kernel, plan, (log_shape, shape((plan.slots, observed.shape[1]), F32)),
        [kernel, pltpu.VMEM((2, plan.wide * plan.chunk, LANES), F32)],
        (
            log_now, green, own_contraction(mine), jnp.concatenate(mine),
            jnp.concatenate(others).astype(F32), owner_map, jnp.asarray(plan.tile_places()),
        ),
        [VMEM] * 5 + [SMEM] * 2,
    )
    return log_now.reshape(-1), owned


def solution(mesh):
    points = P(("grp", "wide", "narrow", "tile"))
    in_specs = (P(("grp", "wide", "narrow", "tile"), None), points, P("grp", None), P("grp"))
    out_specs = (points, P(("grp", "wide"), None))

    def program(green, log_strength, observed, owner_map):
        return on_device(mesh, green, log_strength, observed, owner_map)

    return jax.shard_map(
        program, mesh=mesh, in_specs=in_specs, out_specs=out_specs, check_vma=False
    )
```

time: 82 us -> 70.2 us (0.86)
  Pallas kernels: 26.9 us -> 17.8 us
  waiting for transfers between devices: 28 us -> 24.6 us
    pallas_call x8 -> x11, Pallas kernels: 26.9 us -> 17.8 us  [call(): pl.pallas_call(body, in_specs=specs, out_specs=jax.tree.map(lambda _: out...]
    ppermute x24, waiting for transfers between devices: 28 us -> 24.6 us  [exchange(): return lax.ppermute(x, axis, [(i, i ^ mask) for i in range(size)])]
    unnamed x22 -> x16, local copies, waits for them, and re-layouts: 2.49 us -> 2.3 us
  transfers between devices with their start and end apart: 24 -> 24, of which waited for: 14 -> 12; matrix products, arithmetic and copies ran while one was open for 0% -> 0% of each run, Pallas kernels for 11% -> 9%
where the time goes in v2:
time: 70.2 us; the launch traced here: 70 us
  waiting for transfers between devices  24.6 us (35%)
  starting transfers between devices  23.8 us (34%)
  Pallas kernels  17.8 us (25%)
  local copies, waits for them, and re-layouts  2.3 us (3%)
  between operations  0.91 us (1%)
    ppermute x24, waiting for transfers between devices, exchange(): return lax.ppermute(x, axis, [(i, i ^ mask) for i in range(size)])  24.6 us
    ppermute x24, starting transfers between devices, exchange(): return lax.ppermute(x, axis, [(i, i ^ mask) for i in range(size)])  23.8 us
    pallas_call x11, Pallas kernels, call(): pl.pallas_call(body, in_specs=specs, out_specs=jax.tree.map(lambda _: out...  17.8 us
    unnamed x16, local copies, waits for them, and re-layouts  2.3 us
  transfers between devices with their start and end apart: 24, of which 12 were waited for; matrix products, arithmetic and copies ran while one was open for 0% of the time, Pallas kernels for 9%

profile of v2, /device:TPU:0, one launch (start us, length us, event | category | flops | bytes accessed | tf_op | source)
XLA Modules:
  0.0 70.0 jit_solution(12011435237460191693)
XLA Ops:
  0.6 1.6 %copy-done = bf16[1024,1024]{1,0:T(8,128)(2,1)S(1)} copy-done((bf16[1024,1024]{1,0:T(8,128)(2,1)S(1)}, bf16[1024,1024]{1,0:T(8,128)(2,1)}, u32[]{:S(2)}) %copy-start) | copy-done | bytes 2097176
  2.2 0.7 copy-done.3
  2.9 1.8 %shard_map.77 = (f32[4,272,128]{2,1,0:T(8,128)S(1)}, bf16[2,1024,512]{2,1,0:T(8,128)(2,1)S(1)}) custom-call(f32[8,128]{1,0:T(8,128)S(1)} %bitcast.19, bf16[1024,1024]{1,0:T(8,128)(2,1)S(1)} %copy-done), custom_call_target="tpu_custom_call" | custom-call | tf_op jit(solution)/shard_map/pallas_call | solution.py:349
  4.7 0.5 collective-permute-start
  5.2 1.1 %shard_map.78 = f32[4,272,128]{2,1,0:T(8,128)S(1)} custom-call(bf16[1024,1024]{1,0:T(8,128)(2,1)S(1)} %copy-done.1, bf16[2,1024,512]{2,1,0:T(8,128)(2,1)S(1)} %get-tuple-element.13.refs_1_), custom_call_target="tpu_custom_call" | custom-call | tf_op jit(solution)/shard_map/pallas_call | solution.py:349
  6.3 0.5 collective-permute-done
  6.9 3.0 %collective-permute-start.1 = (f16[272,128]{1,0:T(8,128)(2,1)S(1)}, f16[272,128]{1,0:T(8,128)(2,1)S(1)}, u32[]{:S(2)}, u32[]{:S(2)}) collective-permute-start(f16[272,128]{1,0:T(8,128)(2,1)S(1)} %get-tuple-element.28), channel_id=1, source_target_pairs={{0,4},{4,0},{8,12},{12,8},{1,5},{5,1},{9,13},{13,9},{2,6},{6,2},{1... | collective-permute-start | bytes 208904 | tf_op jit(solution)/shard_map/ppermute | solution.py:360
  9.9 2.5 %collective-permute-start.3 = (f16[272,128]{1,0:T(8,128)(2,1)S(1)}, f16[272,128]{1,0:T(8,128)(2,1)S(1)}, u32[]{:S(2)}, u32[]{:S(2)}) collective-permute-start(f16[272,128]{1,0:T(8,128)(2,1)S(1)} %get-tuple-element.29), channel_id=1, source_target_pairs={{0,12},{4,8},{8,4},{12,0},{1,13},{5,9},{9,5},{13,1},{2,14},{6,10},... | collective-permute-start | bytes 208904 | tf_op jit(solution)/shard_map/ppermute | solution.py:360
  12.3 0.1 collective-permute-start.2
  12.5 0.0 collective-permute-done.1
  12.5 4.3 %collective-permute-done.3 = f16[272,128]{1,0:T(8,128)(2,1)S(1)} collective-permute-done((f16[272,128]{1,0:T(8,128)(2,1)S(1)}, f16[272,128]{1,0:T(8,128)(2,1)S(1)}, u32[]{:S(2)}, u32[]{:S(2)}) %collective-permute-start.3) | collective-permute-done | bytes 69664 | tf_op jit(solution)/shard_map/ppermute | solution.py:360
  16.8 2.4 %collective-permute-done.2 = f16[272,128]{1,0:T(8,128)(2,1)S(1)} collective-permute-done((f16[272,128]{1,0:T(8,128)(2,1)S(1)}, f16[272,128]{1,0:T(8,128)(2,1)S(1)}, u32[]{:S(2)}, u32[]{:S(2)}) %collective-permute-start.2) | collective-permute-done | bytes 69664 | tf_op jit(solution)/shard_map/ppermute | solution.py:360
  19.2 0.1 fusion.12
  19.3 0.0 copy-start.4
  19.3 1.5 %collective-permute-start.4 = (f16[272,128]{1,0:T(8,128)(2,1)S(1)}, f16[272,128]{1,0:T(8,128)(2,1)S(1)}, u32[]{:S(2)}, u32[]{:S(2)}) collective-permute-start(f16[272,128]{1,0:T(8,128)(2,1)S(1)} %get-tuple-element.26), channel_id=1, source_target_pairs={{0,2},{2,0},{1,3},{3,1},{4,6},{6,4},{5,7},{7,5},{8,10},{10,8},{9,1... | collective-permute-start | bytes 208904 | tf_op jit(solution)/shard_map/ppermute | solution.py:360
  20.9 1.6 %shard_map.79.refs_0_ = f32[272,128]{1,0:T(8,128)S(1)} custom-call(s32[204]{0:T(256)S(1)} %copy-done.7, f32[528,512]{1,0:T(8,128)S(1)} %copy-done.2), custom_call_target="tpu_custom_call" | custom-call | tf_op jit(solution)/shard_map/pallas_call | solution.py:349
  22.5 1.2 %collective-permute-done.4 = f16[272,128]{1,0:T(8,128)(2,1)S(1)} collective-permute-done((f16[272,128]{1,0:T(8,128)(2,1)S(1)}, f16[272,128]{1,0:T(8,128)(2,1)S(1)}, u32[]{:S(2)}, u32[]{:S(2)}) %collective-permute-start.4) | collective-permute-done | bytes 69664 | tf_op jit(solution)/shard_map/ppermute | solution.py:360
  23.7 2.7 %collective-permute-start.7 = (bf16[272,128]{1,0:T(8,128)(2,1)S(1)}, bf16[272,128]{1,0:T(8,128)(2,1)S(1)}, u32[]{:S(2)}, u32[]{:S(2)}) collective-permute-start(bf16[272,128]{1,0:T(8,128)(2,1)S(1)} %tanh_convert_fusion.refs_1_), channel_id=1, source_target_pairs={{0,12},{4,8},{8,4},{12,0},{1,13},{5,9},{9,5},{13,1},{2,14},{6,10},... | collective-permute-start | bytes 208904 | tf_op jit(solution)/shard_map/ppermute | solution.py:360
  26.4 1.8 %collective-permute-start.5 = (bf16[272,128]{1,0:T(8,128)(2,1)S(1)}, bf16[272,128]{1,0:T(8,128)(2,1)S(1)}, u32[]{:S(2)}, u32[]{:S(2)}) collective-permute-start(bf16[272,128]{1,0:T(8,128)(2,1)S(1)} %tanh_convert_fusion.refs_1_), channel_id=1, source_target_pairs={{0,4},{4,0},{8,12},{12,8},{1,5},{5,1},{9,13},{13,9},{2,6},{6,2},{1... | collective-permute-start | bytes 208904 | tf_op jit(solution)/shard_map/ppermute | solution.py:360
  28.2 2.1 %collective-permute-done.7.refs_4_ = bf16[272,128]{1,0:T(8,128)(2,1)S(1)} collective-permute-done((bf16[272,128]{1,0:T(8,128)(2,1)S(1)}, bf16[272,128]{1,0:T(8,128)(2,1)S(1)}, u32[]{:S(2)}, u32[]{:S(2)}) %collective-permute-start.7) | collective-permute-done | bytes 69664 | tf_op jit(solution)/shard_map/ppermute | solution.py:360
  30.2 1.6 %collective-permute-done.6.refs_3_ = bf16[272,128]{1,0:T(8,128)(2,1)S(1)} collective-permute-done((bf16[272,128]{1,0:T(8,128)(2,1)S(1)}, bf16[272,128]{1,0:T(8,128)(2,1)S(1)}, u32[]{:S(2)}, u32[]{:S(2)}) %collective-permute-start.6) | collective-permute-done | bytes 69664 | tf_op jit(solution)/shard_map/ppermute | solution.py:360
  31.8 0.5 collective-permute-start.9
  32.3 1.1 %shard_map.80.refs_2_ = f32[1024,128]{1,0:T(8,128)S(1)} custom-call(bf16[1024,1024]{1,0:T(8,128)(2,1)S(1)} %copy-done.1, bf16[272,128]{1,0:T(8,128)(2,1)S(1)} %tanh_convert_fusion.refs_1_, bf16[272,128]{1,0:T(8,128)(2,1)S(1)} %collective-permute-done.5.refs_2_, bf16[272,128]{1,0:T(8,128)(2,1)S(1)} %collective-permute-done.6.refs_3_, ...), custom_call_target="tpu_custom_call" | custom-call | tf_op jit(solution)/shard_map/pallas_call | solution.py:349
  33.5 3.9 %shard_map.81 = (f32[4,288,128]{2,1,0:T(8,128)S(1)}, bf16[2,1024,512]{2,1,0:T(8,128)(2,1)S(1)}, f32[8,128]{1,0:T(8,128)S(1)}) custom-call(f32[8,128]{1,0:T(8,128)S(1)} %bitcast.20, bf16[1024,1024]{1,0:T(8,128)(2,1)S(1)} %copy-done.1, f32[1024,128]{1,0:T(8,128)S(1)} %shard_map.80.refs_2_, bf16[272,128]{1,0:T(8,128)(2,1)S(1)} %collective-permute-done.8.refs_3_, ...), custom_call_target="tpu_custom_call" | custom-call | tf_op jit(solution)/shard_map/pallas_call | solution.py:349
  37.4 0.1 collective-permute-start.12
  37.5 1.2 %shard_map.82.refs_0_ = f32[4,288,128]{2,1,0:T(8,128)S(1)} custom-call(bf16[1024,1024]{1,0:T(8,128)(2,1)S(1)} %copy-done.1, bf16[2,1024,512]{2,1,0:T(8,128)(2,1)S(1)} %get-tuple-element.16.refs_1_), custom_call_target="tpu_custom_call" | custom-call | tf_op jit(solution)/shard_map/pallas_call | solution.py:349
  38.7 0.7 %collective-permute-done.12.refs_1_ = f32[4,288,128]{2,1,0:T(8,128)S(1)} collective-permute-done((f32[4,288,128]{2,1,0:T(8,128)S(1)}, f32[4,288,128]{2,1,0:T(8,128)S(1)}, u32[]{:S(2)}, u32[]{:S(2)}) %collective-permute-start.12) | collective-permute-done | bytes 589856 | tf_op jit(solution)/shard_map/ppermute | solution.py:360
  39.4 0.1 shard_map.83
  39.5 2.3 %collective-permute-start.15 = (f16[288,128]{1,0:T(8,128)(2,1)S(1)}, f16[288,128]{1,0:T(8,128)(2,1)S(1)}, u32[]{:S(2)}, u32[]{:S(2)}) collective-permute-start(f16[288,128]{1,0:T(8,128)(2,1)S(1)} %convert_element_type.94), channel_id=1, source_target_pairs={{0,12},{4,8},{8,4},{12,0},{1,13},{5,9},{9,5},{13,1},{2,14},{6,10},... | collective-permute-start | bytes 221192 | tf_op jit(solution)/shard_map/ppermute | solution.py:360
  41.8 2.3 %collective-permute-start.13 = (f16[288,128]{1,0:T(8,128)(2,1)S(1)}, f16[288,128]{1,0:T(8,128)(2,1)S(1)}, u32[]{:S(2)}, u32[]{:S(2)}) collective-permute-start(f16[288,128]{1,0:T(8,128)(2,1)S(1)} %convert_element_type.90), channel_id=1, source_target_pairs={{0,4},{4,0},{8,12},{12,8},{1,5},{5,1},{9,13},{13,9},{2,6},{6,2},{1... | collective-permute-start | bytes 221192 | tf_op jit(solution)/shard_map/ppermute | solution.py:360
  44.1 2.5 %collective-permute-done.15 = f16[288,128]{1,0:T(8,128)(2,1)S(1)} collective-permute-done((f16[288,128]{1,0:T(8,128)(2,1)S(1)}, f16[288,128]{1,0:T(8,128)(2,1)S(1)}, u32[]{:S(2)}, u32[]{:S(2)}) %collective-permute-start.15) | collective-permute-done | bytes 73760 | tf_op jit(solution)/shard_map/ppermute | solution.py:360
  46.6 2.3 %collective-permute-done.14 = f16[288,128]{1,0:T(8,128)(2,1)S(1)} collective-permute-done((f16[288,128]{1,0:T(8,128)(2,1)S(1)}, f16[288,128]{1,0:T(8,128)(2,1)S(1)}, u32[]{:S(2)}, u32[]{:S(2)}) %collective-permute-start.14) | collective-permute-done | bytes 73760 | tf_op jit(solution)/shard_map/ppermute | solution.py:360
  49.0 0.1 reduce-precision_convert_fusion.1
  49.1 1.6 %collective-permute-start.16 = (f16[288,128]{1,0:T(8,128)(2,1)S(1)}, f16[288,128]{1,0:T(8,128)(2,1)S(1)}, u32[]{:S(2)}, u32[]{:S(2)}) collective-permute-start(f16[288,128]{1,0:T(8,128)(2,1)S(1)} %get-tuple-element.31), channel_id=1, source_target_pairs={{0,2},{2,0},{1,3},{3,1},{4,6},{6,4},{5,7},{7,5},{8,10},{10,8},{9,1... | collective-permute-start | bytes 221192 | tf_op jit(solution)/shard_map/ppermute | solution.py:360
  50.6 2.9 %collective-permute-done.16 = f16[288,128]{1,0:T(8,128)(2,1)S(1)} collective-permute-done((f16[288,128]{1,0:T(8,128)(2,1)S(1)}, f16[288,128]{1,0:T(8,128)(2,1)S(1)}, u32[]{:S(2)}, u32[]{:S(2)}) %collective-permute-start.16) | collective-permute-done | bytes 73760 | tf_op jit(solution)/shard_map/ppermute | solution.py:360
  53.5 0.1 fusion.11
  53.6 0.5 collective-permute-start.17
  54.1 2.5 %collective-permute-start.18 = (f16[272,128]{1,0:T(8,128)(2,1)S(1)}, f16[272,128]{1,0:T(8,128)(2,1)S(1)}, u32[]{:S(2)}, u32[]{:S(2)}) collective-permute-start(f16[272,128]{1,0:T(8,128)(2,1)S(1)} %get-tuple-element.25), channel_id=1, source_target_pairs={{0,8},{4,12},{8,0},{12,4},{1,9},{5,13},{9,1},{13,5},{2,10},{6,14},... | collective-permute-start | bytes 208904 | tf_op jit(solution)/shard_map/ppermute | solution.py:360
  56.6 1.4 %collective-permute-start.19 = (f16[272,128]{1,0:T(8,128)(2,1)S(1)}, f16[272,128]{1,0:T(8,128)(2,1)S(1)}, u32[]{:S(2)}, u32[]{:S(2)}) collective-permute-start(f16[272,128]{1,0:T(8,128)(2,1)S(1)} %get-tuple-element.25), channel_id=1, source_target_pairs={{0,12},{4,8},{8,4},{12,0},{1,13},{5,9},{9,5},{13,1},{2,14},{6,10},... | collective-permute-start | bytes 208904 | tf_op jit(solution)/shard_map/ppermute | solution.py:360
  58.1 0.5 collective-permute-start.21
  58.6 0.9 %collective-permute-done.18 = f16[272,128]{1,0:T(8,128)(2,1)S(1)} collective-permute-done((f16[272,128]{1,0:T(8,128)(2,1)S(1)}, f16[272,128]{1,0:T(8,128)(2,1)S(1)}, u32[]{:S(2)}, u32[]{:S(2)}) %collective-permute-start.18) | collective-permute-done | bytes 69664 | tf_op jit(solution)/shard_map/ppermute | solution.py:360
  59.5 3.2 %collective-permute-done.19 = f16[272,128]{1,0:T(8,128)(2,1)S(1)} collective-permute-done((f16[272,128]{1,0:T(8,128)(2,1)S(1)}, f16[272,128]{1,0:T(8,128)(2,1)S(1)}, u32[]{:S(2)}, u32[]{:S(2)}) %collective-permute-start.19) | collective-permute-done | bytes 69664 | tf_op jit(solution)/shard_map/ppermute | solution.py:360
  62.8 0.0 copy-start.5
  62.8 0.0 copy-start.6
  62.8 1.1 %shard_map.86.refs_2_ = f32[1024,128]{1,0:T(8,128)S(1)} custom-call(bf16[1024,1024]{1,0:T(8,128)(2,1)S(1)} %copy-done.1, f32[272,128]{1,0:T(8,128)S(1)} %get-tuple-element.24.refs_1_, f32[272,128]{1,0:T(8,128)S(1)} %convert_element_type.100.refs_2_, f32[272,128]{1,0:T(8,128)S(1)} %convert_element_type.101.refs_3_, f32[272,128]{1,0:T(8,128)S(1)} %convert_element_type.102.refs_4_), custom_call_target="tpu_custom_call" | custom-call | tf_op jit(solution)/shard_map/pallas_call | solution.py:349
  64.0 0.0 collective-permute-done.23
  64.0 0.1 maximum_convert_fusion.refs_4_
  64.1 5.8 %shard_map.87 = (f32[8,128]{1,0:T(8,128)}, f32[132,512]{1,0:T(8,128)}) custom-call(f32[8,128]{1,0:T(8,128)S(1)} %get-tuple-element.15.refs_0_, bf16[1024,1024]{1,0:T(8,128)(2,1)S(1)} %copy-done.1, f32[1024,128]{1,0:T(8,128)S(1)} %shard_map.86.refs_2_, f32[1088,128]{1,0:T(8,128)S(1)} %pad_maximum_fusion.refs_3_, f32[1088,128]{1,0:T(8,128)S(1)} %maximum_convert_fusion.refs_4_, ...), custom_call_target="tpu_custom_call" | custom-call | tf_op jit(solution)/shard_map/pallas_call | solution.py:349
  (44 shorter events, 0.4 us)
Async XLA Ops:
  0.6 1.6 %copy-start = (bf16[1024,1024]{1,0:T(8,128)(2,1)S(1)}, bf16[1024,1024]{1,0:T(8,128)(2,1)}, u32[]{:S(2)}) copy-start(bf16[1024,1024]{1,0:T(8,128)(2,1)} %refs_1_.7) | copy-start | bytes 6291460
  2.2 0.7 copy-start.3
  2.9 2.3 %copy-start.1 = (bf16[1024,1024]{1,0:T(8,128)(2,1)S(1)}, bf16[1024,1024]{1,0:T(8,128)(2,1)}, u32[]{:S(2)}) copy-start(bf16[1024,1024]{1,0:T(8,128)(2,1)} %refs_1_.7) | copy-start | bytes 6291460
  4.7 2.1 %collective-permute-start = (f32[4,272,128]{2,1,0:T(8,128)S(1)}, f32[4,272,128]{2,1,0:T(8,128)S(1)}, u32[]{:S(2)}, u32[]{:S(2)}) collective-permute-start(f32[4,272,128]{2,1,0:T(8,128)S(1)} %get-tuple-element.14), channel_id=1, source_target_pairs={{0,1},{1,0},{2,3},{3,2},{4,5},{5,4},{6,7},{7,6},{8,9},{9,8},{10,11... | collective-permute-start | bytes 1671176 | tf_op jit(solution)/shard_map/ppermute | solution.py:360
  5.2 15.6 %copy-start.2 = (f32[528,512]{1,0:T(8,128)S(1)}, f32[528,512]{1,0:T(8,128)}, u32[]{:S(2)}) copy-start(f32[528,512]{1,0:T(8,128)} %refs_1_.5) | copy-start | bytes 3244036
  5.2 15.6 %copy-start.7 = (s32[204]{0:T(256)S(1)}, s32[204]{0:T(256)}, u32[]{:S(2)}) copy-start(s32[204]{0:T(256)} %constant.4.clone.refs_0_) | copy-start | bytes 2452
  6.9 5.6 %collective-permute-start.1 = (f16[272,128]{1,0:T(8,128)(2,1)S(1)}, f16[272,128]{1,0:T(8,128)(2,1)S(1)}, u32[]{:S(2)}, u32[]{:S(2)}) collective-permute-start(f16[272,128]{1,0:T(8,128)(2,1)S(1)} %get-tuple-element.28), channel_id=1, source_target_pairs={{0,4},{4,0},{8,12},{12,8},{1,5},{5,1},{9,13},{13,9},{2,6},{6,2},{1... | collective-permute-start | bytes 208904 | tf_op jit(solution)/shard_map/ppermute | solution.py:360
  9.9 6.9 %collective-permute-start.3 = (f16[272,128]{1,0:T(8,128)(2,1)S(1)}, f16[272,128]{1,0:T(8,128)(2,1)S(1)}, u32[]{:S(2)}, u32[]{:S(2)}) collective-permute-start(f16[272,128]{1,0:T(8,128)(2,1)S(1)} %get-tuple-element.29), channel_id=1, source_target_pairs={{0,12},{4,8},{8,4},{12,0},{1,13},{5,9},{9,5},{13,1},{2,14},{6,10},... | collective-permute-start | bytes 208904 | tf_op jit(solution)/shard_map/ppermute | solution.py:360
  12.3 6.8 %collective-permute-start.2 = (f16[272,128]{1,0:T(8,128)(2,1)S(1)}, f16[272,128]{1,0:T(8,128)(2,1)S(1)}, u32[]{:S(2)}, u32[]{:S(2)}) collective-permute-start(f16[272,128]{1,0:T(8,128)(2,1)S(1)} %get-tuple-element.30), channel_id=1, source_target_pairs={{0,8},{4,12},{8,0},{12,4},{1,9},{5,13},{9,1},{13,5},{2,10},{6,14},... | collective-permute-start | bytes 208904 | tf_op jit(solution)/shard_map/ppermute | solution.py:360
  19.3 14.2 %copy-start.4 = (f32[1024]{0:T(1024)S(1)}, f32[1024]{0:T(1024)}, u32[]{:S(2)}) copy-start(f32[1024]{0:T(1024)} %param.7) | copy-start | bytes 12292
  19.3 4.4 %collective-permute-start.4 = (f16[272,128]{1,0:T(8,128)(2,1)S(1)}, f16[272,128]{1,0:T(8,128)(2,1)S(1)}, u32[]{:S(2)}, u32[]{:S(2)}) collective-permute-start(f16[272,128]{1,0:T(8,128)(2,1)S(1)} %get-tuple-element.26), channel_id=1, source_target_pairs={{0,2},{2,0},{1,3},{3,1},{4,6},{6,4},{5,7},{7,5},{8,10},{10,8},{9,1... | collective-permute-start | bytes 208904 | tf_op jit(solution)/shard_map/ppermute | solution.py:360
  23.7 6.5 %collective-permute-start.7 = (bf16[272,128]{1,0:T(8,128)(2,1)S(1)}, bf16[272,128]{1,0:T(8,128)(2,1)S(1)}, u32[]{:S(2)}, u32[]{:S(2)}) collective-permute-start(bf16[272,128]{1,0:T(8,128)(2,1)S(1)} %tanh_convert_fusion.refs_1_), channel_id=1, source_target_pairs={{0,12},{4,8},{8,4},{12,0},{1,13},{5,9},{9,5},{13,1},{2,14},{6,10},... | collective-permute-start | bytes 208904 | tf_op jit(solution)/shard_map/ppermute | solution.py:360
  26.4 5.4 %collective-permute-start.6 = (bf16[272,128]{1,0:T(8,128)(2,1)S(1)}, bf16[272,128]{1,0:T(8,128)(2,1)S(1)}, u32[]{:S(2)}, u32[]{:S(2)}) collective-permute-start(bf16[272,128]{1,0:T(8,128)(2,1)S(1)} %tanh_convert_fusion.refs_1_), channel_id=1, source_target_pairs={{0,8},{4,12},{8,0},{12,4},{1,9},{5,13},{9,1},{13,5},{2,10},{6,14},... | collective-permute-start | bytes 208904 | tf_op jit(solution)/shard_map/ppermute | solution.py:360
  26.4 5.4 %collective-permute-start.5 = (bf16[272,128]{1,0:T(8,128)(2,1)S(1)}, bf16[272,128]{1,0:T(8,128)(2,1)S(1)}, u32[]{:S(2)}, u32[]{:S(2)}) collective-permute-start(bf16[272,128]{1,0:T(8,128)(2,1)S(1)} %tanh_convert_fusion.refs_1_), channel_id=1, source_target_pairs={{0,4},{4,0},{8,12},{12,8},{1,5},{5,1},{9,13},{13,9},{2,6},{6,2},{1... | collective-permute-start | bytes 208904 | tf_op jit(solution)/shard_map/ppermute | solution.py:360
  28.2 5.3 %collective-permute-start.8 = (bf16[272,128]{1,0:T(8,128)(2,1)S(1)}, bf16[272,128]{1,0:T(8,128)(2,1)S(1)}, u32[]{:S(2)}, u32[]{:S(2)}) collective-permute-start(bf16[272,128]{1,0:T(8,128)(2,1)S(1)} %tanh_convert_fusion.refs_1_), channel_id=1, source_target_pairs={{0,1},{1,0},{2,3},{3,2},{4,5},{5,4},{6,7},{7,6},{8,9},{9,8},{10,11... | collective-permute-start | bytes 208904 | tf_op jit(solution)/shard_map/ppermute | solution.py:360
  30.2 3.2 %collective-permute-start.11 = (bf16[272,128]{1,0:T(8,128)(2,1)S(1)}, bf16[272,128]{1,0:T(8,128)(2,1)S(1)}, u32[]{:S(2)}, u32[]{:S(2)}) collective-permute-start(bf16[272,128]{1,0:T(8,128)(2,1)S(1)} %collective-permute-done.7.refs_4_), channel_id=1, source_target_pairs={{0,1},{1,0},{2,3},{3,2},{4,5},{5,4},{6,7},{7,6},{8,9},{9,8},{10,11... | collective-permute-start | bytes 208904 | tf_op jit(solution)/shard_map/ppermute | solution.py:360
  31.8 1.7 %collective-permute-start.10 = (bf16[272,128]{1,0:T(8,128)(2,1)S(1)}, bf16[272,128]{1,0:T(8,128)(2,1)S(1)}, u32[]{:S(2)}, u32[]{:S(2)}) collective-permute-start(bf16[272,128]{1,0:T(8,128)(2,1)S(1)} %collective-permute-done.6.refs_3_), channel_id=1, source_target_pairs={{0,1},{1,0},{2,3},{3,2},{4,5},{5,4},{6,7},{7,6},{8,9},{9,8},{10,11... | collective-permute-start | bytes 208904 | tf_op jit(solution)/shard_map/ppermute | solution.py:360
  31.8 1.7 %collective-permute-start.9 = (bf16[272,128]{1,0:T(8,128)(2,1)S(1)}, bf16[272,128]{1,0:T(8,128)(2,1)S(1)}, u32[]{:S(2)}, u32[]{:S(2)}) collective-permute-start(bf16[272,128]{1,0:T(8,128)(2,1)S(1)} %collective-permute-done.5.refs_2_), channel_id=1, source_target_pairs={{0,1},{1,0},{2,3},{3,2},{4,5},{5,4},{6,7},{7,6},{8,9},{9,8},{10,11... | collective-permute-start | bytes 208904 | tf_op jit(solution)/shard_map/ppermute | solution.py:360
  37.4 2.0 %collective-permute-start.12 = (f32[4,288,128]{2,1,0:T(8,128)S(1)}, f32[4,288,128]{2,1,0:T(8,128)S(1)}, u32[]{:S(2)}, u32[]{:S(2)}) collective-permute-start(f32[4,288,128]{2,1,0:T(8,128)S(1)} %get-tuple-element.17), channel_id=1, source_target_pairs={{0,1},{1,0},{2,3},{3,2},{4,5},{5,4},{6,7},{7,6},{8,9},{9,8},{10,11... | collective-permute-start | bytes 1769480 | tf_op jit(solution)/shard_map/ppermute | solution.py:360
  39.5 7.1 %collective-permute-start.15 = (f16[288,128]{1,0:T(8,128)(2,1)S(1)}, f16[288,128]{1,0:T(8,128)(2,1)S(1)}, u32[]{:S(2)}, u32[]{:S(2)}) collective-permute-start(f16[288,128]{1,0:T(8,128)(2,1)S(1)} %convert_element_type.94), channel_id=1, source_target_pairs={{0,12},{4,8},{8,4},{12,0},{1,13},{5,9},{9,5},{13,1},{2,14},{6,10},... | collective-permute-start | bytes 221192 | tf_op jit(solution)/shard_map/ppermute | solution.py:360
  41.8 7.1 %collective-permute-start.14 = (f16[288,128]{1,0:T(8,128)(2,1)S(1)}, f16[288,128]{1,0:T(8,128)(2,1)S(1)}, u32[]{:S(2)}, u32[]{:S(2)}) collective-permute-start(f16[288,128]{1,0:T(8,128)(2,1)S(1)} %convert_element_type.92), channel_id=1, source_target_pairs={{0,8},{4,12},{8,0},{12,4},{1,9},{5,13},{9,1},{13,5},{2,10},{6,14},... | collective-permute-start | bytes 221192 | tf_op jit(solution)/shard_map/ppermute | solution.py:360
  41.8 7.1 %collective-permute-start.13 = (f16[288,128]{1,0:T(8,128)(2,1)S(1)}, f16[288,128]{1,0:T(8,128)(2,1)S(1)}, u32[]{:S(2)}, u32[]{:S(2)}) collective-permute-start(f16[288,128]{1,0:T(8,128)(2,1)S(1)} %convert_element_type.90), channel_id=1, source_target_pairs={{0,4},{4,0},{8,12},{12,8},{1,5},{5,1},{9,13},{13,9},{2,6},{6,2},{1... | collective-permute-start | bytes 221192 | tf_op jit(solution)/shard_map/ppermute | solution.py:360
  49.1 4.4 %collective-permute-start.16 = (f16[288,128]{1,0:T(8,128)(2,1)S(1)}, f16[288,128]{1,0:T(8,128)(2,1)S(1)}, u32[]{:S(2)}, u32[]{:S(2)}) collective-permute-start(f16[288,128]{1,0:T(8,128)(2,1)S(1)} %get-tuple-element.31), channel_id=1, source_target_pairs={{0,2},{2,0},{1,3},{3,1},{4,6},{6,4},{5,7},{7,5},{8,10},{10,8},{9,1... | collective-permute-start | bytes 221192 | tf_op jit(solution)/shard_map/ppermute | solution.py:360
  53.6 4.5 %collective-permute-start.17 = (f16[272,128]{1,0:T(8,128)(2,1)S(1)}, f16[272,128]{1,0:T(8,128)(2,1)S(1)}, u32[]{:S(2)}, u32[]{:S(2)}) collective-permute-start(f16[272,128]{1,0:T(8,128)(2,1)S(1)} %get-tuple-element.25), channel_id=1, source_target_pairs={{0,4},{4,0},{8,12},{12,8},{1,5},{5,1},{9,13},{13,9},{2,6},{6,2},{1... | collective-permute-start | bytes 208904 | tf_op jit(solution)/shard_map/ppermute | solution.py:360
  54.1 5.4 %collective-permute-start.18 = (f16[272,128]{1,0:T(8,128)(2,1)S(1)}, f16[272,128]{1,0:T(8,128)(2,1)S(1)}, u32[]{:S(2)}, u32[]{:S(2)}) collective-permute-start(f16[272,128]{1,0:T(8,128)(2,1)S(1)} %get-tuple-element.25), channel_id=1, source_target_pairs={{0,8},{4,12},{8,0},{12,4},{1,9},{5,13},{9,1},{13,5},{2,10},{6,14},... | collective-permute-start | bytes 208904 | tf_op jit(solution)/shard_map/ppermute | solution.py:360
  56.6 6.1 %collective-permute-start.19 = (f16[272,128]{1,0:T(8,128)(2,1)S(1)}, f16[272,128]{1,0:T(8,128)(2,1)S(1)}, u32[]{:S(2)}, u32[]{:S(2)}) collective-permute-start(f16[272,128]{1,0:T(8,128)(2,1)S(1)} %get-tuple-element.25), channel_id=1, source_target_pairs={{0,12},{4,8},{8,4},{12,0},{1,13},{5,9},{9,5},{13,1},{2,14},{6,10},... | collective-permute-start | bytes 208904 | tf_op jit(solution)/shard_map/ppermute | solution.py:360
  58.1 5.9 %collective-permute-start.20 = (f16[272,128]{1,0:T(8,128)(2,1)S(1)}, f16[272,128]{1,0:T(8,128)(2,1)S(1)}, u32[]{:S(2)}, u32[]{:S(2)}) collective-permute-start(f16[272,128]{1,0:T(8,128)(2,1)S(1)} %get-tuple-element.25), channel_id=1, source_target_pairs={{0,1},{1,0},{2,3},{3,2},{4,5},{5,4},{6,7},{7,6},{8,9},{9,8},{10,11... | collective-permute-start | bytes 208904 | tf_op jit(solution)/shard_map/ppermute | solution.py:360
  58.1 5.9 %collective-permute-start.21 = (f16[272,128]{1,0:T(8,128)(2,1)S(1)}, f16[272,128]{1,0:T(8,128)(2,1)S(1)}, u32[]{:S(2)}, u32[]{:S(2)}) collective-permute-start(f16[272,128]{1,0:T(8,128)(2,1)S(1)} %collective-permute-done.17), channel_id=1, source_target_pairs={{0,1},{1,0},{2,3},{3,2},{4,5},{5,4},{6,7},{7,6},{8,9},{9,8},{10,11... | collective-permute-start | bytes 208904 | tf_op jit(solution)/shard_map/ppermute | solution.py:360
  59.5 4.5 %collective-permute-start.22 = (f16[272,128]{1,0:T(8,128)(2,1)S(1)}, f16[272,128]{1,0:T(8,128)(2,1)S(1)}, u32[]{:S(2)}, u32[]{:S(2)}) collective-permute-start(f16[272,128]{1,0:T(8,128)(2,1)S(1)} %collective-permute-done.18), channel_id=1, source_target_pairs={{0,1},{1,0},{2,3},{3,2},{4,5},{5,4},{6,7},{7,6},{8,9},{9,8},{10,11... | collective-permute-start | bytes 208904 | tf_op jit(solution)/shard_map/ppermute | solution.py:360
  62.7 1.3 %collective-permute-start.23 = (f16[272,128]{1,0:T(8,128)(2,1)S(1)}, f16[272,128]{1,0:T(8,128)(2,1)S(1)}, u32[]{:S(2)}, u32[]{:S(2)}) collective-permute-start(f16[272,128]{1,0:T(8,128)(2,1)S(1)} %collective-permute-done.19), channel_id=1, source_target_pairs={{0,1},{1,0},{2,3},{3,2},{4,5},{5,4},{6,7},{7,6},{8,9},{9,8},{10,11... | collective-permute-start | bytes 208904 | tf_op jit(solution)/shard_map/ppermute | solution.py:360
  62.8 1.3 %copy-start.5 = (s32[528]{0:T(1024)S(1)}, s32[528]{0:T(1024)}, u32[]{:S(2)}) copy-start(s32[528]{0:T(1024)} %refs_5_.1) | copy-start | bytes 6340
  62.8 1.3 %copy-start.6 = (s32[528]{0:T(1024)S(1)}, s32[528]{0:T(1024)}, u32[]{:S(2)}) copy-start(s32[528]{0:T(1024)} %constant.5.clone.refs_6_) | copy-start | bytes 6340

commit v3 on v2

--- a/solution.py
+++ b/solution.py
@@ -14,10 +14,12 @@
 SUB = 16
 TOP = 14.0
 LN2 = math.log(2.0)
-STRIPS, BATCHES = 17, 4
+STRIPS, BATCHES, PIECES = 17, 4, 4
+LIMIT = 48
 F32, BF16, F16 = jnp.float32, jnp.bfloat16, jnp.float16
 VMEM = pl.BlockSpec(memory_space=pltpu.VMEM)
 SMEM = pl.BlockSpec(memory_space=pltpu.SMEM)
+HBM = pl.BlockSpec(memory_space=pltpu.MemorySpace.HBM)
 
 
 class Plan:
@@ -84,18 +86,16 @@
     return lax.dot_general(a, b, (((over_a,), (over_b,)), ((), ())), preferred_element_type=F32)
 
 
-def swap_groups(x, width):
+def lean(x, shift, width):
+    return pltpu.roll(x, shift, 1, stride=width, stride_axis=0)
+
+
+def settle(x, width):
     n = LANES // width
     row = lax.broadcasted_iota(jnp.int32, (n, LANES), 0)
     run = lax.broadcasted_iota(jnp.int32, (n, LANES), 1) // width
-    d = n // 2
-    while d:
-        up = pltpu.roll(pltpu.roll(x, n - d, 0), width * d, 1)
-        down = up if 2 * d == n else pltpu.roll(pltpu.roll(x, d, 0), LANES - width * d, 1)
-        low, high = (row & d) == 0, (run & d) == 0
-        x = jnp.where(low == high, x, jnp.where(low, up, down))
-        d //= 2
-    return x
+    x = jnp.take_along_axis(x, (run + row + 1) & (n - 1), axis=0)
+    return lean(x, width, width)
 
 
 def unrolled(count, step, body):
@@ -113,64 +113,66 @@
         body(i)
 
 
-def to_column(rows):
-    eye = lax.broadcasted_iota(jnp.int32, (LANES, LANES), 0) == lax.broadcasted_iota(
-        jnp.int32, (LANES, LANES), 1
-    )
+def row_sums(total):
     parts = []
-    for i in range(rows.shape[0]):
-        spread = jnp.broadcast_to(rows[i : i + 1, :], (LANES, LANES))
-        parts.append(jnp.sum(jnp.where(eye, spread, 0.0), axis=1, keepdims=True))
+    for at in range(0, total.shape[0], LANES):
+        parts.append(jnp.sum(total[at : at + LANES].T, axis=0, keepdims=True))
     return jnp.concatenate(parts, axis=0)
 
 
-def to_rows(column, out_ref):
-    eye = lax.broadcasted_iota(jnp.int32, (LANES, LANES), 0) == lax.broadcasted_iota(
-        jnp.int32, (LANES, LANES), 1
-    )
-    for i in range(column.shape[0] // LANES):
-        spread = jnp.broadcast_to(column[i * LANES : (i + 1) * LANES], (LANES, LANES))
-        out_ref[i : i + 1, :] = jnp.sum(jnp.where(eye, spread, 0.0), axis=0, keepdims=True)
-
-
-def weigh(plan, green, strength, weighted):
-    ns = plan.stations
+def weigh_rows(plan, green, strength, weighted, i):
+    column = jnp.broadcast_to(strength[i : i + 1, :], (LANES, LANES)).T
+    at = slice(i * LANES, (i + 1) * LANES)
     for h in range(2):
-        weighted[h] = (green[:, h * ns : (h + 1) * ns].astype(F32) * strength).astype(BF16)
-
-
-def product(plan, half, green, weighted, out):
+        for left in range(0, plan.stations, LANES):
+            part = green[at, h * plan.stations + left : h * plan.stations + left + LANES]
+            weighted[h, at, left : left + LANES] = (part.astype(F32) * column).astype(BF16)
+
+
+def product_part(plan, half, green, weighted, j, at=slice(None)):
+    ns, end = plan.stations, WIDE_BLOCK * (j + 1)
+    sign = (1 - 2 * half).astype(F32)
+    a = green[at, end - WIDE_BLOCK : end]
+    b = green[at, ns + end - WIDE_BLOCK : ns + end]
+    part = contract(weighted[half, at, :end], a, 0, 0)
+    return part + sign * contract(weighted[1 - half, at, :end], b, 0, 0)
+
+
+def pack(plan, j, part, out, most=None):
     z = lax.axis_index("wide")
-    ns, w = plan.stations, plan.width
-    sign = (1 - 2 * half).astype(F32)
+    w = plan.width
     lane = lax.broadcasted_iota(jnp.int32, (w, LANES), 1)
-    most = jnp.zeros((w, LANES), F32)
-    levelled = out.shape[1] > plan.chunk
-    for j in range(ns // WIDE_BLOCK):
-        end = WIDE_BLOCK * (j + 1)
-        a = green[:, end - WIDE_BLOCK : end]
-        b = green[:, ns + end - WIDE_BLOCK : ns + end]
-        part = contract(weighted[half, :, :end], a, 0, 0)
-        part = part + sign * contract(weighted[1 - half, :, :end], b, 0, 0)
-        for k, strip in enumerate(plan.strips):
-            if strip[0][1] * LANES // WIDE_BLOCK != j:
-                continue
-            value = None
-            for row, bj, _, last, shift in strip:
-                left = bj * LANES % WIDE_BLOCK
-                seen = part[row * w : (row + 1) * w, left : left + LANES]
-                seen = pltpu.roll(seen, shift, 1) if shift else seen
-                value = seen if value is None else jnp.where(lane < last, seen, value)
-            at = k % plan.run * w
-            out[(k // plan.run) ^ z, at : at + w, :] = value
-            if levelled:
-                most = jnp.maximum(most, jnp.abs(value))
+    for k, strip in enumerate(plan.strips):
+        if strip[0][1] * LANES // WIDE_BLOCK != j:
+            continue
+        value = None
+        for row, bj, _, last, shift in strip:
+            left = bj * LANES % WIDE_BLOCK
+            seen = part[row * w : (row + 1) * w, left : left + LANES]
+            seen = pltpu.roll(seen, shift, 1) if shift else seen
+            value = seen if value is None else jnp.where(lane < last, seen, value)
+        at = k % plan.run * w
+        out[(k // plan.run) ^ z, at : at + w, :] = value
+        if most is not None:
+            most = jnp.maximum(most, jnp.abs(value))
+    return most
+
+
+def pad(plan, out):
+    z, w = lax.axis_index("wide"), plan.width
     for k in range(len(plan.strips), plan.run * plan.wide):
         at = k % plan.run * w
         out[(k // plan.run) ^ z, at : at + w, :] = jnp.zeros((w, LANES), F32)
-    if levelled:
+
+
+def product(plan, half, green, weighted, out):
+    most = jnp.zeros((plan.width, LANES), F32) if out.shape[1] > plan.chunk else None
+    for j in range(plan.stations // WIDE_BLOCK):
+        most = pack(plan, j, product_part(plan, half, green, weighted, j), out, most)
+    pad(plan, out)
+    if most is not None:
         top = jnp.max(jnp.max(most, axis=0, keepdims=True), axis=1, keepdims=True)
-        level = jnp.ceil(jnp.log2(jnp.maximum(top, 1e-30)))
+        level = jnp.ceil(jnp.log2(jnp.maximum(top, 1e-30))) + (1.0 - TOP)
         out[:, plan.chunk :, :] = jnp.broadcast_to(level, (plan.wide, SUB, LANES))
 
 
@@ -236,14 +238,37 @@
             tiles = jnp.where(row < split, found[1], found[0])
             to = s * plan.width + part * n
             to = to if isinstance(to, int) else pl.multiple_of(to, n)
-            out[pl.ds(to, n), :] = swap_groups(tiles, plan.width)
+            tiles = settle(lean(tiles, 0, plan.width), plan.width)
+            out[pl.ds(to, n), :] = jnp.take_along_axis(tiles, n - 1 - row, axis=0)
 
     unrolled(plan.run, STRIPS, strip)
 
 
-def first_kernel(plan, log_ref, green, send, weighted):
-    weigh(plan, green, jnp.exp(to_column(log_ref[...])), weighted)
-    product(plan, 1 - lax.axis_index("tile"), green, weighted, send)
+def first_kernel(plan, log_hbm, green_hbm, send, weighted, green, log_ref, sums, done):
+    pieces = done.shape[0] - 1
+    size = plan.points // pieces
+    copies = [pltpu.make_async_copy(log_hbm, log_ref, done.at[pieces])]
+    for k in range(pieces):
+        at = pl.ds(k * size, size)
+        copies.append(pltpu.make_async_copy(green_hbm.at[at, :], green.at[at, :], done.at[k]))
+    for copy in copies:
+        copy.start()
+    copies[0].wait()
+    strength = jnp.exp(log_ref[...])
+    half = 1 - lax.axis_index("tile")
+    for k in range(pieces):
+        copies[1 + k].wait()
+        for i in range(k * size // LANES, (k + 1) * size // LANES):
+            weigh_rows(plan, green, strength, weighted, i)
+        at = slice(k * size, (k + 1) * size)
+        for j in range(plan.stations // WIDE_BLOCK):
+            part = product_part(plan, half, green, weighted, j, at)
+            part = part if k == 0 else part + sums[j, : part.shape[0], :]
+            if k < pieces - 1:
+                sums[j, : part.shape[0], :] = part
+            else:
+                pack(plan, j, part, send)
+    pad(plan, send)
 
 
 def own_product_kernel(plan, green, weighted, own):
@@ -260,9 +285,9 @@
 
 def new_log(plan, log_ref, green, total, kernel, log_out):
     total = total[...] + contraction(plan, 1 - lax.axis_index("tile"), green, kernel)
-    log_now = to_column(log_ref[...])
-    log_now = log_now - 0.5 * jnp.exp(log_now) * jnp.sum(total, axis=1, keepdims=True)
-    to_rows(log_now, log_out)
+    log_now = log_ref[...]
+    log_now = log_now - 0.5 * jnp.exp(log_now) * row_sums(total)
+    log_out[...] = log_now
     return log_now
 
 
@@ -271,8 +296,9 @@
     for k, ref in enumerate(tiles):
         stack[k] = ref[...]
     fill_half(plan, lambda slot, at: stack[slot, at : at + plan.width, :], kernel)
-    log_now = new_log(plan, log_ref, green, total, kernel, log_out)
-    weigh(plan, green, jnp.exp(log_now), weighted)
+    strength = jnp.exp(new_log(plan, log_ref, green, total, kernel, log_out))
+    for i in range(plan.points // LANES):
+        weigh_rows(plan, green, strength, weighted, i)
     product(plan, 1 - lax.axis_index("tile"), green, weighted, send)
 
 
@@ -293,14 +319,13 @@
         found = [None, None]
         for m in range(count):
             place = places[owners[z * plan.slots + first + m]]
-            row = pl.multiple_of(((place >> 16) ^ z) * c + ((place >> 4) & 4095), w)
-            shift = ((m - (place & 15)) & (n - 1)) * w
+            at = pl.multiple_of(((place >> 16) ^ z) * c + ((place >> 4) & 4095), w)
+            shift = ((n - 1 - m - (place & 15)) & (n - 1)) * w
             for h in range(2):
-                value = pltpu.roll(tiles[h, pl.ds(row, w), :], shift, 1)
-                found[h] = value if m == 0 else jnp.where(run == m, value, found[h])
-        return [
-            swap_groups(found[h][k * n : (k + 1) * n], w) for h in range(2) for k in range(w // n)
-        ]
+                value = pltpu.roll(tiles[h, pl.ds(at, w), :], shift, 1)
+                found[h] = value if m == 0 else jnp.where(run == n - 1 - m, value, found[h])
+        parts = [found[h][k * n : (k + 1) * n] for h in range(2) for k in range(w // n)]
+        return [settle(lean(x, 0, w), w) for x in parts]
 
     def batch(i):
         first = i * n if isinstance(i, int) else pl.multiple_of(i * n, n)
@@ -315,12 +340,21 @@
             residual[whole * n :, k * LANES : (k + 1) * LANES] = piece[:rest]
 
 
+def scale_kernel(plan, send, out):
+    c = plan.chunk
+    factor = jnp.exp(send[0, c : c + 1, :] * -LN2)
+    for k in range(plan.wide):
+        out[k, :c, :] = send[k, :c, :] * factor
+        out[k, c:, :] = send[k, c:, :]
+
+
 def join_kernel(plan, own, recv, *messages):
     c = plan.chunk
-    level = jnp.maximum(own[0, c : c + 1, :], recv[0, c : c + 1, :]) + (1.0 - TOP)
-    factor = jnp.exp(level * -LN2)
+    mine, other = own[0, c : c + 1, :], recv[0, c : c + 1, :]
+    level = jnp.maximum(mine, other) + 1.0
+    factor, wider = jnp.exp(level * -LN2), jnp.exp((other - level) * LN2)
     for k, out in enumerate(messages):
-        out[:c, :] = (own[k, :c, :] + recv[k, :c, :]) * factor
+        out[:c, :] = own[k, :c, :] * factor + recv[k, :c, :] * wider
         out[c:, :] = jnp.broadcast_to(level, (SUB, LANES))
 
 
@@ -342,17 +376,17 @@
     out[...] = jnp.tanh(total - target[...])
 
 
-def call(kernel, plan, out_shape, scratch, arguments, specs, out_spec=VMEM):
+def call(kernel, plan, out_shape, scratch, arguments, specs, limit=24):
     def body(*refs):
         kernel(plan, *refs)
 
     return pl.pallas_call(
         body,
         in_specs=specs,
-        out_specs=jax.tree.map(lambda _: out_spec, out_shape),
+        out_specs=jax.tree.map(lambda _: VMEM, out_shape),
         out_shape=out_shape,
         scratch_shapes=scratch,
-        compiler_params=pltpu.CompilerParams(vmem_limit_bytes=24 * 1024 * 1024),
+        compiler_params=pltpu.CompilerParams(vmem_limit_bytes=limit * 1024 * 1024),
     )(*arguments)
 
 
@@ -428,13 +462,19 @@
         observed_kernel, plan, shape((plan.chunk, LANES), F32), [],
         (jnp.asarray(plan.strip_table()), observed), [SMEM, VMEM],
     )
-    send, weighted = call(
-        first_kernel, plan, (shape((plan.wide, plan.chunk, LANES), F32), weighted_shape), [],
-        (log_now, green), [VMEM] * 2,
+    columns = plan.stations // WIDE_BLOCK
+    send, weighted, green = call(
+        first_kernel, plan,
+        (shape((plan.wide, plan.chunk, LANES), F32), weighted_shape, shape(green.shape, BF16)),
+        [
+            pltpu.VMEM(log_now.shape, F32),
+            pltpu.VMEM((columns, plan.stations, WIDE_BLOCK), F32),
+            pltpu.SemaphoreType.DMA((PIECES + 1,)),
+        ],
+        (log_now, green), [HBM] * 2, LIMIT,
     )
-    residual = bounded_residual(
-        plan, own_product(weighted, send), exchange(send, "tile", 1, 2), target
-    )
+    recv = exchange(send.astype(F16), "tile", 1, 2).astype(F32)
+    residual = bounded_residual(plan, own_product(weighted, send), recv, target)
     for _ in range(STEPS - 1):
         mine, others = spread(plan, residual.astype(BF16))
         levelled = shape((plan.wide, plan.chunk + SUB, LANES), F32)
@@ -442,9 +482,9 @@
             middle_kernel, plan, (levelled, weighted_shape, log_shape), [kernel, stack],
             (log_now, green, own_contraction(mine), *others), [VMEM] * (3 + len(others)),
         )
-        residual = scaled_residual(
-            plan, own_product(weighted, send), exchange(send, "tile", 1, 2), target
-        )
+        scaled = call(scale_kernel, plan, levelled, [], (send,), [VMEM])
+        recv = exchange(scaled.astype(F16), "tile", 1, 2).astype(F32)
+        residual = scaled_residual(plan, own_product(weighted, send), recv, target)
     mine, others = spread(plan, to_half(residual).astype(F16))
     mine = [x.astype(F32) for x in mine]
     log_now, owned = call(

time: 70.2 us -> 67.4 us (0.960)
  local copies, waits for them, and re-layouts: 2.3 us -> 0.71 us
  waiting for transfers between devices: 24.6 us -> 23.8 us
    unnamed x16 -> x10, local copies, waits for them, and re-layouts: 2.3 us -> 0.71 us
    ppermute x24, waiting for transfers between devices: 24.6 us -> 23.8 us  [exchange(): return lax.ppermute(x, axis, [(i, i ^ mask) for i in range(size)])]
    pallas_call x11 -> x12, Pallas kernels: 17.8 us -> 17.2 us  [call(): pl.pallas_call(body, in_specs=specs, out_specs=jax.tree.map(lambda _: VME...]
where the time goes in v3:
time: 67.4 us; the launch traced here: 67.2 us
  starting transfers between devices  23.8 us (35%)
  waiting for transfers between devices  23.8 us (35%)
  Pallas kernels  17.2 us (26%)
  between operations  0.95 us (1%)
  other arithmetic  0.75 us (1%)
  local copies, waits for them, and re-layouts  0.71 us (1%)
    ppermute x24, waiting for transfers between devices, exchange(): return lax.ppermute(x, axis, [(i, i ^ mask) for i in range(size)])  23.8 us
    ppermute x24, starting transfers between devices, exchange(): return lax.ppermute(x, axis, [(i, i ^ mask) for i in range(size)])  23.8 us
    pallas_call x12, Pallas kernels, call(): pl.pallas_call(body, in_specs=specs, out_specs=jax.tree.map(lambda _: VME...  17.2 us
  transfers between devices with their start and end apart: 24, of which 12 were waited for; matrix products, arithmetic and copies ran while one was open for 0% of the time, Pallas kernels for 9%

profile of v3, /device:TPU:0, one launch (start us, length us, event | category | flops | bytes accessed | tf_op | source)
XLA Modules:
  0.0 67.2 jit_solution(5716878984166623916)
XLA Ops:
  0.6 0.7 %copy-done.1 = f32[1024]{0:T(1024)S(1)} copy-done((f32[1024]{0:T(1024)S(1)}, f32[1024]{0:T(1024)}, u32[]{:S(2)}) %copy-start.1) | copy-done | bytes 4120
  1.3 3.4 %shard_map.77 = (f32[4,272,128]{2,1,0:T(8,128)S(1)}, bf16[2,1024,512]{2,1,0:T(8,128)(2,1)S(1)}, bf16[1024,1024]{1,0:T(8,128)(2,1)S(1)}) custom-call(f32[8,128]{1,0:T(8,128)S(1)} %bitcast.19, bf16[1024,1024]{1,0:T(8,128)(2,1)} %refs_1_.2), custom_call_target="tpu_custom_call" | custom-call | tf_op jit(solution)/shard_map/pallas_call | solution.py:383
  4.8 0.5 collective-permute-start
  5.3 1.1 %shard_map.78 = f32[4,272,128]{2,1,0:T(8,128)S(1)} custom-call(bf16[1024,1024]{1,0:T(8,128)(2,1)S(1)} %get-tuple-element.14.refs_0_.refs_1_, bf16[2,1024,512]{2,1,0:T(8,128)(2,1)S(1)} %get-tuple-element.15.refs_1_), custom_call_target="tpu_custom_call" | custom-call | tf_op jit(solution)/shard_map/pallas_call | solution.py:383
  6.4 0.0 copy-start
  6.4 0.0 copy-start.4
  6.4 0.1 collective-permute-done
  6.5 0.1 fusion.8
  6.6 3.0 %collective-permute-start.1 = (f16[272,128]{1,0:T(8,128)(2,1)S(1)}, f16[272,128]{1,0:T(8,128)(2,1)S(1)}, u32[]{:S(2)}, u32[]{:S(2)}) collective-permute-start(f16[272,128]{1,0:T(8,128)(2,1)S(1)} %get-tuple-element.30), channel_id=1, source_target_pairs={{0,4},{4,0},{8,12},{12,8},{1,5},{5,1},{9,13},{13,9},{2,6},{6,2},{1... | collective-permute-start | bytes 208904 | tf_op jit(solution)/shard_map/ppermute | solution.py:394
  9.6 2.5 %collective-permute-start.3 = (f16[272,128]{1,0:T(8,128)(2,1)S(1)}, f16[272,128]{1,0:T(8,128)(2,1)S(1)}, u32[]{:S(2)}, u32[]{:S(2)}) collective-permute-start(f16[272,128]{1,0:T(8,128)(2,1)S(1)} %get-tuple-element.31), channel_id=1, source_target_pairs={{0,12},{4,8},{8,4},{12,0},{1,13},{5,9},{9,5},{13,1},{2,14},{6,10},... | collective-permute-start | bytes 208904 | tf_op jit(solution)/shard_map/ppermute | solution.py:394
  12.1 0.1 collective-permute-start.2
  12.2 4.3 %collective-permute-done.3 = f16[272,128]{1,0:T(8,128)(2,1)S(1)} collective-permute-done((f16[272,128]{1,0:T(8,128)(2,1)S(1)}, f16[272,128]{1,0:T(8,128)(2,1)S(1)}, u32[]{:S(2)}, u32[]{:S(2)}) %collective-permute-start.3) | collective-permute-done | bytes 69664 | tf_op jit(solution)/shard_map/ppermute | solution.py:394
  16.5 2.4 %collective-permute-done.2 = f16[272,128]{1,0:T(8,128)(2,1)S(1)} collective-permute-done((f16[272,128]{1,0:T(8,128)(2,1)S(1)}, f16[272,128]{1,0:T(8,128)(2,1)S(1)}, u32[]{:S(2)}, u32[]{:S(2)}) %collective-permute-start.2) | collective-permute-done | bytes 69664 | tf_op jit(solution)/shard_map/ppermute | solution.py:394
  18.9 0.1 fusion.12
  19.0 1.5 %collective-permute-start.4 = (f16[272,128]{1,0:T(8,128)(2,1)S(1)}, f16[272,128]{1,0:T(8,128)(2,1)S(1)}, u32[]{:S(2)}, u32[]{:S(2)}) collective-permute-start(f16[272,128]{1,0:T(8,128)(2,1)S(1)} %get-tuple-element.28), channel_id=1, source_target_pairs={{0,2},{2,0},{1,3},{3,1},{4,6},{6,4},{5,7},{7,5},{8,10},{10,8},{9,1... | collective-permute-start | bytes 208904 | tf_op jit(solution)/shard_map/ppermute | solution.py:394
  20.6 1.5 %shard_map.79.refs_0_ = f32[272,128]{1,0:T(8,128)S(1)} custom-call(s32[204]{0:T(256)S(1)} %copy-done.4, f32[528,512]{1,0:T(8,128)S(1)} %copy-done), custom_call_target="tpu_custom_call" | custom-call | tf_op jit(solution)/shard_map/pallas_call | solution.py:383
  22.1 1.3 %collective-permute-done.4 = f16[272,128]{1,0:T(8,128)(2,1)S(1)} collective-permute-done((f16[272,128]{1,0:T(8,128)(2,1)S(1)}, f16[272,128]{1,0:T(8,128)(2,1)S(1)}, u32[]{:S(2)}, u32[]{:S(2)}) %collective-permute-start.4) | collective-permute-done | bytes 69664 | tf_op jit(solution)/shard_map/ppermute | solution.py:394
  23.5 2.7 %collective-permute-start.7 = (bf16[272,128]{1,0:T(8,128)(2,1)S(1)}, bf16[272,128]{1,0:T(8,128)(2,1)S(1)}, u32[]{:S(2)}, u32[]{:S(2)}) collective-permute-start(bf16[272,128]{1,0:T(8,128)(2,1)S(1)} %tanh_convert_fusion.refs_1_), channel_id=1, source_target_pairs={{0,12},{4,8},{8,4},{12,0},{1,13},{5,9},{9,5},{13,1},{2,14},{6,10},... | collective-permute-start | bytes 208904 | tf_op jit(solution)/shard_map/ppermute | solution.py:394
  26.1 1.8 %collective-permute-start.5 = (bf16[272,128]{1,0:T(8,128)(2,1)S(1)}, bf16[272,128]{1,0:T(8,128)(2,1)S(1)}, u32[]{:S(2)}, u32[]{:S(2)}) collective-permute-start(bf16[272,128]{1,0:T(8,128)(2,1)S(1)} %tanh_convert_fusion.refs_1_), channel_id=1, source_target_pairs={{0,4},{4,0},{8,12},{12,8},{1,5},{5,1},{9,13},{13,9},{2,6},{6,2},{1... | collective-permute-start | bytes 208904 | tf_op jit(solution)/shard_map/ppermute | solution.py:394
  27.9 2.1 %collective-permute-done.7.refs_4_ = bf16[272,128]{1,0:T(8,128)(2,1)S(1)} collective-permute-done((bf16[272,128]{1,0:T(8,128)(2,1)S(1)}, bf16[272,128]{1,0:T(8,128)(2,1)S(1)}, u32[]{:S(2)}, u32[]{:S(2)}) %collective-permute-start.7) | collective-permute-done | bytes 69664 | tf_op jit(solution)/shard_map/ppermute | solution.py:394
  30.0 1.6 %collective-permute-done.6.refs_3_ = bf16[272,128]{1,0:T(8,128)(2,1)S(1)} collective-permute-done((bf16[272,128]{1,0:T(8,128)(2,1)S(1)}, bf16[272,128]{1,0:T(8,128)(2,1)S(1)}, u32[]{:S(2)}, u32[]{:S(2)}) %collective-permute-start.6) | collective-permute-done | bytes 69664 | tf_op jit(solution)/shard_map/ppermute | solution.py:394
  31.6 0.5 collective-permute-start.9
  32.1 1.1 %shard_map.80.refs_2_ = f32[1024,128]{1,0:T(8,128)S(1)} custom-call(bf16[1024,1024]{1,0:T(8,128)(2,1)S(1)} %get-tuple-element.14.refs_0_.refs_1_, bf16[272,128]{1,0:T(8,128)(2,1)S(1)} %tanh_convert_fusion.refs_1_, bf16[272,128]{1,0:T(8,128)(2,1)S(1)} %collective-permute-done.5.refs_2_, bf16[272,128]{1,0:T(8,128)(2,1)S(1)} %collective-permute-done.6.refs_3_, ...), custom_call_target="tpu_custom_call" | custom-call | tf_op jit(solution)/shard_map/pallas_call | solution.py:383
  33.3 3.1 %shard_map.81 = (f32[4,288,128]{2,1,0:T(8,128)S(1)}, bf16[2,1024,512]{2,1,0:T(8,128)(2,1)S(1)}, f32[8,128]{1,0:T(8,128)S(1)}) custom-call(f32[8,128]{1,0:T(8,128)S(1)} %bitcast.20, bf16[1024,1024]{1,0:T(8,128)(2,1)S(1)} %get-tuple-element.14.refs_0_.refs_1_, f32[1024,128]{1,0:T(8,128)S(1)} %shard_map.80.refs_2_, ...), custom_call_target="tpu_custom_call" | custom-call | tf_op jit(solution)/shard_map/pallas_call | solution.py:383
  36.3 0.1 shard_map.83
  36.4 0.1 collective-permute-start.12
  36.6 1.2 %shard_map.82.refs_0_ = f32[4,288,128]{2,1,0:T(8,128)S(1)} custom-call(bf16[1024,1024]{1,0:T(8,128)(2,1)S(1)} %get-tuple-element.14.refs_0_.refs_1_, bf16[2,1024,512]{2,1,0:T(8,128)(2,1)S(1)} %get-tuple-element.18.refs_1_), custom_call_target="tpu_custom_call" | custom-call | tf_op jit(solution)/shard_map/pallas_call | solution.py:383
  37.8 0.3 collective-permute-done.12
  38.1 0.1 shard_map.84
  38.3 2.3 %collective-permute-start.15 = (f16[288,128]{1,0:T(8,128)(2,1)S(1)}, f16[288,128]{1,0:T(8,128)(2,1)S(1)}, u32[]{:S(2)}, u32[]{:S(2)}) collective-permute-start(f16[288,128]{1,0:T(8,128)(2,1)S(1)} %convert_element_type.110), channel_id=1, source_target_pairs={{0,12},{4,8},{8,4},{12,0},{1,13},{5,9},{9,5},{13,1},{2,14},{6,10},... | collective-permute-start | bytes 221192 | tf_op jit(solution)/shard_map/ppermute | solution.py:394
  40.5 2.3 %collective-permute-start.13 = (f16[288,128]{1,0:T(8,128)(2,1)S(1)}, f16[288,128]{1,0:T(8,128)(2,1)S(1)}, u32[]{:S(2)}, u32[]{:S(2)}) collective-permute-start(f16[288,128]{1,0:T(8,128)(2,1)S(1)} %convert_element_type.106), channel_id=1, source_target_pairs={{0,4},{4,0},{8,12},{12,8},{1,5},{5,1},{9,13},{13,9},{2,6},{6,2},{1... | collective-permute-start | bytes 221192 | tf_op jit(solution)/shard_map/ppermute | solution.py:394
  42.8 2.5 %collective-permute-done.15 = f16[288,128]{1,0:T(8,128)(2,1)S(1)} collective-permute-done((f16[288,128]{1,0:T(8,128)(2,1)S(1)}, f16[288,128]{1,0:T(8,128)(2,1)S(1)}, u32[]{:S(2)}, u32[]{:S(2)}) %collective-permute-start.15) | collective-permute-done | bytes 73760 | tf_op jit(solution)/shard_map/ppermute | solution.py:394
  45.3 2.3 %collective-permute-done.14 = f16[288,128]{1,0:T(8,128)(2,1)S(1)} collective-permute-done((f16[288,128]{1,0:T(8,128)(2,1)S(1)}, f16[288,128]{1,0:T(8,128)(2,1)S(1)}, u32[]{:S(2)}, u32[]{:S(2)}) %collective-permute-start.14) | collective-permute-done | bytes 73760 | tf_op jit(solution)/shard_map/ppermute | solution.py:394
  47.7 0.1 reduce-precision_convert_fusion.1
  47.8 1.6 %collective-permute-start.16 = (f16[288,128]{1,0:T(8,128)(2,1)S(1)}, f16[288,128]{1,0:T(8,128)(2,1)S(1)}, u32[]{:S(2)}, u32[]{:S(2)}) collective-permute-start(f16[288,128]{1,0:T(8,128)(2,1)S(1)} %get-tuple-element.33), channel_id=1, source_target_pairs={{0,2},{2,0},{1,3},{3,1},{4,6},{6,4},{5,7},{7,5},{8,10},{10,8},{9,1... | collective-permute-start | bytes 221192 | tf_op jit(solution)/shard_map/ppermute | solution.py:394
  49.3 2.9 %collective-permute-done.16 = f16[288,128]{1,0:T(8,128)(2,1)S(1)} collective-permute-done((f16[288,128]{1,0:T(8,128)(2,1)S(1)}, f16[288,128]{1,0:T(8,128)(2,1)S(1)}, u32[]{:S(2)}, u32[]{:S(2)}) %collective-permute-start.16) | collective-permute-done | bytes 73760 | tf_op jit(solution)/shard_map/ppermute | solution.py:394
  52.3 0.1 fusion.11
  52.4 0.5 collective-permute-start.17
  52.8 2.5 %collective-permute-start.18 = (f16[272,128]{1,0:T(8,128)(2,1)S(1)}, f16[272,128]{1,0:T(8,128)(2,1)S(1)}, u32[]{:S(2)}, u32[]{:S(2)}) collective-permute-start(f16[272,128]{1,0:T(8,128)(2,1)S(1)} %get-tuple-element.27), channel_id=1, source_target_pairs={{0,8},{4,12},{8,0},{12,4},{1,9},{5,13},{9,1},{13,5},{2,10},{6,14},... | collective-permute-start | bytes 208904 | tf_op jit(solution)/shard_map/ppermute | solution.py:394
  55.3 1.5 %collective-permute-start.19 = (f16[272,128]{1,0:T(8,128)(2,1)S(1)}, f16[272,128]{1,0:T(8,128)(2,1)S(1)}, u32[]{:S(2)}, u32[]{:S(2)}) collective-permute-start(f16[272,128]{1,0:T(8,128)(2,1)S(1)} %get-tuple-element.27), channel_id=1, source_target_pairs={{0,12},{4,8},{8,4},{12,0},{1,13},{5,9},{9,5},{13,1},{2,14},{6,10},... | collective-permute-start | bytes 208904 | tf_op jit(solution)/shard_map/ppermute | solution.py:394
  56.8 0.5 collective-permute-start.21
  57.3 2.4 %collective-permute-done.18 = f16[272,128]{1,0:T(8,128)(2,1)S(1)} collective-permute-done((f16[272,128]{1,0:T(8,128)(2,1)S(1)}, f16[272,128]{1,0:T(8,128)(2,1)S(1)}, u32[]{:S(2)}, u32[]{:S(2)}) %collective-permute-start.18) | collective-permute-done | bytes 69664 | tf_op jit(solution)/shard_map/ppermute | solution.py:394
  59.7 1.7 %collective-permute-done.19 = f16[272,128]{1,0:T(8,128)(2,1)S(1)} collective-permute-done((f16[272,128]{1,0:T(8,128)(2,1)S(1)}, f16[272,128]{1,0:T(8,128)(2,1)S(1)}, u32[]{:S(2)}, u32[]{:S(2)}) %collective-permute-start.19) | collective-permute-done | bytes 69664 | tf_op jit(solution)/shard_map/ppermute | solution.py:394
  61.5 0.0 copy-start.2
  61.5 0.0 copy-start.3
  61.5 1.2 %shard_map.87.refs_2_ = f32[1024,128]{1,0:T(8,128)S(1)} custom-call(bf16[1024,1024]{1,0:T(8,128)(2,1)S(1)} %get-tuple-element.14.refs_0_.refs_1_, f32[272,128]{1,0:T(8,128)S(1)} %get-tuple-element.26.refs_1_, f32[272,128]{1,0:T(8,128)S(1)} %convert_element_type.116.refs_2_, f32[272,128]{1,0:T(8,128)S(1)} %convert_element_type.117.refs_3_, ...), custom_call_target="tpu_custom_call" | custom-call | tf_op jit(solution)/shard_map/pallas_call | solution.py:383
  62.8 0.1 maximum_convert_fusion.refs_4_
  62.9 4.4 %shard_map.88 = (f32[8,128]{1,0:T(8,128)}, f32[132,512]{1,0:T(8,128)}) custom-call(f32[8,128]{1,0:T(8,128)S(1)} %get-tuple-element.17.refs_0_, bf16[1024,1024]{1,0:T(8,128)(2,1)S(1)} %get-tuple-element.14.refs_0_.refs_1_, f32[1024,128]{1,0:T(8,128)S(1)} %shard_map.87.refs_2_, f32[1088,128]{1,0:T(8,128)S(1)} %pad_maximum_fusion.refs_3_, ...), custom_call_target="tpu_custom_call" | custom-call | tf_op jit(solution)/shard_map/pallas_call | solution.py:383
  (43 shorter events, 0.5 us)
Async XLA Ops:
  0.6 0.7 %copy-start.1 = (f32[1024]{0:T(1024)S(1)}, f32[1024]{0:T(1024)}, u32[]{:S(2)}) copy-start(f32[1024]{0:T(1024)} %param.7) | copy-start | bytes 12292
  4.8 1.7 %collective-permute-start = (f16[4,272,128]{2,1,0:T(8,128)(2,1)S(1)}, f16[4,272,128]{2,1,0:T(8,128)(2,1)S(1)}, u32[]{:S(2)}, u32[]{:S(2)}) collective-permute-start(f16[4,272,128]{2,1,0:T(8,128)(2,1)S(1)} %convert_element_type.90), channel_id=1, source_target_pairs={{0,1},{1,0},{2,3},{3,2},{4,5},{5,4},{6,7},{7,6},{8,9},{9,8},{10,11... | collective-permute-start | bytes 835592 | tf_op jit(solution)/shard_map/ppermute | solution.py:394
  6.4 14.2 %copy-start = (f32[528,512]{1,0:T(8,128)S(1)}, f32[528,512]{1,0:T(8,128)}, u32[]{:S(2)}) copy-start(f32[528,512]{1,0:T(8,128)} %refs_1_.3) | copy-start | bytes 3244036
  6.4 14.2 %copy-start.4 = (s32[204]{0:T(256)S(1)}, s32[204]{0:T(256)}, u32[]{:S(2)}) copy-start(s32[204]{0:T(256)} %constant.4.clone.refs_0_) | copy-start | bytes 2452
  6.6 5.6 %collective-permute-start.1 = (f16[272,128]{1,0:T(8,128)(2,1)S(1)}, f16[272,128]{1,0:T(8,128)(2,1)S(1)}, u32[]{:S(2)}, u32[]{:S(2)}) collective-permute-start(f16[272,128]{1,0:T(8,128)(2,1)S(1)} %get-tuple-element.30), channel_id=1, source_target_pairs={{0,4},{4,0},{8,12},{12,8},{1,5},{5,1},{9,13},{13,9},{2,6},{6,2},{1... | collective-permute-start | bytes 208904 | tf_op jit(solution)/shard_map/ppermute | solution.py:394
  9.6 6.9 %collective-permute-start.3 = (f16[272,128]{1,0:T(8,128)(2,1)S(1)}, f16[272,128]{1,0:T(8,128)(2,1)S(1)}, u32[]{:S(2)}, u32[]{:S(2)}) collective-permute-start(f16[272,128]{1,0:T(8,128)(2,1)S(1)} %get-tuple-element.31), channel_id=1, source_target_pairs={{0,12},{4,8},{8,4},{12,0},{1,13},{5,9},{9,5},{13,1},{2,14},{6,10},... | collective-permute-start | bytes 208904 | tf_op jit(solution)/shard_map/ppermute | solution.py:394
  12.1 6.8 %collective-permute-start.2 = (f16[272,128]{1,0:T(8,128)(2,1)S(1)}, f16[272,128]{1,0:T(8,128)(2,1)S(1)}, u32[]{:S(2)}, u32[]{:S(2)}) collective-permute-start(f16[272,128]{1,0:T(8,128)(2,1)S(1)} %get-tuple-element.32), channel_id=1, source_target_pairs={{0,8},{4,12},{8,0},{12,4},{1,9},{5,13},{9,1},{13,5},{2,10},{6,14},... | collective-permute-start | bytes 208904 | tf_op jit(solution)/shard_map/ppermute | solution.py:394
  19.0 4.4 %collective-permute-start.4 = (f16[272,128]{1,0:T(8,128)(2,1)S(1)}, f16[272,128]{1,0:T(8,128)(2,1)S(1)}, u32[]{:S(2)}, u32[]{:S(2)}) collective-permute-start(f16[272,128]{1,0:T(8,128)(2,1)S(1)} %get-tuple-element.28), channel_id=1, source_target_pairs={{0,2},{2,0},{1,3},{3,1},{4,6},{6,4},{5,7},{7,5},{8,10},{10,8},{9,1... | collective-permute-start | bytes 208904 | tf_op jit(solution)/shard_map/ppermute | solution.py:394
  23.5 6.5 %collective-permute-start.7 = (bf16[272,128]{1,0:T(8,128)(2,1)S(1)}, bf16[272,128]{1,0:T(8,128)(2,1)S(1)}, u32[]{:S(2)}, u32[]{:S(2)}) collective-permute-start(bf16[272,128]{1,0:T(8,128)(2,1)S(1)} %tanh_convert_fusion.refs_1_), channel_id=1, source_target_pairs={{0,12},{4,8},{8,4},{12,0},{1,13},{5,9},{9,5},{13,1},{2,14},{6,10},... | collective-permute-start | bytes 208904 | tf_op jit(solution)/shard_map/ppermute | solution.py:394
  26.1 5.4 %collective-permute-start.6 = (bf16[272,128]{1,0:T(8,128)(2,1)S(1)}, bf16[272,128]{1,0:T(8,128)(2,1)S(1)}, u32[]{:S(2)}, u32[]{:S(2)}) collective-permute-start(bf16[272,128]{1,0:T(8,128)(2,1)S(1)} %tanh_convert_fusion.refs_1_), channel_id=1, source_target_pairs={{0,8},{4,12},{8,0},{12,4},{1,9},{5,13},{9,1},{13,5},{2,10},{6,14},... | collective-permute-start | bytes 208904 | tf_op jit(solution)/shard_map/ppermute | solution.py:394
  26.1 5.4 %collective-permute-start.5 = (bf16[272,128]{1,0:T(8,128)(2,1)S(1)}, bf16[272,128]{1,0:T(8,128)(2,1)S(1)}, u32[]{:S(2)}, u32[]{:S(2)}) collective-permute-start(bf16[272,128]{1,0:T(8,128)(2,1)S(1)} %tanh_convert_fusion.refs_1_), channel_id=1, source_target_pairs={{0,4},{4,0},{8,12},{12,8},{1,5},{5,1},{9,13},{13,9},{2,6},{6,2},{1... | collective-permute-start | bytes 208904 | tf_op jit(solution)/shard_map/ppermute | solution.py:394
  27.9 5.3 %collective-permute-start.8 = (bf16[272,128]{1,0:T(8,128)(2,1)S(1)}, bf16[272,128]{1,0:T(8,128)(2,1)S(1)}, u32[]{:S(2)}, u32[]{:S(2)}) collective-permute-start(bf16[272,128]{1,0:T(8,128)(2,1)S(1)} %tanh_convert_fusion.refs_1_), channel_id=1, source_target_pairs={{0,1},{1,0},{2,3},{3,2},{4,5},{5,4},{6,7},{7,6},{8,9},{9,8},{10,11... | collective-permute-start | bytes 208904 | tf_op jit(solution)/shard_map/ppermute | solution.py:394
  30.0 3.3 %collective-permute-start.11 = (bf16[272,128]{1,0:T(8,128)(2,1)S(1)}, bf16[272,128]{1,0:T(8,128)(2,1)S(1)}, u32[]{:S(2)}, u32[]{:S(2)}) collective-permute-start(bf16[272,128]{1,0:T(8,128)(2,1)S(1)} %collective-permute-done.7.refs_4_), channel_id=1, source_target_pairs={{0,1},{1,0},{2,3},{3,2},{4,5},{5,4},{6,7},{7,6},{8,9},{9,8},{10,11... | collective-permute-start | bytes 208904 | tf_op jit(solution)/shard_map/ppermute | solution.py:394
  31.5 1.7 %collective-permute-start.10 = (bf16[272,128]{1,0:T(8,128)(2,1)S(1)}, bf16[272,128]{1,0:T(8,128)(2,1)S(1)}, u32[]{:S(2)}, u32[]{:S(2)}) collective-permute-start(bf16[272,128]{1,0:T(8,128)(2,1)S(1)} %collective-permute-done.6.refs_3_), channel_id=1, source_target_pairs={{0,1},{1,0},{2,3},{3,2},{4,5},{5,4},{6,7},{7,6},{8,9},{9,8},{10,11... | collective-permute-start | bytes 208904 | tf_op jit(solution)/shard_map/ppermute | solution.py:394
  31.6 1.7 %collective-permute-start.9 = (bf16[272,128]{1,0:T(8,128)(2,1)S(1)}, bf16[272,128]{1,0:T(8,128)(2,1)S(1)}, u32[]{:S(2)}, u32[]{:S(2)}) collective-permute-start(bf16[272,128]{1,0:T(8,128)(2,1)S(1)} %collective-permute-done.5.refs_2_), channel_id=1, source_target_pairs={{0,1},{1,0},{2,3},{3,2},{4,5},{5,4},{6,7},{7,6},{8,9},{9,8},{10,11... | collective-permute-start | bytes 208904 | tf_op jit(solution)/shard_map/ppermute | solution.py:394
  36.4 1.6 %collective-permute-start.12 = (f16[4,288,128]{2,1,0:T(8,128)(2,1)S(1)}, f16[4,288,128]{2,1,0:T(8,128)(2,1)S(1)}, u32[]{:S(2)}, u32[]{:S(2)}) collective-permute-start(f16[4,288,128]{2,1,0:T(8,128)(2,1)S(1)} %convert_element_type.104), channel_id=1, source_target_pairs={{0,1},{1,0},{2,3},{3,2},{4,5},{5,4},{6,7},{7,6},{8,9},{9,8},{10,11... | collective-permute-start | bytes 884744 | tf_op jit(solution)/shard_map/ppermute | solution.py:394
  38.3 7.1 %collective-permute-start.15 = (f16[288,128]{1,0:T(8,128)(2,1)S(1)}, f16[288,128]{1,0:T(8,128)(2,1)S(1)}, u32[]{:S(2)}, u32[]{:S(2)}) collective-permute-start(f16[288,128]{1,0:T(8,128)(2,1)S(1)} %convert_element_type.110), channel_id=1, source_target_pairs={{0,12},{4,8},{8,4},{12,0},{1,13},{5,9},{9,5},{13,1},{2,14},{6,10},... | collective-permute-start | bytes 221192 | tf_op jit(solution)/shard_map/ppermute | solution.py:394
  40.5 7.1 %collective-permute-start.14 = (f16[288,128]{1,0:T(8,128)(2,1)S(1)}, f16[288,128]{1,0:T(8,128)(2,1)S(1)}, u32[]{:S(2)}, u32[]{:S(2)}) collective-permute-start(f16[288,128]{1,0:T(8,128)(2,1)S(1)} %convert_element_type.108), channel_id=1, source_target_pairs={{0,8},{4,12},{8,0},{12,4},{1,9},{5,13},{9,1},{13,5},{2,10},{6,14},... | collective-permute-start | bytes 221192 | tf_op jit(solution)/shard_map/ppermute | solution.py:394
  40.5 7.1 %collective-permute-start.13 = (f16[288,128]{1,0:T(8,128)(2,1)S(1)}, f16[288,128]{1,0:T(8,128)(2,1)S(1)}, u32[]{:S(2)}, u32[]{:S(2)}) collective-permute-start(f16[288,128]{1,0:T(8,128)(2,1)S(1)} %convert_element_type.106), channel_id=1, source_target_pairs={{0,4},{4,0},{8,12},{12,8},{1,5},{5,1},{9,13},{13,9},{2,6},{6,2},{1... | collective-permute-start | bytes 221192 | tf_op jit(solution)/shard_map/ppermute | solution.py:394
  47.8 4.4 %collective-permute-start.16 = (f16[288,128]{1,0:T(8,128)(2,1)S(1)}, f16[288,128]{1,0:T(8,128)(2,1)S(1)}, u32[]{:S(2)}, u32[]{:S(2)}) collective-permute-start(f16[288,128]{1,0:T(8,128)(2,1)S(1)} %get-tuple-element.33), channel_id=1, source_target_pairs={{0,2},{2,0},{1,3},{3,1},{4,6},{6,4},{5,7},{7,5},{8,10},{10,8},{9,1... | collective-permute-start | bytes 221192 | tf_op jit(solution)/shard_map/ppermute | solution.py:394
  52.4 4.5 %collective-permute-start.17 = (f16[272,128]{1,0:T(8,128)(2,1)S(1)}, f16[272,128]{1,0:T(8,128)(2,1)S(1)}, u32[]{:S(2)}, u32[]{:S(2)}) collective-permute-start(f16[272,128]{1,0:T(8,128)(2,1)S(1)} %get-tuple-element.27), channel_id=1, source_target_pairs={{0,4},{4,0},{8,12},{12,8},{1,5},{5,1},{9,13},{13,9},{2,6},{6,2},{1... | collective-permute-start | bytes 208904 | tf_op jit(solution)/shard_map/ppermute | solution.py:394
  52.8 6.9 %collective-permute-start.18 = (f16[272,128]{1,0:T(8,128)(2,1)S(1)}, f16[272,128]{1,0:T(8,128)(2,1)S(1)}, u32[]{:S(2)}, u32[]{:S(2)}) collective-permute-start(f16[272,128]{1,0:T(8,128)(2,1)S(1)} %get-tuple-element.27), channel_id=1, source_target_pairs={{0,8},{4,12},{8,0},{12,4},{1,9},{5,13},{9,1},{13,5},{2,10},{6,14},... | collective-permute-start | bytes 208904 | tf_op jit(solution)/shard_map/ppermute | solution.py:394
  55.3 6.1 %collective-permute-start.19 = (f16[272,128]{1,0:T(8,128)(2,1)S(1)}, f16[272,128]{1,0:T(8,128)(2,1)S(1)}, u32[]{:S(2)}, u32[]{:S(2)}) collective-permute-start(f16[272,128]{1,0:T(8,128)(2,1)S(1)} %get-tuple-element.27), channel_id=1, source_target_pairs={{0,12},{4,8},{8,4},{12,0},{1,13},{5,9},{9,5},{13,1},{2,14},{6,10},... | collective-permute-start | bytes 208904 | tf_op jit(solution)/shard_map/ppermute | solution.py:394
  56.8 5.9 %collective-permute-start.20 = (f16[272,128]{1,0:T(8,128)(2,1)S(1)}, f16[272,128]{1,0:T(8,128)(2,1)S(1)}, u32[]{:S(2)}, u32[]{:S(2)}) collective-permute-start(f16[272,128]{1,0:T(8,128)(2,1)S(1)} %get-tuple-element.27), channel_id=1, source_target_pairs={{0,1},{1,0},{2,3},{3,2},{4,5},{5,4},{6,7},{7,6},{8,9},{9,8},{10,11... | collective-permute-start | bytes 208904 | tf_op jit(solution)/shard_map/ppermute | solution.py:394
  56.8 5.9 %collective-permute-start.21 = (f16[272,128]{1,0:T(8,128)(2,1)S(1)}, f16[272,128]{1,0:T(8,128)(2,1)S(1)}, u32[]{:S(2)}, u32[]{:S(2)}) collective-permute-start(f16[272,128]{1,0:T(8,128)(2,1)S(1)} %collective-permute-done.17), channel_id=1, source_target_pairs={{0,1},{1,0},{2,3},{3,2},{4,5},{5,4},{6,7},{7,6},{8,9},{9,8},{10,11... | collective-permute-start | bytes 208904 | tf_op jit(solution)/shard_map/ppermute | solution.py:394
  59.7 3.0 %collective-permute-start.22 = (f16[272,128]{1,0:T(8,128)(2,1)S(1)}, f16[272,128]{1,0:T(8,128)(2,1)S(1)}, u32[]{:S(2)}, u32[]{:S(2)}) collective-permute-start(f16[272,128]{1,0:T(8,128)(2,1)S(1)} %collective-permute-done.18), channel_id=1, source_target_pairs={{0,1},{1,0},{2,3},{3,2},{4,5},{5,4},{6,7},{7,6},{8,9},{9,8},{10,11... | collective-permute-start | bytes 208904 | tf_op jit(solution)/shard_map/ppermute | solution.py:394
  61.5 1.3 %collective-permute-start.23 = (f16[272,128]{1,0:T(8,128)(2,1)S(1)}, f16[272,128]{1,0:T(8,128)(2,1)S(1)}, u32[]{:S(2)}, u32[]{:S(2)}) collective-permute-start(f16[272,128]{1,0:T(8,128)(2,1)S(1)} %collective-permute-done.19), channel_id=1, source_target_pairs={{0,1},{1,0},{2,3},{3,2},{4,5},{5,4},{6,7},{7,6},{8,9},{9,8},{10,11... | collective-permute-start | bytes 208904 | tf_op jit(solution)/shard_map/ppermute | solution.py:394
  61.5 1.3 %copy-start.2 = (s32[528]{0:T(1024)S(1)}, s32[528]{0:T(1024)}, u32[]{:S(2)}) copy-start(s32[528]{0:T(1024)} %refs_5_.1) | copy-start | bytes 6340
  61.5 1.3 %copy-start.3 = (s32[528]{0:T(1024)S(1)}, s32[528]{0:T(1024)}, u32[]{:S(2)}) copy-start(s32[528]{0:T(1024)} %constant.5.clone.refs_6_) | copy-start | bytes 6340

commit v4 on v3

--- a/solution.py
+++ b/solution.py
@@ -15,7 +15,6 @@
 TOP = 14.0
 LN2 = math.log(2.0)
 STRIPS, BATCHES, PIECES = 17, 4, 4
-LIMIT = 48
 F32, BF16, F16 = jnp.float32, jnp.bfloat16, jnp.float16
 VMEM = pl.BlockSpec(memory_space=pltpu.VMEM)
 SMEM = pl.BlockSpec(memory_space=pltpu.SMEM)
@@ -36,6 +35,7 @@
         self.run = -(-len(self.strips) // self.wide)
         self.chunk = self.run * self.width
         self.slots = owner_map.shape[0] // self.wide
+        self.order = [*range(min(2, self.wide)), *range(self.wide - 1, 1, -1)]
 
     def list_strips(self):
         side, per, w = self.stations // LANES, self.group, self.width
@@ -129,13 +129,13 @@
             weighted[h, at, left : left + LANES] = (part.astype(F32) * column).astype(BF16)
 
 
-def product_part(plan, half, green, weighted, j, at=slice(None)):
+def product_part(plan, half, green, weighted, j):
     ns, end = plan.stations, WIDE_BLOCK * (j + 1)
     sign = (1 - 2 * half).astype(F32)
-    a = green[at, end - WIDE_BLOCK : end]
-    b = green[at, ns + end - WIDE_BLOCK : ns + end]
-    part = contract(weighted[half, at, :end], a, 0, 0)
-    return part + sign * contract(weighted[1 - half, at, :end], b, 0, 0)
+    a = green[:, end - WIDE_BLOCK : end]
+    b = green[:, ns + end - WIDE_BLOCK : ns + end]
+    part = contract(weighted[half, :, :end], a, 0, 0)
+    return part + sign * contract(weighted[1 - half, :, :end], b, 0, 0)
 
 
 def pack(plan, j, part, out, most=None):
@@ -244,7 +244,7 @@
     unrolled(plan.run, STRIPS, strip)
 
 
-def first_kernel(plan, log_hbm, green_hbm, send, weighted, green, log_ref, sums, done):
+def first_kernel(plan, log_hbm, green_hbm, send, weighted, green, log_ref, done):
     pieces = done.shape[0] - 1
     size = plan.points // pieces
     copies = [pltpu.make_async_copy(log_hbm, log_ref, done.at[pieces])]
@@ -255,20 +255,11 @@
         copy.start()
     copies[0].wait()
     strength = jnp.exp(log_ref[...])
-    half = 1 - lax.axis_index("tile")
     for k in range(pieces):
         copies[1 + k].wait()
         for i in range(k * size // LANES, (k + 1) * size // LANES):
             weigh_rows(plan, green, strength, weighted, i)
-        at = slice(k * size, (k + 1) * size)
-        for j in range(plan.stations // WIDE_BLOCK):
-            part = product_part(plan, half, green, weighted, j, at)
-            part = part if k == 0 else part + sums[j, : part.shape[0], :]
-            if k < pieces - 1:
-                sums[j, : part.shape[0], :] = part
-            else:
-                pack(plan, j, part, send)
-    pad(plan, send)
+    product(plan, 1 - lax.axis_index("tile"), green, weighted, send)
 
 
 def own_product_kernel(plan, green, weighted, own):
@@ -277,7 +268,7 @@
 
 def own_contraction_kernel(plan, green, *refs):
     *tiles, total, kernel, stack = refs
-    for k, ref in enumerate(tiles):
+    for k, ref in zip(plan.order, tiles):
         stack[k] = ref[...].astype(BF16)
     fill_half(plan, lambda slot, at: stack[slot, at : at + plan.width, :], kernel)
     total[...] = contraction(plan, lax.axis_index("tile"), green, kernel)
@@ -293,7 +284,7 @@
 
 def middle_kernel(plan, log_ref, green, total, *refs):
     *tiles, send, weighted, log_out, kernel, stack = refs
-    for k, ref in enumerate(tiles):
+    for k, ref in zip(plan.order, tiles):
         stack[k] = ref[...]
     fill_half(plan, lambda slot, at: stack[slot, at : at + plan.width, :], kernel)
     strength = jnp.exp(new_log(plan, log_ref, green, total, kernel, log_out))
@@ -302,17 +293,20 @@
     product(plan, 1 - lax.axis_index("tile"), green, weighted, send)
 
 
-def last_kernel(plan, log_ref, green, total, mine, others, owners, places, log_out, residual, kernel, tiles):
+def last_kernel(plan, log_ref, green, total, owners, places, *refs):
+    *refs, log_out, residual, kernel, tiles = refs
+    mine, others = refs[: plan.wide], refs[plan.wide :]
     core, z = lax.axis_index("tile"), lax.axis_index("wide")
     n, w, c = plan.group, plan.width, plan.chunk
+    for k, left, right in zip(plan.order, mine, others):
+        tiles[core, k * c : (k + 1) * c, :] = left[...]
+        tiles[1 - core, k * c : (k + 1) * c, :] = right[...]
     fill_half(
         plan,
-        lambda slot, at: others[pl.ds(pl.multiple_of(slot * c + at, w), w), :],
+        lambda slot, at: tiles[1 - core, pl.ds(pl.multiple_of(slot * c + at, w), w), :],
         kernel,
     )
     new_log(plan, log_ref, green, total, kernel, log_out)
-    tiles[core] = mine[...]
-    tiles[1 - core] = others[...]
     run = lax.broadcasted_iota(jnp.int32, (w, LANES), 1) // w
 
     def rows_of(first, count):
@@ -376,7 +370,7 @@
     out[...] = jnp.tanh(total - target[...])
 
 
-def call(kernel, plan, out_shape, scratch, arguments, specs, limit=24):
+def call(kernel, plan, out_shape, scratch, arguments, specs):
     def body(*refs):
         kernel(plan, *refs)
 
@@ -386,7 +380,7 @@
         out_specs=jax.tree.map(lambda _: VMEM, out_shape),
         out_shape=out_shape,
         scratch_shapes=scratch,
-        compiler_params=pltpu.CompilerParams(vmem_limit_bytes=limit * 1024 * 1024),
+        compiler_params=pltpu.CompilerParams(vmem_limit_bytes=24 * 1024 * 1024),
     )(*arguments)
 
 
@@ -401,7 +395,7 @@
 def bounded_residual(plan, own, recv, target):
     sums = [own[k] + recv[k] for k in range(plan.wide)]
     total = sums[0]
-    for x in [exchange(sums[k].astype(F16), "wide", k, plan.wide) for k in range(1, plan.wide)]:
+    for x in [exchange(sums[k].astype(F16), "wide", k, plan.wide) for k in range(plan.wide - 1, 0, -1)]:
         total = total + x.astype(F32)
     mask = 1
     while mask < plan.narrow:
@@ -419,7 +413,7 @@
 
     sums = call(join_kernel, plan, (message,) * plan.wide, [], (own, recv), [VMEM] * 2)
     parts = [sums[0]]
-    for k in range(1, plan.wide):
+    for k in [*range(plan.wide - 1, 2, -1), *range(1, min(3, plan.wide))]:
         parts.append(exchange(sums[k].astype(F16), "wide", k, plan.wide).astype(F32))
     total = to_half(join(*parts))
     mask = 1
@@ -435,7 +429,7 @@
 
 
 def spread(plan, chunk):
-    mine = [chunk] + [exchange(chunk, "wide", k, plan.wide) for k in range(1, plan.wide)]
+    mine = [chunk] + [exchange(chunk, "wide", k, plan.wide) for k in plan.order[1:]]
     return mine, [exchange(x, "tile", 1, 2) for x in mine]
 
 
@@ -462,16 +456,15 @@
         observed_kernel, plan, shape((plan.chunk, LANES), F32), [],
         (jnp.asarray(plan.strip_table()), observed), [SMEM, VMEM],
     )
-    columns = plan.stations // WIDE_BLOCK
     send, weighted, green = call(
         first_kernel, plan,
         (shape((plan.wide, plan.chunk, LANES), F32), weighted_shape, shape(green.shape, BF16)),
         [
             pltpu.VMEM(log_now.shape, F32),
-            pltpu.VMEM((columns, plan.stations, WIDE_BLOCK), F32),
             pltpu.SemaphoreType.DMA((PIECES + 1,)),
         ],
-        (log_now, green), [HBM] * 2, LIMIT,
+        [pltpu.with_memory_space_constraint(x, pltpu.MemorySpace.HBM) for x in (log_now, green)],
+        [HBM] * 2,
     )
     recv = exchange(send.astype(F16), "tile", 1, 2).astype(F32)
     residual = bounded_residual(plan, own_product(weighted, send), recv, target)
@@ -491,10 +484,10 @@
         last_kernel, plan, (log_shape, shape((plan.slots, observed.shape[1]), F32)),
         [kernel, pltpu.VMEM((2, plan.wide * plan.chunk, LANES), F32)],
         (
-            log_now, green, own_contraction(mine), jnp.concatenate(mine),
-            jnp.concatenate(others).astype(F32), owner_map, jnp.asarray(plan.tile_places()),
+            log_now, green, own_contraction(mine), owner_map, jnp.asarray(plan.tile_places()),
+            *mine, *[x.astype(F32) for x in others],
         ),
-        [VMEM] * 5 + [SMEM] * 2,
+        [VMEM] * 3 + [SMEM] * 2 + [VMEM] * (2 * plan.wide),
     )
     return log_now.reshape(-1), owned
 

time: 67.4 us -> 64.6 us (0.958)
  starting transfers between devices: 23.8 us -> 22.2 us
  local copies, waits for them, and re-layouts: 0.71 us -> 0.03 us
    ppermute x24, starting transfers between devices: 23.8 us -> 22.2 us  [exchange(): return lax.ppermute(x, axis, [(i, i ^ mask) for i in range(size)])]
  transfers between devices with their start and end apart: 24 -> 24, of which waited for: 12 -> 15; matrix products, arithmetic and copies ran while one was open for 0% -> 0% of each run, Pallas kernels for 9% -> 9%
where the time goes in v4:
time: 64.6 us; the launch traced here: 64.4 us
  waiting for transfers between devices  23.9 us (37%)
  starting transfers between devices  22.2 us (34%)
  Pallas kernels  16.6 us (26%)
  between operations  0.97 us (2%)
  other arithmetic  0.71 us (1%)
    ppermute x24, waiting for transfers between devices, exchange(): return lax.ppermute(x, axis, [(i, i ^ mask) for i in range(size)])  23.9 us
    ppermute x24, starting transfers between devices, exchange(): return lax.ppermute(x, axis, [(i, i ^ mask) for i in range(size)])  22.2 us
    pallas_call x12, Pallas kernels, call(): pl.pallas_call(body, in_specs=specs, out_specs=jax.tree.map(lambda _: VME...  16.6 us
  transfers between devices with their start and end apart: 24, of which 15 were waited for; matrix products, arithmetic and copies ran while one was open for 0% of the time, Pallas kernels for 9%

profile of v4, /device:TPU:0, one launch (start us, length us, event | category | flops | bytes accessed | tf_op | source)
XLA Modules:
  0.0 64.4 jit_solution(10165313976781589063)
XLA Ops:
  0.6 2.9 %shard_map.77 = (f32[4,272,128]{2,1,0:T(8,128)S(1)}, bf16[2,1024,512]{2,1,0:T(8,128)(2,1)S(1)}, bf16[1024,1024]{1,0:T(8,128)(2,1)S(1)}) custom-call(f32[8,128]{1,0:T(8,128)} %bitcast.19, bf16[1024,1024]{1,0:T(8,128)(2,1)} %refs_1_.2), custom_call_target="tpu_custom_call" | custom-call | tf_op jit(solution)/shard_map/pallas_call | solution.py:377
  3.6 0.5 collective-permute-start
  4.1 1.1 %shard_map.78 = f32[4,272,128]{2,1,0:T(8,128)S(1)} custom-call(bf16[1024,1024]{1,0:T(8,128)(2,1)S(1)} %get-tuple-element.14.refs_0_.refs_1_, bf16[2,1024,512]{2,1,0:T(8,128)(2,1)S(1)} %get-tuple-element.15.refs_1_), custom_call_target="tpu_custom_call" | custom-call | tf_op jit(solution)/shard_map/pallas_call | solution.py:377
  5.2 0.0 copy-start
  5.2 0.0 copy-start.4
  5.2 0.1 collective-permute-done
  5.3 0.1 fusion.8
  5.4 5.0 %collective-permute-start.1 = (f16[272,128]{1,0:T(8,128)(2,1)S(1)}, f16[272,128]{1,0:T(8,128)(2,1)S(1)}, u32[]{:S(2)}, u32[]{:S(2)}) collective-permute-start(f16[272,128]{1,0:T(8,128)(2,1)S(1)} %get-tuple-element.30), channel_id=1, source_target_pairs={{0,12},{4,8},{8,4},{12,0},{1,13},{5,9},{9,5},{13,1},{2,14},{6,10},... | collective-permute-start | bytes 208904 | tf_op jit(solution)/shard_map/ppermute | solution.py:388
  10.4 0.6 collective-permute-start.2
  11.1 2.4 %collective-permute-done.1 = f16[272,128]{1,0:T(8,128)(2,1)S(1)} collective-permute-done((f16[272,128]{1,0:T(8,128)(2,1)S(1)}, f16[272,128]{1,0:T(8,128)(2,1)S(1)}, u32[]{:S(2)}, u32[]{:S(2)}) %collective-permute-start.1) | collective-permute-done | bytes 69664 | tf_op jit(solution)/shard_map/ppermute | solution.py:388
  13.4 2.1 %collective-permute-done.3 = f16[272,128]{1,0:T(8,128)(2,1)S(1)} collective-permute-done((f16[272,128]{1,0:T(8,128)(2,1)S(1)}, f16[272,128]{1,0:T(8,128)(2,1)S(1)}, u32[]{:S(2)}, u32[]{:S(2)}) %collective-permute-start.3) | collective-permute-done | bytes 69664 | tf_op jit(solution)/shard_map/ppermute | solution.py:388
  15.6 0.8 %collective-permute-done.2 = f16[272,128]{1,0:T(8,128)(2,1)S(1)} collective-permute-done((f16[272,128]{1,0:T(8,128)(2,1)S(1)}, f16[272,128]{1,0:T(8,128)(2,1)S(1)}, u32[]{:S(2)}, u32[]{:S(2)}) %collective-permute-start.2) | collective-permute-done | bytes 69664 | tf_op jit(solution)/shard_map/ppermute | solution.py:388
  16.4 0.1 fusion.12
  16.5 0.0 copy-start.1
  16.5 1.6 %collective-permute-start.4 = (f16[272,128]{1,0:T(8,128)(2,1)S(1)}, f16[272,128]{1,0:T(8,128)(2,1)S(1)}, u32[]{:S(2)}, u32[]{:S(2)}) collective-permute-start(f16[272,128]{1,0:T(8,128)(2,1)S(1)} %get-tuple-element.28), channel_id=1, source_target_pairs={{0,2},{2,0},{1,3},{3,1},{4,6},{6,4},{5,7},{7,5},{8,10},{10,8},{9,1... | collective-permute-start | bytes 208904 | tf_op jit(solution)/shard_map/ppermute | solution.py:388
  18.1 1.5 %shard_map.79.refs_0_ = f32[272,128]{1,0:T(8,128)S(1)} custom-call(s32[204]{0:T(256)S(1)} %copy-done.4, f32[528,512]{1,0:T(8,128)S(1)} %copy-done), custom_call_target="tpu_custom_call" | custom-call | tf_op jit(solution)/shard_map/pallas_call | solution.py:377
  19.6 1.3 %collective-permute-done.4 = f16[272,128]{1,0:T(8,128)(2,1)S(1)} collective-permute-done((f16[272,128]{1,0:T(8,128)(2,1)S(1)}, f16[272,128]{1,0:T(8,128)(2,1)S(1)}, u32[]{:S(2)}, u32[]{:S(2)}) %collective-permute-start.4) | collective-permute-done | bytes 69664 | tf_op jit(solution)/shard_map/ppermute | solution.py:388
  21.0 2.2 %collective-permute-start.7 = (bf16[272,128]{1,0:T(8,128)(2,1)S(1)}, bf16[272,128]{1,0:T(8,128)(2,1)S(1)}, u32[]{:S(2)}, u32[]{:S(2)}) collective-permute-start(bf16[272,128]{1,0:T(8,128)(2,1)S(1)} %tanh_convert_fusion.refs_1_), channel_id=1, source_target_pairs={{0,8},{4,12},{8,0},{12,4},{1,9},{5,13},{9,1},{13,5},{2,10},{6,14},... | collective-permute-start | bytes 208904 | tf_op jit(solution)/shard_map/ppermute | solution.py:388
  23.2 1.5 %collective-permute-start.6 = (bf16[272,128]{1,0:T(8,128)(2,1)S(1)}, bf16[272,128]{1,0:T(8,128)(2,1)S(1)}, u32[]{:S(2)}, u32[]{:S(2)}) collective-permute-start(bf16[272,128]{1,0:T(8,128)(2,1)S(1)} %tanh_convert_fusion.refs_1_), channel_id=1, source_target_pairs={{0,12},{4,8},{8,4},{12,0},{1,13},{5,9},{9,5},{13,1},{2,14},{6,10},... | collective-permute-start | bytes 208904 | tf_op jit(solution)/shard_map/ppermute | solution.py:388
  24.7 2.3 %collective-permute-done.7.refs_4_ = bf16[272,128]{1,0:T(8,128)(2,1)S(1)} collective-permute-done((bf16[272,128]{1,0:T(8,128)(2,1)S(1)}, bf16[272,128]{1,0:T(8,128)(2,1)S(1)}, u32[]{:S(2)}, u32[]{:S(2)}) %collective-permute-start.7) | collective-permute-done | bytes 69664 | tf_op jit(solution)/shard_map/ppermute | solution.py:388
  27.0 2.3 %collective-permute-done.6.refs_3_ = bf16[272,128]{1,0:T(8,128)(2,1)S(1)} collective-permute-done((bf16[272,128]{1,0:T(8,128)(2,1)S(1)}, bf16[272,128]{1,0:T(8,128)(2,1)S(1)}, u32[]{:S(2)}, u32[]{:S(2)}) %collective-permute-start.6) | collective-permute-done | bytes 69664 | tf_op jit(solution)/shard_map/ppermute | solution.py:388
  29.4 0.4 collective-permute-done.5.refs_2_
  29.7 0.1 collective-permute-start.9
  29.9 1.1 %shard_map.80.refs_2_ = f32[1024,128]{1,0:T(8,128)S(1)} custom-call(bf16[1024,1024]{1,0:T(8,128)(2,1)S(1)} %get-tuple-element.14.refs_0_.refs_1_, bf16[272,128]{1,0:T(8,128)(2,1)S(1)} %tanh_convert_fusion.refs_1_, bf16[272,128]{1,0:T(8,128)(2,1)S(1)} %collective-permute-done.5.refs_2_, bf16[272,128]{1,0:T(8,128)(2,1)S(1)} %collective-permute-done.6.refs_3_, ...), custom_call_target="tpu_custom_call" | custom-call | tf_op jit(solution)/shard_map/pallas_call | solution.py:377
  31.1 3.1 %shard_map.81 = (f32[4,288,128]{2,1,0:T(8,128)S(1)}, bf16[2,1024,512]{2,1,0:T(8,128)(2,1)S(1)}, f32[8,128]{1,0:T(8,128)S(1)}) custom-call(f32[8,128]{1,0:T(8,128)S(1)} %bitcast.20, bf16[1024,1024]{1,0:T(8,128)(2,1)S(1)} %get-tuple-element.14.refs_0_.refs_1_, f32[1024,128]{1,0:T(8,128)S(1)} %shard_map.80.refs_2_, ...), custom_call_target="tpu_custom_call" | custom-call | tf_op jit(solution)/shard_map/pallas_call | solution.py:377
  34.2 0.1 shard_map.83
  34.3 0.4 collective-permute-start.12
  34.7 1.2 %shard_map.82.refs_0_ = f32[4,288,128]{2,1,0:T(8,128)S(1)} custom-call(bf16[1024,1024]{1,0:T(8,128)(2,1)S(1)} %get-tuple-element.14.refs_0_.refs_1_, bf16[2,1024,512]{2,1,0:T(8,128)(2,1)S(1)} %get-tuple-element.18.refs_1_), custom_call_target="tpu_custom_call" | custom-call | tf_op jit(solution)/shard_map/pallas_call | solution.py:377
  36.0 0.1 shard_map.84
  36.1 0.9 %collective-permute-start.15 = (f16[288,128]{1,0:T(8,128)(2,1)S(1)}, f16[288,128]{1,0:T(8,128)(2,1)S(1)}, u32[]{:S(2)}, u32[]{:S(2)}) collective-permute-start(f16[288,128]{1,0:T(8,128)(2,1)S(1)} %convert_element_type.119), channel_id=1, source_target_pairs={{0,8},{4,12},{8,0},{12,4},{1,9},{5,13},{9,1},{13,5},{2,10},{6,14},... | collective-permute-start | bytes 221192 | tf_op jit(solution)/shard_map/ppermute | solution.py:388
  37.0 1.6 %collective-permute-start.14 = (f16[288,128]{1,0:T(8,128)(2,1)S(1)}, f16[288,128]{1,0:T(8,128)(2,1)S(1)}, u32[]{:S(2)}, u32[]{:S(2)}) collective-permute-start(f16[288,128]{1,0:T(8,128)(2,1)S(1)} %convert_element_type.117), channel_id=1, source_target_pairs={{0,4},{4,0},{8,12},{12,8},{1,5},{5,1},{9,13},{13,9},{2,6},{6,2},{1... | collective-permute-start | bytes 221192 | tf_op jit(solution)/shard_map/ppermute | solution.py:388
  38.6 2.0 %collective-permute-start.13 = (f16[288,128]{1,0:T(8,128)(2,1)S(1)}, f16[288,128]{1,0:T(8,128)(2,1)S(1)}, u32[]{:S(2)}, u32[]{:S(2)}) collective-permute-start(f16[288,128]{1,0:T(8,128)(2,1)S(1)} %convert_element_type.115), channel_id=1, source_target_pairs={{0,12},{4,8},{8,4},{12,0},{1,13},{5,9},{9,5},{13,1},{2,14},{6,10},... | collective-permute-start | bytes 221192 | tf_op jit(solution)/shard_map/ppermute | solution.py:388
  40.6 2.1 %collective-permute-done.15 = f16[288,128]{1,0:T(8,128)(2,1)S(1)} collective-permute-done((f16[288,128]{1,0:T(8,128)(2,1)S(1)}, f16[288,128]{1,0:T(8,128)(2,1)S(1)}, u32[]{:S(2)}, u32[]{:S(2)}) %collective-permute-start.15) | collective-permute-done | bytes 73760 | tf_op jit(solution)/shard_map/ppermute | solution.py:388
  42.7 0.1 collective-permute-done.14
  42.9 2.0 %collective-permute-done.13 = f16[288,128]{1,0:T(8,128)(2,1)S(1)} collective-permute-done((f16[288,128]{1,0:T(8,128)(2,1)S(1)}, f16[288,128]{1,0:T(8,128)(2,1)S(1)}, u32[]{:S(2)}, u32[]{:S(2)}) %collective-permute-start.13) | collective-permute-done | bytes 73760 | tf_op jit(solution)/shard_map/ppermute | solution.py:388
  45.0 0.1 reduce-precision_convert_fusion.1
  45.1 1.6 %collective-permute-start.16 = (f16[288,128]{1,0:T(8,128)(2,1)S(1)}, f16[288,128]{1,0:T(8,128)(2,1)S(1)}, u32[]{:S(2)}, u32[]{:S(2)}) collective-permute-start(f16[288,128]{1,0:T(8,128)(2,1)S(1)} %get-tuple-element.33), channel_id=1, source_target_pairs={{0,2},{2,0},{1,3},{3,1},{4,6},{6,4},{5,7},{7,5},{8,10},{10,8},{9,1... | collective-permute-start | bytes 221192 | tf_op jit(solution)/shard_map/ppermute | solution.py:388
  46.6 2.9 %collective-permute-done.16 = f16[288,128]{1,0:T(8,128)(2,1)S(1)} collective-permute-done((f16[288,128]{1,0:T(8,128)(2,1)S(1)}, f16[288,128]{1,0:T(8,128)(2,1)S(1)}, u32[]{:S(2)}, u32[]{:S(2)}) %collective-permute-start.16) | collective-permute-done | bytes 73760 | tf_op jit(solution)/shard_map/ppermute | solution.py:388
  49.6 0.1 fusion.11
  49.7 2.3 %collective-permute-start.19 = (f16[272,128]{1,0:T(8,128)(2,1)S(1)}, f16[272,128]{1,0:T(8,128)(2,1)S(1)}, u32[]{:S(2)}, u32[]{:S(2)}) collective-permute-start(f16[272,128]{1,0:T(8,128)(2,1)S(1)} %get-tuple-element.27), channel_id=1, source_target_pairs={{0,8},{4,12},{8,0},{12,4},{1,9},{5,13},{9,1},{13,5},{2,10},{6,14},... | collective-permute-start | bytes 208904 | tf_op jit(solution)/shard_map/ppermute | solution.py:388
  52.0 1.6 %collective-permute-start.18 = (f16[272,128]{1,0:T(8,128)(2,1)S(1)}, f16[272,128]{1,0:T(8,128)(2,1)S(1)}, u32[]{:S(2)}, u32[]{:S(2)}) collective-permute-start(f16[272,128]{1,0:T(8,128)(2,1)S(1)} %get-tuple-element.27), channel_id=1, source_target_pairs={{0,12},{4,8},{8,4},{12,0},{1,13},{5,9},{9,5},{13,1},{2,14},{6,10},... | collective-permute-start | bytes 208904 | tf_op jit(solution)/shard_map/ppermute | solution.py:388
  53.5 1.4 %collective-permute-done.19 = f16[272,128]{1,0:T(8,128)(2,1)S(1)} collective-permute-done((f16[272,128]{1,0:T(8,128)(2,1)S(1)}, f16[272,128]{1,0:T(8,128)(2,1)S(1)}, u32[]{:S(2)}, u32[]{:S(2)}) %collective-permute-start.19) | collective-permute-done | bytes 69664 | tf_op jit(solution)/shard_map/ppermute | solution.py:388
  55.0 3.2 %collective-permute-done.18 = f16[272,128]{1,0:T(8,128)(2,1)S(1)} collective-permute-done((f16[272,128]{1,0:T(8,128)(2,1)S(1)}, f16[272,128]{1,0:T(8,128)(2,1)S(1)}, u32[]{:S(2)}, u32[]{:S(2)}) %collective-permute-start.18) | collective-permute-done | bytes 69664 | tf_op jit(solution)/shard_map/ppermute | solution.py:388
  58.2 0.4 collective-permute-done.17
  58.6 0.1 collective-permute-start.21
  58.7 0.0 copy-start.3
  58.8 1.1 %shard_map.87.refs_2_ = f32[1024,128]{1,0:T(8,128)S(1)} custom-call(bf16[1024,1024]{1,0:T(8,128)(2,1)S(1)} %get-tuple-element.14.refs_0_.refs_1_, f32[272,128]{1,0:T(8,128)S(1)} %get-tuple-element.26.refs_1_.refs_5_, f32[272,128]{1,0:T(8,128)S(1)} %convert_element_type.125.refs_2_.refs_6_, f32[272,128]{1,0:T(8,128)S(1)} %convert_element_type.126.refs_3_.refs_7_, ...), custom_call_target="tpu_custom_call" | custom-call | tf_op jit(solution)/shard_map/pallas_call | solution.py:377
  60.1 4.4 %shard_map.88 = (f32[8,128]{1,0:T(8,128)}, f32[132,512]{1,0:T(8,128)}) custom-call(f32[8,128]{1,0:T(8,128)S(1)} %get-tuple-element.17.refs_0_, bf16[1024,1024]{1,0:T(8,128)(2,1)S(1)} %get-tuple-element.14.refs_0_.refs_1_, f32[1024,128]{1,0:T(8,128)S(1)} %shard_map.87.refs_2_, s32[528]{0:T(1024)S(1)} %copy-done.2, s32[528]{0:T(1024)S(1)} %copy-done.3, ...), custom_call_target="tpu_custom_call" | custom-call | tf_op jit(solution)/shard_map/pallas_call | solution.py:377
  (45 shorter events, 0.5 us)
Async XLA Ops:
  3.6 1.7 %collective-permute-start = (f16[4,272,128]{2,1,0:T(8,128)(2,1)S(1)}, f16[4,272,128]{2,1,0:T(8,128)(2,1)S(1)}, u32[]{:S(2)}, u32[]{:S(2)}) collective-permute-start(f16[4,272,128]{2,1,0:T(8,128)(2,1)S(1)} %convert_element_type.99), channel_id=1, source_target_pairs={{0,1},{1,0},{2,3},{3,2},{4,5},{5,4},{6,7},{7,6},{8,9},{9,8},{10,11... | collective-permute-start | bytes 835592 | tf_op jit(solution)/shard_map/ppermute | solution.py:388
  5.2 12.9 %copy-start = (f32[528,512]{1,0:T(8,128)S(1)}, f32[528,512]{1,0:T(8,128)}, u32[]{:S(2)}) copy-start(f32[528,512]{1,0:T(8,128)} %refs_1_.3) | copy-start | bytes 3244036
  5.2 12.9 %copy-start.4 = (s32[204]{0:T(256)S(1)}, s32[204]{0:T(256)}, u32[]{:S(2)}) copy-start(s32[204]{0:T(256)} %constant.4.clone.refs_0_) | copy-start | bytes 2452
  5.4 8.0 %collective-permute-start.1 = (f16[272,128]{1,0:T(8,128)(2,1)S(1)}, f16[272,128]{1,0:T(8,128)(2,1)S(1)}, u32[]{:S(2)}, u32[]{:S(2)}) collective-permute-start(f16[272,128]{1,0:T(8,128)(2,1)S(1)} %get-tuple-element.30), channel_id=1, source_target_pairs={{0,12},{4,8},{8,4},{12,0},{1,13},{5,9},{9,5},{13,1},{2,14},{6,10},... | collective-permute-start | bytes 208904 | tf_op jit(solution)/shard_map/ppermute | solution.py:388
  10.4 5.1 %collective-permute-start.3 = (f16[272,128]{1,0:T(8,128)(2,1)S(1)}, f16[272,128]{1,0:T(8,128)(2,1)S(1)}, u32[]{:S(2)}, u32[]{:S(2)}) collective-permute-start(f16[272,128]{1,0:T(8,128)(2,1)S(1)} %get-tuple-element.31), channel_id=1, source_target_pairs={{0,4},{4,0},{8,12},{12,8},{1,5},{5,1},{9,13},{13,9},{2,6},{6,2},{1... | collective-permute-start | bytes 208904 | tf_op jit(solution)/shard_map/ppermute | solution.py:388
  10.4 6.0 %collective-permute-start.2 = (f16[272,128]{1,0:T(8,128)(2,1)S(1)}, f16[272,128]{1,0:T(8,128)(2,1)S(1)}, u32[]{:S(2)}, u32[]{:S(2)}) collective-permute-start(f16[272,128]{1,0:T(8,128)(2,1)S(1)} %get-tuple-element.32), channel_id=1, source_target_pairs={{0,8},{4,12},{8,0},{12,4},{1,9},{5,13},{9,1},{13,5},{2,10},{6,14},... | collective-permute-start | bytes 208904 | tf_op jit(solution)/shard_map/ppermute | solution.py:388
  16.5 14.5 %copy-start.1 = (f32[1024]{0:T(1024)S(1)}, f32[1024]{0:T(1024)}, u32[]{:S(2)}) copy-start(f32[1024]{0:T(1024)} %param.7) | copy-start | bytes 12292
  16.5 4.4 %collective-permute-start.4 = (f16[272,128]{1,0:T(8,128)(2,1)S(1)}, f16[272,128]{1,0:T(8,128)(2,1)S(1)}, u32[]{:S(2)}, u32[]{:S(2)}) collective-permute-start(f16[272,128]{1,0:T(8,128)(2,1)S(1)} %get-tuple-element.28), channel_id=1, source_target_pairs={{0,2},{2,0},{1,3},{3,1},{4,6},{6,4},{5,7},{7,5},{8,10},{10,8},{9,1... | collective-permute-start | bytes 208904 | tf_op jit(solution)/shard_map/ppermute | solution.py:388
  21.0 6.1 %collective-permute-start.7 = (bf16[272,128]{1,0:T(8,128)(2,1)S(1)}, bf16[272,128]{1,0:T(8,128)(2,1)S(1)}, u32[]{:S(2)}, u32[]{:S(2)}) collective-permute-start(bf16[272,128]{1,0:T(8,128)(2,1)S(1)} %tanh_convert_fusion.refs_1_), channel_id=1, source_target_pairs={{0,8},{4,12},{8,0},{12,4},{1,9},{5,13},{9,1},{13,5},{2,10},{6,14},... | collective-permute-start | bytes 208904 | tf_op jit(solution)/shard_map/ppermute | solution.py:388
  23.2 6.2 %collective-permute-start.6 = (bf16[272,128]{1,0:T(8,128)(2,1)S(1)}, bf16[272,128]{1,0:T(8,128)(2,1)S(1)}, u32[]{:S(2)}, u32[]{:S(2)}) collective-permute-start(bf16[272,128]{1,0:T(8,128)(2,1)S(1)} %tanh_convert_fusion.refs_1_), channel_id=1, source_target_pairs={{0,12},{4,8},{8,4},{12,0},{1,13},{5,9},{9,5},{13,1},{2,14},{6,10},... | collective-permute-start | bytes 208904 | tf_op jit(solution)/shard_map/ppermute | solution.py:388
  24.7 5.1 %collective-permute-start.5 = (bf16[272,128]{1,0:T(8,128)(2,1)S(1)}, bf16[272,128]{1,0:T(8,128)(2,1)S(1)}, u32[]{:S(2)}, u32[]{:S(2)}) collective-permute-start(bf16[272,128]{1,0:T(8,128)(2,1)S(1)} %tanh_convert_fusion.refs_1_), channel_id=1, source_target_pairs={{0,4},{4,0},{8,12},{12,8},{1,5},{5,1},{9,13},{13,9},{2,6},{6,2},{1... | collective-permute-start | bytes 208904 | tf_op jit(solution)/shard_map/ppermute | solution.py:388
  24.7 6.3 %collective-permute-start.8 = (bf16[272,128]{1,0:T(8,128)(2,1)S(1)}, bf16[272,128]{1,0:T(8,128)(2,1)S(1)}, u32[]{:S(2)}, u32[]{:S(2)}) collective-permute-start(bf16[272,128]{1,0:T(8,128)(2,1)S(1)} %tanh_convert_fusion.refs_1_), channel_id=1, source_target_pairs={{0,1},{1,0},{2,3},{3,2},{4,5},{5,4},{6,7},{7,6},{8,9},{9,8},{10,11... | collective-permute-start | bytes 208904 | tf_op jit(solution)/shard_map/ppermute | solution.py:388
  27.0 4.0 %collective-permute-start.11 = (bf16[272,128]{1,0:T(8,128)(2,1)S(1)}, bf16[272,128]{1,0:T(8,128)(2,1)S(1)}, u32[]{:S(2)}, u32[]{:S(2)}) collective-permute-start(bf16[272,128]{1,0:T(8,128)(2,1)S(1)} %collective-permute-done.7.refs_4_), channel_id=1, source_target_pairs={{0,1},{1,0},{2,3},{3,2},{4,5},{5,4},{6,7},{7,6},{8,9},{9,8},{10,11... | collective-permute-start | bytes 208904 | tf_op jit(solution)/shard_map/ppermute | solution.py:388
  29.4 1.7 %collective-permute-start.10 = (bf16[272,128]{1,0:T(8,128)(2,1)S(1)}, bf16[272,128]{1,0:T(8,128)(2,1)S(1)}, u32[]{:S(2)}, u32[]{:S(2)}) collective-permute-start(bf16[272,128]{1,0:T(8,128)(2,1)S(1)} %collective-permute-done.6.refs_3_), channel_id=1, source_target_pairs={{0,1},{1,0},{2,3},{3,2},{4,5},{5,4},{6,7},{7,6},{8,9},{9,8},{10,11... | collective-permute-start | bytes 208904 | tf_op jit(solution)/shard_map/ppermute | solution.py:388
  29.7 1.3 %collective-permute-start.9 = (bf16[272,128]{1,0:T(8,128)(2,1)S(1)}, bf16[272,128]{1,0:T(8,128)(2,1)S(1)}, u32[]{:S(2)}, u32[]{:S(2)}) collective-permute-start(bf16[272,128]{1,0:T(8,128)(2,1)S(1)} %collective-permute-done.5.refs_2_), channel_id=1, source_target_pairs={{0,1},{1,0},{2,3},{3,2},{4,5},{5,4},{6,7},{7,6},{8,9},{9,8},{10,11... | collective-permute-start | bytes 208904 | tf_op jit(solution)/shard_map/ppermute | solution.py:388
  34.3 1.6 %collective-permute-start.12 = (f16[4,288,128]{2,1,0:T(8,128)(2,1)S(1)}, f16[4,288,128]{2,1,0:T(8,128)(2,1)S(1)}, u32[]{:S(2)}, u32[]{:S(2)}) collective-permute-start(f16[4,288,128]{2,1,0:T(8,128)(2,1)S(1)} %convert_element_type.113), channel_id=1, source_target_pairs={{0,1},{1,0},{2,3},{3,2},{4,5},{5,4},{6,7},{7,6},{8,9},{9,8},{10,11... | collective-permute-start | bytes 884744 | tf_op jit(solution)/shard_map/ppermute | solution.py:388
  36.1 6.6 %collective-permute-start.15 = (f16[288,128]{1,0:T(8,128)(2,1)S(1)}, f16[288,128]{1,0:T(8,128)(2,1)S(1)}, u32[]{:S(2)}, u32[]{:S(2)}) collective-permute-start(f16[288,128]{1,0:T(8,128)(2,1)S(1)} %convert_element_type.119), channel_id=1, source_target_pairs={{0,8},{4,12},{8,0},{12,4},{1,9},{5,13},{9,1},{13,5},{2,10},{6,14},... | collective-permute-start | bytes 221192 | tf_op jit(solution)/shard_map/ppermute | solution.py:388
  37.0 5.9 %collective-permute-start.14 = (f16[288,128]{1,0:T(8,128)(2,1)S(1)}, f16[288,128]{1,0:T(8,128)(2,1)S(1)}, u32[]{:S(2)}, u32[]{:S(2)}) collective-permute-start(f16[288,128]{1,0:T(8,128)(2,1)S(1)} %convert_element_type.117), channel_id=1, source_target_pairs={{0,4},{4,0},{8,12},{12,8},{1,5},{5,1},{9,13},{13,9},{2,6},{6,2},{1... | collective-permute-start | bytes 221192 | tf_op jit(solution)/shard_map/ppermute | solution.py:388
  38.6 6.3 %collective-permute-start.13 = (f16[288,128]{1,0:T(8,128)(2,1)S(1)}, f16[288,128]{1,0:T(8,128)(2,1)S(1)}, u32[]{:S(2)}, u32[]{:S(2)}) collective-permute-start(f16[288,128]{1,0:T(8,128)(2,1)S(1)} %convert_element_type.115), channel_id=1, source_target_pairs={{0,12},{4,8},{8,4},{12,0},{1,13},{5,9},{9,5},{13,1},{2,14},{6,10},... | collective-permute-start | bytes 221192 | tf_op jit(solution)/shard_map/ppermute | solution.py:388
  45.1 4.4 %collective-permute-start.16 = (f16[288,128]{1,0:T(8,128)(2,1)S(1)}, f16[288,128]{1,0:T(8,128)(2,1)S(1)}, u32[]{:S(2)}, u32[]{:S(2)}) collective-permute-start(f16[288,128]{1,0:T(8,128)(2,1)S(1)} %get-tuple-element.33), channel_id=1, source_target_pairs={{0,2},{2,0},{1,3},{3,1},{4,6},{6,4},{5,7},{7,5},{8,10},{10,8},{9,1... | collective-permute-start | bytes 221192 | tf_op jit(solution)/shard_map/ppermute | solution.py:388
  49.7 5.3 %collective-permute-start.19 = (f16[272,128]{1,0:T(8,128)(2,1)S(1)}, f16[272,128]{1,0:T(8,128)(2,1)S(1)}, u32[]{:S(2)}, u32[]{:S(2)}) collective-permute-start(f16[272,128]{1,0:T(8,128)(2,1)S(1)} %get-tuple-element.27), channel_id=1, source_target_pairs={{0,8},{4,12},{8,0},{12,4},{1,9},{5,13},{9,1},{13,5},{2,10},{6,14},... | collective-permute-start | bytes 208904 | tf_op jit(solution)/shard_map/ppermute | solution.py:388
  52.0 6.2 %collective-permute-start.18 = (f16[272,128]{1,0:T(8,128)(2,1)S(1)}, f16[272,128]{1,0:T(8,128)(2,1)S(1)}, u32[]{:S(2)}, u32[]{:S(2)}) collective-permute-start(f16[272,128]{1,0:T(8,128)(2,1)S(1)} %get-tuple-element.27), channel_id=1, source_target_pairs={{0,12},{4,8},{8,4},{12,0},{1,13},{5,9},{9,5},{13,1},{2,14},{6,10},... | collective-permute-start | bytes 208904 | tf_op jit(solution)/shard_map/ppermute | solution.py:388
  53.5 5.1 %collective-permute-start.17 = (f16[272,128]{1,0:T(8,128)(2,1)S(1)}, f16[272,128]{1,0:T(8,128)(2,1)S(1)}, u32[]{:S(2)}, u32[]{:S(2)}) collective-permute-start(f16[272,128]{1,0:T(8,128)(2,1)S(1)} %get-tuple-element.27), channel_id=1, source_target_pairs={{0,4},{4,0},{8,12},{12,8},{1,5},{5,1},{9,13},{13,9},{2,6},{6,2},{1... | collective-permute-start | bytes 208904 | tf_op jit(solution)/shard_map/ppermute | solution.py:388
  53.5 6.4 %collective-permute-start.20 = (f16[272,128]{1,0:T(8,128)(2,1)S(1)}, f16[272,128]{1,0:T(8,128)(2,1)S(1)}, u32[]{:S(2)}, u32[]{:S(2)}) collective-permute-start(f16[272,128]{1,0:T(8,128)(2,1)S(1)} %get-tuple-element.27), channel_id=1, source_target_pairs={{0,1},{1,0},{2,3},{3,2},{4,5},{5,4},{6,7},{7,6},{8,9},{9,8},{10,11... | collective-permute-start | bytes 208904 | tf_op jit(solution)/shard_map/ppermute | solution.py:388
  55.0 5.0 %collective-permute-start.23 = (f16[272,128]{1,0:T(8,128)(2,1)S(1)}, f16[272,128]{1,0:T(8,128)(2,1)S(1)}, u32[]{:S(2)}, u32[]{:S(2)}) collective-permute-start(f16[272,128]{1,0:T(8,128)(2,1)S(1)} %collective-permute-done.19), channel_id=1, source_target_pairs={{0,1},{1,0},{2,3},{3,2},{4,5},{5,4},{6,7},{7,6},{8,9},{9,8},{10,11... | collective-permute-start | bytes 208904 | tf_op jit(solution)/shard_map/ppermute | solution.py:388
  58.2 1.8 %collective-permute-start.22 = (f16[272,128]{1,0:T(8,128)(2,1)S(1)}, f16[272,128]{1,0:T(8,128)(2,1)S(1)}, u32[]{:S(2)}, u32[]{:S(2)}) collective-permute-start(f16[272,128]{1,0:T(8,128)(2,1)S(1)} %collective-permute-done.18), channel_id=1, source_target_pairs={{0,1},{1,0},{2,3},{3,2},{4,5},{5,4},{6,7},{7,6},{8,9},{9,8},{10,11... | collective-permute-start | bytes 208904 | tf_op jit(solution)/shard_map/ppermute | solution.py:388
  58.6 1.4 %collective-permute-start.21 = (f16[272,128]{1,0:T(8,128)(2,1)S(1)}, f16[272,128]{1,0:T(8,128)(2,1)S(1)}, u32[]{:S(2)}, u32[]{:S(2)}) collective-permute-start(f16[272,128]{1,0:T(8,128)(2,1)S(1)} %collective-permute-done.17), channel_id=1, source_target_pairs={{0,1},{1,0},{2,3},{3,2},{4,5},{5,4},{6,7},{7,6},{8,9},{9,8},{10,11... | collective-permute-start | bytes 208904 | tf_op jit(solution)/shard_map/ppermute | solution.py:388
  58.7 1.3 %copy-start.2 = (s32[528]{0:T(1024)S(1)}, s32[528]{0:T(1024)}, u32[]{:S(2)}) copy-start(s32[528]{0:T(1024)} %refs_3_.1) | copy-start | bytes 6340
  58.7 1.3 %copy-start.3 = (s32[528]{0:T(1024)S(1)}, s32[528]{0:T(1024)}, u32[]{:S(2)}) copy-start(s32[528]{0:T(1024)} %constant.5.clone.refs_4_) | copy-start | bytes 6340

commit v5 on v4

--- a/solution.py
+++ b/solution.py
@@ -14,11 +14,15 @@
 SUB = 16
 TOP = 14.0
 LN2 = math.log(2.0)
-STRIPS, BATCHES, PIECES = 17, 4, 4
+STRIPS, PIECES, BLOCK = 17, 4, 256
 F32, BF16, F16 = jnp.float32, jnp.bfloat16, jnp.float16
 VMEM = pl.BlockSpec(memory_space=pltpu.VMEM)
 SMEM = pl.BlockSpec(memory_space=pltpu.SMEM)
 HBM = pl.BlockSpec(memory_space=pltpu.MemorySpace.HBM)
+
+
+def doubling(first, size):
+    return [1 << k for k in range(first.bit_length() - 1, (size - 1).bit_length())]
 
 
 class Plan:
@@ -31,11 +35,26 @@
         self.group = LANES // self.width
         self.wide = mesh.shape["wide"]
         self.narrow = mesh.shape["narrow"]
+        self.ways, self.near, self.far = self.list_masks()
         self.strips = self.list_strips()
-        self.run = -(-len(self.strips) // self.wide)
+        self.run = -(-len(self.strips) // self.ways)
         self.chunk = self.run * self.width
         self.slots = owner_map.shape[0] // self.wide
-        self.order = [*range(min(2, self.wide)), *range(self.wide - 1, 1, -1)]
+        self.order = [k for k in (0, 2, 1, 3) if k < self.ways]
+        self.sums1 = [k for k in (3, 2, 1) if k < self.ways]
+        self.sums2 = [k for k in (2, 1, 3) if k < self.ways]
+
+    def list_masks(self):
+        bits = [step for step, size in ((1, self.narrow), (self.narrow, self.wide)) if size > 1]
+        near = [0]
+        for bit in bits:
+            near += [mask ^ bit for mask in near]
+        far = [self.narrow * (3 if k == 2 else k) for k in doubling(2, self.wide)]
+        return len(near), near, far + doubling(2, self.narrow)
+
+    def corner(self):
+        x, z = lax.axis_index("narrow"), lax.axis_index("wide")
+        return (x & 1) + ((z ^ (z >> 1)) & 1) * min(2, self.narrow)
 
     def list_strips(self):
         side, per, w = self.stations // LANES, self.group, self.width
@@ -61,7 +80,7 @@
         return row * self.blocks - row * (row - 1) // 2 + col - row
 
     def strip_table(self):
-        table = np.zeros((3, self.run * self.wide), np.int32)
+        table = np.zeros((3, self.run * self.ways), np.int32)
         for k, strip in enumerate(self.strips):
             row, j, first, _, _ = strip[0]
             table[0, k] = self.tile(row, j * self.group)
@@ -139,7 +158,7 @@
 
 
 def pack(plan, j, part, out, most=None):
-    z = lax.axis_index("wide")
+    z = plan.corner()
     w = plan.width
     lane = lax.broadcasted_iota(jnp.int32, (w, LANES), 1)
     for k, strip in enumerate(plan.strips):
@@ -159,8 +178,8 @@
 
 
 def pad(plan, out):
-    z, w = lax.axis_index("wide"), plan.width
-    for k in range(len(plan.strips), plan.run * plan.wide):
+    z, w = plan.corner(), plan.width
+    for k in range(len(plan.strips), plan.run * plan.ways):
         at = k % plan.run * w
         out[(k // plan.run) ^ z, at : at + w, :] = jnp.zeros((w, LANES), F32)
 
@@ -173,11 +192,11 @@
     if most is not None:
         top = jnp.max(jnp.max(most, axis=0, keepdims=True), axis=1, keepdims=True)
         level = jnp.ceil(jnp.log2(jnp.maximum(top, 1e-30))) + (1.0 - TOP)
-        out[:, plan.chunk :, :] = jnp.broadcast_to(level, (plan.wide, SUB, LANES))
+        out[:, plan.chunk :, :] = jnp.broadcast_to(level, (plan.ways, SUB, LANES))
 
 
 def fill_half(plan, load, kernel):
-    z = lax.axis_index("wide")
+    z = plan.corner()
     w = plan.width
     lane = lax.broadcasted_iota(jnp.int32, (w, LANES), 1)
     for k, strip in enumerate(plan.strips):
@@ -196,7 +215,7 @@
         )
 
 
-def contraction(plan, half, green, kernel):
+def contraction(plan, half, green, kernel, at=slice(None)):
     ns = plan.stations
     near = pl.multiple_of(half * ns, LANES)
     far = pl.multiple_of((1 - half) * ns, LANES)
@@ -205,10 +224,10 @@
     for j in range(ns // WIDE_BLOCK):
         end = WIDE_BLOCK * (j + 1)
         block = kernel[:end, end - WIDE_BLOCK : end]
-        u = contract(green[:, pl.ds(near, end)], block, 1, 0)
-        v = contract(green[:, pl.ds(far, end)], block, 1, 0) * sign
-        x = green[:, end - WIDE_BLOCK : end].astype(F32)
-        y = green[:, ns + end - WIDE_BLOCK : ns + end].astype(F32)
+        u = contract(green[at, pl.ds(near, end)], block, 1, 0)
+        v = contract(green[at, pl.ds(far, end)], block, 1, 0) * sign
+        x = green[at, end - WIDE_BLOCK : end].astype(F32)
+        y = green[at, ns + end - WIDE_BLOCK : ns + end].astype(F32)
         part = u * x + v * y
         for left in range(0, WIDE_BLOCK, LANES):
             seen = part[:, left : left + LANES]
@@ -217,9 +236,9 @@
 
 
 def observed_kernel(plan, table, observed, out):
-    core, z = lax.axis_index("tile"), lax.axis_index("wide")
+    core, z = lax.axis_index("tile"), plan.corner()
     left = pl.multiple_of(core * plan.area, LANES)
-    n, count = plan.group, plan.run * plan.wide
+    n, count = plan.group, plan.run * plan.ways
     row = lax.broadcasted_iota(jnp.int32, (n, LANES), 0)
     last = observed.shape[0] // n * n - n
 
@@ -294,9 +313,9 @@
 
 
 def last_kernel(plan, log_ref, green, total, owners, places, *refs):
-    *refs, log_out, residual, kernel, tiles = refs
-    mine, others = refs[: plan.wide], refs[plan.wide :]
-    core, z = lax.axis_index("tile"), lax.axis_index("wide")
+    *refs, log_out, residual, kernel, tiles, sums = refs
+    mine, others = refs[: plan.ways], refs[plan.ways :]
+    core, z, owned = lax.axis_index("tile"), plan.corner(), lax.axis_index("wide") * plan.slots
     n, w, c = plan.group, plan.width, plan.chunk
     for k, left, right in zip(plan.order, mine, others):
         tiles[core, k * c : (k + 1) * c, :] = left[...]
@@ -306,13 +325,12 @@
         lambda slot, at: tiles[1 - core, pl.ds(pl.multiple_of(slot * c + at, w), w), :],
         kernel,
     )
-    new_log(plan, log_ref, green, total, kernel, log_out)
     run = lax.broadcasted_iota(jnp.int32, (w, LANES), 1) // w
 
     def rows_of(first, count):
         found = [None, None]
         for m in range(count):
-            place = places[owners[z * plan.slots + first + m]]
+            place = places[owners[owned + first + m]]
             at = pl.multiple_of(((place >> 16) ^ z) * c + ((place >> 4) & 4095), w)
             shift = ((n - 1 - m - (place & 15)) & (n - 1)) * w
             for h in range(2):
@@ -327,7 +345,23 @@
             residual[pl.ds(first, n), k * LANES : (k + 1) * LANES] = piece
 
     whole = plan.slots // n
-    unrolled(whole, BATCHES, batch)
+    steps = plan.points // BLOCK
+    batches, rows = whole // steps, BLOCK // LANES
+
+    def step(p, carry):
+        at = pl.ds(pl.multiple_of(p * BLOCK, BLOCK), BLOCK)
+        part = row_sums(total[at, :] + contraction(plan, 1 - core, green, kernel, at))
+        for i in range(rows):
+            sums[pl.ds(p * rows + i, 1), :] = part[i : i + 1, :]
+        for k in range(batches):
+            batch(p * batches + k)
+        return carry
+
+    lax.fori_loop(0, steps, step, 0)
+    for i in range(batches * steps, whole):
+        batch(i)
+    log_now = log_ref[...]
+    log_out[...] = log_now - 0.5 * jnp.exp(log_now) * sums[...]
     rest = plan.slots - whole * n
     if rest:
         for k, piece in enumerate(rows_of(whole * n, rest)):
@@ -337,7 +371,7 @@
 def scale_kernel(plan, send, out):
     c = plan.chunk
     factor = jnp.exp(send[0, c : c + 1, :] * -LN2)
-    for k in range(plan.wide):
+    for k in range(plan.ways):
         out[k, :c, :] = send[k, :c, :] * factor
         out[k, c:, :] = send[k, c:, :]
 
@@ -364,9 +398,10 @@
     out[c:, :] = jnp.broadcast_to(level, (SUB, LANES))
 
 
-def tanh_kernel(plan, target, left, right, out):
+def tanh_kernel(plan, target, *refs):
+    *parts, out = refs
     c = plan.chunk
-    total = sum(x[:c, :] * jnp.exp(x[c : c + 1, :] * LN2) for x in (left, right))
+    total = sum(x[:c, :] * jnp.exp(x[c : c + 1, :] * LN2) for x in parts)
     out[...] = jnp.tanh(total - target[...])
 
 
@@ -384,8 +419,13 @@
     )(*arguments)
 
 
-def exchange(x, axis, mask, size):
-    return lax.ppermute(x, axis, [(i, i ^ mask) for i in range(size)])
+def swap_cores(x):
+    return lax.ppermute(x, "tile", [(0, 1), (1, 0)])
+
+
+def exchange(plan, x, mask):
+    pairs = [(i, i ^ mask) for i in range(plan.wide * plan.narrow)]
+    return lax.ppermute(x, ("wide", "narrow"), pairs)
 
 
 def to_half(x):
@@ -393,15 +433,13 @@
 
 
 def bounded_residual(plan, own, recv, target):
-    sums = [own[k] + recv[k] for k in range(plan.wide)]
+    sums = [own[k] + recv[k] for k in range(plan.ways)]
     total = sums[0]
-    for x in [exchange(sums[k].astype(F16), "wide", k, plan.wide) for k in range(plan.wide - 1, 0, -1)]:
+    for x in [exchange(plan, sums[k].astype(F16), plan.near[k]) for k in plan.sums1]:
         total = total + x.astype(F32)
-    mask = 1
-    while mask < plan.narrow:
+    for mask in plan.far:
         total = to_half(total)
-        total = total + exchange(total.astype(F16), "narrow", mask, plan.narrow).astype(F32)
-        mask *= 2
+        total = total + exchange(plan, total.astype(F16), mask).astype(F32)
     return jnp.tanh(total - target)
 
 
@@ -411,26 +449,23 @@
     def join(*parts):
         return call(sum_kernel, plan, message, [], parts, [VMEM] * len(parts))
 
-    sums = call(join_kernel, plan, (message,) * plan.wide, [], (own, recv), [VMEM] * 2)
+    sums = call(join_kernel, plan, (message,) * plan.ways, [], (own, recv), [VMEM] * 2)
     parts = [sums[0]]
-    for k in [*range(plan.wide - 1, 2, -1), *range(1, min(3, plan.wide))]:
-        parts.append(exchange(sums[k].astype(F16), "wide", k, plan.wide).astype(F32))
-    total = to_half(join(*parts))
-    mask = 1
-    while mask < plan.narrow:
-        other = exchange(total.astype(F16), "narrow", mask, plan.narrow).astype(F32)
-        mask *= 2
-        if mask < plan.narrow:
-            total = to_half(join(total, other))
+    for k in plan.sums2:
+        parts.append(exchange(plan, sums[k].astype(F16), plan.near[k]).astype(F32))
+    parts = [join(*parts)]
+    for mask in plan.far:
+        total = to_half(join(*parts) if len(parts) > 1 else parts[0])
+        parts = [total, exchange(plan, total.astype(F16), mask).astype(F32)]
     return call(
         tanh_kernel, plan, jax.ShapeDtypeStruct(target.shape, F32), [],
-        (target, total, other), [VMEM] * 3,
+        (target, *parts), [VMEM] * (1 + len(parts)),
     )
 
 
 def spread(plan, chunk):
-    mine = [chunk] + [exchange(chunk, "wide", k, plan.wide) for k in plan.order[1:]]
-    return mine, [exchange(x, "tile", 1, 2) for x in mine]
+    mine = [chunk] + [exchange(plan, chunk, plan.near[k]) for k in plan.order[1:]]
+    return mine, [swap_cores(x) for x in mine]
 
 
 def on_device(mesh, green, log_strength, observed, owner_map):
@@ -441,7 +476,7 @@
     weighted_shape = shape((2, plan.points, plan.stations), BF16)
     total_shape = shape((plan.points, LANES), F32)
     kernel = pltpu.VMEM((plan.stations, plan.stations), BF16)
-    stack = pltpu.VMEM((plan.wide, plan.chunk, LANES), BF16)
+    stack = pltpu.VMEM((plan.ways, plan.chunk, LANES), BF16)
 
     def own_product(weighted, like):
         return call(own_product_kernel, plan, shape(like.shape, F32), [], (green, weighted), [VMEM] * 2)
@@ -458,7 +493,7 @@
     )
     send, weighted, green = call(
         first_kernel, plan,
-        (shape((plan.wide, plan.chunk, LANES), F32), weighted_shape, shape(green.shape, BF16)),
+        (shape((plan.ways, plan.chunk, LANES), F32), weighted_shape, shape(green.shape, BF16)),
         [
             pltpu.VMEM(log_now.shape, F32),
             pltpu.SemaphoreType.DMA((PIECES + 1,)),
@@ -466,28 +501,31 @@
         [pltpu.with_memory_space_constraint(x, pltpu.MemorySpace.HBM) for x in (log_now, green)],
         [HBM] * 2,
     )
-    recv = exchange(send.astype(F16), "tile", 1, 2).astype(F32)
+    recv = swap_cores(send.astype(F16)).astype(F32)
     residual = bounded_residual(plan, own_product(weighted, send), recv, target)
     for _ in range(STEPS - 1):
         mine, others = spread(plan, residual.astype(BF16))
-        levelled = shape((plan.wide, plan.chunk + SUB, LANES), F32)
+        levelled = shape((plan.ways, plan.chunk + SUB, LANES), F32)
         send, weighted, log_now = call(
             middle_kernel, plan, (levelled, weighted_shape, log_shape), [kernel, stack],
             (log_now, green, own_contraction(mine), *others), [VMEM] * (3 + len(others)),
         )
         scaled = call(scale_kernel, plan, levelled, [], (send,), [VMEM])
-        recv = exchange(scaled.astype(F16), "tile", 1, 2).astype(F32)
+        recv = swap_cores(scaled.astype(F16)).astype(F32)
         residual = scaled_residual(plan, own_product(weighted, send), recv, target)
     mine, others = spread(plan, to_half(residual).astype(F16))
     mine = [x.astype(F32) for x in mine]
     log_now, owned = call(
         last_kernel, plan, (log_shape, shape((plan.slots, observed.shape[1]), F32)),
-        [kernel, pltpu.VMEM((2, plan.wide * plan.chunk, LANES), F32)],
+        [
+            kernel, pltpu.VMEM((2, plan.ways * plan.chunk, LANES), F32),
+            pltpu.VMEM(log_now.shape, F32),
+        ],
         (
             log_now, green, own_contraction(mine), owner_map, jnp.asarray(plan.tile_places()),
             *mine, *[x.astype(F32) for x in others],
         ),
-        [VMEM] * 3 + [SMEM] * 2 + [VMEM] * (2 * plan.wide),
+        [VMEM] * 3 + [SMEM] * 2 + [VMEM] * (2 * plan.ways),
     )
     return log_now.reshape(-1), owned
 

time: 64.6 us -> 59 us (0.913)
  waiting for transfers between devices: 23.9 us -> 18.1 us
  starting transfers between devices: 22.2 us -> 22.9 us
    ppermute x24, waiting for transfers between devices: 23.9 us -> 18.1 us  [the longest x14 17.9 us: exchange(): return lax.ppermute(x, ('wide', 'narrow'), pairs)]
    ppermute x24, starting transfers between devices: 22.2 us -> 22.9 us  [the longest x14 21.3 us: exchange(): return lax.ppermute(x, ('wide', 'narrow'), pairs)]
  transfers between devices with their start and end apart: 24 -> 24, of which waited for: 15 -> 16; matrix products, arithmetic and copies ran while one was open for 0% -> 0% of each run, Pallas kernels for 9% -> 10%
where the time goes in v5:
time: 59 us; the launch traced here: 58.8 us
  starting transfers between devices  22.9 us (39%)
  waiting for transfers between devices  18.1 us (31%)
  Pallas kernels  16.1 us (27%)
  between operations  0.96 us (2%)
  other arithmetic  0.71 us (1%)
    ppermute x14, starting transfers between devices, exchange(): return lax.ppermute(x, ('wide', 'narrow'), pairs)  21.3 us
    ppermute x14, waiting for transfers between devices, exchange(): return lax.ppermute(x, ('wide', 'narrow'), pairs)  17.9 us
    pallas_call x12, Pallas kernels, call(): pl.pallas_call(body, in_specs=specs, out_specs=jax.tree.map(lambda _: VME...  16.1 us
    ppermute x10, starting transfers between devices, swap_cores(): return lax.ppermute(x, 'tile', [(0, 1), (1, 0)])  1.63 us
  transfers between devices with their start and end apart: 24, of which 16 were waited for; matrix products, arithmetic and copies ran while one was open for 0% of the time, Pallas kernels for 10%

profile of v5, /device:TPU:0, one launch (start us, length us, event | category | flops | bytes accessed | tf_op | source)
XLA Modules:
  0.0 58.8 jit_solution(10653336301403559041)
XLA Ops:
  0.6 2.9 %shard_map.77 = (f32[4,272,128]{2,1,0:T(8,128)S(1)}, bf16[2,1024,512]{2,1,0:T(8,128)(2,1)S(1)}, bf16[1024,1024]{1,0:T(8,128)(2,1)S(1)}) custom-call(f32[8,128]{1,0:T(8,128)} %bitcast.19, bf16[1024,1024]{1,0:T(8,128)(2,1)} %refs_1_.2), custom_call_target="tpu_custom_call" | custom-call | tf_op jit(solution)/shard_map/pallas_call | solution.py:412
  3.6 0.5 collective-permute-start
  4.1 1.1 %shard_map.78 = f32[4,272,128]{2,1,0:T(8,128)S(1)} custom-call(bf16[1024,1024]{1,0:T(8,128)(2,1)S(1)} %get-tuple-element.14.refs_0_.refs_1_, bf16[2,1024,512]{2,1,0:T(8,128)(2,1)S(1)} %get-tuple-element.15.refs_1_), custom_call_target="tpu_custom_call" | custom-call | tf_op jit(solution)/shard_map/pallas_call | solution.py:412
  5.2 0.1 collective-permute-done
  5.3 0.1 fusion.8
  5.4 3.9 %collective-permute-start.1 = (f16[272,128]{1,0:T(8,128)(2,1)S(1)}, f16[272,128]{1,0:T(8,128)(2,1)S(1)}, u32[]{:S(2)}, u32[]{:S(2)}) collective-permute-start(f16[272,128]{1,0:T(8,128)(2,1)S(1)} %get-tuple-element.30), channel_id=1, source_target_pairs={{0,6},{2,4},{4,2},{6,0},{8,14},{10,12},{12,10},{14,8},{1,7},{3,5},... | collective-permute-start | bytes 208904 | tf_op jit(solution)/shard_map/ppermute | solution.py:428
  9.3 0.5 collective-permute-start.3
  9.9 0.1 collective-permute-start.2
  10.0 1.9 %collective-permute-done.1 = f16[272,128]{1,0:T(8,128)(2,1)S(1)} collective-permute-done((f16[272,128]{1,0:T(8,128)(2,1)S(1)}, f16[272,128]{1,0:T(8,128)(2,1)S(1)}, u32[]{:S(2)}, u32[]{:S(2)}) %collective-permute-start.1) | collective-permute-done | bytes 69664 | tf_op jit(solution)/shard_map/ppermute | solution.py:428
  11.9 1.8 %collective-permute-done.3 = f16[272,128]{1,0:T(8,128)(2,1)S(1)} collective-permute-done((f16[272,128]{1,0:T(8,128)(2,1)S(1)}, f16[272,128]{1,0:T(8,128)(2,1)S(1)}, u32[]{:S(2)}, u32[]{:S(2)}) %collective-permute-start.3) | collective-permute-done | bytes 69664 | tf_op jit(solution)/shard_map/ppermute | solution.py:428
  13.7 0.5 collective-permute-done.2
  14.2 0.1 fusion.12
  14.3 3.0 %collective-permute-start.4 = (f16[272,128]{1,0:T(8,128)(2,1)S(1)}, f16[272,128]{1,0:T(8,128)(2,1)S(1)}, u32[]{:S(2)}, u32[]{:S(2)}) collective-permute-start(f16[272,128]{1,0:T(8,128)(2,1)S(1)} %get-tuple-element.28), channel_id=1, source_target_pairs={{0,12},{2,14},{4,8},{6,10},{8,4},{10,6},{12,0},{14,2},{1,13},{3,15... | collective-permute-start | bytes 208904 | tf_op jit(solution)/shard_map/ppermute | solution.py:428
  17.3 1.5 %shard_map.79.refs_0_ = f32[272,128]{1,0:T(8,128)S(1)} custom-call(s32[204]{0:T(256)S(1)} %copy-done.4, f32[528,512]{1,0:T(8,128)S(1)} %copy-done), custom_call_target="tpu_custom_call" | custom-call | tf_op jit(solution)/shard_map/pallas_call | solution.py:412
  18.8 1.7 %collective-permute-done.4 = f16[272,128]{1,0:T(8,128)(2,1)S(1)} collective-permute-done((f16[272,128]{1,0:T(8,128)(2,1)S(1)}, f16[272,128]{1,0:T(8,128)(2,1)S(1)}, u32[]{:S(2)}, u32[]{:S(2)}) %collective-permute-start.4) | collective-permute-done | bytes 69664 | tf_op jit(solution)/shard_map/ppermute | solution.py:428
  20.5 0.6 collective-permute-start.7
  21.1 1.3 %collective-permute-start.6 = (bf16[272,128]{1,0:T(8,128)(2,1)S(1)}, bf16[272,128]{1,0:T(8,128)(2,1)S(1)}, u32[]{:S(2)}, u32[]{:S(2)}) collective-permute-start(bf16[272,128]{1,0:T(8,128)(2,1)S(1)} %tanh_convert_fusion.refs_1_), channel_id=1, source_target_pairs={{0,2},{2,0},{4,6},{6,4},{8,10},{10,8},{12,14},{14,12},{1,3},{3,1},... | collective-permute-start | bytes 208904 | tf_op jit(solution)/shard_map/ppermute | solution.py:428
  22.5 1.6 %collective-permute-start.5 = (bf16[272,128]{1,0:T(8,128)(2,1)S(1)}, bf16[272,128]{1,0:T(8,128)(2,1)S(1)}, u32[]{:S(2)}, u32[]{:S(2)}) collective-permute-start(bf16[272,128]{1,0:T(8,128)(2,1)S(1)} %tanh_convert_fusion.refs_1_), channel_id=1, source_target_pairs={{0,4},{2,6},{4,0},{6,2},{8,12},{10,14},{12,8},{14,10},{1,5},{3,7},... | collective-permute-start | bytes 208904 | tf_op jit(solution)/shard_map/ppermute | solution.py:428
  24.1 1.8 %collective-permute-done.7.refs_4_ = bf16[272,128]{1,0:T(8,128)(2,1)S(1)} collective-permute-done((bf16[272,128]{1,0:T(8,128)(2,1)S(1)}, bf16[272,128]{1,0:T(8,128)(2,1)S(1)}, u32[]{:S(2)}, u32[]{:S(2)}) %collective-permute-start.7) | collective-permute-done | bytes 69664 | tf_op jit(solution)/shard_map/ppermute | solution.py:428
  25.9 0.2 collective-permute-done.6.refs_3_
  26.2 0.3 collective-permute-start.10
  26.4 0.3 collective-permute-done.5.refs_2_
  26.8 1.1 %shard_map.80.refs_2_ = f32[1024,128]{1,0:T(8,128)S(1)} custom-call(bf16[1024,1024]{1,0:T(8,128)(2,1)S(1)} %get-tuple-element.14.refs_0_.refs_1_, bf16[272,128]{1,0:T(8,128)(2,1)S(1)} %tanh_convert_fusion.refs_1_, bf16[272,128]{1,0:T(8,128)(2,1)S(1)} %collective-permute-done.5.refs_2_, bf16[272,128]{1,0:T(8,128)(2,1)S(1)} %collective-permute-done.6.refs_3_, ...), custom_call_target="tpu_custom_call" | custom-call | tf_op jit(solution)/shard_map/pallas_call | solution.py:412
  27.9 0.1 collective-permute-done.9.refs_4_
  28.0 3.1 %shard_map.81 = (f32[4,288,128]{2,1,0:T(8,128)S(1)}, bf16[2,1024,512]{2,1,0:T(8,128)(2,1)S(1)}, f32[8,128]{1,0:T(8,128)S(1)}) custom-call(f32[8,128]{1,0:T(8,128)S(1)} %bitcast.20, bf16[1024,1024]{1,0:T(8,128)(2,1)S(1)} %get-tuple-element.14.refs_0_.refs_1_, f32[1024,128]{1,0:T(8,128)S(1)} %shard_map.80.refs_2_, ...), custom_call_target="tpu_custom_call" | custom-call | tf_op jit(solution)/shard_map/pallas_call | solution.py:412
  31.1 0.1 shard_map.83
  31.2 0.5 collective-permute-start.12
  31.7 1.2 %shard_map.82.refs_0_ = f32[4,288,128]{2,1,0:T(8,128)S(1)} custom-call(bf16[1024,1024]{1,0:T(8,128)(2,1)S(1)} %get-tuple-element.14.refs_0_.refs_1_, bf16[2,1024,512]{2,1,0:T(8,128)(2,1)S(1)} %get-tuple-element.18.refs_1_), custom_call_target="tpu_custom_call" | custom-call | tf_op jit(solution)/shard_map/pallas_call | solution.py:412
  33.0 0.1 shard_map.84
  33.1 2.6 %collective-permute-start.15 = (f16[288,128]{1,0:T(8,128)(2,1)S(1)}, f16[288,128]{1,0:T(8,128)(2,1)S(1)}, u32[]{:S(2)}, u32[]{:S(2)}) collective-permute-start(f16[288,128]{1,0:T(8,128)(2,1)S(1)} %convert_element_type.119), channel_id=1, source_target_pairs={{0,6},{2,4},{4,2},{6,0},{8,14},{10,12},{12,10},{14,8},{1,7},{3,5},... | collective-permute-start | bytes 221192 | tf_op jit(solution)/shard_map/ppermute | solution.py:428
  35.8 0.5 collective-permute-start.14
  36.3 0.5 collective-permute-start.13
  36.8 1.9 %collective-permute-done.15 = f16[288,128]{1,0:T(8,128)(2,1)S(1)} collective-permute-done((f16[288,128]{1,0:T(8,128)(2,1)S(1)}, f16[288,128]{1,0:T(8,128)(2,1)S(1)}, u32[]{:S(2)}, u32[]{:S(2)}) %collective-permute-start.15) | collective-permute-done | bytes 73760 | tf_op jit(solution)/shard_map/ppermute | solution.py:428
  38.7 1.5 %collective-permute-done.14 = f16[288,128]{1,0:T(8,128)(2,1)S(1)} collective-permute-done((f16[288,128]{1,0:T(8,128)(2,1)S(1)}, f16[288,128]{1,0:T(8,128)(2,1)S(1)}, u32[]{:S(2)}, u32[]{:S(2)}) %collective-permute-start.14) | collective-permute-done | bytes 73760 | tf_op jit(solution)/shard_map/ppermute | solution.py:428
  40.2 0.5 collective-permute-done.13
  40.8 0.1 reduce-precision_convert_fusion.1
  40.9 3.0 %collective-permute-start.16 = (f16[288,128]{1,0:T(8,128)(2,1)S(1)}, f16[288,128]{1,0:T(8,128)(2,1)S(1)}, u32[]{:S(2)}, u32[]{:S(2)}) collective-permute-start(f16[288,128]{1,0:T(8,128)(2,1)S(1)} %get-tuple-element.33), channel_id=1, source_target_pairs={{0,12},{2,14},{4,8},{6,10},{8,4},{10,6},{12,0},{14,2},{1,13},{3,15... | collective-permute-start | bytes 221192 | tf_op jit(solution)/shard_map/ppermute | solution.py:428
  43.9 3.2 %collective-permute-done.16 = f16[288,128]{1,0:T(8,128)(2,1)S(1)} collective-permute-done((f16[288,128]{1,0:T(8,128)(2,1)S(1)}, f16[288,128]{1,0:T(8,128)(2,1)S(1)}, u32[]{:S(2)}, u32[]{:S(2)}) %collective-permute-start.16) | collective-permute-done | bytes 73760 | tf_op jit(solution)/shard_map/ppermute | solution.py:428
  47.2 0.1 fusion.11
  47.3 0.8 %collective-permute-start.19 = (f16[272,128]{1,0:T(8,128)(2,1)S(1)}, f16[272,128]{1,0:T(8,128)(2,1)S(1)}, u32[]{:S(2)}, u32[]{:S(2)}) collective-permute-start(f16[272,128]{1,0:T(8,128)(2,1)S(1)} %get-tuple-element.27), channel_id=1, source_target_pairs={{0,6},{2,4},{4,2},{6,0},{8,14},{10,12},{12,10},{14,8},{1,7},{3,5},... | collective-permute-start | bytes 208904 | tf_op jit(solution)/shard_map/ppermute | solution.py:428
  48.1 0.9 %collective-permute-start.18 = (f16[272,128]{1,0:T(8,128)(2,1)S(1)}, f16[272,128]{1,0:T(8,128)(2,1)S(1)}, u32[]{:S(2)}, u32[]{:S(2)}) collective-permute-start(f16[272,128]{1,0:T(8,128)(2,1)S(1)} %get-tuple-element.27), channel_id=1, source_target_pairs={{0,2},{2,0},{4,6},{6,4},{8,10},{10,8},{12,14},{14,12},{1,3},{3,1},... | collective-permute-start | bytes 208904 | tf_op jit(solution)/shard_map/ppermute | solution.py:428
  48.9 1.9 %collective-permute-start.17 = (f16[272,128]{1,0:T(8,128)(2,1)S(1)}, f16[272,128]{1,0:T(8,128)(2,1)S(1)}, u32[]{:S(2)}, u32[]{:S(2)}) collective-permute-start(f16[272,128]{1,0:T(8,128)(2,1)S(1)} %get-tuple-element.27), channel_id=1, source_target_pairs={{0,4},{2,6},{4,0},{6,2},{8,12},{10,14},{12,8},{14,10},{1,5},{3,7},... | collective-permute-start | bytes 208904 | tf_op jit(solution)/shard_map/ppermute | solution.py:428
  50.8 1.8 %collective-permute-done.19 = f16[272,128]{1,0:T(8,128)(2,1)S(1)} collective-permute-done((f16[272,128]{1,0:T(8,128)(2,1)S(1)}, f16[272,128]{1,0:T(8,128)(2,1)S(1)}, u32[]{:S(2)}, u32[]{:S(2)}) %collective-permute-start.19) | collective-permute-done | bytes 69664 | tf_op jit(solution)/shard_map/ppermute | solution.py:428
  52.7 0.5 collective-permute-done.18
  53.2 0.2 collective-permute-done.17
  53.3 0.3 collective-permute-start.21
  53.7 1.1 %shard_map.87.refs_2_ = f32[1024,128]{1,0:T(8,128)S(1)} custom-call(bf16[1024,1024]{1,0:T(8,128)(2,1)S(1)} %get-tuple-element.14.refs_0_.refs_1_, f32[272,128]{1,0:T(8,128)S(1)} %get-tuple-element.26.refs_1_.refs_5_, f32[272,128]{1,0:T(8,128)S(1)} %convert_element_type.125.refs_2_.refs_6_, f32[272,128]{1,0:T(8,128)S(1)} %convert_element_type.126.refs_3_.refs_7_, ...), custom_call_target="tpu_custom_call" | custom-call | tf_op jit(solution)/shard_map/pallas_call | solution.py:412
  55.0 3.8 %shard_map.88 = (f32[8,128]{1,0:T(8,128)}, f32[132,512]{1,0:T(8,128)}) custom-call(f32[8,128]{1,0:T(8,128)S(1)} %get-tuple-element.17.refs_0_, bf16[1024,1024]{1,0:T(8,128)(2,1)S(1)} %get-tuple-element.14.refs_0_.refs_1_, f32[1024,128]{1,0:T(8,128)S(1)} %shard_map.87.refs_2_, s32[528]{0:T(1024)S(1)} %copy-done.2, s32[528]{0:T(1024)S(1)} %copy-done.3, ...), custom_call_target="tpu_custom_call" | custom-call | tf_op jit(solution)/shard_map/pallas_call | solution.py:412
  (45 shorter events, 0.6 us)
Async XLA Ops:
  3.6 1.7 %collective-permute-start = (f16[4,272,128]{2,1,0:T(8,128)(2,1)S(1)}, f16[4,272,128]{2,1,0:T(8,128)(2,1)S(1)}, u32[]{:S(2)}, u32[]{:S(2)}) collective-permute-start(f16[4,272,128]{2,1,0:T(8,128)(2,1)S(1)} %convert_element_type.99), channel_id=1, source_target_pairs={{0,1},{1,0},{2,3},{3,2},{4,5},{5,4},{6,7},{7,6},{8,9},{9,8},{10,11... | collective-permute-start | bytes 835592 | tf_op jit(solution)/shard_map/ppermute | solution.py:423
  5.2 12.1 %copy-start = (f32[528,512]{1,0:T(8,128)S(1)}, f32[528,512]{1,0:T(8,128)}, u32[]{:S(2)}) copy-start(f32[528,512]{1,0:T(8,128)} %refs_1_.3) | copy-start | bytes 3244036
  5.2 12.1 %copy-start.4 = (s32[204]{0:T(256)S(1)}, s32[204]{0:T(256)}, u32[]{:S(2)}) copy-start(s32[204]{0:T(256)} %constant.4.clone.refs_0_) | copy-start | bytes 2452
  5.4 6.4 %collective-permute-start.1 = (f16[272,128]{1,0:T(8,128)(2,1)S(1)}, f16[272,128]{1,0:T(8,128)(2,1)S(1)}, u32[]{:S(2)}, u32[]{:S(2)}) collective-permute-start(f16[272,128]{1,0:T(8,128)(2,1)S(1)} %get-tuple-element.30), channel_id=1, source_target_pairs={{0,6},{2,4},{4,2},{6,0},{8,14},{10,12},{12,10},{14,8},{1,7},{3,5},... | collective-permute-start | bytes 208904 | tf_op jit(solution)/shard_map/ppermute | solution.py:428
  9.3 4.3 %collective-permute-start.3 = (f16[272,128]{1,0:T(8,128)(2,1)S(1)}, f16[272,128]{1,0:T(8,128)(2,1)S(1)}, u32[]{:S(2)}, u32[]{:S(2)}) collective-permute-start(f16[272,128]{1,0:T(8,128)(2,1)S(1)} %get-tuple-element.31), channel_id=1, source_target_pairs={{0,2},{2,0},{4,6},{6,4},{8,10},{10,8},{12,14},{14,12},{1,3},{3,1},... | collective-permute-start | bytes 208904 | tf_op jit(solution)/shard_map/ppermute | solution.py:428
  9.9 4.3 %collective-permute-start.2 = (f16[272,128]{1,0:T(8,128)(2,1)S(1)}, f16[272,128]{1,0:T(8,128)(2,1)S(1)}, u32[]{:S(2)}, u32[]{:S(2)}) collective-permute-start(f16[272,128]{1,0:T(8,128)(2,1)S(1)} %get-tuple-element.32), channel_id=1, source_target_pairs={{0,4},{2,6},{4,0},{6,2},{8,12},{10,14},{12,8},{14,10},{1,5},{3,7},... | collective-permute-start | bytes 208904 | tf_op jit(solution)/shard_map/ppermute | solution.py:428
  14.3 13.7 %copy-start.1 = (f32[1024]{0:T(1024)S(1)}, f32[1024]{0:T(1024)}, u32[]{:S(2)}) copy-start(f32[1024]{0:T(1024)} %param.7) | copy-start | bytes 12292
  14.3 6.2 %collective-permute-start.4 = (f16[272,128]{1,0:T(8,128)(2,1)S(1)}, f16[272,128]{1,0:T(8,128)(2,1)S(1)}, u32[]{:S(2)}, u32[]{:S(2)}) collective-permute-start(f16[272,128]{1,0:T(8,128)(2,1)S(1)} %get-tuple-element.28), channel_id=1, source_target_pairs={{0,12},{2,14},{4,8},{6,10},{8,4},{10,6},{12,0},{14,2},{1,13},{3,15... | collective-permute-start | bytes 208904 | tf_op jit(solution)/shard_map/ppermute | solution.py:428
  20.5 5.4 %collective-permute-start.7 = (bf16[272,128]{1,0:T(8,128)(2,1)S(1)}, bf16[272,128]{1,0:T(8,128)(2,1)S(1)}, u32[]{:S(2)}, u32[]{:S(2)}) collective-permute-start(bf16[272,128]{1,0:T(8,128)(2,1)S(1)} %tanh_convert_fusion.refs_1_), channel_id=1, source_target_pairs={{0,6},{2,4},{4,2},{6,0},{8,14},{10,12},{12,10},{14,8},{1,7},{3,5},... | collective-permute-start | bytes 208904 | tf_op jit(solution)/shard_map/ppermute | solution.py:428
  21.1 5.1 %collective-permute-start.6 = (bf16[272,128]{1,0:T(8,128)(2,1)S(1)}, bf16[272,128]{1,0:T(8,128)(2,1)S(1)}, u32[]{:S(2)}, u32[]{:S(2)}) collective-permute-start(bf16[272,128]{1,0:T(8,128)(2,1)S(1)} %tanh_convert_fusion.refs_1_), channel_id=1, source_target_pairs={{0,2},{2,0},{4,6},{6,4},{8,10},{10,8},{12,14},{14,12},{1,3},{3,1},... | collective-permute-start | bytes 208904 | tf_op jit(solution)/shard_map/ppermute | solution.py:428
  22.5 4.3 %collective-permute-start.5 = (bf16[272,128]{1,0:T(8,128)(2,1)S(1)}, bf16[272,128]{1,0:T(8,128)(2,1)S(1)}, u32[]{:S(2)}, u32[]{:S(2)}) collective-permute-start(bf16[272,128]{1,0:T(8,128)(2,1)S(1)} %tanh_convert_fusion.refs_1_), channel_id=1, source_target_pairs={{0,4},{2,6},{4,0},{6,2},{8,12},{10,14},{12,8},{14,10},{1,5},{3,7},... | collective-permute-start | bytes 208904 | tf_op jit(solution)/shard_map/ppermute | solution.py:428
  24.1 3.8 %collective-permute-start.8 = (bf16[272,128]{1,0:T(8,128)(2,1)S(1)}, bf16[272,128]{1,0:T(8,128)(2,1)S(1)}, u32[]{:S(2)}, u32[]{:S(2)}) collective-permute-start(bf16[272,128]{1,0:T(8,128)(2,1)S(1)} %tanh_convert_fusion.refs_1_), channel_id=1, source_target_pairs={{0,1},{1,0},{2,3},{3,2},{4,5},{5,4},{6,7},{7,6},{8,9},{9,8},{10,11... | collective-permute-start | bytes 208904 | tf_op jit(solution)/shard_map/ppermute | solution.py:423
  25.9 2.0 %collective-permute-start.11 = (bf16[272,128]{1,0:T(8,128)(2,1)S(1)}, bf16[272,128]{1,0:T(8,128)(2,1)S(1)}, u32[]{:S(2)}, u32[]{:S(2)}) collective-permute-start(bf16[272,128]{1,0:T(8,128)(2,1)S(1)} %collective-permute-done.7.refs_4_), channel_id=1, source_target_pairs={{0,1},{1,0},{2,3},{3,2},{4,5},{5,4},{6,7},{7,6},{8,9},{9,8},{10,11... | collective-permute-start | bytes 208904 | tf_op jit(solution)/shard_map/ppermute | solution.py:423
  26.2 1.8 %collective-permute-start.10 = (bf16[272,128]{1,0:T(8,128)(2,1)S(1)}, bf16[272,128]{1,0:T(8,128)(2,1)S(1)}, u32[]{:S(2)}, u32[]{:S(2)}) collective-permute-start(bf16[272,128]{1,0:T(8,128)(2,1)S(1)} %collective-permute-done.6.refs_3_), channel_id=1, source_target_pairs={{0,1},{1,0},{2,3},{3,2},{4,5},{5,4},{6,7},{7,6},{8,9},{9,8},{10,11... | collective-permute-start | bytes 208904 | tf_op jit(solution)/shard_map/ppermute | solution.py:423
  26.8 1.3 %collective-permute-start.9 = (bf16[272,128]{1,0:T(8,128)(2,1)S(1)}, bf16[272,128]{1,0:T(8,128)(2,1)S(1)}, u32[]{:S(2)}, u32[]{:S(2)}) collective-permute-start(bf16[272,128]{1,0:T(8,128)(2,1)S(1)} %collective-permute-done.5.refs_2_), channel_id=1, source_target_pairs={{0,1},{1,0},{2,3},{3,2},{4,5},{5,4},{6,7},{7,6},{8,9},{9,8},{10,11... | collective-permute-start | bytes 208904 | tf_op jit(solution)/shard_map/ppermute | solution.py:423
  31.2 1.7 %collective-permute-start.12 = (f16[4,288,128]{2,1,0:T(8,128)(2,1)S(1)}, f16[4,288,128]{2,1,0:T(8,128)(2,1)S(1)}, u32[]{:S(2)}, u32[]{:S(2)}) collective-permute-start(f16[4,288,128]{2,1,0:T(8,128)(2,1)S(1)} %convert_element_type.113), channel_id=1, source_target_pairs={{0,1},{1,0},{2,3},{3,2},{4,5},{5,4},{6,7},{7,6},{8,9},{9,8},{10,11... | collective-permute-start | bytes 884744 | tf_op jit(solution)/shard_map/ppermute | solution.py:423
  33.1 5.5 %collective-permute-start.15 = (f16[288,128]{1,0:T(8,128)(2,1)S(1)}, f16[288,128]{1,0:T(8,128)(2,1)S(1)}, u32[]{:S(2)}, u32[]{:S(2)}) collective-permute-start(f16[288,128]{1,0:T(8,128)(2,1)S(1)} %convert_element_type.119), channel_id=1, source_target_pairs={{0,6},{2,4},{4,2},{6,0},{8,14},{10,12},{12,10},{14,8},{1,7},{3,5},... | collective-permute-start | bytes 221192 | tf_op jit(solution)/shard_map/ppermute | solution.py:428
  35.8 4.4 %collective-permute-start.14 = (f16[288,128]{1,0:T(8,128)(2,1)S(1)}, f16[288,128]{1,0:T(8,128)(2,1)S(1)}, u32[]{:S(2)}, u32[]{:S(2)}) collective-permute-start(f16[288,128]{1,0:T(8,128)(2,1)S(1)} %convert_element_type.117), channel_id=1, source_target_pairs={{0,2},{2,0},{4,6},{6,4},{8,10},{10,8},{12,14},{14,12},{1,3},{3,1},... | collective-permute-start | bytes 221192 | tf_op jit(solution)/shard_map/ppermute | solution.py:428
  36.3 4.4 %collective-permute-start.13 = (f16[288,128]{1,0:T(8,128)(2,1)S(1)}, f16[288,128]{1,0:T(8,128)(2,1)S(1)}, u32[]{:S(2)}, u32[]{:S(2)}) collective-permute-start(f16[288,128]{1,0:T(8,128)(2,1)S(1)} %convert_element_type.115), channel_id=1, source_target_pairs={{0,4},{2,6},{4,0},{6,2},{8,12},{10,14},{12,8},{14,10},{1,5},{3,7},... | collective-permute-start | bytes 221192 | tf_op jit(solution)/shard_map/ppermute | solution.py:428
  40.9 6.2 %collective-permute-start.16 = (f16[288,128]{1,0:T(8,128)(2,1)S(1)}, f16[288,128]{1,0:T(8,128)(2,1)S(1)}, u32[]{:S(2)}, u32[]{:S(2)}) collective-permute-start(f16[288,128]{1,0:T(8,128)(2,1)S(1)} %get-tuple-element.33), channel_id=1, source_target_pairs={{0,12},{2,14},{4,8},{6,10},{8,4},{10,6},{12,0},{14,2},{1,13},{3,15... | collective-permute-start | bytes 221192 | tf_op jit(solution)/shard_map/ppermute | solution.py:428
  47.3 5.4 %collective-permute-start.19 = (f16[272,128]{1,0:T(8,128)(2,1)S(1)}, f16[272,128]{1,0:T(8,128)(2,1)S(1)}, u32[]{:S(2)}, u32[]{:S(2)}) collective-permute-start(f16[272,128]{1,0:T(8,128)(2,1)S(1)} %get-tuple-element.27), channel_id=1, source_target_pairs={{0,6},{2,4},{4,2},{6,0},{8,14},{10,12},{12,10},{14,8},{1,7},{3,5},... | collective-permute-start | bytes 208904 | tf_op jit(solution)/shard_map/ppermute | solution.py:428
  48.1 5.1 %collective-permute-start.18 = (f16[272,128]{1,0:T(8,128)(2,1)S(1)}, f16[272,128]{1,0:T(8,128)(2,1)S(1)}, u32[]{:S(2)}, u32[]{:S(2)}) collective-permute-start(f16[272,128]{1,0:T(8,128)(2,1)S(1)} %get-tuple-element.27), channel_id=1, source_target_pairs={{0,2},{2,0},{4,6},{6,4},{8,10},{10,8},{12,14},{14,12},{1,3},{3,1},... | collective-permute-start | bytes 208904 | tf_op jit(solution)/shard_map/ppermute | solution.py:428
  48.9 4.4 %collective-permute-start.17 = (f16[272,128]{1,0:T(8,128)(2,1)S(1)}, f16[272,128]{1,0:T(8,128)(2,1)S(1)}, u32[]{:S(2)}, u32[]{:S(2)}) collective-permute-start(f16[272,128]{1,0:T(8,128)(2,1)S(1)} %get-tuple-element.27), channel_id=1, source_target_pairs={{0,4},{2,6},{4,0},{6,2},{8,12},{10,14},{12,8},{14,10},{1,5},{3,7},... | collective-permute-start | bytes 208904 | tf_op jit(solution)/shard_map/ppermute | solution.py:428
  50.8 4.1 %collective-permute-start.20 = (f16[272,128]{1,0:T(8,128)(2,1)S(1)}, f16[272,128]{1,0:T(8,128)(2,1)S(1)}, u32[]{:S(2)}, u32[]{:S(2)}) collective-permute-start(f16[272,128]{1,0:T(8,128)(2,1)S(1)} %get-tuple-element.27), channel_id=1, source_target_pairs={{0,1},{1,0},{2,3},{3,2},{4,5},{5,4},{6,7},{7,6},{8,9},{9,8},{10,11... | collective-permute-start | bytes 208904 | tf_op jit(solution)/shard_map/ppermute | solution.py:423
  52.6 2.3 %collective-permute-start.23 = (f16[272,128]{1,0:T(8,128)(2,1)S(1)}, f16[272,128]{1,0:T(8,128)(2,1)S(1)}, u32[]{:S(2)}, u32[]{:S(2)}) collective-permute-start(f16[272,128]{1,0:T(8,128)(2,1)S(1)} %collective-permute-done.19), channel_id=1, source_target_pairs={{0,1},{1,0},{2,3},{3,2},{4,5},{5,4},{6,7},{7,6},{8,9},{9,8},{10,11... | collective-permute-start | bytes 208904 | tf_op jit(solution)/shard_map/ppermute | solution.py:423
  53.1 1.8 %collective-permute-start.22 = (f16[272,128]{1,0:T(8,128)(2,1)S(1)}, f16[272,128]{1,0:T(8,128)(2,1)S(1)}, u32[]{:S(2)}, u32[]{:S(2)}) collective-permute-start(f16[272,128]{1,0:T(8,128)(2,1)S(1)} %collective-permute-done.18), channel_id=1, source_target_pairs={{0,1},{1,0},{2,3},{3,2},{4,5},{5,4},{6,7},{7,6},{8,9},{9,8},{10,11... | collective-permute-start | bytes 208904 | tf_op jit(solution)/shard_map/ppermute | solution.py:423
  53.3 1.6 %collective-permute-start.21 = (f16[272,128]{1,0:T(8,128)(2,1)S(1)}, f16[272,128]{1,0:T(8,128)(2,1)S(1)}, u32[]{:S(2)}, u32[]{:S(2)}) collective-permute-start(f16[272,128]{1,0:T(8,128)(2,1)S(1)} %collective-permute-done.17), channel_id=1, source_target_pairs={{0,1},{1,0},{2,3},{3,2},{4,5},{5,4},{6,7},{7,6},{8,9},{9,8},{10,11... | collective-permute-start | bytes 208904 | tf_op jit(solution)/shard_map/ppermute | solution.py:423
  53.7 1.3 %copy-start.2 = (s32[528]{0:T(1024)S(1)}, s32[528]{0:T(1024)}, u32[]{:S(2)}) copy-start(s32[528]{0:T(1024)} %refs_3_.1) | copy-start | bytes 6340
  53.7 1.3 %copy-start.3 = (s32[528]{0:T(1024)S(1)}, s32[528]{0:T(1024)}, u32[]{:S(2)}) copy-start(s32[528]{0:T(1024)} %constant.5.clone.refs_4_) | copy-start | bytes 6340

commit v6 on v5

--- a/solution.py
+++ b/solution.py
@@ -55,6 +55,10 @@
     def corner(self):
         x, z = lax.axis_index("narrow"), lax.axis_index("wide")
         return (x & 1) + ((z ^ (z >> 1)) & 1) * min(2, self.narrow)
+
+    def half(self):
+        x, z = lax.axis_index("narrow"), lax.axis_index("wide")
+        return lax.axis_index("tile") ^ ((x ^ z ^ (z >> 1)) & 1)
 
     def list_strips(self):
         side, per, w = self.stations // LANES, self.group, self.width
@@ -235,9 +239,15 @@
     return total
 
 
-def observed_kernel(plan, table, observed, out):
-    core, z = lax.axis_index("tile"), plan.corner()
-    left = pl.multiple_of(core * plan.area, LANES)
+def observed_kernel(plan, table, observed, owners, places, out, owners_out, places_out, done):
+    copies = [
+        pltpu.make_async_copy(owners, owners_out, done.at[0]),
+        pltpu.make_async_copy(places, places_out, done.at[1]),
+    ]
+    for copy in copies:
+        copy.start()
+    z = plan.corner()
+    left = pl.multiple_of(plan.half() * plan.area, LANES)
     n, count = plan.group, plan.run * plan.ways
     row = lax.broadcasted_iota(jnp.int32, (n, LANES), 0)
     last = observed.shape[0] // n * n - n
@@ -261,6 +271,8 @@
             out[pl.ds(to, n), :] = jnp.take_along_axis(tiles, n - 1 - row, axis=0)
 
     unrolled(plan.run, STRIPS, strip)
+    for copy in copies:
+        copy.wait()
 
 
 def first_kernel(plan, log_hbm, green_hbm, send, weighted, green, log_ref, done):
@@ -278,11 +290,11 @@
         copies[1 + k].wait()
         for i in range(k * size // LANES, (k + 1) * size // LANES):
             weigh_rows(plan, green, strength, weighted, i)
-    product(plan, 1 - lax.axis_index("tile"), green, weighted, send)
+    product(plan, 1 - plan.half(), green, weighted, send)
 
 
 def own_product_kernel(plan, green, weighted, own):
-    product(plan, lax.axis_index("tile"), green, weighted, own)
+    product(plan, plan.half(), green, weighted, own)
 
 
 def own_contraction_kernel(plan, green, *refs):
@@ -290,11 +302,11 @@
     for k, ref in zip(plan.order, tiles):
         stack[k] = ref[...].astype(BF16)
     fill_half(plan, lambda slot, at: stack[slot, at : at + plan.width, :], kernel)
-    total[...] = contraction(plan, lax.axis_index("tile"), green, kernel)
+    total[...] = contraction(plan, plan.half(), green, kernel)
 
 
 def new_log(plan, log_ref, green, total, kernel, log_out):
-    total = total[...] + contraction(plan, 1 - lax.axis_index("tile"), green, kernel)
+    total = total[...] + contraction(plan, 1 - plan.half(), green, kernel)
     log_now = log_ref[...]
     log_now = log_now - 0.5 * jnp.exp(log_now) * row_sums(total)
     log_out[...] = log_now
@@ -309,20 +321,20 @@
     strength = jnp.exp(new_log(plan, log_ref, green, total, kernel, log_out))
     for i in range(plan.points // LANES):
         weigh_rows(plan, green, strength, weighted, i)
-    product(plan, 1 - lax.axis_index("tile"), green, weighted, send)
+    product(plan, 1 - plan.half(), green, weighted, send)
 
 
 def last_kernel(plan, log_ref, green, total, owners, places, *refs):
     *refs, log_out, residual, kernel, tiles, sums = refs
     mine, others = refs[: plan.ways], refs[plan.ways :]
-    core, z, owned = lax.axis_index("tile"), plan.corner(), lax.axis_index("wide") * plan.slots
+    half, z, owned = plan.half(), plan.corner(), lax.axis_index("wide") * plan.slots
     n, w, c = plan.group, plan.width, plan.chunk
     for k, left, right in zip(plan.order, mine, others):
-        tiles[core, k * c : (k + 1) * c, :] = left[...]
-        tiles[1 - core, k * c : (k + 1) * c, :] = right[...]
+        tiles[half, k * c : (k + 1) * c, :] = left[...]
+        tiles[1 - half, k * c : (k + 1) * c, :] = right[...]
     fill_half(
         plan,
-        lambda slot, at: tiles[1 - core, pl.ds(pl.multiple_of(slot * c + at, w), w), :],
+        lambda slot, at: tiles[1 - half, pl.ds(pl.multiple_of(slot * c + at, w), w), :],
         kernel,
     )
     run = lax.broadcasted_iota(jnp.int32, (w, LANES), 1) // w
@@ -350,7 +362,7 @@
 
     def step(p, carry):
         at = pl.ds(pl.multiple_of(p * BLOCK, BLOCK), BLOCK)
-        part = row_sums(total[at, :] + contraction(plan, 1 - core, green, kernel, at))
+        part = row_sums(total[at, :] + contraction(plan, 1 - half, green, kernel, at))
         for i in range(rows):
             sums[pl.ds(p * rows + i, 1), :] = part[i : i + 1, :]
         for k in range(batches):
@@ -405,14 +417,14 @@
     out[...] = jnp.tanh(total - target[...])
 
 
-def call(kernel, plan, out_shape, scratch, arguments, specs):
+def call(kernel, plan, out_shape, scratch, arguments, specs, out_specs=None):
     def body(*refs):
         kernel(plan, *refs)
 
     return pl.pallas_call(
         body,
         in_specs=specs,
-        out_specs=jax.tree.map(lambda _: VMEM, out_shape),
+        out_specs=out_specs or jax.tree.map(lambda _: VMEM, out_shape),
         out_shape=out_shape,
         scratch_shapes=scratch,
         compiler_params=pltpu.CompilerParams(vmem_limit_bytes=24 * 1024 * 1024),
@@ -424,8 +436,10 @@
 
 
 def exchange(plan, x, mask):
-    pairs = [(i, i ^ mask) for i in range(plan.wide * plan.narrow)]
-    return lax.ppermute(x, ("wide", "narrow"), pairs)
+    dz, dx = divmod(mask, plan.narrow)
+    mask = 2 * mask + ((dx ^ dz ^ (dz >> 1)) & 1)
+    pairs = [(i, i ^ mask) for i in range(2 * plan.wide * plan.narrow)]
+    return lax.ppermute(x, ("wide", "narrow", "tile"), pairs)
 
 
 def to_half(x):
@@ -487,9 +501,13 @@
             [VMEM] * (1 + len(tiles)),
         )
 
-    target = call(
-        observed_kernel, plan, shape((plan.chunk, LANES), F32), [],
-        (jnp.asarray(plan.strip_table()), observed), [SMEM, VMEM],
+    places = jnp.asarray(plan.tile_places())
+    tables = [pltpu.SMEM(x.shape, jnp.int32) for x in (owner_map, places)]
+    target, *tables = call(
+        observed_kernel, plan, (shape((plan.chunk, LANES), F32), *tables),
+        [pltpu.SemaphoreType.DMA((2,))],
+        (jnp.asarray(plan.strip_table()), observed, owner_map, places), [SMEM, VMEM, HBM, HBM],
+        (VMEM, SMEM, SMEM),
     )
     send, weighted, green = call(
         first_kernel, plan,
@@ -522,7 +540,7 @@
             pltpu.VMEM(log_now.shape, F32),
         ],
         (
-            log_now, green, own_contraction(mine), owner_map, jnp.asarray(plan.tile_places()),
+            log_now, green, own_contraction(mine), *tables,
             *mine, *[x.astype(F32) for x in others],
         ),
         [VMEM] * 3 + [SMEM] * 2 + [VMEM] * (2 * plan.ways),

time: 59 us -> 57.8 us (0.980)
  starting transfers between devices: 22.9 us -> 21.8 us
    ppermute x14, starting transfers between devices: 21.3 us -> 20.1 us  [exchange(): return lax.ppermute(x, ('wide', 'narrow', 'tile'), pairs)]
  transfers between devices with their start and end apart: 24 -> 24, of which waited for: 16 -> 11; matrix products, arithmetic and copies ran while one was open for 0% -> 0% of each run, Pallas kernels for 10% -> 11%
where the time goes in v6:
time: 57.8 us; the launch traced here: 57.6 us
  starting transfers between devices  21.8 us (38%)
  waiting for transfers between devices  18.3 us (32%)
  Pallas kernels  15.8 us (27%)
  between operations  0.97 us (2%)
  other arithmetic  0.71 us (1%)
    ppermute x14, starting transfers between devices, exchange(): return lax.ppermute(x, ('wide', 'narrow', 'tile'), pairs)  20.1 us
    ppermute x14, waiting for transfers between devices, exchange(): return lax.ppermute(x, ('wide', 'narrow', 'tile'), pairs)  18 us
    pallas_call x12, Pallas kernels, call(): pl.pallas_call(body, in_specs=specs, out_specs=out_specs or jax.tree.map(...  15.8 us
    ppermute x10, starting transfers between devices, swap_cores(): return lax.ppermute(x, 'tile', [(0, 1), (1, 0)])  1.7 us
  transfers between devices with their start and end apart: 24, of which 11 were waited for; matrix products, arithmetic and copies ran while one was open for 0% of the time, Pallas kernels for 11%

profile of v6, /device:TPU:0, one launch (start us, length us, event | category | flops | bytes accessed | tf_op | source)
XLA Modules:
  0.0 57.6 jit_solution(8103670208692501406)
XLA Ops:
  0.6 2.9 %shard_map.77 = (f32[4,272,128]{2,1,0:T(8,128)S(1)}, bf16[2,1024,512]{2,1,0:T(8,128)(2,1)S(1)}, bf16[1024,1024]{1,0:T(8,128)(2,1)S(1)}) custom-call(f32[8,128]{1,0:T(8,128)} %bitcast.19, bf16[1024,1024]{1,0:T(8,128)(2,1)} %refs_1_.2), custom_call_target="tpu_custom_call" | custom-call | tf_op jit(solution)/shard_map/pallas_call | solution.py:424
  3.6 0.5 collective-permute-start
  4.1 1.1 %shard_map.78 = f32[4,272,128]{2,1,0:T(8,128)S(1)} custom-call(bf16[1024,1024]{1,0:T(8,128)(2,1)S(1)} %get-tuple-element.17.refs_0_.refs_1_, bf16[2,1024,512]{2,1,0:T(8,128)(2,1)S(1)} %get-tuple-element.18.refs_1_), custom_call_target="tpu_custom_call" | custom-call | tf_op jit(solution)/shard_map/pallas_call | solution.py:424
  5.2 0.0 copy-start
  5.2 0.0 copy-start.2
  5.2 0.0 copy-start.3
  5.2 0.0 copy-start.4
  5.2 0.0 collective-permute-done
  5.3 0.1 fusion.8
  5.4 3.9 %collective-permute-start.1 = (f16[272,128]{1,0:T(8,128)(2,1)S(1)}, f16[272,128]{1,0:T(8,128)(2,1)S(1)}, u32[]{:S(2)}, u32[]{:S(2)}) collective-permute-start(f16[272,128]{1,0:T(8,128)(2,1)S(1)} %get-tuple-element.36), channel_id=1, source_target_pairs={{0,6},{1,7},{2,4},{3,5},{4,2},{5,3},{6,0},{7,1},{8,14},{9,15},{10,... | collective-permute-start | bytes 208904 | tf_op jit(solution)/shard_map/ppermute | solution.py:442
  9.3 0.0 collective-permute-start.3
  9.3 0.4 collective-permute-start.2
  9.7 2.2 %collective-permute-done.1 = f16[272,128]{1,0:T(8,128)(2,1)S(1)} collective-permute-done((f16[272,128]{1,0:T(8,128)(2,1)S(1)}, f16[272,128]{1,0:T(8,128)(2,1)S(1)}, u32[]{:S(2)}, u32[]{:S(2)}) %collective-permute-start.1) | collective-permute-done | bytes 69664 | tf_op jit(solution)/shard_map/ppermute | solution.py:442
  11.9 1.9 %collective-permute-done.3 = f16[272,128]{1,0:T(8,128)(2,1)S(1)} collective-permute-done((f16[272,128]{1,0:T(8,128)(2,1)S(1)}, f16[272,128]{1,0:T(8,128)(2,1)S(1)}, u32[]{:S(2)}, u32[]{:S(2)}) %collective-permute-start.3) | collective-permute-done | bytes 69664 | tf_op jit(solution)/shard_map/ppermute | solution.py:442
  13.7 0.1 fusion.12
  13.9 0.0 copy-start.1
  13.9 3.3 %collective-permute-start.4 = (f16[272,128]{1,0:T(8,128)(2,1)S(1)}, f16[272,128]{1,0:T(8,128)(2,1)S(1)}, u32[]{:S(2)}, u32[]{:S(2)}) collective-permute-start(f16[272,128]{1,0:T(8,128)(2,1)S(1)} %get-tuple-element.34), channel_id=1, source_target_pairs={{0,12},{1,13},{2,14},{3,15},{4,8},{5,9},{6,10},{7,11},{8,4},{9,5},... | collective-permute-start | bytes 208904 | tf_op jit(solution)/shard_map/ppermute | solution.py:442
  17.2 2.0 %shard_map.79 = (f32[272,128]{1,0:T(8,128)S(1)}, s32[528]{0:T(1024)S(4)}, s32[528]{0:T(1024)S(4)}) custom-call(s32[204]{0:T(256)S(1)} %copy-done.4, f32[528,512]{1,0:T(8,128)S(1)} %copy-done, s32[528]{0:T(1024)S(1)} %copy-done.2, s32[528]{0:T(1024)S(1)} %copy-done.3), custom_call_target="tpu_custom_call" | custom-call | tf_op jit(solution)/shard_map/pallas_call | solution.py:424
  19.2 0.9 %collective-permute-done.4 = f16[272,128]{1,0:T(8,128)(2,1)S(1)} collective-permute-done((f16[272,128]{1,0:T(8,128)(2,1)S(1)}, f16[272,128]{1,0:T(8,128)(2,1)S(1)}, u32[]{:S(2)}, u32[]{:S(2)}) %collective-permute-start.4) | collective-permute-done | bytes 69664 | tf_op jit(solution)/shard_map/ppermute | solution.py:442
  20.2 1.8 %collective-permute-start.7 = (bf16[272,128]{1,0:T(8,128)(2,1)S(1)}, bf16[272,128]{1,0:T(8,128)(2,1)S(1)}, u32[]{:S(2)}, u32[]{:S(2)}) collective-permute-start(bf16[272,128]{1,0:T(8,128)(2,1)S(1)} %tanh_convert_fusion.refs_1_), channel_id=1, source_target_pairs={{0,6},{1,7},{2,4},{3,5},{4,2},{5,3},{6,0},{7,1},{8,14},{9,15},{10,... | collective-permute-start | bytes 208904 | tf_op jit(solution)/shard_map/ppermute | solution.py:442
  21.9 1.5 %collective-permute-start.5 = (bf16[272,128]{1,0:T(8,128)(2,1)S(1)}, bf16[272,128]{1,0:T(8,128)(2,1)S(1)}, u32[]{:S(2)}, u32[]{:S(2)}) collective-permute-start(bf16[272,128]{1,0:T(8,128)(2,1)S(1)} %tanh_convert_fusion.refs_1_), channel_id=1, source_target_pairs={{0,5},{1,4},{2,7},{3,6},{4,1},{5,0},{6,3},{7,2},{8,13},{9,12},{10,... | collective-permute-start | bytes 208904 | tf_op jit(solution)/shard_map/ppermute | solution.py:442
  23.4 2.1 %collective-permute-done.7.refs_4_ = bf16[272,128]{1,0:T(8,128)(2,1)S(1)} collective-permute-done((bf16[272,128]{1,0:T(8,128)(2,1)S(1)}, bf16[272,128]{1,0:T(8,128)(2,1)S(1)}, u32[]{:S(2)}, u32[]{:S(2)}) %collective-permute-start.7) | collective-permute-done | bytes 69664 | tf_op jit(solution)/shard_map/ppermute | solution.py:442
  25.5 1.2 %collective-permute-done.6.refs_3_ = bf16[272,128]{1,0:T(8,128)(2,1)S(1)} collective-permute-done((bf16[272,128]{1,0:T(8,128)(2,1)S(1)}, bf16[272,128]{1,0:T(8,128)(2,1)S(1)}, u32[]{:S(2)}, u32[]{:S(2)}) %collective-permute-start.6) | collective-permute-done | bytes 69664 | tf_op jit(solution)/shard_map/ppermute | solution.py:442
  26.7 0.5 collective-permute-start.9
  27.2 1.1 %shard_map.80.refs_2_ = f32[1024,128]{1,0:T(8,128)S(1)} custom-call(bf16[1024,1024]{1,0:T(8,128)(2,1)S(1)} %get-tuple-element.17.refs_0_.refs_1_, bf16[272,128]{1,0:T(8,128)(2,1)S(1)} %tanh_convert_fusion.refs_1_, bf16[272,128]{1,0:T(8,128)(2,1)S(1)} %collective-permute-done.5.refs_2_, bf16[272,128]{1,0:T(8,128)(2,1)S(1)} %collective-permute-done.6.refs_3_, ...), custom_call_target="tpu_custom_call" | custom-call | tf_op jit(solution)/shard_map/pallas_call | solution.py:424
  28.4 3.0 %shard_map.81 = (f32[4,288,128]{2,1,0:T(8,128)S(1)}, bf16[2,1024,512]{2,1,0:T(8,128)(2,1)S(1)}, f32[8,128]{1,0:T(8,128)S(1)}) custom-call(f32[8,128]{1,0:T(8,128)S(1)} %bitcast.20, bf16[1024,1024]{1,0:T(8,128)(2,1)S(1)} %get-tuple-element.17.refs_0_.refs_1_, f32[1024,128]{1,0:T(8,128)S(1)} %shard_map.80.refs_2_, ...), custom_call_target="tpu_custom_call" | custom-call | tf_op jit(solution)/shard_map/pallas_call | solution.py:424
  31.4 0.1 shard_map.83
  31.5 0.1 collective-permute-start.12
  31.6 1.2 %shard_map.82.refs_0_ = f32[4,288,128]{2,1,0:T(8,128)S(1)} custom-call(bf16[1024,1024]{1,0:T(8,128)(2,1)S(1)} %get-tuple-element.17.refs_0_.refs_1_, bf16[2,1024,512]{2,1,0:T(8,128)(2,1)S(1)} %get-tuple-element.22.refs_1_), custom_call_target="tpu_custom_call" | custom-call | tf_op jit(solution)/shard_map/pallas_call | solution.py:424
  32.8 0.3 collective-permute-done.12
  33.2 0.1 shard_map.84
  33.3 1.5 %collective-permute-start.15 = (f16[288,128]{1,0:T(8,128)(2,1)S(1)}, f16[288,128]{1,0:T(8,128)(2,1)S(1)}, u32[]{:S(2)}, u32[]{:S(2)}) collective-permute-start(f16[288,128]{1,0:T(8,128)(2,1)S(1)} %convert_element_type.119), channel_id=1, source_target_pairs={{0,6},{1,7},{2,4},{3,5},{4,2},{5,3},{6,0},{7,1},{8,14},{9,15},{10,... | collective-permute-start | bytes 221192 | tf_op jit(solution)/shard_map/ppermute | solution.py:442
  34.8 0.3 collective-permute-start.14
  35.1 1.6 %collective-permute-start.13 = (f16[288,128]{1,0:T(8,128)(2,1)S(1)}, f16[288,128]{1,0:T(8,128)(2,1)S(1)}, u32[]{:S(2)}, u32[]{:S(2)}) collective-permute-start(f16[288,128]{1,0:T(8,128)(2,1)S(1)} %convert_element_type.115), channel_id=1, source_target_pairs={{0,5},{1,4},{2,7},{3,6},{4,1},{5,0},{6,3},{7,2},{8,13},{9,12},{10,... | collective-permute-start | bytes 221192 | tf_op jit(solution)/shard_map/ppermute | solution.py:442
  36.7 2.1 %collective-permute-done.15 = f16[288,128]{1,0:T(8,128)(2,1)S(1)} collective-permute-done((f16[288,128]{1,0:T(8,128)(2,1)S(1)}, f16[288,128]{1,0:T(8,128)(2,1)S(1)}, u32[]{:S(2)}, u32[]{:S(2)}) %collective-permute-start.15) | collective-permute-done | bytes 73760 | tf_op jit(solution)/shard_map/ppermute | solution.py:442
  38.7 1.4 %collective-permute-done.14 = f16[288,128]{1,0:T(8,128)(2,1)S(1)} collective-permute-done((f16[288,128]{1,0:T(8,128)(2,1)S(1)}, f16[288,128]{1,0:T(8,128)(2,1)S(1)}, u32[]{:S(2)}, u32[]{:S(2)}) %collective-permute-start.14) | collective-permute-done | bytes 73760 | tf_op jit(solution)/shard_map/ppermute | solution.py:442
  40.3 0.1 reduce-precision_convert_fusion.1
  40.3 2.6 %collective-permute-start.16 = (f16[288,128]{1,0:T(8,128)(2,1)S(1)}, f16[288,128]{1,0:T(8,128)(2,1)S(1)}, u32[]{:S(2)}, u32[]{:S(2)}) collective-permute-start(f16[288,128]{1,0:T(8,128)(2,1)S(1)} %get-tuple-element.39), channel_id=1, source_target_pairs={{0,12},{1,13},{2,14},{3,15},{4,8},{5,9},{6,10},{7,11},{8,4},{9,5},... | collective-permute-start | bytes 221192 | tf_op jit(solution)/shard_map/ppermute | solution.py:442
  42.9 3.7 %collective-permute-done.16 = f16[288,128]{1,0:T(8,128)(2,1)S(1)} collective-permute-done((f16[288,128]{1,0:T(8,128)(2,1)S(1)}, f16[288,128]{1,0:T(8,128)(2,1)S(1)}, u32[]{:S(2)}, u32[]{:S(2)}) %collective-permute-start.16) | collective-permute-done | bytes 73760 | tf_op jit(solution)/shard_map/ppermute | solution.py:442
  46.7 0.1 fusion.11
  46.8 1.3 %collective-permute-start.19 = (f16[272,128]{1,0:T(8,128)(2,1)S(1)}, f16[272,128]{1,0:T(8,128)(2,1)S(1)}, u32[]{:S(2)}, u32[]{:S(2)}) collective-permute-start(f16[272,128]{1,0:T(8,128)(2,1)S(1)} %get-tuple-element.33), channel_id=1, source_target_pairs={{0,6},{1,7},{2,4},{3,5},{4,2},{5,3},{6,0},{7,1},{8,14},{9,15},{10,... | collective-permute-start | bytes 208904 | tf_op jit(solution)/shard_map/ppermute | solution.py:442
  48.1 2.0 %collective-permute-start.17 = (f16[272,128]{1,0:T(8,128)(2,1)S(1)}, f16[272,128]{1,0:T(8,128)(2,1)S(1)}, u32[]{:S(2)}, u32[]{:S(2)}) collective-permute-start(f16[272,128]{1,0:T(8,128)(2,1)S(1)} %get-tuple-element.33), channel_id=1, source_target_pairs={{0,5},{1,4},{2,7},{3,6},{4,1},{5,0},{6,3},{7,2},{8,13},{9,12},{10,... | collective-permute-start | bytes 208904 | tf_op jit(solution)/shard_map/ppermute | solution.py:442
  50.0 2.4 %collective-permute-done.19 = f16[272,128]{1,0:T(8,128)(2,1)S(1)} collective-permute-done((f16[272,128]{1,0:T(8,128)(2,1)S(1)}, f16[272,128]{1,0:T(8,128)(2,1)S(1)}, u32[]{:S(2)}, u32[]{:S(2)}) %collective-permute-start.19) | collective-permute-done | bytes 69664 | tf_op jit(solution)/shard_map/ppermute | solution.py:442
  52.4 0.2 collective-permute-done.18
  52.6 0.3 collective-permute-start.22
  52.9 0.2 collective-permute-start.21
  53.2 1.1 %shard_map.87.refs_2_ = f32[1024,128]{1,0:T(8,128)S(1)} custom-call(bf16[1024,1024]{1,0:T(8,128)(2,1)S(1)} %get-tuple-element.17.refs_0_.refs_1_, f32[272,128]{1,0:T(8,128)S(1)} %get-tuple-element.32.refs_1_.refs_5_, f32[272,128]{1,0:T(8,128)S(1)} %convert_element_type.125.refs_2_.refs_6_, f32[272,128]{1,0:T(8,128)S(1)} %convert_element_type.126.refs_3_.refs_7_, ...), custom_call_target="tpu_custom_call" | custom-call | tf_op jit(solution)/shard_map/pallas_call | solution.py:424
  54.5 3.2 %shard_map.88 = (f32[8,128]{1,0:T(8,128)}, f32[132,512]{1,0:T(8,128)}) custom-call(f32[8,128]{1,0:T(8,128)S(1)} %get-tuple-element.21.refs_0_, bf16[1024,1024]{1,0:T(8,128)(2,1)S(1)} %get-tuple-element.17.refs_0_.refs_1_, f32[1024,128]{1,0:T(8,128)S(1)} %shard_map.87.refs_2_, s32[528]{0:T(1024)S(4)} %get-tuple-element.28.refs_3_, ...), custom_call_target="tpu_custom_call" | custom-call | tf_op jit(solution)/shard_map/pallas_call | solution.py:424
  (45 shorter events, 0.5 us)
Async XLA Ops:
  3.6 1.7 %collective-permute-start = (f16[4,272,128]{2,1,0:T(8,128)(2,1)S(1)}, f16[4,272,128]{2,1,0:T(8,128)(2,1)S(1)}, u32[]{:S(2)}, u32[]{:S(2)}) collective-permute-start(f16[4,272,128]{2,1,0:T(8,128)(2,1)S(1)} %convert_element_type.99), channel_id=1, source_target_pairs={{0,1},{1,0},{2,3},{3,2},{4,5},{5,4},{6,7},{7,6},{8,9},{9,8},{10,11... | collective-permute-start | bytes 835592 | tf_op jit(solution)/shard_map/ppermute | solution.py:435
  5.2 12.0 %copy-start = (f32[528,512]{1,0:T(8,128)S(1)}, f32[528,512]{1,0:T(8,128)}, u32[]{:S(2)}) copy-start(f32[528,512]{1,0:T(8,128)} %refs_1_.3) | copy-start | bytes 3244036
  5.2 12.0 %copy-start.2 = (s32[528]{0:T(1024)S(1)}, s32[528]{0:T(1024)}, u32[]{:S(2)}) copy-start(s32[528]{0:T(1024)} %refs_2_.1) | copy-start | bytes 6340
  5.2 12.0 %copy-start.3 = (s32[528]{0:T(1024)S(1)}, s32[528]{0:T(1024)}, u32[]{:S(2)}) copy-start(s32[528]{0:T(1024)} %constant.4.clone.refs_3_) | copy-start | bytes 6340
  5.2 12.0 %copy-start.4 = (s32[204]{0:T(256)S(1)}, s32[204]{0:T(256)}, u32[]{:S(2)}) copy-start(s32[204]{0:T(256)} %constant.5.clone.refs_0_) | copy-start | bytes 2452
  5.4 6.5 %collective-permute-start.1 = (f16[272,128]{1,0:T(8,128)(2,1)S(1)}, f16[272,128]{1,0:T(8,128)(2,1)S(1)}, u32[]{:S(2)}, u32[]{:S(2)}) collective-permute-start(f16[272,128]{1,0:T(8,128)(2,1)S(1)} %get-tuple-element.36), channel_id=1, source_target_pairs={{0,6},{1,7},{2,4},{3,5},{4,2},{5,3},{6,0},{7,1},{8,14},{9,15},{10,... | collective-permute-start | bytes 208904 | tf_op jit(solution)/shard_map/ppermute | solution.py:442
  9.3 4.4 %collective-permute-start.3 = (f16[272,128]{1,0:T(8,128)(2,1)S(1)}, f16[272,128]{1,0:T(8,128)(2,1)S(1)}, u32[]{:S(2)}, u32[]{:S(2)}) collective-permute-start(f16[272,128]{1,0:T(8,128)(2,1)S(1)} %get-tuple-element.37), channel_id=1, source_target_pairs={{0,3},{1,2},{2,1},{3,0},{4,7},{5,6},{6,5},{7,4},{8,11},{9,10},{10,... | collective-permute-start | bytes 208904 | tf_op jit(solution)/shard_map/ppermute | solution.py:442
  9.3 4.4 %collective-permute-start.2 = (f16[272,128]{1,0:T(8,128)(2,1)S(1)}, f16[272,128]{1,0:T(8,128)(2,1)S(1)}, u32[]{:S(2)}, u32[]{:S(2)}) collective-permute-start(f16[272,128]{1,0:T(8,128)(2,1)S(1)} %get-tuple-element.38), channel_id=1, source_target_pairs={{0,5},{1,4},{2,7},{3,6},{4,1},{5,0},{6,3},{7,2},{8,13},{9,12},{10,... | collective-permute-start | bytes 208904 | tf_op jit(solution)/shard_map/ppermute | solution.py:442
  13.9 14.5 %copy-start.1 = (f32[1024]{0:T(1024)S(1)}, f32[1024]{0:T(1024)}, u32[]{:S(2)}) copy-start(f32[1024]{0:T(1024)} %param.7) | copy-start | bytes 12292
  13.9 6.2 %collective-permute-start.4 = (f16[272,128]{1,0:T(8,128)(2,1)S(1)}, f16[272,128]{1,0:T(8,128)(2,1)S(1)}, u32[]{:S(2)}, u32[]{:S(2)}) collective-permute-start(f16[272,128]{1,0:T(8,128)(2,1)S(1)} %get-tuple-element.34), channel_id=1, source_target_pairs={{0,12},{1,13},{2,14},{3,15},{4,8},{5,9},{6,10},{7,11},{8,4},{9,5},... | collective-permute-start | bytes 208904 | tf_op jit(solution)/shard_map/ppermute | solution.py:442
  20.2 5.4 %collective-permute-start.7 = (bf16[272,128]{1,0:T(8,128)(2,1)S(1)}, bf16[272,128]{1,0:T(8,128)(2,1)S(1)}, u32[]{:S(2)}, u32[]{:S(2)}) collective-permute-start(bf16[272,128]{1,0:T(8,128)(2,1)S(1)} %tanh_convert_fusion.refs_1_), channel_id=1, source_target_pairs={{0,6},{1,7},{2,4},{3,5},{4,2},{5,3},{6,0},{7,1},{8,14},{9,15},{10,... | collective-permute-start | bytes 208904 | tf_op jit(solution)/shard_map/ppermute | solution.py:442
  21.9 4.8 %collective-permute-start.6 = (bf16[272,128]{1,0:T(8,128)(2,1)S(1)}, bf16[272,128]{1,0:T(8,128)(2,1)S(1)}, u32[]{:S(2)}, u32[]{:S(2)}) collective-permute-start(bf16[272,128]{1,0:T(8,128)(2,1)S(1)} %tanh_convert_fusion.refs_1_), channel_id=1, source_target_pairs={{0,3},{1,2},{2,1},{3,0},{4,7},{5,6},{6,5},{7,4},{8,11},{9,10},{10,... | collective-permute-start | bytes 208904 | tf_op jit(solution)/shard_map/ppermute | solution.py:442
  21.9 4.8 %collective-permute-start.5 = (bf16[272,128]{1,0:T(8,128)(2,1)S(1)}, bf16[272,128]{1,0:T(8,128)(2,1)S(1)}, u32[]{:S(2)}, u32[]{:S(2)}) collective-permute-start(bf16[272,128]{1,0:T(8,128)(2,1)S(1)} %tanh_convert_fusion.refs_1_), channel_id=1, source_target_pairs={{0,5},{1,4},{2,7},{3,6},{4,1},{5,0},{6,3},{7,2},{8,13},{9,12},{10,... | collective-permute-start | bytes 208904 | tf_op jit(solution)/shard_map/ppermute | solution.py:442
  23.4 4.9 %collective-permute-start.8 = (bf16[272,128]{1,0:T(8,128)(2,1)S(1)}, bf16[272,128]{1,0:T(8,128)(2,1)S(1)}, u32[]{:S(2)}, u32[]{:S(2)}) collective-permute-start(bf16[272,128]{1,0:T(8,128)(2,1)S(1)} %tanh_convert_fusion.refs_1_), channel_id=1, source_target_pairs={{0,1},{1,0},{2,3},{3,2},{4,5},{5,4},{6,7},{7,6},{8,9},{9,8},{10,11... | collective-permute-start | bytes 208904 | tf_op jit(solution)/shard_map/ppermute | solution.py:435
  25.5 2.8 %collective-permute-start.11 = (bf16[272,128]{1,0:T(8,128)(2,1)S(1)}, bf16[272,128]{1,0:T(8,128)(2,1)S(1)}, u32[]{:S(2)}, u32[]{:S(2)}) collective-permute-start(bf16[272,128]{1,0:T(8,128)(2,1)S(1)} %collective-permute-done.7.refs_4_), channel_id=1, source_target_pairs={{0,1},{1,0},{2,3},{3,2},{4,5},{5,4},{6,7},{7,6},{8,9},{9,8},{10,11... | collective-permute-start | bytes 208904 | tf_op jit(solution)/shard_map/ppermute | solution.py:435
  26.7 1.7 %collective-permute-start.10 = (bf16[272,128]{1,0:T(8,128)(2,1)S(1)}, bf16[272,128]{1,0:T(8,128)(2,1)S(1)}, u32[]{:S(2)}, u32[]{:S(2)}) collective-permute-start(bf16[272,128]{1,0:T(8,128)(2,1)S(1)} %collective-permute-done.6.refs_3_), channel_id=1, source_target_pairs={{0,1},{1,0},{2,3},{3,2},{4,5},{5,4},{6,7},{7,6},{8,9},{9,8},{10,11... | collective-permute-start | bytes 208904 | tf_op jit(solution)/shard_map/ppermute | solution.py:435
  26.7 1.7 %collective-permute-start.9 = (bf16[272,128]{1,0:T(8,128)(2,1)S(1)}, bf16[272,128]{1,0:T(8,128)(2,1)S(1)}, u32[]{:S(2)}, u32[]{:S(2)}) collective-permute-start(bf16[272,128]{1,0:T(8,128)(2,1)S(1)} %collective-permute-done.5.refs_2_), channel_id=1, source_target_pairs={{0,1},{1,0},{2,3},{3,2},{4,5},{5,4},{6,7},{7,6},{8,9},{9,8},{10,11... | collective-permute-start | bytes 208904 | tf_op jit(solution)/shard_map/ppermute | solution.py:435
  31.5 1.6 %collective-permute-start.12 = (f16[4,288,128]{2,1,0:T(8,128)(2,1)S(1)}, f16[4,288,128]{2,1,0:T(8,128)(2,1)S(1)}, u32[]{:S(2)}, u32[]{:S(2)}) collective-permute-start(f16[4,288,128]{2,1,0:T(8,128)(2,1)S(1)} %convert_element_type.113), channel_id=1, source_target_pairs={{0,1},{1,0},{2,3},{3,2},{4,5},{5,4},{6,7},{7,6},{8,9},{9,8},{10,11... | collective-permute-start | bytes 884744 | tf_op jit(solution)/shard_map/ppermute | solution.py:435
  33.3 5.4 %collective-permute-start.15 = (f16[288,128]{1,0:T(8,128)(2,1)S(1)}, f16[288,128]{1,0:T(8,128)(2,1)S(1)}, u32[]{:S(2)}, u32[]{:S(2)}) collective-permute-start(f16[288,128]{1,0:T(8,128)(2,1)S(1)} %convert_element_type.119), channel_id=1, source_target_pairs={{0,6},{1,7},{2,4},{3,5},{4,2},{5,3},{6,0},{7,1},{8,14},{9,15},{10,... | collective-permute-start | bytes 221192 | tf_op jit(solution)/shard_map/ppermute | solution.py:442
  34.8 5.3 %collective-permute-start.14 = (f16[288,128]{1,0:T(8,128)(2,1)S(1)}, f16[288,128]{1,0:T(8,128)(2,1)S(1)}, u32[]{:S(2)}, u32[]{:S(2)}) collective-permute-start(f16[288,128]{1,0:T(8,128)(2,1)S(1)} %convert_element_type.117), channel_id=1, source_target_pairs={{0,3},{1,2},{2,1},{3,0},{4,7},{5,6},{6,5},{7,4},{8,11},{9,10},{10,... | collective-permute-start | bytes 221192 | tf_op jit(solution)/shard_map/ppermute | solution.py:442
  35.1 5.1 %collective-permute-start.13 = (f16[288,128]{1,0:T(8,128)(2,1)S(1)}, f16[288,128]{1,0:T(8,128)(2,1)S(1)}, u32[]{:S(2)}, u32[]{:S(2)}) collective-permute-start(f16[288,128]{1,0:T(8,128)(2,1)S(1)} %convert_element_type.115), channel_id=1, source_target_pairs={{0,5},{1,4},{2,7},{3,6},{4,1},{5,0},{6,3},{7,2},{8,13},{9,12},{10,... | collective-permute-start | bytes 221192 | tf_op jit(solution)/shard_map/ppermute | solution.py:442
  40.3 6.3 %collective-permute-start.16 = (f16[288,128]{1,0:T(8,128)(2,1)S(1)}, f16[288,128]{1,0:T(8,128)(2,1)S(1)}, u32[]{:S(2)}, u32[]{:S(2)}) collective-permute-start(f16[288,128]{1,0:T(8,128)(2,1)S(1)} %get-tuple-element.39), channel_id=1, source_target_pairs={{0,12},{1,13},{2,14},{3,15},{4,8},{5,9},{6,10},{7,11},{8,4},{9,5},... | collective-permute-start | bytes 221192 | tf_op jit(solution)/shard_map/ppermute | solution.py:442
  46.8 5.6 %collective-permute-start.19 = (f16[272,128]{1,0:T(8,128)(2,1)S(1)}, f16[272,128]{1,0:T(8,128)(2,1)S(1)}, u32[]{:S(2)}, u32[]{:S(2)}) collective-permute-start(f16[272,128]{1,0:T(8,128)(2,1)S(1)} %get-tuple-element.33), channel_id=1, source_target_pairs={{0,6},{1,7},{2,4},{3,5},{4,2},{5,3},{6,0},{7,1},{8,14},{9,15},{10,... | collective-permute-start | bytes 208904 | tf_op jit(solution)/shard_map/ppermute | solution.py:442
  48.1 4.6 %collective-permute-start.18 = (f16[272,128]{1,0:T(8,128)(2,1)S(1)}, f16[272,128]{1,0:T(8,128)(2,1)S(1)}, u32[]{:S(2)}, u32[]{:S(2)}) collective-permute-start(f16[272,128]{1,0:T(8,128)(2,1)S(1)} %get-tuple-element.33), channel_id=1, source_target_pairs={{0,3},{1,2},{2,1},{3,0},{4,7},{5,6},{6,5},{7,4},{8,11},{9,10},{10,... | collective-permute-start | bytes 208904 | tf_op jit(solution)/shard_map/ppermute | solution.py:442
  48.1 4.8 %collective-permute-start.17 = (f16[272,128]{1,0:T(8,128)(2,1)S(1)}, f16[272,128]{1,0:T(8,128)(2,1)S(1)}, u32[]{:S(2)}, u32[]{:S(2)}) collective-permute-start(f16[272,128]{1,0:T(8,128)(2,1)S(1)} %get-tuple-element.33), channel_id=1, source_target_pairs={{0,5},{1,4},{2,7},{3,6},{4,1},{5,0},{6,3},{7,2},{8,13},{9,12},{10,... | collective-permute-start | bytes 208904 | tf_op jit(solution)/shard_map/ppermute | solution.py:442
  50.0 4.3 %collective-permute-start.20 = (f16[272,128]{1,0:T(8,128)(2,1)S(1)}, f16[272,128]{1,0:T(8,128)(2,1)S(1)}, u32[]{:S(2)}, u32[]{:S(2)}) collective-permute-start(f16[272,128]{1,0:T(8,128)(2,1)S(1)} %get-tuple-element.33), channel_id=1, source_target_pairs={{0,1},{1,0},{2,3},{3,2},{4,5},{5,4},{6,7},{7,6},{8,9},{9,8},{10,11... | collective-permute-start | bytes 208904 | tf_op jit(solution)/shard_map/ppermute | solution.py:435
  52.4 2.0 %collective-permute-start.23 = (f16[272,128]{1,0:T(8,128)(2,1)S(1)}, f16[272,128]{1,0:T(8,128)(2,1)S(1)}, u32[]{:S(2)}, u32[]{:S(2)}) collective-permute-start(f16[272,128]{1,0:T(8,128)(2,1)S(1)} %collective-permute-done.19), channel_id=1, source_target_pairs={{0,1},{1,0},{2,3},{3,2},{4,5},{5,4},{6,7},{7,6},{8,9},{9,8},{10,11... | collective-permute-start | bytes 208904 | tf_op jit(solution)/shard_map/ppermute | solution.py:435
  52.6 1.8 %collective-permute-start.22 = (f16[272,128]{1,0:T(8,128)(2,1)S(1)}, f16[272,128]{1,0:T(8,128)(2,1)S(1)}, u32[]{:S(2)}, u32[]{:S(2)}) collective-permute-start(f16[272,128]{1,0:T(8,128)(2,1)S(1)} %collective-permute-done.18), channel_id=1, source_target_pairs={{0,1},{1,0},{2,3},{3,2},{4,5},{5,4},{6,7},{7,6},{8,9},{9,8},{10,11... | collective-permute-start | bytes 208904 | tf_op jit(solution)/shard_map/ppermute | solution.py:435
  52.9 1.5 %collective-permute-start.21 = (f16[272,128]{1,0:T(8,128)(2,1)S(1)}, f16[272,128]{1,0:T(8,128)(2,1)S(1)}, u32[]{:S(2)}, u32[]{:S(2)}) collective-permute-start(f16[272,128]{1,0:T(8,128)(2,1)S(1)} %collective-permute-done.17), channel_id=1, source_target_pairs={{0,1},{1,0},{2,3},{3,2},{4,5},{5,4},{6,7},{7,6},{8,9},{9,8},{10,11... | collective-permute-start | bytes 208904 | tf_op jit(solution)/shard_map/ppermute | solution.py:435

commit v7 on v6

--- a/solution.py
+++ b/solution.py
@@ -11,7 +11,7 @@
 STEPS = 2
 LANES = 128
 WIDE_BLOCK = 256
-SUB = 16
+SUB = 8
 TOP = 14.0
 LN2 = math.log(2.0)
 STRIPS, PIECES, BLOCK = 17, 4, 256
@@ -58,7 +58,7 @@
 
     def half(self):
         x, z = lax.axis_index("narrow"), lax.axis_index("wide")
-        return lax.axis_index("tile") ^ ((x ^ z ^ (z >> 1)) & 1)
+        return lax.axis_index("tile") ^ ((x ^ z) & 1)
 
     def list_strips(self):
         side, per, w = self.stations // LANES, self.group, self.width
@@ -437,7 +437,7 @@
 
 def exchange(plan, x, mask):
     dz, dx = divmod(mask, plan.narrow)
-    mask = 2 * mask + ((dx ^ dz ^ (dz >> 1)) & 1)
+    mask = 2 * mask + ((dx ^ dz) & 1)
     pairs = [(i, i ^ mask) for i in range(2 * plan.wide * plan.narrow)]
     return lax.ppermute(x, ("wide", "narrow", "tile"), pairs)
 

time: 57.8 us -> 57.1 us (0.988)
  waiting for transfers between devices: 18.3 us -> 16.6 us
  starting transfers between devices: 21.8 us -> 22.8 us
    ppermute x14, waiting for transfers between devices: 18 us -> 16.5 us  [exchange(): return lax.ppermute(x, ('wide', 'narrow', 'tile'), pairs)]
    ppermute x10, starting transfers between devices: 1.7 us -> 2.76 us  [swap_cores(): return lax.ppermute(x, 'tile', [(0, 1), (1, 0)])]
  transfers between devices with their start and end apart: 24 -> 24, of which waited for: 11 -> 10; matrix products, arithmetic and copies ran while one was open for 0% -> 0% of each run, Pallas kernels for 11% -> 12%
where the time goes in v7:
time: 57.1 us; the launch traced here: 56.9 us
  starting transfers between devices  22.8 us (40%)
  waiting for transfers between devices  16.6 us (29%)
  Pallas kernels  15.8 us (28%)
  between operations  0.99 us (2%)
  other arithmetic  0.72 us (1%)
    ppermute x14, starting transfers between devices, exchange(): return lax.ppermute(x, ('wide', 'narrow', 'tile'), pairs)  20 us
    ppermute x14, waiting for transfers between devices, exchange(): return lax.ppermute(x, ('wide', 'narrow', 'tile'), pairs)  16.5 us
    pallas_call x12, Pallas kernels, call(): pl.pallas_call(body, in_specs=specs, out_specs=out_specs or jax.tree.map(...  15.8 us
    ppermute x10, starting transfers between devices, swap_cores(): return lax.ppermute(x, 'tile', [(0, 1), (1, 0)])  2.76 us
  transfers between devices with their start and end apart: 24, of which 10 were waited for; matrix products, arithmetic and copies ran while one was open for 0% of the time, Pallas kernels for 12%

profile of v7, /device:TPU:0, one launch (start us, length us, event | category | flops | bytes accessed | tf_op | source)
XLA Modules:
  0.0 56.9 jit_solution(6644984273241170059)
XLA Ops:
  0.6 2.9 %shard_map.77 = (f32[4,272,128]{2,1,0:T(8,128)S(1)}, bf16[2,1024,512]{2,1,0:T(8,128)(2,1)S(1)}, bf16[1024,1024]{1,0:T(8,128)(2,1)S(1)}) custom-call(f32[8,128]{1,0:T(8,128)} %bitcast.19, bf16[1024,1024]{1,0:T(8,128)(2,1)} %refs_1_.2), custom_call_target="tpu_custom_call" | custom-call | tf_op jit(solution)/shard_map/pallas_call | solution.py:424
  3.6 0.5 collective-permute-start
  4.1 1.1 %shard_map.78 = f32[4,272,128]{2,1,0:T(8,128)S(1)} custom-call(bf16[1024,1024]{1,0:T(8,128)(2,1)S(1)} %get-tuple-element.17.refs_0_.refs_1_, bf16[2,1024,512]{2,1,0:T(8,128)(2,1)S(1)} %get-tuple-element.18.refs_1_), custom_call_target="tpu_custom_call" | custom-call | tf_op jit(solution)/shard_map/pallas_call | solution.py:424
  5.2 0.0 copy-start.3
  5.2 0.0 copy-start.4
  5.2 0.0 collective-permute-done
  5.3 0.1 fusion.8
  5.4 3.9 %collective-permute-start.1 = (f16[272,128]{1,0:T(8,128)(2,1)S(1)}, f16[272,128]{1,0:T(8,128)(2,1)S(1)}, u32[]{:S(2)}, u32[]{:S(2)}) collective-permute-start(f16[272,128]{1,0:T(8,128)(2,1)S(1)} %get-tuple-element.36), channel_id=1, source_target_pairs={{0,6},{1,7},{2,4},{3,5},{4,2},{5,3},{6,0},{7,1},{8,14},{9,15},{10,... | collective-permute-start | bytes 208904 | tf_op jit(solution)/shard_map/ppermute | solution.py:442
  9.3 0.4 collective-permute-start.2
  9.7 2.2 %collective-permute-done.1 = f16[272,128]{1,0:T(8,128)(2,1)S(1)} collective-permute-done((f16[272,128]{1,0:T(8,128)(2,1)S(1)}, f16[272,128]{1,0:T(8,128)(2,1)S(1)}, u32[]{:S(2)}, u32[]{:S(2)}) %collective-permute-start.1) | collective-permute-done | bytes 69664 | tf_op jit(solution)/shard_map/ppermute | solution.py:442
  11.9 1.9 %collective-permute-done.3 = f16[272,128]{1,0:T(8,128)(2,1)S(1)} collective-permute-done((f16[272,128]{1,0:T(8,128)(2,1)S(1)}, f16[272,128]{1,0:T(8,128)(2,1)S(1)}, u32[]{:S(2)}, u32[]{:S(2)}) %collective-permute-start.3) | collective-permute-done | bytes 69664 | tf_op jit(solution)/shard_map/ppermute | solution.py:442
  13.7 0.1 fusion.12
  13.9 0.0 copy-start.1
  13.9 3.0 %collective-permute-start.4 = (f16[272,128]{1,0:T(8,128)(2,1)S(1)}, f16[272,128]{1,0:T(8,128)(2,1)S(1)}, u32[]{:S(2)}, u32[]{:S(2)}) collective-permute-start(f16[272,128]{1,0:T(8,128)(2,1)S(1)} %get-tuple-element.34), channel_id=1, source_target_pairs={{0,13},{1,12},{2,15},{3,14},{4,9},{5,8},{6,11},{7,10},{8,5},{9,4},... | collective-permute-start | bytes 208904 | tf_op jit(solution)/shard_map/ppermute | solution.py:442
  16.9 2.0 %shard_map.79 = (f32[272,128]{1,0:T(8,128)S(1)}, s32[528]{0:T(1024)S(4)}, s32[528]{0:T(1024)S(4)}) custom-call(s32[204]{0:T(256)S(1)} %copy-done.4, f32[528,512]{1,0:T(8,128)S(1)} %copy-done, s32[528]{0:T(1024)S(1)} %copy-done.2, s32[528]{0:T(1024)S(1)} %copy-done.3), custom_call_target="tpu_custom_call" | custom-call | tf_op jit(solution)/shard_map/pallas_call | solution.py:424
  18.9 1.1 %collective-permute-done.4 = f16[272,128]{1,0:T(8,128)(2,1)S(1)} collective-permute-done((f16[272,128]{1,0:T(8,128)(2,1)S(1)}, f16[272,128]{1,0:T(8,128)(2,1)S(1)}, u32[]{:S(2)}, u32[]{:S(2)}) %collective-permute-start.4) | collective-permute-done | bytes 69664 | tf_op jit(solution)/shard_map/ppermute | solution.py:442
  20.1 0.1 collective-permute-start.7
  20.2 1.7 %collective-permute-start.6 = (bf16[272,128]{1,0:T(8,128)(2,1)S(1)}, bf16[272,128]{1,0:T(8,128)(2,1)S(1)}, u32[]{:S(2)}, u32[]{:S(2)}) collective-permute-start(bf16[272,128]{1,0:T(8,128)(2,1)S(1)} %tanh_convert_fusion.refs_1_), channel_id=1, source_target_pairs={{0,3},{1,2},{2,1},{3,0},{4,7},{5,6},{6,5},{7,4},{8,11},{9,10},{10,... | collective-permute-start | bytes 208904 | tf_op jit(solution)/shard_map/ppermute | solution.py:442
  21.9 1.5 %collective-permute-start.5 = (bf16[272,128]{1,0:T(8,128)(2,1)S(1)}, bf16[272,128]{1,0:T(8,128)(2,1)S(1)}, u32[]{:S(2)}, u32[]{:S(2)}) collective-permute-start(bf16[272,128]{1,0:T(8,128)(2,1)S(1)} %tanh_convert_fusion.refs_1_), channel_id=1, source_target_pairs={{0,5},{1,4},{2,7},{3,6},{4,1},{5,0},{6,3},{7,2},{8,13},{9,12},{10,... | collective-permute-start | bytes 208904 | tf_op jit(solution)/shard_map/ppermute | solution.py:442
  23.4 2.1 %collective-permute-done.7.refs_4_ = bf16[272,128]{1,0:T(8,128)(2,1)S(1)} collective-permute-done((bf16[272,128]{1,0:T(8,128)(2,1)S(1)}, bf16[272,128]{1,0:T(8,128)(2,1)S(1)}, u32[]{:S(2)}, u32[]{:S(2)}) %collective-permute-start.7) | collective-permute-done | bytes 69664 | tf_op jit(solution)/shard_map/ppermute | solution.py:442
  25.4 0.1 collective-permute-done.6.refs_3_
  25.5 0.8 %collective-permute-start.10 = (bf16[272,128]{1,0:T(8,128)(2,1)S(1)}, bf16[272,128]{1,0:T(8,128)(2,1)S(1)}, u32[]{:S(2)}, u32[]{:S(2)}) collective-permute-start(bf16[272,128]{1,0:T(8,128)(2,1)S(1)} %collective-permute-done.6.refs_3_), channel_id=1, source_target_pairs={{0,1},{1,0},{2,3},{3,2},{4,5},{5,4},{6,7},{7,6},{8,9},{9,8},{10,11... | collective-permute-start | bytes 208904 | tf_op jit(solution)/shard_map/ppermute | solution.py:435
  26.3 0.2 collective-permute-start.9
  26.5 1.1 %shard_map.80.refs_2_ = f32[1024,128]{1,0:T(8,128)S(1)} custom-call(bf16[1024,1024]{1,0:T(8,128)(2,1)S(1)} %get-tuple-element.17.refs_0_.refs_1_, bf16[272,128]{1,0:T(8,128)(2,1)S(1)} %tanh_convert_fusion.refs_1_, bf16[272,128]{1,0:T(8,128)(2,1)S(1)} %collective-permute-done.5.refs_2_, bf16[272,128]{1,0:T(8,128)(2,1)S(1)} %collective-permute-done.6.refs_3_, ...), custom_call_target="tpu_custom_call" | custom-call | tf_op jit(solution)/shard_map/pallas_call | solution.py:424
  27.7 3.0 %shard_map.81 = (f32[4,280,128]{2,1,0:T(8,128)S(1)}, bf16[2,1024,512]{2,1,0:T(8,128)(2,1)S(1)}, f32[8,128]{1,0:T(8,128)S(1)}) custom-call(f32[8,128]{1,0:T(8,128)S(1)} %bitcast.20, bf16[1024,1024]{1,0:T(8,128)(2,1)S(1)} %get-tuple-element.17.refs_0_.refs_1_, f32[1024,128]{1,0:T(8,128)S(1)} %shard_map.80.refs_2_, ...), custom_call_target="tpu_custom_call" | custom-call | tf_op jit(solution)/shard_map/pallas_call | solution.py:424
  30.6 0.1 shard_map.83
  30.7 0.4 collective-permute-start.12
  31.1 1.2 %shard_map.82.refs_0_ = f32[4,280,128]{2,1,0:T(8,128)S(1)} custom-call(bf16[1024,1024]{1,0:T(8,128)(2,1)S(1)} %get-tuple-element.17.refs_0_.refs_1_, bf16[2,1024,512]{2,1,0:T(8,128)(2,1)S(1)} %get-tuple-element.22.refs_1_), custom_call_target="tpu_custom_call" | custom-call | tf_op jit(solution)/shard_map/pallas_call | solution.py:424
  32.4 0.1 shard_map.84
  32.5 1.8 %collective-permute-start.15 = (f16[280,128]{1,0:T(8,128)(2,1)S(1)}, f16[280,128]{1,0:T(8,128)(2,1)S(1)}, u32[]{:S(2)}, u32[]{:S(2)}) collective-permute-start(f16[280,128]{1,0:T(8,128)(2,1)S(1)} %convert_element_type.119), channel_id=1, source_target_pairs={{0,6},{1,7},{2,4},{3,5},{4,2},{5,3},{6,0},{7,1},{8,14},{9,15},{10,... | collective-permute-start | bytes 215048 | tf_op jit(solution)/shard_map/ppermute | solution.py:442
  34.3 0.7 %collective-permute-start.14 = (f16[280,128]{1,0:T(8,128)(2,1)S(1)}, f16[280,128]{1,0:T(8,128)(2,1)S(1)}, u32[]{:S(2)}, u32[]{:S(2)}) collective-permute-start(f16[280,128]{1,0:T(8,128)(2,1)S(1)} %convert_element_type.117), channel_id=1, source_target_pairs={{0,3},{1,2},{2,1},{3,0},{4,7},{5,6},{6,5},{7,4},{8,11},{9,10},{10,... | collective-permute-start | bytes 215048 | tf_op jit(solution)/shard_map/ppermute | solution.py:442
  35.0 0.9 %collective-permute-start.13 = (f16[280,128]{1,0:T(8,128)(2,1)S(1)}, f16[280,128]{1,0:T(8,128)(2,1)S(1)}, u32[]{:S(2)}, u32[]{:S(2)}) collective-permute-start(f16[280,128]{1,0:T(8,128)(2,1)S(1)} %convert_element_type.115), channel_id=1, source_target_pairs={{0,5},{1,4},{2,7},{3,6},{4,1},{5,0},{6,3},{7,2},{8,13},{9,12},{10,... | collective-permute-start | bytes 215048 | tf_op jit(solution)/shard_map/ppermute | solution.py:442
  35.9 2.2 %collective-permute-done.15 = f16[280,128]{1,0:T(8,128)(2,1)S(1)} collective-permute-done((f16[280,128]{1,0:T(8,128)(2,1)S(1)}, f16[280,128]{1,0:T(8,128)(2,1)S(1)}, u32[]{:S(2)}, u32[]{:S(2)}) %collective-permute-start.15) | collective-permute-done | bytes 71712 | tf_op jit(solution)/shard_map/ppermute | solution.py:442
  38.1 1.4 %collective-permute-done.14 = f16[280,128]{1,0:T(8,128)(2,1)S(1)} collective-permute-done((f16[280,128]{1,0:T(8,128)(2,1)S(1)}, f16[280,128]{1,0:T(8,128)(2,1)S(1)}, u32[]{:S(2)}, u32[]{:S(2)}) %collective-permute-start.14) | collective-permute-done | bytes 71712 | tf_op jit(solution)/shard_map/ppermute | solution.py:442
  39.6 0.1 shard_map.85
  39.6 0.1 reduce-precision_convert_fusion.1
  39.7 2.8 %collective-permute-start.16 = (f16[280,128]{1,0:T(8,128)(2,1)S(1)}, f16[280,128]{1,0:T(8,128)(2,1)S(1)}, u32[]{:S(2)}, u32[]{:S(2)}) collective-permute-start(f16[280,128]{1,0:T(8,128)(2,1)S(1)} %get-tuple-element.39), channel_id=1, source_target_pairs={{0,13},{1,12},{2,15},{3,14},{4,9},{5,8},{6,11},{7,10},{8,5},{9,4},... | collective-permute-start | bytes 215048 | tf_op jit(solution)/shard_map/ppermute | solution.py:442
  42.5 3.4 %collective-permute-done.16 = f16[280,128]{1,0:T(8,128)(2,1)S(1)} collective-permute-done((f16[280,128]{1,0:T(8,128)(2,1)S(1)}, f16[280,128]{1,0:T(8,128)(2,1)S(1)}, u32[]{:S(2)}, u32[]{:S(2)}) %collective-permute-start.16) | collective-permute-done | bytes 71712 | tf_op jit(solution)/shard_map/ppermute | solution.py:442
  46.0 0.1 fusion.11
  46.1 0.1 collective-permute-start.19
  46.1 1.8 %collective-permute-start.18 = (f16[272,128]{1,0:T(8,128)(2,1)S(1)}, f16[272,128]{1,0:T(8,128)(2,1)S(1)}, u32[]{:S(2)}, u32[]{:S(2)}) collective-permute-start(f16[272,128]{1,0:T(8,128)(2,1)S(1)} %get-tuple-element.33), channel_id=1, source_target_pairs={{0,3},{1,2},{2,1},{3,0},{4,7},{5,6},{6,5},{7,4},{8,11},{9,10},{10,... | collective-permute-start | bytes 208904 | tf_op jit(solution)/shard_map/ppermute | solution.py:442
  48.0 1.4 %collective-permute-start.17 = (f16[272,128]{1,0:T(8,128)(2,1)S(1)}, f16[272,128]{1,0:T(8,128)(2,1)S(1)}, u32[]{:S(2)}, u32[]{:S(2)}) collective-permute-start(f16[272,128]{1,0:T(8,128)(2,1)S(1)} %get-tuple-element.33), channel_id=1, source_target_pairs={{0,5},{1,4},{2,7},{3,6},{4,1},{5,0},{6,3},{7,2},{8,13},{9,12},{10,... | collective-permute-start | bytes 208904 | tf_op jit(solution)/shard_map/ppermute | solution.py:442
  49.3 2.1 %collective-permute-done.19 = f16[272,128]{1,0:T(8,128)(2,1)S(1)} collective-permute-done((f16[272,128]{1,0:T(8,128)(2,1)S(1)}, f16[272,128]{1,0:T(8,128)(2,1)S(1)}, u32[]{:S(2)}, u32[]{:S(2)}) %collective-permute-start.19) | collective-permute-done | bytes 69664 | tf_op jit(solution)/shard_map/ppermute | solution.py:442
  51.4 0.2 collective-permute-done.18
  51.6 0.6 %collective-permute-start.22 = (f16[272,128]{1,0:T(8,128)(2,1)S(1)}, f16[272,128]{1,0:T(8,128)(2,1)S(1)}, u32[]{:S(2)}, u32[]{:S(2)}) collective-permute-start(f16[272,128]{1,0:T(8,128)(2,1)S(1)} %collective-permute-done.18), channel_id=1, source_target_pairs={{0,1},{1,0},{2,3},{3,2},{4,5},{5,4},{6,7},{7,6},{8,9},{9,8},{10,11... | collective-permute-start | bytes 208904 | tf_op jit(solution)/shard_map/ppermute | solution.py:435
  52.1 0.3 collective-permute-start.21
  52.5 1.1 %shard_map.87.refs_2_ = f32[1024,128]{1,0:T(8,128)S(1)} custom-call(bf16[1024,1024]{1,0:T(8,128)(2,1)S(1)} %get-tuple-element.17.refs_0_.refs_1_, f32[272,128]{1,0:T(8,128)S(1)} %get-tuple-element.32.refs_1_.refs_5_, f32[272,128]{1,0:T(8,128)S(1)} %convert_element_type.125.refs_2_.refs_6_, f32[272,128]{1,0:T(8,128)S(1)} %convert_element_type.126.refs_3_.refs_7_, ...), custom_call_target="tpu_custom_call" | custom-call | tf_op jit(solution)/shard_map/pallas_call | solution.py:424
  53.7 3.2 %shard_map.88 = (f32[8,128]{1,0:T(8,128)}, f32[132,512]{1,0:T(8,128)}) custom-call(f32[8,128]{1,0:T(8,128)S(1)} %get-tuple-element.21.refs_0_, bf16[1024,1024]{1,0:T(8,128)(2,1)S(1)} %get-tuple-element.17.refs_0_.refs_1_, f32[1024,128]{1,0:T(8,128)S(1)} %shard_map.87.refs_2_, s32[528]{0:T(1024)S(4)} %get-tuple-element.28.refs_3_, ...), custom_call_target="tpu_custom_call" | custom-call | tf_op jit(solution)/shard_map/pallas_call | solution.py:424
  (45 shorter events, 0.5 us)
Async XLA Ops:
  3.6 1.7 %collective-permute-start = (f16[4,272,128]{2,1,0:T(8,128)(2,1)S(1)}, f16[4,272,128]{2,1,0:T(8,128)(2,1)S(1)}, u32[]{:S(2)}, u32[]{:S(2)}) collective-permute-start(f16[4,272,128]{2,1,0:T(8,128)(2,1)S(1)} %convert_element_type.99), channel_id=1, source_target_pairs={{0,1},{1,0},{2,3},{3,2},{4,5},{5,4},{6,7},{7,6},{8,9},{9,8},{10,11... | collective-permute-start | bytes 835592 | tf_op jit(solution)/shard_map/ppermute | solution.py:435
  5.2 11.7 %copy-start = (f32[528,512]{1,0:T(8,128)S(1)}, f32[528,512]{1,0:T(8,128)}, u32[]{:S(2)}) copy-start(f32[528,512]{1,0:T(8,128)} %refs_1_.3) | copy-start | bytes 3244036
  5.2 11.7 %copy-start.2 = (s32[528]{0:T(1024)S(1)}, s32[528]{0:T(1024)}, u32[]{:S(2)}) copy-start(s32[528]{0:T(1024)} %refs_2_.1) | copy-start | bytes 6340
  5.2 11.7 %copy-start.3 = (s32[528]{0:T(1024)S(1)}, s32[528]{0:T(1024)}, u32[]{:S(2)}) copy-start(s32[528]{0:T(1024)} %constant.4.clone.refs_3_) | copy-start | bytes 6340
  5.2 11.7 %copy-start.4 = (s32[204]{0:T(256)S(1)}, s32[204]{0:T(256)}, u32[]{:S(2)}) copy-start(s32[204]{0:T(256)} %constant.5.clone.refs_0_) | copy-start | bytes 2452
  5.4 6.5 %collective-permute-start.1 = (f16[272,128]{1,0:T(8,128)(2,1)S(1)}, f16[272,128]{1,0:T(8,128)(2,1)S(1)}, u32[]{:S(2)}, u32[]{:S(2)}) collective-permute-start(f16[272,128]{1,0:T(8,128)(2,1)S(1)} %get-tuple-element.36), channel_id=1, source_target_pairs={{0,6},{1,7},{2,4},{3,5},{4,2},{5,3},{6,0},{7,1},{8,14},{9,15},{10,... | collective-permute-start | bytes 208904 | tf_op jit(solution)/shard_map/ppermute | solution.py:442
  9.3 4.4 %collective-permute-start.3 = (f16[272,128]{1,0:T(8,128)(2,1)S(1)}, f16[272,128]{1,0:T(8,128)(2,1)S(1)}, u32[]{:S(2)}, u32[]{:S(2)}) collective-permute-start(f16[272,128]{1,0:T(8,128)(2,1)S(1)} %get-tuple-element.37), channel_id=1, source_target_pairs={{0,3},{1,2},{2,1},{3,0},{4,7},{5,6},{6,5},{7,4},{8,11},{9,10},{10,... | collective-permute-start | bytes 208904 | tf_op jit(solution)/shard_map/ppermute | solution.py:442
  9.3 4.4 %collective-permute-start.2 = (f16[272,128]{1,0:T(8,128)(2,1)S(1)}, f16[272,128]{1,0:T(8,128)(2,1)S(1)}, u32[]{:S(2)}, u32[]{:S(2)}) collective-permute-start(f16[272,128]{1,0:T(8,128)(2,1)S(1)} %get-tuple-element.38), channel_id=1, source_target_pairs={{0,5},{1,4},{2,7},{3,6},{4,1},{5,0},{6,3},{7,2},{8,13},{9,12},{10,... | collective-permute-start | bytes 208904 | tf_op jit(solution)/shard_map/ppermute | solution.py:442
  13.9 13.8 %copy-start.1 = (f32[1024]{0:T(1024)S(1)}, f32[1024]{0:T(1024)}, u32[]{:S(2)}) copy-start(f32[1024]{0:T(1024)} %param.7) | copy-start | bytes 12292
  13.9 6.1 %collective-permute-start.4 = (f16[272,128]{1,0:T(8,128)(2,1)S(1)}, f16[272,128]{1,0:T(8,128)(2,1)S(1)}, u32[]{:S(2)}, u32[]{:S(2)}) collective-permute-start(f16[272,128]{1,0:T(8,128)(2,1)S(1)} %get-tuple-element.34), channel_id=1, source_target_pairs={{0,13},{1,12},{2,15},{3,14},{4,9},{5,8},{6,11},{7,10},{8,5},{9,4},... | collective-permute-start | bytes 208904 | tf_op jit(solution)/shard_map/ppermute | solution.py:442
  20.1 5.3 %collective-permute-start.7 = (bf16[272,128]{1,0:T(8,128)(2,1)S(1)}, bf16[272,128]{1,0:T(8,128)(2,1)S(1)}, u32[]{:S(2)}, u32[]{:S(2)}) collective-permute-start(bf16[272,128]{1,0:T(8,128)(2,1)S(1)} %tanh_convert_fusion.refs_1_), channel_id=1, source_target_pairs={{0,6},{1,7},{2,4},{3,5},{4,2},{5,3},{6,0},{7,1},{8,14},{9,15},{10,... | collective-permute-start | bytes 208904 | tf_op jit(solution)/shard_map/ppermute | solution.py:442
  20.2 5.3 %collective-permute-start.6 = (bf16[272,128]{1,0:T(8,128)(2,1)S(1)}, bf16[272,128]{1,0:T(8,128)(2,1)S(1)}, u32[]{:S(2)}, u32[]{:S(2)}) collective-permute-start(bf16[272,128]{1,0:T(8,128)(2,1)S(1)} %tanh_convert_fusion.refs_1_), channel_id=1, source_target_pairs={{0,3},{1,2},{2,1},{3,0},{4,7},{5,6},{6,5},{7,4},{8,11},{9,10},{10,... | collective-permute-start | bytes 208904 | tf_op jit(solution)/shard_map/ppermute | solution.py:442
  21.9 4.5 %collective-permute-start.5 = (bf16[272,128]{1,0:T(8,128)(2,1)S(1)}, bf16[272,128]{1,0:T(8,128)(2,1)S(1)}, u32[]{:S(2)}, u32[]{:S(2)}) collective-permute-start(bf16[272,128]{1,0:T(8,128)(2,1)S(1)} %tanh_convert_fusion.refs_1_), channel_id=1, source_target_pairs={{0,5},{1,4},{2,7},{3,6},{4,1},{5,0},{6,3},{7,2},{8,13},{9,12},{10,... | collective-permute-start | bytes 208904 | tf_op jit(solution)/shard_map/ppermute | solution.py:442
  23.4 4.3 %collective-permute-start.8 = (bf16[272,128]{1,0:T(8,128)(2,1)S(1)}, bf16[272,128]{1,0:T(8,128)(2,1)S(1)}, u32[]{:S(2)}, u32[]{:S(2)}) collective-permute-start(bf16[272,128]{1,0:T(8,128)(2,1)S(1)} %tanh_convert_fusion.refs_1_), channel_id=1, source_target_pairs={{0,1},{1,0},{2,3},{3,2},{4,5},{5,4},{6,7},{7,6},{8,9},{9,8},{10,11... | collective-permute-start | bytes 208904 | tf_op jit(solution)/shard_map/ppermute | solution.py:435
  25.4 2.2 %collective-permute-start.11 = (bf16[272,128]{1,0:T(8,128)(2,1)S(1)}, bf16[272,128]{1,0:T(8,128)(2,1)S(1)}, u32[]{:S(2)}, u32[]{:S(2)}) collective-permute-start(bf16[272,128]{1,0:T(8,128)(2,1)S(1)} %collective-permute-done.7.refs_4_), channel_id=1, source_target_pairs={{0,1},{1,0},{2,3},{3,2},{4,5},{5,4},{6,7},{7,6},{8,9},{9,8},{10,11... | collective-permute-start | bytes 208904 | tf_op jit(solution)/shard_map/ppermute | solution.py:435
  25.5 2.1 %collective-permute-start.10 = (bf16[272,128]{1,0:T(8,128)(2,1)S(1)}, bf16[272,128]{1,0:T(8,128)(2,1)S(1)}, u32[]{:S(2)}, u32[]{:S(2)}) collective-permute-start(bf16[272,128]{1,0:T(8,128)(2,1)S(1)} %collective-permute-done.6.refs_3_), channel_id=1, source_target_pairs={{0,1},{1,0},{2,3},{3,2},{4,5},{5,4},{6,7},{7,6},{8,9},{9,8},{10,11... | collective-permute-start | bytes 208904 | tf_op jit(solution)/shard_map/ppermute | solution.py:435
  26.3 1.3 %collective-permute-start.9 = (bf16[272,128]{1,0:T(8,128)(2,1)S(1)}, bf16[272,128]{1,0:T(8,128)(2,1)S(1)}, u32[]{:S(2)}, u32[]{:S(2)}) collective-permute-start(bf16[272,128]{1,0:T(8,128)(2,1)S(1)} %collective-permute-done.5.refs_2_), channel_id=1, source_target_pairs={{0,1},{1,0},{2,3},{3,2},{4,5},{5,4},{6,7},{7,6},{8,9},{9,8},{10,11... | collective-permute-start | bytes 208904 | tf_op jit(solution)/shard_map/ppermute | solution.py:435
  30.7 1.6 %collective-permute-start.12 = (f16[4,280,128]{2,1,0:T(8,128)(2,1)S(1)}, f16[4,280,128]{2,1,0:T(8,128)(2,1)S(1)}, u32[]{:S(2)}, u32[]{:S(2)}) collective-permute-start(f16[4,280,128]{2,1,0:T(8,128)(2,1)S(1)} %convert_element_type.113), channel_id=1, source_target_pairs={{0,1},{1,0},{2,3},{3,2},{4,5},{5,4},{6,7},{7,6},{8,9},{9,8},{10,11... | collective-permute-start | bytes 860168 | tf_op jit(solution)/shard_map/ppermute | solution.py:435
  32.5 5.5 %collective-permute-start.15 = (f16[280,128]{1,0:T(8,128)(2,1)S(1)}, f16[280,128]{1,0:T(8,128)(2,1)S(1)}, u32[]{:S(2)}, u32[]{:S(2)}) collective-permute-start(f16[280,128]{1,0:T(8,128)(2,1)S(1)} %convert_element_type.119), channel_id=1, source_target_pairs={{0,6},{1,7},{2,4},{3,5},{4,2},{5,3},{6,0},{7,1},{8,14},{9,15},{10,... | collective-permute-start | bytes 215048 | tf_op jit(solution)/shard_map/ppermute | solution.py:442
  34.3 5.2 %collective-permute-start.14 = (f16[280,128]{1,0:T(8,128)(2,1)S(1)}, f16[280,128]{1,0:T(8,128)(2,1)S(1)}, u32[]{:S(2)}, u32[]{:S(2)}) collective-permute-start(f16[280,128]{1,0:T(8,128)(2,1)S(1)} %convert_element_type.117), channel_id=1, source_target_pairs={{0,3},{1,2},{2,1},{3,0},{4,7},{5,6},{6,5},{7,4},{8,11},{9,10},{10,... | collective-permute-start | bytes 215048 | tf_op jit(solution)/shard_map/ppermute | solution.py:442
  35.0 4.5 %collective-permute-start.13 = (f16[280,128]{1,0:T(8,128)(2,1)S(1)}, f16[280,128]{1,0:T(8,128)(2,1)S(1)}, u32[]{:S(2)}, u32[]{:S(2)}) collective-permute-start(f16[280,128]{1,0:T(8,128)(2,1)S(1)} %convert_element_type.115), channel_id=1, source_target_pairs={{0,5},{1,4},{2,7},{3,6},{4,1},{5,0},{6,3},{7,2},{8,13},{9,12},{10,... | collective-permute-start | bytes 215048 | tf_op jit(solution)/shard_map/ppermute | solution.py:442
  39.7 6.2 %collective-permute-start.16 = (f16[280,128]{1,0:T(8,128)(2,1)S(1)}, f16[280,128]{1,0:T(8,128)(2,1)S(1)}, u32[]{:S(2)}, u32[]{:S(2)}) collective-permute-start(f16[280,128]{1,0:T(8,128)(2,1)S(1)} %get-tuple-element.39), channel_id=1, source_target_pairs={{0,13},{1,12},{2,15},{3,14},{4,9},{5,8},{6,11},{7,10},{8,5},{9,4},... | collective-permute-start | bytes 215048 | tf_op jit(solution)/shard_map/ppermute | solution.py:442
  46.1 5.3 %collective-permute-start.19 = (f16[272,128]{1,0:T(8,128)(2,1)S(1)}, f16[272,128]{1,0:T(8,128)(2,1)S(1)}, u32[]{:S(2)}, u32[]{:S(2)}) collective-permute-start(f16[272,128]{1,0:T(8,128)(2,1)S(1)} %get-tuple-element.33), channel_id=1, source_target_pairs={{0,6},{1,7},{2,4},{3,5},{4,2},{5,3},{6,0},{7,1},{8,14},{9,15},{10,... | collective-permute-start | bytes 208904 | tf_op jit(solution)/shard_map/ppermute | solution.py:442
  46.1 5.4 %collective-permute-start.18 = (f16[272,128]{1,0:T(8,128)(2,1)S(1)}, f16[272,128]{1,0:T(8,128)(2,1)S(1)}, u32[]{:S(2)}, u32[]{:S(2)}) collective-permute-start(f16[272,128]{1,0:T(8,128)(2,1)S(1)} %get-tuple-element.33), channel_id=1, source_target_pairs={{0,3},{1,2},{2,1},{3,0},{4,7},{5,6},{6,5},{7,4},{8,11},{9,10},{10,... | collective-permute-start | bytes 208904 | tf_op jit(solution)/shard_map/ppermute | solution.py:442
  48.0 4.2 %collective-permute-start.17 = (f16[272,128]{1,0:T(8,128)(2,1)S(1)}, f16[272,128]{1,0:T(8,128)(2,1)S(1)}, u32[]{:S(2)}, u32[]{:S(2)}) collective-permute-start(f16[272,128]{1,0:T(8,128)(2,1)S(1)} %get-tuple-element.33), channel_id=1, source_target_pairs={{0,5},{1,4},{2,7},{3,6},{4,1},{5,0},{6,3},{7,2},{8,13},{9,12},{10,... | collective-permute-start | bytes 208904 | tf_op jit(solution)/shard_map/ppermute | solution.py:442
  49.3 4.3 %collective-permute-start.20 = (f16[272,128]{1,0:T(8,128)(2,1)S(1)}, f16[272,128]{1,0:T(8,128)(2,1)S(1)}, u32[]{:S(2)}, u32[]{:S(2)}) collective-permute-start(f16[272,128]{1,0:T(8,128)(2,1)S(1)} %get-tuple-element.33), channel_id=1, source_target_pairs={{0,1},{1,0},{2,3},{3,2},{4,5},{5,4},{6,7},{7,6},{8,9},{9,8},{10,11... | collective-permute-start | bytes 208904 | tf_op jit(solution)/shard_map/ppermute | solution.py:435
  51.4 2.3 %collective-permute-start.23 = (f16[272,128]{1,0:T(8,128)(2,1)S(1)}, f16[272,128]{1,0:T(8,128)(2,1)S(1)}, u32[]{:S(2)}, u32[]{:S(2)}) collective-permute-start(f16[272,128]{1,0:T(8,128)(2,1)S(1)} %collective-permute-done.19), channel_id=1, source_target_pairs={{0,1},{1,0},{2,3},{3,2},{4,5},{5,4},{6,7},{7,6},{8,9},{9,8},{10,11... | collective-permute-start | bytes 208904 | tf_op jit(solution)/shard_map/ppermute | solution.py:435
  51.6 2.1 %collective-permute-start.22 = (f16[272,128]{1,0:T(8,128)(2,1)S(1)}, f16[272,128]{1,0:T(8,128)(2,1)S(1)}, u32[]{:S(2)}, u32[]{:S(2)}) collective-permute-start(f16[272,128]{1,0:T(8,128)(2,1)S(1)} %collective-permute-done.18), channel_id=1, source_target_pairs={{0,1},{1,0},{2,3},{3,2},{4,5},{5,4},{6,7},{7,6},{8,9},{9,8},{10,11... | collective-permute-start | bytes 208904 | tf_op jit(solution)/shard_map/ppermute | solution.py:435
  52.1 1.6 %collective-permute-start.21 = (f16[272,128]{1,0:T(8,128)(2,1)S(1)}, f16[272,128]{1,0:T(8,128)(2,1)S(1)}, u32[]{:S(2)}, u32[]{:S(2)}) collective-permute-start(f16[272,128]{1,0:T(8,128)(2,1)S(1)} %collective-permute-done.17), channel_id=1, source_target_pairs={{0,1},{1,0},{2,3},{3,2},{4,5},{5,4},{6,7},{7,6},{8,9},{9,8},{10,11... | collective-permute-start | bytes 208904 | tf_op jit(solution)/shard_map/ppermute | solution.py:435

commit v8 on v7

--- a/solution.py
+++ b/solution.py
@@ -143,8 +143,13 @@
     return jnp.concatenate(parts, axis=0)
 
 
+def columns_of(rows):
+    blank = jnp.zeros((LANES - rows.shape[0], LANES), F32)
+    return jnp.concatenate([rows, blank], axis=0).T
+
+
 def weigh_rows(plan, green, strength, weighted, i):
-    column = jnp.broadcast_to(strength[i : i + 1, :], (LANES, LANES)).T
+    column = jnp.broadcast_to(strength[:, i : i + 1], (LANES, LANES))
     at = slice(i * LANES, (i + 1) * LANES)
     for h in range(2):
         for left in range(0, plan.stations, LANES):
@@ -285,7 +290,7 @@
     for copy in copies:
         copy.start()
     copies[0].wait()
-    strength = jnp.exp(log_ref[...])
+    strength = columns_of(jnp.exp(log_ref[...]))
     for k in range(pieces):
         copies[1 + k].wait()
         for i in range(k * size // LANES, (k + 1) * size // LANES):
@@ -318,7 +323,7 @@
     for k, ref in zip(plan.order, tiles):
         stack[k] = ref[...]
     fill_half(plan, lambda slot, at: stack[slot, at : at + plan.width, :], kernel)
-    strength = jnp.exp(new_log(plan, log_ref, green, total, kernel, log_out))
+    strength = columns_of(jnp.exp(new_log(plan, log_ref, green, total, kernel, log_out)))
     for i in range(plan.points // LANES):
         weigh_rows(plan, green, strength, weighted, i)
     product(plan, 1 - plan.half(), green, weighted, send)
@@ -369,15 +374,15 @@
             batch(p * batches + k)
         return carry
 
+    rest = plan.slots - whole * n
+    if rest:
+        for k, piece in enumerate(rows_of(whole * n, rest)):
+            residual[whole * n :, k * LANES : (k + 1) * LANES] = piece[:rest]
     lax.fori_loop(0, steps, step, 0)
     for i in range(batches * steps, whole):
         batch(i)
     log_now = log_ref[...]
     log_out[...] = log_now - 0.5 * jnp.exp(log_now) * sums[...]
-    rest = plan.slots - whole * n
-    if rest:
-        for k, piece in enumerate(rows_of(whole * n, rest)):
-            residual[whole * n :, k * LANES : (k + 1) * LANES] = piece[:rest]
 
 
 def scale_kernel(plan, send, out):

time: 57.1 us -> 57.1 us (level)
  no operation moved by 1% of the time
where the time goes in v8:
time: 57.1 us; the launch traced here: 56.9 us
  starting transfers between devices  22.7 us (40%)
  waiting for transfers between devices  16.6 us (29%)
  Pallas kernels  15.8 us (28%)
  between operations  0.99 us (2%)
  other arithmetic  0.72 us (1%)
    ppermute x14, starting transfers between devices, exchange(): return lax.ppermute(x, ('wide', 'narrow', 'tile'), pairs)  20 us
    ppermute x14, waiting for transfers between devices, exchange(): return lax.ppermute(x, ('wide', 'narrow', 'tile'), pairs)  16.5 us
    pallas_call x12, Pallas kernels, call(): pl.pallas_call(body, in_specs=specs, out_specs=out_specs or jax.tree.map(...  15.8 us
    ppermute x10, starting transfers between devices, swap_cores(): return lax.ppermute(x, 'tile', [(0, 1), (1, 0)])  2.73 us
  transfers between devices with their start and end apart: 24, of which 10 were waited for; matrix products, arithmetic and copies ran while one was open for 0% of the time, Pallas kernels for 12%

profile of v8, /device:TPU:0, one launch (start us, length us, event | category | flops | bytes accessed | tf_op | source)
XLA Modules:
  0.0 56.9 jit_solution(3163928310380039975)
XLA Ops:
  0.6 2.9 %shard_map.77 = (f32[4,272,128]{2,1,0:T(8,128)S(1)}, bf16[2,1024,512]{2,1,0:T(8,128)(2,1)S(1)}, bf16[1024,1024]{1,0:T(8,128)(2,1)S(1)}) custom-call(f32[8,128]{1,0:T(8,128)} %bitcast.19, bf16[1024,1024]{1,0:T(8,128)(2,1)} %refs_1_.2), custom_call_target="tpu_custom_call" | custom-call | tf_op jit(solution)/shard_map/pallas_call | solution.py:429
  3.6 0.5 collective-permute-start
  4.1 1.1 %shard_map.78 = f32[4,272,128]{2,1,0:T(8,128)S(1)} custom-call(bf16[1024,1024]{1,0:T(8,128)(2,1)S(1)} %get-tuple-element.17.refs_0_.refs_1_, bf16[2,1024,512]{2,1,0:T(8,128)(2,1)S(1)} %get-tuple-element.18.refs_1_), custom_call_target="tpu_custom_call" | custom-call | tf_op jit(solution)/shard_map/pallas_call | solution.py:429
  5.2 0.0 copy-start.2
  5.2 0.0 copy-start.3
  5.2 0.0 copy-start.4
  5.2 0.0 collective-permute-done
  5.3 0.1 fusion.8
  5.4 3.9 %collective-permute-start.1 = (f16[272,128]{1,0:T(8,128)(2,1)S(1)}, f16[272,128]{1,0:T(8,128)(2,1)S(1)}, u32[]{:S(2)}, u32[]{:S(2)}) collective-permute-start(f16[272,128]{1,0:T(8,128)(2,1)S(1)} %get-tuple-element.36), channel_id=1, source_target_pairs={{0,6},{1,7},{2,4},{3,5},{4,2},{5,3},{6,0},{7,1},{8,14},{9,15},{10,... | collective-permute-start | bytes 208904 | tf_op jit(solution)/shard_map/ppermute | solution.py:447
  9.3 0.4 collective-permute-start.2
  9.7 2.2 %collective-permute-done.1 = f16[272,128]{1,0:T(8,128)(2,1)S(1)} collective-permute-done((f16[272,128]{1,0:T(8,128)(2,1)S(1)}, f16[272,128]{1,0:T(8,128)(2,1)S(1)}, u32[]{:S(2)}, u32[]{:S(2)}) %collective-permute-start.1) | collective-permute-done | bytes 69664 | tf_op jit(solution)/shard_map/ppermute | solution.py:447
  11.9 1.9 %collective-permute-done.3 = f16[272,128]{1,0:T(8,128)(2,1)S(1)} collective-permute-done((f16[272,128]{1,0:T(8,128)(2,1)S(1)}, f16[272,128]{1,0:T(8,128)(2,1)S(1)}, u32[]{:S(2)}, u32[]{:S(2)}) %collective-permute-start.3) | collective-permute-done | bytes 69664 | tf_op jit(solution)/shard_map/ppermute | solution.py:447
  13.7 0.1 fusion.12
  13.9 3.0 %collective-permute-start.4 = (f16[272,128]{1,0:T(8,128)(2,1)S(1)}, f16[272,128]{1,0:T(8,128)(2,1)S(1)}, u32[]{:S(2)}, u32[]{:S(2)}) collective-permute-start(f16[272,128]{1,0:T(8,128)(2,1)S(1)} %get-tuple-element.34), channel_id=1, source_target_pairs={{0,13},{1,12},{2,15},{3,14},{4,9},{5,8},{6,11},{7,10},{8,5},{9,4},... | collective-permute-start | bytes 208904 | tf_op jit(solution)/shard_map/ppermute | solution.py:447
  16.9 2.0 %shard_map.79 = (f32[272,128]{1,0:T(8,128)S(1)}, s32[528]{0:T(1024)S(4)}, s32[528]{0:T(1024)S(4)}) custom-call(s32[204]{0:T(256)S(1)} %copy-done.4, f32[528,512]{1,0:T(8,128)S(1)} %copy-done, s32[528]{0:T(1024)S(1)} %copy-done.2, s32[528]{0:T(1024)S(1)} %copy-done.3), custom_call_target="tpu_custom_call" | custom-call | tf_op jit(solution)/shard_map/pallas_call | solution.py:429
  18.9 1.1 %collective-permute-done.4 = f16[272,128]{1,0:T(8,128)(2,1)S(1)} collective-permute-done((f16[272,128]{1,0:T(8,128)(2,1)S(1)}, f16[272,128]{1,0:T(8,128)(2,1)S(1)}, u32[]{:S(2)}, u32[]{:S(2)}) %collective-permute-start.4) | collective-permute-done | bytes 69664 | tf_op jit(solution)/shard_map/ppermute | solution.py:447
  20.1 0.1 collective-permute-start.7
  20.2 1.7 %collective-permute-start.6 = (bf16[272,128]{1,0:T(8,128)(2,1)S(1)}, bf16[272,128]{1,0:T(8,128)(2,1)S(1)}, u32[]{:S(2)}, u32[]{:S(2)}) collective-permute-start(bf16[272,128]{1,0:T(8,128)(2,1)S(1)} %tanh_convert_fusion.refs_1_), channel_id=1, source_target_pairs={{0,3},{1,2},{2,1},{3,0},{4,7},{5,6},{6,5},{7,4},{8,11},{9,10},{10,... | collective-permute-start | bytes 208904 | tf_op jit(solution)/shard_map/ppermute | solution.py:447
  21.9 1.5 %collective-permute-start.5 = (bf16[272,128]{1,0:T(8,128)(2,1)S(1)}, bf16[272,128]{1,0:T(8,128)(2,1)S(1)}, u32[]{:S(2)}, u32[]{:S(2)}) collective-permute-start(bf16[272,128]{1,0:T(8,128)(2,1)S(1)} %tanh_convert_fusion.refs_1_), channel_id=1, source_target_pairs={{0,5},{1,4},{2,7},{3,6},{4,1},{5,0},{6,3},{7,2},{8,13},{9,12},{10,... | collective-permute-start | bytes 208904 | tf_op jit(solution)/shard_map/ppermute | solution.py:447
  23.4 2.1 %collective-permute-done.7.refs_4_ = bf16[272,128]{1,0:T(8,128)(2,1)S(1)} collective-permute-done((bf16[272,128]{1,0:T(8,128)(2,1)S(1)}, bf16[272,128]{1,0:T(8,128)(2,1)S(1)}, u32[]{:S(2)}, u32[]{:S(2)}) %collective-permute-start.7) | collective-permute-done | bytes 69664 | tf_op jit(solution)/shard_map/ppermute | solution.py:447
  25.4 0.1 collective-permute-done.6.refs_3_
  25.5 0.8 %collective-permute-start.10 = (bf16[272,128]{1,0:T(8,128)(2,1)S(1)}, bf16[272,128]{1,0:T(8,128)(2,1)S(1)}, u32[]{:S(2)}, u32[]{:S(2)}) collective-permute-start(bf16[272,128]{1,0:T(8,128)(2,1)S(1)} %collective-permute-done.6.refs_3_), channel_id=1, source_target_pairs={{0,1},{1,0},{2,3},{3,2},{4,5},{5,4},{6,7},{7,6},{8,9},{9,8},{10,11... | collective-permute-start | bytes 208904 | tf_op jit(solution)/shard_map/ppermute | solution.py:440
  26.3 0.2 collective-permute-start.9
  26.5 1.1 %shard_map.80.refs_2_ = f32[1024,128]{1,0:T(8,128)S(1)} custom-call(bf16[1024,1024]{1,0:T(8,128)(2,1)S(1)} %get-tuple-element.17.refs_0_.refs_1_, bf16[272,128]{1,0:T(8,128)(2,1)S(1)} %tanh_convert_fusion.refs_1_, bf16[272,128]{1,0:T(8,128)(2,1)S(1)} %collective-permute-done.5.refs_2_, bf16[272,128]{1,0:T(8,128)(2,1)S(1)} %collective-permute-done.6.refs_3_, ...), custom_call_target="tpu_custom_call" | custom-call | tf_op jit(solution)/shard_map/pallas_call | solution.py:429
  27.7 3.0 %shard_map.81 = (f32[4,280,128]{2,1,0:T(8,128)S(1)}, bf16[2,1024,512]{2,1,0:T(8,128)(2,1)S(1)}, f32[8,128]{1,0:T(8,128)S(1)}) custom-call(f32[8,128]{1,0:T(8,128)S(1)} %bitcast.20, bf16[1024,1024]{1,0:T(8,128)(2,1)S(1)} %get-tuple-element.17.refs_0_.refs_1_, f32[1024,128]{1,0:T(8,128)S(1)} %shard_map.80.refs_2_, ...), custom_call_target="tpu_custom_call" | custom-call | tf_op jit(solution)/shard_map/pallas_call | solution.py:429
  30.7 0.1 shard_map.83
  30.8 0.4 collective-permute-start.12
  31.2 1.2 %shard_map.82.refs_0_ = f32[4,280,128]{2,1,0:T(8,128)S(1)} custom-call(bf16[1024,1024]{1,0:T(8,128)(2,1)S(1)} %get-tuple-element.17.refs_0_.refs_1_, bf16[2,1024,512]{2,1,0:T(8,128)(2,1)S(1)} %get-tuple-element.22.refs_1_), custom_call_target="tpu_custom_call" | custom-call | tf_op jit(solution)/shard_map/pallas_call | solution.py:429
  32.5 0.1 shard_map.84
  32.6 1.8 %collective-permute-start.15 = (f16[280,128]{1,0:T(8,128)(2,1)S(1)}, f16[280,128]{1,0:T(8,128)(2,1)S(1)}, u32[]{:S(2)}, u32[]{:S(2)}) collective-permute-start(f16[280,128]{1,0:T(8,128)(2,1)S(1)} %convert_element_type.119), channel_id=1, source_target_pairs={{0,6},{1,7},{2,4},{3,5},{4,2},{5,3},{6,0},{7,1},{8,14},{9,15},{10,... | collective-permute-start | bytes 215048 | tf_op jit(solution)/shard_map/ppermute | solution.py:447
  34.4 0.7 %collective-permute-start.14 = (f16[280,128]{1,0:T(8,128)(2,1)S(1)}, f16[280,128]{1,0:T(8,128)(2,1)S(1)}, u32[]{:S(2)}, u32[]{:S(2)}) collective-permute-start(f16[280,128]{1,0:T(8,128)(2,1)S(1)} %convert_element_type.117), channel_id=1, source_target_pairs={{0,3},{1,2},{2,1},{3,0},{4,7},{5,6},{6,5},{7,4},{8,11},{9,10},{10,... | collective-permute-start | bytes 215048 | tf_op jit(solution)/shard_map/ppermute | solution.py:447
  35.1 0.9 %collective-permute-start.13 = (f16[280,128]{1,0:T(8,128)(2,1)S(1)}, f16[280,128]{1,0:T(8,128)(2,1)S(1)}, u32[]{:S(2)}, u32[]{:S(2)}) collective-permute-start(f16[280,128]{1,0:T(8,128)(2,1)S(1)} %convert_element_type.115), channel_id=1, source_target_pairs={{0,5},{1,4},{2,7},{3,6},{4,1},{5,0},{6,3},{7,2},{8,13},{9,12},{10,... | collective-permute-start | bytes 215048 | tf_op jit(solution)/shard_map/ppermute | solution.py:447
  36.0 2.2 %collective-permute-done.15 = f16[280,128]{1,0:T(8,128)(2,1)S(1)} collective-permute-done((f16[280,128]{1,0:T(8,128)(2,1)S(1)}, f16[280,128]{1,0:T(8,128)(2,1)S(1)}, u32[]{:S(2)}, u32[]{:S(2)}) %collective-permute-start.15) | collective-permute-done | bytes 71712 | tf_op jit(solution)/shard_map/ppermute | solution.py:447
  38.1 1.4 %collective-permute-done.14 = f16[280,128]{1,0:T(8,128)(2,1)S(1)} collective-permute-done((f16[280,128]{1,0:T(8,128)(2,1)S(1)}, f16[280,128]{1,0:T(8,128)(2,1)S(1)}, u32[]{:S(2)}, u32[]{:S(2)}) %collective-permute-start.14) | collective-permute-done | bytes 71712 | tf_op jit(solution)/shard_map/ppermute | solution.py:447
  39.6 0.1 shard_map.85
  39.7 0.1 reduce-precision_convert_fusion.1
  39.8 2.8 %collective-permute-start.16 = (f16[280,128]{1,0:T(8,128)(2,1)S(1)}, f16[280,128]{1,0:T(8,128)(2,1)S(1)}, u32[]{:S(2)}, u32[]{:S(2)}) collective-permute-start(f16[280,128]{1,0:T(8,128)(2,1)S(1)} %get-tuple-element.39), channel_id=1, source_target_pairs={{0,13},{1,12},{2,15},{3,14},{4,9},{5,8},{6,11},{7,10},{8,5},{9,4},... | collective-permute-start | bytes 215048 | tf_op jit(solution)/shard_map/ppermute | solution.py:447
  42.6 3.4 %collective-permute-done.16 = f16[280,128]{1,0:T(8,128)(2,1)S(1)} collective-permute-done((f16[280,128]{1,0:T(8,128)(2,1)S(1)}, f16[280,128]{1,0:T(8,128)(2,1)S(1)}, u32[]{:S(2)}, u32[]{:S(2)}) %collective-permute-start.16) | collective-permute-done | bytes 71712 | tf_op jit(solution)/shard_map/ppermute | solution.py:447
  46.0 0.1 fusion.11
  46.1 0.1 collective-permute-start.19
  46.2 1.9 %collective-permute-start.18 = (f16[272,128]{1,0:T(8,128)(2,1)S(1)}, f16[272,128]{1,0:T(8,128)(2,1)S(1)}, u32[]{:S(2)}, u32[]{:S(2)}) collective-permute-start(f16[272,128]{1,0:T(8,128)(2,1)S(1)} %get-tuple-element.33), channel_id=1, source_target_pairs={{0,3},{1,2},{2,1},{3,0},{4,7},{5,6},{6,5},{7,4},{8,11},{9,10},{10,... | collective-permute-start | bytes 208904 | tf_op jit(solution)/shard_map/ppermute | solution.py:447
  48.1 1.3 %collective-permute-start.17 = (f16[272,128]{1,0:T(8,128)(2,1)S(1)}, f16[272,128]{1,0:T(8,128)(2,1)S(1)}, u32[]{:S(2)}, u32[]{:S(2)}) collective-permute-start(f16[272,128]{1,0:T(8,128)(2,1)S(1)} %get-tuple-element.33), channel_id=1, source_target_pairs={{0,5},{1,4},{2,7},{3,6},{4,1},{5,0},{6,3},{7,2},{8,13},{9,12},{10,... | collective-permute-start | bytes 208904 | tf_op jit(solution)/shard_map/ppermute | solution.py:447
  49.4 2.1 %collective-permute-done.19 = f16[272,128]{1,0:T(8,128)(2,1)S(1)} collective-permute-done((f16[272,128]{1,0:T(8,128)(2,1)S(1)}, f16[272,128]{1,0:T(8,128)(2,1)S(1)}, u32[]{:S(2)}, u32[]{:S(2)}) %collective-permute-start.19) | collective-permute-done | bytes 69664 | tf_op jit(solution)/shard_map/ppermute | solution.py:447
  51.5 0.2 collective-permute-done.18
  51.7 0.5 collective-permute-start.22
  52.2 0.3 collective-permute-start.21
  52.5 1.1 %shard_map.87.refs_2_ = f32[1024,128]{1,0:T(8,128)S(1)} custom-call(bf16[1024,1024]{1,0:T(8,128)(2,1)S(1)} %get-tuple-element.17.refs_0_.refs_1_, f32[272,128]{1,0:T(8,128)S(1)} %get-tuple-element.32.refs_1_.refs_5_, f32[272,128]{1,0:T(8,128)S(1)} %convert_element_type.125.refs_2_.refs_6_, f32[272,128]{1,0:T(8,128)S(1)} %convert_element_type.126.refs_3_.refs_7_, ...), custom_call_target="tpu_custom_call" | custom-call | tf_op jit(solution)/shard_map/pallas_call | solution.py:429
  53.8 3.1 %shard_map.88 = (f32[8,128]{1,0:T(8,128)}, f32[132,512]{1,0:T(8,128)}) custom-call(f32[8,128]{1,0:T(8,128)S(1)} %get-tuple-element.21.refs_0_, bf16[1024,1024]{1,0:T(8,128)(2,1)S(1)} %get-tuple-element.17.refs_0_.refs_1_, f32[1024,128]{1,0:T(8,128)S(1)} %shard_map.87.refs_2_, s32[528]{0:T(1024)S(4)} %get-tuple-element.28.refs_3_, ...), custom_call_target="tpu_custom_call" | custom-call | tf_op jit(solution)/shard_map/pallas_call | solution.py:429
  (45 shorter events, 0.5 us)
Async XLA Ops:
  3.6 1.7 %collective-permute-start = (f16[4,272,128]{2,1,0:T(8,128)(2,1)S(1)}, f16[4,272,128]{2,1,0:T(8,128)(2,1)S(1)}, u32[]{:S(2)}, u32[]{:S(2)}) collective-permute-start(f16[4,272,128]{2,1,0:T(8,128)(2,1)S(1)} %convert_element_type.99), channel_id=1, source_target_pairs={{0,1},{1,0},{2,3},{3,2},{4,5},{5,4},{6,7},{7,6},{8,9},{9,8},{10,11... | collective-permute-start | bytes 835592 | tf_op jit(solution)/shard_map/ppermute | solution.py:440
  5.2 11.7 %copy-start = (f32[528,512]{1,0:T(8,128)S(1)}, f32[528,512]{1,0:T(8,128)}, u32[]{:S(2)}) copy-start(f32[528,512]{1,0:T(8,128)} %refs_1_.3) | copy-start | bytes 3244036
  5.2 11.7 %copy-start.2 = (s32[528]{0:T(1024)S(1)}, s32[528]{0:T(1024)}, u32[]{:S(2)}) copy-start(s32[528]{0:T(1024)} %refs_2_.1) | copy-start | bytes 6340
  5.2 11.7 %copy-start.3 = (s32[528]{0:T(1024)S(1)}, s32[528]{0:T(1024)}, u32[]{:S(2)}) copy-start(s32[528]{0:T(1024)} %constant.4.clone.refs_3_) | copy-start | bytes 6340
  5.2 11.7 %copy-start.4 = (s32[204]{0:T(256)S(1)}, s32[204]{0:T(256)}, u32[]{:S(2)}) copy-start(s32[204]{0:T(256)} %constant.5.clone.refs_0_) | copy-start | bytes 2452
  5.4 6.5 %collective-permute-start.1 = (f16[272,128]{1,0:T(8,128)(2,1)S(1)}, f16[272,128]{1,0:T(8,128)(2,1)S(1)}, u32[]{:S(2)}, u32[]{:S(2)}) collective-permute-start(f16[272,128]{1,0:T(8,128)(2,1)S(1)} %get-tuple-element.36), channel_id=1, source_target_pairs={{0,6},{1,7},{2,4},{3,5},{4,2},{5,3},{6,0},{7,1},{8,14},{9,15},{10,... | collective-permute-start | bytes 208904 | tf_op jit(solution)/shard_map/ppermute | solution.py:447
  9.3 4.4 %collective-permute-start.3 = (f16[272,128]{1,0:T(8,128)(2,1)S(1)}, f16[272,128]{1,0:T(8,128)(2,1)S(1)}, u32[]{:S(2)}, u32[]{:S(2)}) collective-permute-start(f16[272,128]{1,0:T(8,128)(2,1)S(1)} %get-tuple-element.37), channel_id=1, source_target_pairs={{0,3},{1,2},{2,1},{3,0},{4,7},{5,6},{6,5},{7,4},{8,11},{9,10},{10,... | collective-permute-start | bytes 208904 | tf_op jit(solution)/shard_map/ppermute | solution.py:447
  9.3 4.4 %collective-permute-start.2 = (f16[272,128]{1,0:T(8,128)(2,1)S(1)}, f16[272,128]{1,0:T(8,128)(2,1)S(1)}, u32[]{:S(2)}, u32[]{:S(2)}) collective-permute-start(f16[272,128]{1,0:T(8,128)(2,1)S(1)} %get-tuple-element.38), channel_id=1, source_target_pairs={{0,5},{1,4},{2,7},{3,6},{4,1},{5,0},{6,3},{7,2},{8,13},{9,12},{10,... | collective-permute-start | bytes 208904 | tf_op jit(solution)/shard_map/ppermute | solution.py:447
  13.9 13.8 %copy-start.1 = (f32[1024]{0:T(1024)S(1)}, f32[1024]{0:T(1024)}, u32[]{:S(2)}) copy-start(f32[1024]{0:T(1024)} %param.7) | copy-start | bytes 12292
  13.9 6.2 %collective-permute-start.4 = (f16[272,128]{1,0:T(8,128)(2,1)S(1)}, f16[272,128]{1,0:T(8,128)(2,1)S(1)}, u32[]{:S(2)}, u32[]{:S(2)}) collective-permute-start(f16[272,128]{1,0:T(8,128)(2,1)S(1)} %get-tuple-element.34), channel_id=1, source_target_pairs={{0,13},{1,12},{2,15},{3,14},{4,9},{5,8},{6,11},{7,10},{8,5},{9,4},... | collective-permute-start | bytes 208904 | tf_op jit(solution)/shard_map/ppermute | solution.py:447
  20.1 5.3 %collective-permute-start.7 = (bf16[272,128]{1,0:T(8,128)(2,1)S(1)}, bf16[272,128]{1,0:T(8,128)(2,1)S(1)}, u32[]{:S(2)}, u32[]{:S(2)}) collective-permute-start(bf16[272,128]{1,0:T(8,128)(2,1)S(1)} %tanh_convert_fusion.refs_1_), channel_id=1, source_target_pairs={{0,6},{1,7},{2,4},{3,5},{4,2},{5,3},{6,0},{7,1},{8,14},{9,15},{10,... | collective-permute-start | bytes 208904 | tf_op jit(solution)/shard_map/ppermute | solution.py:447
  20.2 5.3 %collective-permute-start.6 = (bf16[272,128]{1,0:T(8,128)(2,1)S(1)}, bf16[272,128]{1,0:T(8,128)(2,1)S(1)}, u32[]{:S(2)}, u32[]{:S(2)}) collective-permute-start(bf16[272,128]{1,0:T(8,128)(2,1)S(1)} %tanh_convert_fusion.refs_1_), channel_id=1, source_target_pairs={{0,3},{1,2},{2,1},{3,0},{4,7},{5,6},{6,5},{7,4},{8,11},{9,10},{10,... | collective-permute-start | bytes 208904 | tf_op jit(solution)/shard_map/ppermute | solution.py:447
  21.9 4.5 %collective-permute-start.5 = (bf16[272,128]{1,0:T(8,128)(2,1)S(1)}, bf16[272,128]{1,0:T(8,128)(2,1)S(1)}, u32[]{:S(2)}, u32[]{:S(2)}) collective-permute-start(bf16[272,128]{1,0:T(8,128)(2,1)S(1)} %tanh_convert_fusion.refs_1_), channel_id=1, source_target_pairs={{0,5},{1,4},{2,7},{3,6},{4,1},{5,0},{6,3},{7,2},{8,13},{9,12},{10,... | collective-permute-start | bytes 208904 | tf_op jit(solution)/shard_map/ppermute | solution.py:447
  23.4 4.2 %collective-permute-start.8 = (bf16[272,128]{1,0:T(8,128)(2,1)S(1)}, bf16[272,128]{1,0:T(8,128)(2,1)S(1)}, u32[]{:S(2)}, u32[]{:S(2)}) collective-permute-start(bf16[272,128]{1,0:T(8,128)(2,1)S(1)} %tanh_convert_fusion.refs_1_), channel_id=1, source_target_pairs={{0,1},{1,0},{2,3},{3,2},{4,5},{5,4},{6,7},{7,6},{8,9},{9,8},{10,11... | collective-permute-start | bytes 208904 | tf_op jit(solution)/shard_map/ppermute | solution.py:440
  25.4 2.2 %collective-permute-start.11 = (bf16[272,128]{1,0:T(8,128)(2,1)S(1)}, bf16[272,128]{1,0:T(8,128)(2,1)S(1)}, u32[]{:S(2)}, u32[]{:S(2)}) collective-permute-start(bf16[272,128]{1,0:T(8,128)(2,1)S(1)} %collective-permute-done.7.refs_4_), channel_id=1, source_target_pairs={{0,1},{1,0},{2,3},{3,2},{4,5},{5,4},{6,7},{7,6},{8,9},{9,8},{10,11... | collective-permute-start | bytes 208904 | tf_op jit(solution)/shard_map/ppermute | solution.py:440
  25.5 2.1 %collective-permute-start.10 = (bf16[272,128]{1,0:T(8,128)(2,1)S(1)}, bf16[272,128]{1,0:T(8,128)(2,1)S(1)}, u32[]{:S(2)}, u32[]{:S(2)}) collective-permute-start(bf16[272,128]{1,0:T(8,128)(2,1)S(1)} %collective-permute-done.6.refs_3_), channel_id=1, source_target_pairs={{0,1},{1,0},{2,3},{3,2},{4,5},{5,4},{6,7},{7,6},{8,9},{9,8},{10,11... | collective-permute-start | bytes 208904 | tf_op jit(solution)/shard_map/ppermute | solution.py:440
  26.3 1.3 %collective-permute-start.9 = (bf16[272,128]{1,0:T(8,128)(2,1)S(1)}, bf16[272,128]{1,0:T(8,128)(2,1)S(1)}, u32[]{:S(2)}, u32[]{:S(2)}) collective-permute-start(bf16[272,128]{1,0:T(8,128)(2,1)S(1)} %collective-permute-done.5.refs_2_), channel_id=1, source_target_pairs={{0,1},{1,0},{2,3},{3,2},{4,5},{5,4},{6,7},{7,6},{8,9},{9,8},{10,11... | collective-permute-start | bytes 208904 | tf_op jit(solution)/shard_map/ppermute | solution.py:440
  30.8 1.6 %collective-permute-start.12 = (f16[4,280,128]{2,1,0:T(8,128)(2,1)S(1)}, f16[4,280,128]{2,1,0:T(8,128)(2,1)S(1)}, u32[]{:S(2)}, u32[]{:S(2)}) collective-permute-start(f16[4,280,128]{2,1,0:T(8,128)(2,1)S(1)} %convert_element_type.113), channel_id=1, source_target_pairs={{0,1},{1,0},{2,3},{3,2},{4,5},{5,4},{6,7},{7,6},{8,9},{9,8},{10,11... | collective-permute-start | bytes 860168 | tf_op jit(solution)/shard_map/ppermute | solution.py:440
  32.6 5.5 %collective-permute-start.15 = (f16[280,128]{1,0:T(8,128)(2,1)S(1)}, f16[280,128]{1,0:T(8,128)(2,1)S(1)}, u32[]{:S(2)}, u32[]{:S(2)}) collective-permute-start(f16[280,128]{1,0:T(8,128)(2,1)S(1)} %convert_element_type.119), channel_id=1, source_target_pairs={{0,6},{1,7},{2,4},{3,5},{4,2},{5,3},{6,0},{7,1},{8,14},{9,15},{10,... | collective-permute-start | bytes 215048 | tf_op jit(solution)/shard_map/ppermute | solution.py:447
  34.4 5.2 %collective-permute-start.14 = (f16[280,128]{1,0:T(8,128)(2,1)S(1)}, f16[280,128]{1,0:T(8,128)(2,1)S(1)}, u32[]{:S(2)}, u32[]{:S(2)}) collective-permute-start(f16[280,128]{1,0:T(8,128)(2,1)S(1)} %convert_element_type.117), channel_id=1, source_target_pairs={{0,3},{1,2},{2,1},{3,0},{4,7},{5,6},{6,5},{7,4},{8,11},{9,10},{10,... | collective-permute-start | bytes 215048 | tf_op jit(solution)/shard_map/ppermute | solution.py:447
  35.1 4.5 %collective-permute-start.13 = (f16[280,128]{1,0:T(8,128)(2,1)S(1)}, f16[280,128]{1,0:T(8,128)(2,1)S(1)}, u32[]{:S(2)}, u32[]{:S(2)}) collective-permute-start(f16[280,128]{1,0:T(8,128)(2,1)S(1)} %convert_element_type.115), channel_id=1, source_target_pairs={{0,5},{1,4},{2,7},{3,6},{4,1},{5,0},{6,3},{7,2},{8,13},{9,12},{10,... | collective-permute-start | bytes 215048 | tf_op jit(solution)/shard_map/ppermute | solution.py:447
  39.8 6.2 %collective-permute-start.16 = (f16[280,128]{1,0:T(8,128)(2,1)S(1)}, f16[280,128]{1,0:T(8,128)(2,1)S(1)}, u32[]{:S(2)}, u32[]{:S(2)}) collective-permute-start(f16[280,128]{1,0:T(8,128)(2,1)S(1)} %get-tuple-element.39), channel_id=1, source_target_pairs={{0,13},{1,12},{2,15},{3,14},{4,9},{5,8},{6,11},{7,10},{8,5},{9,4},... | collective-permute-start | bytes 215048 | tf_op jit(solution)/shard_map/ppermute | solution.py:447
  46.1 5.3 %collective-permute-start.19 = (f16[272,128]{1,0:T(8,128)(2,1)S(1)}, f16[272,128]{1,0:T(8,128)(2,1)S(1)}, u32[]{:S(2)}, u32[]{:S(2)}) collective-permute-start(f16[272,128]{1,0:T(8,128)(2,1)S(1)} %get-tuple-element.33), channel_id=1, source_target_pairs={{0,6},{1,7},{2,4},{3,5},{4,2},{5,3},{6,0},{7,1},{8,14},{9,15},{10,... | collective-permute-start | bytes 208904 | tf_op jit(solution)/shard_map/ppermute | solution.py:447
  46.2 5.4 %collective-permute-start.18 = (f16[272,128]{1,0:T(8,128)(2,1)S(1)}, f16[272,128]{1,0:T(8,128)(2,1)S(1)}, u32[]{:S(2)}, u32[]{:S(2)}) collective-permute-start(f16[272,128]{1,0:T(8,128)(2,1)S(1)} %get-tuple-element.33), channel_id=1, source_target_pairs={{0,3},{1,2},{2,1},{3,0},{4,7},{5,6},{6,5},{7,4},{8,11},{9,10},{10,... | collective-permute-start | bytes 208904 | tf_op jit(solution)/shard_map/ppermute | solution.py:447
  48.1 4.1 %collective-permute-start.17 = (f16[272,128]{1,0:T(8,128)(2,1)S(1)}, f16[272,128]{1,0:T(8,128)(2,1)S(1)}, u32[]{:S(2)}, u32[]{:S(2)}) collective-permute-start(f16[272,128]{1,0:T(8,128)(2,1)S(1)} %get-tuple-element.33), channel_id=1, source_target_pairs={{0,5},{1,4},{2,7},{3,6},{4,1},{5,0},{6,3},{7,2},{8,13},{9,12},{10,... | collective-permute-start | bytes 208904 | tf_op jit(solution)/shard_map/ppermute | solution.py:447
  49.4 4.3 %collective-permute-start.20 = (f16[272,128]{1,0:T(8,128)(2,1)S(1)}, f16[272,128]{1,0:T(8,128)(2,1)S(1)}, u32[]{:S(2)}, u32[]{:S(2)}) collective-permute-start(f16[272,128]{1,0:T(8,128)(2,1)S(1)} %get-tuple-element.33), channel_id=1, source_target_pairs={{0,1},{1,0},{2,3},{3,2},{4,5},{5,4},{6,7},{7,6},{8,9},{9,8},{10,11... | collective-permute-start | bytes 208904 | tf_op jit(solution)/shard_map/ppermute | solution.py:440
  51.5 2.2 %collective-permute-start.23 = (f16[272,128]{1,0:T(8,128)(2,1)S(1)}, f16[272,128]{1,0:T(8,128)(2,1)S(1)}, u32[]{:S(2)}, u32[]{:S(2)}) collective-permute-start(f16[272,128]{1,0:T(8,128)(2,1)S(1)} %collective-permute-done.19), channel_id=1, source_target_pairs={{0,1},{1,0},{2,3},{3,2},{4,5},{5,4},{6,7},{7,6},{8,9},{9,8},{10,11... | collective-permute-start | bytes 208904 | tf_op jit(solution)/shard_map/ppermute | solution.py:440
  51.7 2.1 %collective-permute-start.22 = (f16[272,128]{1,0:T(8,128)(2,1)S(1)}, f16[272,128]{1,0:T(8,128)(2,1)S(1)}, u32[]{:S(2)}, u32[]{:S(2)}) collective-permute-start(f16[272,128]{1,0:T(8,128)(2,1)S(1)} %collective-permute-done.18), channel_id=1, source_target_pairs={{0,1},{1,0},{2,3},{3,2},{4,5},{5,4},{6,7},{7,6},{8,9},{9,8},{10,11... | collective-permute-start | bytes 208904 | tf_op jit(solution)/shard_map/ppermute | solution.py:440
  52.2 1.6 %collective-permute-start.21 = (f16[272,128]{1,0:T(8,128)(2,1)S(1)}, f16[272,128]{1,0:T(8,128)(2,1)S(1)}, u32[]{:S(2)}, u32[]{:S(2)}) collective-permute-start(f16[272,128]{1,0:T(8,128)(2,1)S(1)} %collective-permute-done.17), channel_id=1, source_target_pairs={{0,1},{1,0},{2,3},{3,2},{4,5},{5,4},{6,7},{7,6},{8,9},{9,8},{10,11... | collective-permute-start | bytes 208904 | tf_op jit(solution)/shard_map/ppermute | solution.py:440

commit v9 on v8

--- a/solution.py
+++ b/solution.py
@@ -319,14 +319,15 @@
 
 
 def middle_kernel(plan, log_ref, green, total, *refs):
-    *tiles, send, weighted, log_out, kernel, stack = refs
+    *tiles, send, weighted, log_out, kernel, stack, sums = refs
     for k, ref in zip(plan.order, tiles):
         stack[k] = ref[...]
     fill_half(plan, lambda slot, at: stack[slot, at : at + plan.width, :], kernel)
     strength = columns_of(jnp.exp(new_log(plan, log_ref, green, total, kernel, log_out)))
     for i in range(plan.points // LANES):
         weigh_rows(plan, green, strength, weighted, i)
-    product(plan, 1 - plan.half(), green, weighted, send)
+    product(plan, 1 - plan.half(), green, weighted, sums)
+    scale(plan, sums, send)
 
 
 def last_kernel(plan, log_ref, green, total, owners, places, *refs):
@@ -385,7 +386,7 @@
     log_out[...] = log_now - 0.5 * jnp.exp(log_now) * sums[...]
 
 
-def scale_kernel(plan, send, out):
+def scale(plan, send, out):
     c = plan.chunk
     factor = jnp.exp(send[0, c : c + 1, :] * -LN2)
     for k in range(plan.ways):
@@ -530,11 +531,11 @@
         mine, others = spread(plan, residual.astype(BF16))
         levelled = shape((plan.ways, plan.chunk + SUB, LANES), F32)
         send, weighted, log_now = call(
-            middle_kernel, plan, (levelled, weighted_shape, log_shape), [kernel, stack],
+            middle_kernel, plan, (levelled, weighted_shape, log_shape),
+            [kernel, stack, pltpu.VMEM(levelled.shape, F32)],
             (log_now, green, own_contraction(mine), *others), [VMEM] * (3 + len(others)),
         )
-        scaled = call(scale_kernel, plan, levelled, [], (send,), [VMEM])
-        recv = swap_cores(scaled.astype(F16)).astype(F32)
+        recv = swap_cores(send.astype(F16)).astype(F32)
         residual = scaled_residual(plan, own_product(weighted, send), recv, target)
     mine, others = spread(plan, to_half(residual).astype(F16))
     mine = [x.astype(F32) for x in mine]

time: 57.1 us -> 57.1 us (level)
    pallas_call x12 -> x11, Pallas kernels: 15.8 us -> 15.8 us  [call(): pl.pallas_call(body, in_specs=specs, out_specs=out_specs or jax.tree.map(...]
where the time goes in v9:
time: 57.1 us; the launch traced here: 56.9 us
  starting transfers between devices  22.7 us (40%)
  waiting for transfers between devices  16.6 us (29%)
  Pallas kernels  15.8 us (28%)
  between operations  0.99 us (2%)
  other arithmetic  0.72 us (1%)
    ppermute x14, starting transfers between devices, exchange(): return lax.ppermute(x, ('wide', 'narrow', 'tile'), pairs)  20 us
    ppermute x14, waiting for transfers between devices, exchange(): return lax.ppermute(x, ('wide', 'narrow', 'tile'), pairs)  16.5 us
    pallas_call x11, Pallas kernels, call(): pl.pallas_call(body, in_specs=specs, out_specs=out_specs or jax.tree.map(...  15.8 us
    ppermute x10, starting transfers between devices, swap_cores(): return lax.ppermute(x, 'tile', [(0, 1), (1, 0)])  2.73 us
  transfers between devices with their start and end apart: 24, of which 10 were waited for; matrix products, arithmetic and copies ran while one was open for 0% of the time, Pallas kernels for 12%

profile of v9, /device:TPU:0, one launch (start us, length us, event | category | flops | bytes accessed | tf_op | source)
XLA Modules:
  0.0 56.9 jit_solution(17752739158261729108)
XLA Ops:
  0.6 2.9 %shard_map.77 = (f32[4,272,128]{2,1,0:T(8,128)S(1)}, bf16[2,1024,512]{2,1,0:T(8,128)(2,1)S(1)}, bf16[1024,1024]{1,0:T(8,128)(2,1)S(1)}) custom-call(f32[8,128]{1,0:T(8,128)} %bitcast.19, bf16[1024,1024]{1,0:T(8,128)(2,1)} %refs_1_.2), custom_call_target="tpu_custom_call" | custom-call | tf_op jit(solution)/shard_map/pallas_call | solution.py:430
  3.6 0.5 collective-permute-start
  4.1 1.1 %shard_map.78 = f32[4,272,128]{2,1,0:T(8,128)S(1)} custom-call(bf16[1024,1024]{1,0:T(8,128)(2,1)S(1)} %get-tuple-element.17.refs_0_.refs_1_, bf16[2,1024,512]{2,1,0:T(8,128)(2,1)S(1)} %get-tuple-element.18.refs_1_), custom_call_target="tpu_custom_call" | custom-call | tf_op jit(solution)/shard_map/pallas_call | solution.py:430
  5.2 0.0 copy-start
  5.2 0.0 copy-start.3
  5.2 0.0 copy-start.4
  5.2 0.0 collective-permute-done
  5.3 0.1 fusion.8
  5.4 3.9 %collective-permute-start.1 = (f16[272,128]{1,0:T(8,128)(2,1)S(1)}, f16[272,128]{1,0:T(8,128)(2,1)S(1)}, u32[]{:S(2)}, u32[]{:S(2)}) collective-permute-start(f16[272,128]{1,0:T(8,128)(2,1)S(1)} %get-tuple-element.36), channel_id=1, source_target_pairs={{0,6},{1,7},{2,4},{3,5},{4,2},{5,3},{6,0},{7,1},{8,14},{9,15},{10,... | collective-permute-start | bytes 208904 | tf_op jit(solution)/shard_map/ppermute | solution.py:448
  9.3 0.4 collective-permute-start.2
  9.7 2.2 %collective-permute-done.1 = f16[272,128]{1,0:T(8,128)(2,1)S(1)} collective-permute-done((f16[272,128]{1,0:T(8,128)(2,1)S(1)}, f16[272,128]{1,0:T(8,128)(2,1)S(1)}, u32[]{:S(2)}, u32[]{:S(2)}) %collective-permute-start.1) | collective-permute-done | bytes 69664 | tf_op jit(solution)/shard_map/ppermute | solution.py:448
  11.9 1.9 %collective-permute-done.3 = f16[272,128]{1,0:T(8,128)(2,1)S(1)} collective-permute-done((f16[272,128]{1,0:T(8,128)(2,1)S(1)}, f16[272,128]{1,0:T(8,128)(2,1)S(1)}, u32[]{:S(2)}, u32[]{:S(2)}) %collective-permute-start.3) | collective-permute-done | bytes 69664 | tf_op jit(solution)/shard_map/ppermute | solution.py:448
  13.7 0.1 fusion.12
  13.9 0.0 copy-start.1
  13.9 3.0 %collective-permute-start.4 = (f16[272,128]{1,0:T(8,128)(2,1)S(1)}, f16[272,128]{1,0:T(8,128)(2,1)S(1)}, u32[]{:S(2)}, u32[]{:S(2)}) collective-permute-start(f16[272,128]{1,0:T(8,128)(2,1)S(1)} %get-tuple-element.34), channel_id=1, source_target_pairs={{0,13},{1,12},{2,15},{3,14},{4,9},{5,8},{6,11},{7,10},{8,5},{9,4},... | collective-permute-start | bytes 208904 | tf_op jit(solution)/shard_map/ppermute | solution.py:448
  16.9 2.0 %shard_map.79 = (f32[272,128]{1,0:T(8,128)S(1)}, s32[528]{0:T(1024)S(4)}, s32[528]{0:T(1024)S(4)}) custom-call(s32[204]{0:T(256)S(1)} %copy-done.4, f32[528,512]{1,0:T(8,128)S(1)} %copy-done, s32[528]{0:T(1024)S(1)} %copy-done.2, s32[528]{0:T(1024)S(1)} %copy-done.3), custom_call_target="tpu_custom_call" | custom-call | tf_op jit(solution)/shard_map/pallas_call | solution.py:430
  18.9 1.1 %collective-permute-done.4 = f16[272,128]{1,0:T(8,128)(2,1)S(1)} collective-permute-done((f16[272,128]{1,0:T(8,128)(2,1)S(1)}, f16[272,128]{1,0:T(8,128)(2,1)S(1)}, u32[]{:S(2)}, u32[]{:S(2)}) %collective-permute-start.4) | collective-permute-done | bytes 69664 | tf_op jit(solution)/shard_map/ppermute | solution.py:448
  20.1 0.1 collective-permute-start.7
  20.2 1.7 %collective-permute-start.6 = (bf16[272,128]{1,0:T(8,128)(2,1)S(1)}, bf16[272,128]{1,0:T(8,128)(2,1)S(1)}, u32[]{:S(2)}, u32[]{:S(2)}) collective-permute-start(bf16[272,128]{1,0:T(8,128)(2,1)S(1)} %tanh_convert_fusion.refs_1_), channel_id=1, source_target_pairs={{0,3},{1,2},{2,1},{3,0},{4,7},{5,6},{6,5},{7,4},{8,11},{9,10},{10,... | collective-permute-start | bytes 208904 | tf_op jit(solution)/shard_map/ppermute | solution.py:448
  21.9 1.5 %collective-permute-start.5 = (bf16[272,128]{1,0:T(8,128)(2,1)S(1)}, bf16[272,128]{1,0:T(8,128)(2,1)S(1)}, u32[]{:S(2)}, u32[]{:S(2)}) collective-permute-start(bf16[272,128]{1,0:T(8,128)(2,1)S(1)} %tanh_convert_fusion.refs_1_), channel_id=1, source_target_pairs={{0,5},{1,4},{2,7},{3,6},{4,1},{5,0},{6,3},{7,2},{8,13},{9,12},{10,... | collective-permute-start | bytes 208904 | tf_op jit(solution)/shard_map/ppermute | solution.py:448
  23.4 2.1 %collective-permute-done.7.refs_4_ = bf16[272,128]{1,0:T(8,128)(2,1)S(1)} collective-permute-done((bf16[272,128]{1,0:T(8,128)(2,1)S(1)}, bf16[272,128]{1,0:T(8,128)(2,1)S(1)}, u32[]{:S(2)}, u32[]{:S(2)}) %collective-permute-start.7) | collective-permute-done | bytes 69664 | tf_op jit(solution)/shard_map/ppermute | solution.py:448
  25.4 0.1 collective-permute-done.6.refs_3_
  25.5 0.8 %collective-permute-start.10 = (bf16[272,128]{1,0:T(8,128)(2,1)S(1)}, bf16[272,128]{1,0:T(8,128)(2,1)S(1)}, u32[]{:S(2)}, u32[]{:S(2)}) collective-permute-start(bf16[272,128]{1,0:T(8,128)(2,1)S(1)} %collective-permute-done.6.refs_3_), channel_id=1, source_target_pairs={{0,1},{1,0},{2,3},{3,2},{4,5},{5,4},{6,7},{7,6},{8,9},{9,8},{10,11... | collective-permute-start | bytes 208904 | tf_op jit(solution)/shard_map/ppermute | solution.py:441
  26.3 0.2 collective-permute-start.9
  26.5 1.1 %shard_map.80.refs_2_ = f32[1024,128]{1,0:T(8,128)S(1)} custom-call(bf16[1024,1024]{1,0:T(8,128)(2,1)S(1)} %get-tuple-element.17.refs_0_.refs_1_, bf16[272,128]{1,0:T(8,128)(2,1)S(1)} %tanh_convert_fusion.refs_1_, bf16[272,128]{1,0:T(8,128)(2,1)S(1)} %collective-permute-done.5.refs_2_, bf16[272,128]{1,0:T(8,128)(2,1)S(1)} %collective-permute-done.6.refs_3_, ...), custom_call_target="tpu_custom_call" | custom-call | tf_op jit(solution)/shard_map/pallas_call | solution.py:430
  27.7 3.1 %shard_map.81 = (f32[4,280,128]{2,1,0:T(8,128)S(1)}, bf16[2,1024,512]{2,1,0:T(8,128)(2,1)S(1)}, f32[8,128]{1,0:T(8,128)S(1)}) custom-call(f32[8,128]{1,0:T(8,128)S(1)} %bitcast.20, bf16[1024,1024]{1,0:T(8,128)(2,1)S(1)} %get-tuple-element.17.refs_0_.refs_1_, f32[1024,128]{1,0:T(8,128)S(1)} %shard_map.80.refs_2_, ...), custom_call_target="tpu_custom_call" | custom-call | tf_op jit(solution)/shard_map/pallas_call | solution.py:430
  30.8 0.4 collective-permute-start.12
  31.2 1.2 %shard_map.82.refs_0_ = f32[4,280,128]{2,1,0:T(8,128)S(1)} custom-call(bf16[1024,1024]{1,0:T(8,128)(2,1)S(1)} %get-tuple-element.17.refs_0_.refs_1_, bf16[2,1024,512]{2,1,0:T(8,128)(2,1)S(1)} %get-tuple-element.22.refs_1_), custom_call_target="tpu_custom_call" | custom-call | tf_op jit(solution)/shard_map/pallas_call | solution.py:430
  32.5 0.1 shard_map.83
  32.6 1.8 %collective-permute-start.15 = (f16[280,128]{1,0:T(8,128)(2,1)S(1)}, f16[280,128]{1,0:T(8,128)(2,1)S(1)}, u32[]{:S(2)}, u32[]{:S(2)}) collective-permute-start(f16[280,128]{1,0:T(8,128)(2,1)S(1)} %convert_element_type.119), channel_id=1, source_target_pairs={{0,6},{1,7},{2,4},{3,5},{4,2},{5,3},{6,0},{7,1},{8,14},{9,15},{10,... | collective-permute-start | bytes 215048 | tf_op jit(solution)/shard_map/ppermute | solution.py:448
  34.4 0.7 %collective-permute-start.14 = (f16[280,128]{1,0:T(8,128)(2,1)S(1)}, f16[280,128]{1,0:T(8,128)(2,1)S(1)}, u32[]{:S(2)}, u32[]{:S(2)}) collective-permute-start(f16[280,128]{1,0:T(8,128)(2,1)S(1)} %convert_element_type.117), channel_id=1, source_target_pairs={{0,3},{1,2},{2,1},{3,0},{4,7},{5,6},{6,5},{7,4},{8,11},{9,10},{10,... | collective-permute-start | bytes 215048 | tf_op jit(solution)/shard_map/ppermute | solution.py:448
  35.1 0.9 %collective-permute-start.13 = (f16[280,128]{1,0:T(8,128)(2,1)S(1)}, f16[280,128]{1,0:T(8,128)(2,1)S(1)}, u32[]{:S(2)}, u32[]{:S(2)}) collective-permute-start(f16[280,128]{1,0:T(8,128)(2,1)S(1)} %convert_element_type.115), channel_id=1, source_target_pairs={{0,5},{1,4},{2,7},{3,6},{4,1},{5,0},{6,3},{7,2},{8,13},{9,12},{10,... | collective-permute-start | bytes 215048 | tf_op jit(solution)/shard_map/ppermute | solution.py:448
  36.0 2.2 %collective-permute-done.15 = f16[280,128]{1,0:T(8,128)(2,1)S(1)} collective-permute-done((f16[280,128]{1,0:T(8,128)(2,1)S(1)}, f16[280,128]{1,0:T(8,128)(2,1)S(1)}, u32[]{:S(2)}, u32[]{:S(2)}) %collective-permute-start.15) | collective-permute-done | bytes 71712 | tf_op jit(solution)/shard_map/ppermute | solution.py:448
  38.1 1.4 %collective-permute-done.14 = f16[280,128]{1,0:T(8,128)(2,1)S(1)} collective-permute-done((f16[280,128]{1,0:T(8,128)(2,1)S(1)}, f16[280,128]{1,0:T(8,128)(2,1)S(1)}, u32[]{:S(2)}, u32[]{:S(2)}) %collective-permute-start.14) | collective-permute-done | bytes 71712 | tf_op jit(solution)/shard_map/ppermute | solution.py:448
  39.6 0.1 shard_map.84
  39.7 0.1 reduce-precision_convert_fusion.1
  39.8 2.8 %collective-permute-start.16 = (f16[280,128]{1,0:T(8,128)(2,1)S(1)}, f16[280,128]{1,0:T(8,128)(2,1)S(1)}, u32[]{:S(2)}, u32[]{:S(2)}) collective-permute-start(f16[280,128]{1,0:T(8,128)(2,1)S(1)} %get-tuple-element.39), channel_id=1, source_target_pairs={{0,13},{1,12},{2,15},{3,14},{4,9},{5,8},{6,11},{7,10},{8,5},{9,4},... | collective-permute-start | bytes 215048 | tf_op jit(solution)/shard_map/ppermute | solution.py:448
  42.6 3.4 %collective-permute-done.16 = f16[280,128]{1,0:T(8,128)(2,1)S(1)} collective-permute-done((f16[280,128]{1,0:T(8,128)(2,1)S(1)}, f16[280,128]{1,0:T(8,128)(2,1)S(1)}, u32[]{:S(2)}, u32[]{:S(2)}) %collective-permute-start.16) | collective-permute-done | bytes 71712 | tf_op jit(solution)/shard_map/ppermute | solution.py:448
  46.0 0.1 fusion.11
  46.1 0.1 collective-permute-start.19
  46.2 1.9 %collective-permute-start.18 = (f16[272,128]{1,0:T(8,128)(2,1)S(1)}, f16[272,128]{1,0:T(8,128)(2,1)S(1)}, u32[]{:S(2)}, u32[]{:S(2)}) collective-permute-start(f16[272,128]{1,0:T(8,128)(2,1)S(1)} %get-tuple-element.33), channel_id=1, source_target_pairs={{0,3},{1,2},{2,1},{3,0},{4,7},{5,6},{6,5},{7,4},{8,11},{9,10},{10,... | collective-permute-start | bytes 208904 | tf_op jit(solution)/shard_map/ppermute | solution.py:448
  48.1 1.3 %collective-permute-start.17 = (f16[272,128]{1,0:T(8,128)(2,1)S(1)}, f16[272,128]{1,0:T(8,128)(2,1)S(1)}, u32[]{:S(2)}, u32[]{:S(2)}) collective-permute-start(f16[272,128]{1,0:T(8,128)(2,1)S(1)} %get-tuple-element.33), channel_id=1, source_target_pairs={{0,5},{1,4},{2,7},{3,6},{4,1},{5,0},{6,3},{7,2},{8,13},{9,12},{10,... | collective-permute-start | bytes 208904 | tf_op jit(solution)/shard_map/ppermute | solution.py:448
  49.4 2.1 %collective-permute-done.19 = f16[272,128]{1,0:T(8,128)(2,1)S(1)} collective-permute-done((f16[272,128]{1,0:T(8,128)(2,1)S(1)}, f16[272,128]{1,0:T(8,128)(2,1)S(1)}, u32[]{:S(2)}, u32[]{:S(2)}) %collective-permute-start.19) | collective-permute-done | bytes 69664 | tf_op jit(solution)/shard_map/ppermute | solution.py:448
  51.5 0.2 collective-permute-done.18
  51.6 0.5 collective-permute-start.22
  52.2 0.3 collective-permute-start.21
  52.5 1.1 %shard_map.86.refs_2_ = f32[1024,128]{1,0:T(8,128)S(1)} custom-call(bf16[1024,1024]{1,0:T(8,128)(2,1)S(1)} %get-tuple-element.17.refs_0_.refs_1_, f32[272,128]{1,0:T(8,128)S(1)} %get-tuple-element.32.refs_1_.refs_5_, f32[272,128]{1,0:T(8,128)S(1)} %convert_element_type.125.refs_2_.refs_6_, f32[272,128]{1,0:T(8,128)S(1)} %convert_element_type.126.refs_3_.refs_7_, ...), custom_call_target="tpu_custom_call" | custom-call | tf_op jit(solution)/shard_map/pallas_call | solution.py:430
  53.8 3.1 %shard_map.87 = (f32[8,128]{1,0:T(8,128)}, f32[132,512]{1,0:T(8,128)}) custom-call(f32[8,128]{1,0:T(8,128)S(1)} %get-tuple-element.21.refs_0_, bf16[1024,1024]{1,0:T(8,128)(2,1)S(1)} %get-tuple-element.17.refs_0_.refs_1_, f32[1024,128]{1,0:T(8,128)S(1)} %shard_map.86.refs_2_, s32[528]{0:T(1024)S(4)} %get-tuple-element.28.refs_3_, ...), custom_call_target="tpu_custom_call" | custom-call | tf_op jit(solution)/shard_map/pallas_call | solution.py:430
  (44 shorter events, 0.5 us)
Async XLA Ops:
  3.6 1.7 %collective-permute-start = (f16[4,272,128]{2,1,0:T(8,128)(2,1)S(1)}, f16[4,272,128]{2,1,0:T(8,128)(2,1)S(1)}, u32[]{:S(2)}, u32[]{:S(2)}) collective-permute-start(f16[4,272,128]{2,1,0:T(8,128)(2,1)S(1)} %convert_element_type.99), channel_id=1, source_target_pairs={{0,1},{1,0},{2,3},{3,2},{4,5},{5,4},{6,7},{7,6},{8,9},{9,8},{10,11... | collective-permute-start | bytes 835592 | tf_op jit(solution)/shard_map/ppermute | solution.py:441
  5.2 11.7 %copy-start = (f32[528,512]{1,0:T(8,128)S(1)}, f32[528,512]{1,0:T(8,128)}, u32[]{:S(2)}) copy-start(f32[528,512]{1,0:T(8,128)} %refs_1_.3) | copy-start | bytes 3244036
  5.2 11.7 %copy-start.2 = (s32[528]{0:T(1024)S(1)}, s32[528]{0:T(1024)}, u32[]{:S(2)}) copy-start(s32[528]{0:T(1024)} %refs_2_.1) | copy-start | bytes 6340
  5.2 11.7 %copy-start.3 = (s32[528]{0:T(1024)S(1)}, s32[528]{0:T(1024)}, u32[]{:S(2)}) copy-start(s32[528]{0:T(1024)} %constant.4.clone.refs_3_) | copy-start | bytes 6340
  5.2 11.7 %copy-start.4 = (s32[204]{0:T(256)S(1)}, s32[204]{0:T(256)}, u32[]{:S(2)}) copy-start(s32[204]{0:T(256)} %constant.5.clone.refs_0_) | copy-start | bytes 2452
  5.4 6.5 %collective-permute-start.1 = (f16[272,128]{1,0:T(8,128)(2,1)S(1)}, f16[272,128]{1,0:T(8,128)(2,1)S(1)}, u32[]{:S(2)}, u32[]{:S(2)}) collective-permute-start(f16[272,128]{1,0:T(8,128)(2,1)S(1)} %get-tuple-element.36), channel_id=1, source_target_pairs={{0,6},{1,7},{2,4},{3,5},{4,2},{5,3},{6,0},{7,1},{8,14},{9,15},{10,... | collective-permute-start | bytes 208904 | tf_op jit(solution)/shard_map/ppermute | solution.py:448
  9.3 4.4 %collective-permute-start.3 = (f16[272,128]{1,0:T(8,128)(2,1)S(1)}, f16[272,128]{1,0:T(8,128)(2,1)S(1)}, u32[]{:S(2)}, u32[]{:S(2)}) collective-permute-start(f16[272,128]{1,0:T(8,128)(2,1)S(1)} %get-tuple-element.37), channel_id=1, source_target_pairs={{0,3},{1,2},{2,1},{3,0},{4,7},{5,6},{6,5},{7,4},{8,11},{9,10},{10,... | collective-permute-start | bytes 208904 | tf_op jit(solution)/shard_map/ppermute | solution.py:448
  9.3 4.4 %collective-permute-start.2 = (f16[272,128]{1,0:T(8,128)(2,1)S(1)}, f16[272,128]{1,0:T(8,128)(2,1)S(1)}, u32[]{:S(2)}, u32[]{:S(2)}) collective-permute-start(f16[272,128]{1,0:T(8,128)(2,1)S(1)} %get-tuple-element.38), channel_id=1, source_target_pairs={{0,5},{1,4},{2,7},{3,6},{4,1},{5,0},{6,3},{7,2},{8,13},{9,12},{10,... | collective-permute-start | bytes 208904 | tf_op jit(solution)/shard_map/ppermute | solution.py:448
  13.9 13.8 %copy-start.1 = (f32[1024]{0:T(1024)S(1)}, f32[1024]{0:T(1024)}, u32[]{:S(2)}) copy-start(f32[1024]{0:T(1024)} %param.7) | copy-start | bytes 12292
  13.9 6.2 %collective-permute-start.4 = (f16[272,128]{1,0:T(8,128)(2,1)S(1)}, f16[272,128]{1,0:T(8,128)(2,1)S(1)}, u32[]{:S(2)}, u32[]{:S(2)}) collective-permute-start(f16[272,128]{1,0:T(8,128)(2,1)S(1)} %get-tuple-element.34), channel_id=1, source_target_pairs={{0,13},{1,12},{2,15},{3,14},{4,9},{5,8},{6,11},{7,10},{8,5},{9,4},... | collective-permute-start | bytes 208904 | tf_op jit(solution)/shard_map/ppermute | solution.py:448
  20.1 5.3 %collective-permute-start.7 = (bf16[272,128]{1,0:T(8,128)(2,1)S(1)}, bf16[272,128]{1,0:T(8,128)(2,1)S(1)}, u32[]{:S(2)}, u32[]{:S(2)}) collective-permute-start(bf16[272,128]{1,0:T(8,128)(2,1)S(1)} %tanh_convert_fusion.refs_1_), channel_id=1, source_target_pairs={{0,6},{1,7},{2,4},{3,5},{4,2},{5,3},{6,0},{7,1},{8,14},{9,15},{10,... | collective-permute-start | bytes 208904 | tf_op jit(solution)/shard_map/ppermute | solution.py:448
  20.2 5.3 %collective-permute-start.6 = (bf16[272,128]{1,0:T(8,128)(2,1)S(1)}, bf16[272,128]{1,0:T(8,128)(2,1)S(1)}, u32[]{:S(2)}, u32[]{:S(2)}) collective-permute-start(bf16[272,128]{1,0:T(8,128)(2,1)S(1)} %tanh_convert_fusion.refs_1_), channel_id=1, source_target_pairs={{0,3},{1,2},{2,1},{3,0},{4,7},{5,6},{6,5},{7,4},{8,11},{9,10},{10,... | collective-permute-start | bytes 208904 | tf_op jit(solution)/shard_map/ppermute | solution.py:448
  21.9 4.5 %collective-permute-start.5 = (bf16[272,128]{1,0:T(8,128)(2,1)S(1)}, bf16[272,128]{1,0:T(8,128)(2,1)S(1)}, u32[]{:S(2)}, u32[]{:S(2)}) collective-permute-start(bf16[272,128]{1,0:T(8,128)(2,1)S(1)} %tanh_convert_fusion.refs_1_), channel_id=1, source_target_pairs={{0,5},{1,4},{2,7},{3,6},{4,1},{5,0},{6,3},{7,2},{8,13},{9,12},{10,... | collective-permute-start | bytes 208904 | tf_op jit(solution)/shard_map/ppermute | solution.py:448
  23.4 4.2 %collective-permute-start.8 = (bf16[272,128]{1,0:T(8,128)(2,1)S(1)}, bf16[272,128]{1,0:T(8,128)(2,1)S(1)}, u32[]{:S(2)}, u32[]{:S(2)}) collective-permute-start(bf16[272,128]{1,0:T(8,128)(2,1)S(1)} %tanh_convert_fusion.refs_1_), channel_id=1, source_target_pairs={{0,1},{1,0},{2,3},{3,2},{4,5},{5,4},{6,7},{7,6},{8,9},{9,8},{10,11... | collective-permute-start | bytes 208904 | tf_op jit(solution)/shard_map/ppermute | solution.py:441
  25.4 2.2 %collective-permute-start.11 = (bf16[272,128]{1,0:T(8,128)(2,1)S(1)}, bf16[272,128]{1,0:T(8,128)(2,1)S(1)}, u32[]{:S(2)}, u32[]{:S(2)}) collective-permute-start(bf16[272,128]{1,0:T(8,128)(2,1)S(1)} %collective-permute-done.7.refs_4_), channel_id=1, source_target_pairs={{0,1},{1,0},{2,3},{3,2},{4,5},{5,4},{6,7},{7,6},{8,9},{9,8},{10,11... | collective-permute-start | bytes 208904 | tf_op jit(solution)/shard_map/ppermute | solution.py:441
  25.5 2.1 %collective-permute-start.10 = (bf16[272,128]{1,0:T(8,128)(2,1)S(1)}, bf16[272,128]{1,0:T(8,128)(2,1)S(1)}, u32[]{:S(2)}, u32[]{:S(2)}) collective-permute-start(bf16[272,128]{1,0:T(8,128)(2,1)S(1)} %collective-permute-done.6.refs_3_), channel_id=1, source_target_pairs={{0,1},{1,0},{2,3},{3,2},{4,5},{5,4},{6,7},{7,6},{8,9},{9,8},{10,11... | collective-permute-start | bytes 208904 | tf_op jit(solution)/shard_map/ppermute | solution.py:441
  26.3 1.3 %collective-permute-start.9 = (bf16[272,128]{1,0:T(8,128)(2,1)S(1)}, bf16[272,128]{1,0:T(8,128)(2,1)S(1)}, u32[]{:S(2)}, u32[]{:S(2)}) collective-permute-start(bf16[272,128]{1,0:T(8,128)(2,1)S(1)} %collective-permute-done.5.refs_2_), channel_id=1, source_target_pairs={{0,1},{1,0},{2,3},{3,2},{4,5},{5,4},{6,7},{7,6},{8,9},{9,8},{10,11... | collective-permute-start | bytes 208904 | tf_op jit(solution)/shard_map/ppermute | solution.py:441
  30.8 1.6 %collective-permute-start.12 = (f16[4,280,128]{2,1,0:T(8,128)(2,1)S(1)}, f16[4,280,128]{2,1,0:T(8,128)(2,1)S(1)}, u32[]{:S(2)}, u32[]{:S(2)}) collective-permute-start(f16[4,280,128]{2,1,0:T(8,128)(2,1)S(1)} %convert_element_type.113), channel_id=1, source_target_pairs={{0,1},{1,0},{2,3},{3,2},{4,5},{5,4},{6,7},{7,6},{8,9},{9,8},{10,11... | collective-permute-start | bytes 860168 | tf_op jit(solution)/shard_map/ppermute | solution.py:441
  32.6 5.5 %collective-permute-start.15 = (f16[280,128]{1,0:T(8,128)(2,1)S(1)}, f16[280,128]{1,0:T(8,128)(2,1)S(1)}, u32[]{:S(2)}, u32[]{:S(2)}) collective-permute-start(f16[280,128]{1,0:T(8,128)(2,1)S(1)} %convert_element_type.119), channel_id=1, source_target_pairs={{0,6},{1,7},{2,4},{3,5},{4,2},{5,3},{6,0},{7,1},{8,14},{9,15},{10,... | collective-permute-start | bytes 215048 | tf_op jit(solution)/shard_map/ppermute | solution.py:448
  34.4 5.2 %collective-permute-start.14 = (f16[280,128]{1,0:T(8,128)(2,1)S(1)}, f16[280,128]{1,0:T(8,128)(2,1)S(1)}, u32[]{:S(2)}, u32[]{:S(2)}) collective-permute-start(f16[280,128]{1,0:T(8,128)(2,1)S(1)} %convert_element_type.117), channel_id=1, source_target_pairs={{0,3},{1,2},{2,1},{3,0},{4,7},{5,6},{6,5},{7,4},{8,11},{9,10},{10,... | collective-permute-start | bytes 215048 | tf_op jit(solution)/shard_map/ppermute | solution.py:448
  35.1 4.5 %collective-permute-start.13 = (f16[280,128]{1,0:T(8,128)(2,1)S(1)}, f16[280,128]{1,0:T(8,128)(2,1)S(1)}, u32[]{:S(2)}, u32[]{:S(2)}) collective-permute-start(f16[280,128]{1,0:T(8,128)(2,1)S(1)} %convert_element_type.115), channel_id=1, source_target_pairs={{0,5},{1,4},{2,7},{3,6},{4,1},{5,0},{6,3},{7,2},{8,13},{9,12},{10,... | collective-permute-start | bytes 215048 | tf_op jit(solution)/shard_map/ppermute | solution.py:448
  39.8 6.2 %collective-permute-start.16 = (f16[280,128]{1,0:T(8,128)(2,1)S(1)}, f16[280,128]{1,0:T(8,128)(2,1)S(1)}, u32[]{:S(2)}, u32[]{:S(2)}) collective-permute-start(f16[280,128]{1,0:T(8,128)(2,1)S(1)} %get-tuple-element.39), channel_id=1, source_target_pairs={{0,13},{1,12},{2,15},{3,14},{4,9},{5,8},{6,11},{7,10},{8,5},{9,4},... | collective-permute-start | bytes 215048 | tf_op jit(solution)/shard_map/ppermute | solution.py:448
  46.1 5.3 %collective-permute-start.19 = (f16[272,128]{1,0:T(8,128)(2,1)S(1)}, f16[272,128]{1,0:T(8,128)(2,1)S(1)}, u32[]{:S(2)}, u32[]{:S(2)}) collective-permute-start(f16[272,128]{1,0:T(8,128)(2,1)S(1)} %get-tuple-element.33), channel_id=1, source_target_pairs={{0,6},{1,7},{2,4},{3,5},{4,2},{5,3},{6,0},{7,1},{8,14},{9,15},{10,... | collective-permute-start | bytes 208904 | tf_op jit(solution)/shard_map/ppermute | solution.py:448
  46.2 5.4 %collective-permute-start.18 = (f16[272,128]{1,0:T(8,128)(2,1)S(1)}, f16[272,128]{1,0:T(8,128)(2,1)S(1)}, u32[]{:S(2)}, u32[]{:S(2)}) collective-permute-start(f16[272,128]{1,0:T(8,128)(2,1)S(1)} %get-tuple-element.33), channel_id=1, source_target_pairs={{0,3},{1,2},{2,1},{3,0},{4,7},{5,6},{6,5},{7,4},{8,11},{9,10},{10,... | collective-permute-start | bytes 208904 | tf_op jit(solution)/shard_map/ppermute | solution.py:448
  48.1 4.1 %collective-permute-start.17 = (f16[272,128]{1,0:T(8,128)(2,1)S(1)}, f16[272,128]{1,0:T(8,128)(2,1)S(1)}, u32[]{:S(2)}, u32[]{:S(2)}) collective-permute-start(f16[272,128]{1,0:T(8,128)(2,1)S(1)} %get-tuple-element.33), channel_id=1, source_target_pairs={{0,5},{1,4},{2,7},{3,6},{4,1},{5,0},{6,3},{7,2},{8,13},{9,12},{10,... | collective-permute-start | bytes 208904 | tf_op jit(solution)/shard_map/ppermute | solution.py:448
  49.4 4.3 %collective-permute-start.20 = (f16[272,128]{1,0:T(8,128)(2,1)S(1)}, f16[272,128]{1,0:T(8,128)(2,1)S(1)}, u32[]{:S(2)}, u32[]{:S(2)}) collective-permute-start(f16[272,128]{1,0:T(8,128)(2,1)S(1)} %get-tuple-element.33), channel_id=1, source_target_pairs={{0,1},{1,0},{2,3},{3,2},{4,5},{5,4},{6,7},{7,6},{8,9},{9,8},{10,11... | collective-permute-start | bytes 208904 | tf_op jit(solution)/shard_map/ppermute | solution.py:441
  51.5 2.2 %collective-permute-start.23 = (f16[272,128]{1,0:T(8,128)(2,1)S(1)}, f16[272,128]{1,0:T(8,128)(2,1)S(1)}, u32[]{:S(2)}, u32[]{:S(2)}) collective-permute-start(f16[272,128]{1,0:T(8,128)(2,1)S(1)} %collective-permute-done.19), channel_id=1, source_target_pairs={{0,1},{1,0},{2,3},{3,2},{4,5},{5,4},{6,7},{7,6},{8,9},{9,8},{10,11... | collective-permute-start | bytes 208904 | tf_op jit(solution)/shard_map/ppermute | solution.py:441
  51.6 2.1 %collective-permute-start.22 = (f16[272,128]{1,0:T(8,128)(2,1)S(1)}, f16[272,128]{1,0:T(8,128)(2,1)S(1)}, u32[]{:S(2)}, u32[]{:S(2)}) collective-permute-start(f16[272,128]{1,0:T(8,128)(2,1)S(1)} %collective-permute-done.18), channel_id=1, source_target_pairs={{0,1},{1,0},{2,3},{3,2},{4,5},{5,4},{6,7},{7,6},{8,9},{9,8},{10,11... | collective-permute-start | bytes 208904 | tf_op jit(solution)/shard_map/ppermute | solution.py:441
  52.2 1.6 %collective-permute-start.21 = (f16[272,128]{1,0:T(8,128)(2,1)S(1)}, f16[272,128]{1,0:T(8,128)(2,1)S(1)}, u32[]{:S(2)}, u32[]{:S(2)}) collective-permute-start(f16[272,128]{1,0:T(8,128)(2,1)S(1)} %collective-permute-done.17), channel_id=1, source_target_pairs={{0,1},{1,0},{2,3},{3,2},{4,5},{5,4},{6,7},{7,6},{8,9},{9,8},{10,11... | collective-permute-start | bytes 208904 | tf_op jit(solution)/shard_map/ppermute | solution.py:441
